TPU v7x, 32 devices: a whole 2x2x4 slice. The times are simulated.
32 devices in a mesh: alpha: 8 (over z, core), beta: 4 (over y, x).
Axes of the slice: x: 2, y: 2, z: 4, core: 2. Of those that a mesh axis runs over, the one named last changes fastest.
Arguments:
- start_vector: float32 [256, 98304], P('alpha', 'beta'), may hold values from -6 to 6
- precondition: float32 [256, 98304], P('alpha', 'beta'), may hold values from 1 to 10
- alpha_hamiltonian: float32 [256, 256], replicated, may hold values from -0.375 to 0.375
- alpha_pairs: float32 [2, 256, 256], replicated, may hold values from -0.375 to 0.375
- pair_tables: float32 [4, 128, 128], replicated, may hold values from -0.375 to 0.375
- source_blocks: int32 [768, 2], P('beta'), may hold values from 0 to 767
- pair_index: int32 [768, 2], P('beta'), may hold values from 0 to 3
- phase_signs: int32 [768, 2], P('beta'), may hold values from -1 to 1, as said below
- cross_pairs: int32 [2, 768], P(None, 'beta'), may hold values from 0 to 3
- cross_signs: int32 [2, 768], P(None, 'beta'), may hold values from -1 to 1, as said below
Outputs:
- correction: float32 [256, 98304], P('alpha', 'beta')
- sigma_next: float32 [256, 98304], P('alpha', 'beta')
Inputs may be any that keep to these rules, and one draw needn't show every extreme that they name: `phase_signs`: each entry is -1 or 1. `cross_signs`: each entry is -1 or 1.
All inputs are finite; a program needn't handle non-finite values.
Results may differ from a plain program's by a relative error of at most 0.000076.
Values sent between devices are 32-bit elements; how exact they have to be, the bound alone decides.
No kernel may reach another device: no remote copies, remote signals or barrier semaphores. Data moves between devices by JAX's collectives and lax.ppermute only.
A program may use at most 256 MiB of HBM per device.

v0:
```python
import jax
import jax.numpy as jnp
from jax import lax
from jax.sharding import PartitionSpec as P

SB = 128
NPAIR = 4
Q = 2


highest = lax.Precision.HIGHEST


def pair_images(vector, pair_tables):
    row_count, col_count = vector.shape
    block_count = col_count // SB
    flat = vector.reshape(row_count * block_count, SB)
    side_by_side = jnp.transpose(pair_tables, (1, 0, 2)).reshape(SB, NPAIR * SB)
    images = jnp.dot(flat, side_by_side, precision=highest)
    return images.reshape(row_count, block_count * NPAIR, SB)


def cross_terms(images, pairs, signs):
    block_count = pairs.shape[0]
    chosen = jnp.arange(block_count, dtype=jnp.int32) * NPAIR + pairs
    picked = images[:, chosen] * signs.astype(jnp.float32)[None, :, None]
    return picked.reshape(images.shape[0], block_count * SB)


def local(
    start_vector,
    precondition,
    alpha_hamiltonian,
    alpha_pairs,
    pair_tables,
    source_blocks,
    pair_index,
    phase_signs,
    cross_pairs,
    cross_signs,
):
    signed_tables = pair_tables[pair_index] * phase_signs.astype(jnp.float32)[:, :, None, None]

    def sigma_local(vector):
        row_count, col_count = vector.shape
        piece = lax.all_gather(vector, "beta", axis=1, tiled=True)
        piece_blocks = piece.shape[1] // SB
        blocked = piece.reshape(row_count, piece_blocks, SB)
        inside = ((source_blocks >= 0) & (source_blocks < piece_blocks)).astype(jnp.float32)
        picked = blocked[:, jnp.clip(source_blocks, 0, piece_blocks - 1)] * inside[None, :, :, None]
        beta_term = jnp.einsum("rtkc,tkcd->rtd", picked, signed_tables, precision=highest).reshape(
            row_count, col_count
        )
        own_images = pair_images(vector, pair_tables)
        crossed = [cross_terms(own_images, cross_pairs[n], cross_signs[n]) for n in range(Q)]
        stacked = jnp.stack([vector] + crossed)
        moved = lax.all_to_all(stacked, "alpha", split_axis=2, concat_axis=1, tiled=True)
        columns = moved[0]
        crossed_columns = moved[1:]
        combined = jnp.dot(alpha_hamiltonian, columns, precision=highest)
        combined = combined + jnp.einsum(
            "qij,qjc->ic", alpha_pairs, crossed_columns, precision=highest
        )
        returned = lax.all_to_all(combined, "alpha", split_axis=0, concat_axis=1, tiled=True)
        return beta_term + returned

    first = sigma_local(start_vector)
    intersection, squared = lax.psum(
        (jnp.sum(start_vector * first), jnp.sum(start_vector * start_vector)), ("alpha", "beta")
    )
    theta = intersection / squared
    correction = (first - theta * start_vector) / precondition
    return (correction, sigma_local(correction))


def solution(mesh):
    placed = (
        P("alpha", "beta"),
        P("alpha", "beta"),
        P(),
        P(),
        P(),
        P("beta", None),
        P("beta", None),
        P("beta", None),
        P(None, "beta"),
        P(None, "beta"),
    )
    return jax.shard_map(
        local,
        mesh=mesh,
        in_specs=placed,
        out_specs=(P("alpha", "beta"), P("alpha", "beta")),
        check_vma=False,
    )
```

profile of v0, /device:TPU:0, one launch (start us, length us, event | category | flops | bytes accessed | tf_op | source)
XLA Modules:
  0.0 1309.9 jit_solution(9489412977470924519)
XLA Ops:
  8.3 3.4 reshape.222
  11.7 13.5 %fusion.22 = f32[6144,512]{1,0:T(8,128)} fusion(f32[6144,128]{1,0:T(8,128)} %reshape.222, f32[128,512]{0,1:T(8,128)S(1)} %bitcast.135), kind=kOutput, calls=%fused_computation.54 | convolution fusion | flops 4831838208 | bytes 15990784 | tf_op jit(solution)/shard_map/dot_general | solution.py:19
  25.3 13.4 %reshape.224 = f32[32,768,128]{2,1,0:T(8,128)} reshape(f32[6144,512]{1,0:T(8,128)} %fusion.22) | data formatting | bytes 25165824 | tf_op jit(solution)/shard_map/reshape | solution.py:20
  38.7 16.4 %copy.63 = f32[32,768,128]{2,0,1:T(8,128)} copy(f32[32,768,128]{2,1,0:T(8,128)} %reshape.224) | data formatting | bytes 25165824 | tf_op jit(solution)/shard_map/reshape | solution.py:20
  55.1 7.0 gather_fusion.2
  62.1 5.4 copy.64
  67.5 3.7 gather.32
  71.2 7.0 gather_fusion.3
  78.2 5.4 copy.66
  83.6 3.4 gather.34
  87.2 3.5 broadcast_multiply_fusion.1
  91.0 4.3 pad_maximum_fusion
  95.3 36.0 %copy.67 = f32[3,32,24576]{1,0,2:T(4,128)} copy(f32[3,32,24576]{2,1,0:T(8,128)} %pad_maximum_fusion) | data formatting | bytes 18874368 | tf_op jit(solution)/shard_map/stack | solution.py:56
  131.3 60.4 %reshape.295 = f32[8,1,294912]{2,1,0:T(1,128)} reshape(f32[24576,3,32]{2,1,0:T(4,128)} %bitcast.110) | data formatting | bytes 18874368
  191.7 6.3 all-to-all-start
  198.8 205.7 %all-to-all-done = f32[8,1,294912]{2,1,0:T(1,128)} async-done(((f32[8,1,294912]{2,1,0:T(1,128)}), f32[8,1,294912]{2,1,0:T(1,128)}, u32[]{:S(2)}, u32[]{:S(2)}) %all-to-all-start) | async-done | bytes 9437216 | tf_op jit(solution)/shard_map/all_to_all | solution.py:57
  405.1 28.3 %reduce = f32[8,294912]{1,0:T(8,128)} reduce(f32[8,1,294912]{2,1,0:T(1,128)} %all-to-all-done, f32[]{:T(128)} %broadcast.176), dimensions={1}, to_apply=%all_to_all.50.reduce_sub_computation | reduce | bytes 18874372 | tf_op jit(solution)/shard_map/all_to_all | solution.py:57
  433.3 63.5 %reshape.296 = f32[24576,3,32]{2,1,0:T(4,128)} reshape(f32[8,294912]{1,0:T(8,128)} %reduce) | data formatting | bytes 18874368
  496.8 37.0 %copy.68 = f32[3,32,8,3072]{3,1,2,0:T(8,128)} copy(f32[3,32,8,3072]{1,0,3,2:T(4,128)} %bitcast.111) | data formatting | bytes 18874368 | tf_op jit(solution)/shard_map/all_to_all | solution.py:57
  533.8 3.2 slice.61
  537.0 2.1 slice.60
  539.1 6.2 convolution_bitcast_fusion.1
  545.3 4.8 convolution_add_fusion.1
  550.1 5.0 all-to-all-start.1
  555.5 9.9 gather_fusion
  566.1 10.9 copy_bitcast_fusion.1
  577.0 8.1 gather_fusion.1
  585.1 21.0 %fusion.12 = f32[192,4,8,128]{3,2,1,0:T(8,128)} fusion(f32[192,2,32,128]{3,2,1,0:T(8,128)} %bitcast.125, f32[192,2]{1,0:T(8,128)S(1)} %copy.60, f32[192,2,128,128]{3,2,1,0:T(8,128)} %bitcast.108, f32[192,2]{1,0:T(8,128)S(1)} %copy.57), kind=kOutput, calls=%fused_computation.32 | convolution fusion | flops 2423783424 | bytes 34606080 | tf_op jit(solution)/shard_map/rtkc,tkcd->rtd/dot_general | solution.py:51
  606.1 20.6 %all-to-all-done.1 = f32[8,32,3072]{2,1,0:T(8,128)} async-done(((f32[8,32,3072]{2,1,0:T(8,128)}), f32[8,32,3072]{2,1,0:T(8,128)}, u32[]{:S(2)}, u32[]{:S(2)}) %all-to-all-start.1) | async-done | bytes 3145760 | tf_op jit(solution)/shard_map/all_to_all | solution.py:64
  626.7 2.4 copy.84
  629.5 2.0 copy-done.5
  633.3 38.2 %all-reduce = (f32[]{:T(128)}, f32[]{:T(128)}) all-reduce(f32[]{:T(128)} %get-tuple-element.3, f32[]{:T(128)} %get-tuple-element.2), channel_id=1, replica_groups=mesh['alpha'=8,'beta'=4] {'alpha','beta'}, use_global_device_ids=true, to_apply=%region_1.2 | all-reduce | flops 2 | bytes 16 | tf_op jit(solution)/shard_map/psum | solution.py:68
  672.7 6.9 subtract_divide_fusion
  679.6 3.3 reshape.227
  683.0 13.5 %fusion.23 = f32[6144,512]{1,0:T(8,128)} fusion(f32[6144,128]{1,0:T(8,128)} %reshape.227, f32[128,512]{0,1:T(8,128)S(1)} %bitcast.136), kind=kOutput, calls=%fused_computation.55 | convolution fusion | flops 4831838208 | bytes 15990784 | tf_op jit(solution)/shard_map/dot_general | solution.py:19
  696.5 13.4 %reshape.228 = f32[32,768,128]{2,1,0:T(8,128)} reshape(f32[6144,512]{1,0:T(8,128)} %fusion.23) | data formatting | bytes 25165824 | tf_op jit(solution)/shard_map/reshape | solution.py:20
  709.9 16.4 %copy.72 = f32[32,768,128]{2,0,1:T(8,128)} copy(f32[32,768,128]{2,1,0:T(8,128)} %reshape.228) | data formatting | bytes 25165824 | tf_op jit(solution)/shard_map/reshape | solution.py:20
  726.2 7.1 gather_fusion.5
  733.3 7.1 gather_fusion.6
  740.5 5.3 copy.73
  745.8 3.6 gather.37
  749.4 4.0 broadcast_multiply_fusion.2
  753.4 3.5 copy.75
  756.9 3.4 gather.39
  760.3 2.3 broadcast_multiply_fusion
  764.0 4.3 pad_maximum_fusion.1
  768.4 36.0 %copy.76 = f32[3,32,24576]{1,0,2:T(4,128)} copy(f32[3,32,24576]{2,1,0:T(8,128)} %pad_maximum_fusion.1) | data formatting | bytes 18874368 | tf_op jit(solution)/shard_map/stack | solution.py:56
  804.4 60.5 %reshape.297 = f32[8,1,294912]{2,1,0:T(1,128)} reshape(f32[24576,3,32]{2,1,0:T(4,128)} %bitcast.112) | data formatting | bytes 18874368
  865.0 5.1 all-to-all-start.2
  870.8 205.6 %all-to-all-done.2 = f32[8,1,294912]{2,1,0:T(1,128)} async-done(((f32[8,1,294912]{2,1,0:T(1,128)}), f32[8,1,294912]{2,1,0:T(1,128)}, u32[]{:S(2)}, u32[]{:S(2)}) %all-to-all-start.2) | async-done | bytes 9437216 | tf_op jit(solution)/shard_map/all_to_all | solution.py:57
  1076.4 28.6 %reduce.1 = f32[8,294912]{1,0:T(8,128)} reduce(f32[8,1,294912]{2,1,0:T(1,128)} %all-to-all-done.2, f32[]{:T(128)} %broadcast.176), dimensions={1}, to_apply=%all_to_all.57.reduce_sub_computation | reduce | bytes 18874372 | tf_op jit(solution)/shard_map/all_to_all | solution.py:57
  1105.0 63.3 %reshape.298 = f32[24576,3,32]{2,1,0:T(4,128)} reshape(f32[8,294912]{1,0:T(8,128)} %reduce.1) | data formatting | bytes 18874368
  1168.2 37.0 %copy.77 = f32[3,32,8,3072]{3,1,2,0:T(8,128)} copy(f32[3,32,8,3072]{1,0,3,2:T(4,128)} %bitcast.113) | data formatting | bytes 18874368 | tf_op jit(solution)/shard_map/all_to_all | solution.py:57
  1205.3 3.2 slice.63
  1208.4 2.1 slice.62
  1210.6 6.2 convolution_bitcast_fusion
  1216.8 4.8 convolution_add_fusion
  1221.6 4.7 all-to-all-start.3
  1226.3 10.9 copy_bitcast_fusion
  1237.2 8.2 gather_fusion.4
  1245.4 21.0 %fusion.17 = f32[192,4,8,128]{3,2,1,0:T(8,128)} fusion(f32[192,2,32,128]{3,2,1,0:T(8,128)} %bitcast.124, f32[192,2]{1,0:T(8,128)S(1)} %copy-done.23, f32[192,2,128,128]{3,2,1,0:T(8,128)} %bitcast.109, f32[192,2]{1,0:T(8,128)S(1)} %copy-done.21), kind=kOutput, calls=%fused_computation.33 | convolution fusion | flops 2423783424 | bytes 34606080 | tf_op jit(solution)/shard_map/rtkc,tkcd->rtd/dot_general | solution.py:51
  1266.4 31.4 %all-to-all-done.3 = f32[8,32,3072]{2,1,0:T(8,128)} async-done(((f32[8,32,3072]{2,1,0:T(8,128)}), f32[8,32,3072]{2,1,0:T(8,128)}, u32[]{:S(2)}, u32[]{:S(2)}) %all-to-all-start.3) | async-done | bytes 3145760 | tf_op jit(solution)/shard_map/all_to_all | solution.py:64
  1297.8 2.4 copy.86
  1300.7 2.0 bitcast_add_fusion
  (88 shorter events, 8.8 us)
Async XLA Ops:
  7.2 531.9 %copy-start = (f32[2,256,256]{2,1,0:T(8,128)S(1)}, f32[2,256,256]{2,1,0:T(8,128)}, u32[]{:S(2)}) copy-start(f32[2,256,256]{2,1,0:T(8,128)} %param.13) | copy-start | bytes 1572868
  8.3 3.4 copy-start.12
  38.7 16.4 %copy-start.27 = (s32[2,192]{1,0:T(2,128)S(1)}, s32[2,192]{1,0:T(2,128)}, u32[]{:S(2)}) copy-start(s32[2,192]{1,0:T(2,128)} %param.18) | copy-start | bytes 4612
  55.1 7.0 copy-start.24
  71.2 7.0 copy-start.25
  83.6 3.4 copy-start.28
  87.1 3.7 copy-start.16
  87.2 3.6 copy-start.18
  87.2 3.8 copy-start.2
  191.7 212.8 %all-to-all-start = ((f32[8,1,294912]{2,1,0:T(1,128)}), f32[8,1,294912]{2,1,0:T(1,128)}, u32[]{:S(2)}, u32[]{:S(2)}) async-start(f32[8,1,294912]{2,1,0:T(1,128)} %reshape.295), calls=%async_computation | async-start | bytes 18874368 | tf_op jit(solution)/shard_map/all_to_all | solution.py:57
  198.0 368.0 %all-gather.3.cloned.1.call-start = ((), (), s32[]{:S(2)}) async-start(), calls=%async_computation.4 | async-start | bytes 15728640 | tf_op jit(solution)/shard_map/all_gather | solution.py:46
  539.1 6.2 copy-start.14
  550.1 5.0 copy-start.29
  550.1 5.3 copy-start.1
  550.1 76.5 %all-to-all-start.1 = ((f32[8,32,3072]{2,1,0:T(8,128)}), f32[8,32,3072]{2,1,0:T(8,128)}, u32[]{:S(2)}, u32[]{:S(2)}) async-start(f32[8,32,3072]{2,1,0:T(8,128)} %bitcast.126), calls=%async_computation.1 | async-start | bytes 6291456 | tf_op jit(solution)/shard_map/all_to_all | solution.py:64
  555.5 10.0 copy-start.26
  555.5 10.2 copy-start.30
  565.8 19.2 %copy-start.20 = (f32[192,2]{1,0:T(8,128)}, f32[192,2]{1,0:T(8,128)S(1)}, u32[]{:S(2)}) copy-start(f32[192,2]{1,0:T(8,128)S(1)} %copy.57) | copy-start | bytes 4612
  566.0 19.1 %copy-start.22 = (f32[192,2]{1,0:T(8,128)}, f32[192,2]{1,0:T(8,128)S(1)}, u32[]{:S(2)}) copy-start(f32[192,2]{1,0:T(8,128)S(1)} %copy.60) | copy-start | bytes 4612
  566.0 10.9 copy-start.10
  626.7 2.8 copy-start.3
  626.7 4.8 copy-start.5
  629.0 4.3 copy-start.6
  679.6 3.4 copy-start.13
  745.8 3.6 copy-start.19
  749.4 4.0 copy-start.9
  756.9 3.4 copy-start.17
  760.3 2.8 copy-start.4
  760.3 3.8 copy-start.7
  865.0 211.4 %all-to-all-start.2 = ((f32[8,1,294912]{2,1,0:T(1,128)}), f32[8,1,294912]{2,1,0:T(1,128)}, u32[]{:S(2)}, u32[]{:S(2)}) async-start(f32[8,1,294912]{2,1,0:T(1,128)} %reshape.297), calls=%async_computation.2 | async-start | bytes 18874368 | tf_op jit(solution)/shard_map/all_to_all | solution.py:57
  870.0 356.3 %all-gather.5.cloned.1.call-start = ((), (), s32[]{:S(2)}) async-start(), calls=%async_computation.5 | async-start | bytes 15728640 | tf_op jit(solution)/shard_map/all_gather | solution.py:46
  1210.6 6.2 copy-start.15
  1221.6 76.3 %all-to-all-start.3 = ((f32[8,32,3072]{2,1,0:T(8,128)}), f32[8,32,3072]{2,1,0:T(8,128)}, u32[]{:S(2)}, u32[]{:S(2)}) async-start(f32[8,32,3072]{2,1,0:T(8,128)} %bitcast.127), calls=%async_computation.3 | async-start | bytes 6291456 | tf_op jit(solution)/shard_map/all_to_all | solution.py:64
  1226.3 10.9 copy-start.11
  1237.2 8.2 copy-start.21
  1237.2 8.2 copy-start.23
  1297.8 2.8 copy-start.8
Sparse Core Ops, SparseCore 0:
  200.7 124.0 all-gather.2
  873.3 123.8 all-gather.4
where the time goes:
time: 1320 us; the launch traced here: 1310 us
  local copies, waits for them, and re-layouts  593 us (45%)
  waiting for transfers between devices  465 us (35%)
  matrix products  91.1 us (7%)
  other arithmetic  86 us (7%)
  blocking collectives  38.2 us (3%)
  starting transfers between devices  21.2 us (2%)
  between operations  16.2 us (1%)
    all_to_all x2, waiting for transfers between devices, sigma_local(): lax.all_to_all(stacked, 'alpha', split_axis=2, concat_axis=1, tiled=True)  411 us
    unnamed x67, local copies, waits for them, and re-layouts  254 us
    all_to_all x3, local copies, waits for them, and re-layouts, sigma_local(): lax.all_to_all(stacked, 'alpha', split_axis=2, concat_axis=1, tiled=True)  74.6 us
    another operation x2, local copies, waits for them, and re-layouts, sigma_local(): stacked = jnp.stack([vector] + crossed)  72.1 us
    gather x12, local copies, waits for them, and re-layouts, cross_terms(): picked = images[:, chosen] * signs.astype(jnp.float32)[None, :, None]  61.8 us
    reshape x4, local copies, waits for them, and re-layouts, pair_images(): return images.reshape(row_count, block_count * NPAIR, SB)  59.5 us
    all_to_all x2, other arithmetic, sigma_local(): lax.all_to_all(stacked, 'alpha', split_axis=2, concat_axis=1, tiled=True)  56.8 us
    all_to_all x2, waiting for transfers between devices, sigma_local(): lax.all_to_all(combined, 'alpha', split_axis=0, concat_axis=1, tiled=True)  52 us
  transfers between devices with their start and end apart: 6, of which 4 were waited for; matrix products, arithmetic and copies ran while one was open for 29% of the time, Pallas kernels for 0%

commit v1 on v0

v1 whole, which is shorter than its diff:
```python
import jax
import jax.numpy as jnp
from jax import lax
from jax.experimental import pallas as pl
from jax.experimental.pallas import tpu as pltpu
from jax.sharding import PartitionSpec as P

SB = 128
CHUNKS = 2
VMEM_BYTES = 48 * 1024 * 1024
f32 = jnp.float32
bf16 = jnp.bfloat16


def params():
    return pltpu.CompilerParams(vmem_limit_bytes=VMEM_BYTES)


def divisor(number, most):
    return max(d for d in range(1, most + 1) if number % d == 0)


def halves(x):
    high = x.astype(bf16)
    return high, (x - high.astype(f32)).astype(bf16)


def mul(a, b):
    return jnp.dot(a, b, preferred_element_type=f32)


def cost(flops, count):
    return pl.CostEstimate(flops=flops, bytes_accessed=count, transcendentals=0)


def pack(vector, place, chunk, n, width):
    rows = vector.shape[0]

    def kernel(place_ref, *refs):
        for source, target in zip(refs[: n - 1], refs[n - 1 :]):
            target[...] = source[...]

    def part(k):
        return lambda g, place: (0, chunk * n + lax.rem(place[0] + k, n))

    return pl.pallas_call(
        kernel,
        grid_spec=pltpu.PrefetchScalarGridSpec(
            num_scalar_prefetch=1,
            grid=(1,),
            in_specs=[pl.BlockSpec((rows, width), part(k)) for k in range(1, n)],
            out_specs=[pl.BlockSpec((rows, width), lambda g, place: (0, 0))] * (n - 1),
        ),
        out_shape=[jax.ShapeDtypeStruct((rows, width), f32)] * (n - 1),
        compiler_params=params(),
        cost_estimate=cost(0, 8 * (n - 1) * rows * width),
        name="pack",
    )(place, *[vector] * (n - 1))


def rotate(parts, n, back=False):
    moved = []
    for k, part in enumerate(parts, 1):
        pairs = [(i, ((i // 2 + k) % n) * 2 + i % 2) for i in range(2 * n)]
        moved.append(lax.ppermute(part, "alpha", pairs))
    return moved


def alpha_partial(own, own_chunk, received, couplings, pair_tables, cross_pairs, cross_signs, place, chunk, n, width):
    rows = own.shape[0]
    deep = n * rows
    out_rows, depth = couplings.shape
    npair = pair_tables.shape[0]
    nq = cross_pairs.shape[0]
    blocks = width // SB
    per = divisor(blocks, 4)
    steps = blocks // per
    wide = per * SB

    def kernel(place_ref, pairs_ref, signs_ref, *refs):
        sources = refs[:n]
        a_ref, t_ref, mine_ref, other_ref, a_twice, a_low, t_high, t_low, b = refs[n:]
        g = pl.program_id(0)
        z = place_ref[0]

        @pl.when(g == 0)
        def _():
            high, low = halves(a_ref[...])
            a_twice[:, :depth] = high
            a_twice[:, depth:] = high
            a_low[...] = low
            for p in range(npair):
                high, low = halves(t_ref[p])
                t_high[p] = high
                t_low[p] = low

        for k in range(n):
            high, low = halves(sources[k][...])
            start = pl.multiple_of(lax.rem(z + n - k, n) * rows, rows)
            b[pl.ds(start, rows), :] = high
            b[pl.ds(depth + start, rows), :] = low
        first = (chunk * n + z) * blocks + g * per
        for t in range(per):
            at = slice(t * SB, (t + 1) * SB)
            high = b[:deep, at]
            both = jnp.concatenate([high, b[depth : depth + deep, at]], axis=1)
            for q in range(nq):
                p = pairs_ref[q, first + t]
                table = t_high[p]
                x = mul(both, jnp.concatenate([table, table], axis=0)) + mul(high, t_low[p])
                x = x * signs_ref[q, first + t].astype(f32)
                x_high, x_low = halves(x)
                row = (q + 1) * deep
                b[row : row + deep, at] = x_high
                b[depth + row : depth + row + deep, at] = x_low
        total = mul(a_twice[...], b[...]) + mul(a_low[...], b[:depth, :])
        mine_ref[...] = total[:deep]
        other_ref[...] = total[deep:]

    if own_chunk is None:
        own_spec = pl.BlockSpec((rows, wide), lambda g, place, *_: (0, g))
    else:
        own_spec = pl.BlockSpec((rows, wide), lambda g, place, *_: (0, (own_chunk * n + place[0]) * steps + g))
    part_spec = pl.BlockSpec((rows, wide), lambda g, *_: (0, g))
    return pl.pallas_call(
        kernel,
        grid_spec=pltpu.PrefetchScalarGridSpec(
            num_scalar_prefetch=3,
            grid=(steps,),
            in_specs=[own_spec]
            + [part_spec] * (n - 1)
            + [
                pl.BlockSpec(couplings.shape, lambda g, *_: (0, 0)),
                pl.BlockSpec(pair_tables.shape, lambda g, *_: (0, 0, 0)),
            ],
            out_specs=[pl.BlockSpec((deep, wide), lambda g, *_: (0, g))] * 2,
            scratch_shapes=[
                pltpu.VMEM((out_rows, 2 * depth), bf16),
                pltpu.VMEM((out_rows, depth), bf16),
                pltpu.VMEM(pair_tables.shape, bf16),
                pltpu.VMEM(pair_tables.shape, bf16),
                pltpu.VMEM((2 * depth, wide), bf16),
            ],
        ),
        out_shape=[jax.ShapeDtypeStruct((deep, width), f32)] * 2,
        compiler_params=params(),
        cost_estimate=cost(6 * out_rows * depth * width, 4 * width * rows * n * 3),
        name="alpha_partial",
    )(place, cross_pairs, cross_signs, own, *received, couplings, pair_tables)


def join(mine, other, vectors, place, n, width, with_dot):
    deep = mine.shape[0]
    rows = deep // n
    blocks = width // SB
    steps = divisor(blocks, 4)
    wide = width // steps

    def kernel(place_ref, mine_ref, other_ref, *refs):
        v_refs = refs[: len(vectors)]
        outs = refs[len(vectors) : len(vectors) + n]
        z = place_ref[0]
        dot = jnp.zeros((rows, wide), f32)
        for k in range(n):
            at = pl.ds(pl.multiple_of(lax.rem(z + k, n) * rows, rows), rows)
            total = mine_ref[at, :] + other_ref[at, :]
            outs[k][...] = total
            if with_dot:
                dot = dot + total * v_refs[(n - k) % n][...]
        if with_dot:
            refs[-1][...] = jnp.sum(dot, axis=0, keepdims=True)

    def fixed(place):
        return (0, 0)

    part_spec = pl.BlockSpec((rows, wide), lambda g, place: (0, g))
    v_specs = [part_spec] * len(vectors)
    arrays = list(vectors)
    if with_dot:
        own, own_chunk = vectors[0]
        v_specs[0] = pl.BlockSpec((rows, wide), lambda g, place: (0, (own_chunk * n + place[0]) * steps + g))
        arrays[0] = own
    out = pl.pallas_call(
        kernel,
        grid_spec=pltpu.PrefetchScalarGridSpec(
            num_scalar_prefetch=1,
            grid=(steps,),
            in_specs=[pl.BlockSpec((deep, wide), lambda g, place: (0, g))] * 2 + v_specs,
            out_specs=[part_spec] * n + ([pl.BlockSpec((1, wide), lambda g, place: (0, g))] if with_dot else []),
        ),
        out_shape=[jax.ShapeDtypeStruct((rows, width), f32)] * n
        + ([jax.ShapeDtypeStruct((1, width), f32)] if with_dot else []),
        compiler_params=params(),
        cost_estimate=cost(2 * deep * width, 4 * 4 * deep * width),
        name="join",
    )(place, mine, other, *arrays)
    return out[:n], (jnp.sum(out[n]) if with_dot else None)


def gather_blocks(vector, lists):
    rows = vector.shape[0]
    count, cap = lists.shape

    def kernel(lists_ref, v_ref, *outs):
        for k in range(count):

            @pl.loop(0, cap, unroll=8)
            def _(j):
                at = pl.multiple_of(lists_ref[k, j] * SB, SB)
                outs[k][j] = v_ref[:, pl.ds(at, SB)]

    return pl.pallas_call(
        kernel,
        grid_spec=pltpu.PrefetchScalarGridSpec(
            num_scalar_prefetch=1,
            grid=(1,),
            in_specs=[pl.BlockSpec(vector.shape, lambda g, lists: (0, 0))],
            out_specs=[pl.BlockSpec((cap, rows, SB), lambda g, lists: (0, 0, 0))] * count,
        ),
        out_shape=[jax.ShapeDtypeStruct((cap, rows, SB), f32)] * count,
        compiler_params=params(),
        cost_estimate=cost(0, 4 * vector.size + 4 * count * cap * rows * SB),
        name="gather_blocks",
    )(lists, vector)


def beta_sum(vector, received, slots, own_signs, far_signs, pair_index, pair_tables, with_dot):
    rows, cols = vector.shape
    blocks = cols // SB
    npair = pair_tables.shape[0]
    kb = slots.shape[0]
    cap = received[0].shape[0]
    far = len(received)
    per = divisor(blocks, 16)
    steps = blocks // per

    def kernel(slots_ref, own_ref, far_ref, pair_ref, *refs):
        v_ref, t_ref = refs[:2]
        r_refs = refs[2 : 2 + far]
        outs = refs[2 + far : -5]
        pool, wide, t_high, t_low, sems = refs[-5:]
        g = pl.program_id(0)

        @pl.when(g == 0)
        def _():
            copies = [
                pltpu.make_async_copy(r_refs[i], pool.at[pl.ds(i * cap, cap)], sems.at[i]) for i in range(far)
            ]
            for copy in copies:
                copy.start()
            for p in range(npair):
                high, low = halves(t_ref[p])
                t_high[p * SB : (p + 1) * SB, :] = high
                t_low[p * SB : (p + 1) * SB, :] = low
            for copy in copies:
                copy.wait()

        wide[...] = jnp.zeros_like(wide)
        for t in range(per):
            target = g * per + t
            for k in range(kb):
                slot = slots_ref[k, target]
                own = v_ref[:, pl.ds(pl.multiple_of(lax.min(slot, blocks - 1) * SB, SB), SB)]
                other = pool[lax.max(slot - blocks, 0)]
                block = own * own_ref[k, target].astype(f32) + other * far_ref[k, target].astype(f32)
                at = pl.ds(pl.multiple_of(pair_ref[k, target] * SB, SB), SB)
                wide[t * rows : (t + 1) * rows, at] += block
        high, low = halves(wide[...])
        total = mul(high, t_high[...]) + mul(low, t_high[...]) + mul(high, t_low[...])
        dot = jnp.zeros((rows, SB), f32)
        square = jnp.zeros((rows, SB), f32)
        for t in range(per):
            piece = total[t * rows : (t + 1) * rows]
            outs[0][:, t * SB : (t + 1) * SB] = piece
            if with_dot:
                v = v_ref[:, pl.ds(pl.multiple_of((g * per + t) * SB, SB), SB)]
                dot = dot + piece * v
                square = square + v * v
        if with_dot:

            @pl.when(g == 0)
            def _():
                outs[1][...] = dot
                outs[2][...] = square

            @pl.when(g > 0)
            def _():
                outs[1][...] += dot
                outs[2][...] += square

    out = pl.pallas_call(
        kernel,
        grid_spec=pltpu.PrefetchScalarGridSpec(
            num_scalar_prefetch=4,
            grid=(steps,),
            in_specs=[
                pl.BlockSpec((rows, cols), lambda g, *_: (0, 0)),
                pl.BlockSpec(pair_tables.shape, lambda g, *_: (0, 0, 0)),
            ]
            + [pl.BlockSpec(memory_space=pl.ANY)] * far,
            out_specs=[pl.BlockSpec((rows, per * SB), lambda g, *_: (0, g))]
            + ([pl.BlockSpec((rows, SB), lambda g, *_: (0, 0))] * 2 if with_dot else []),
            scratch_shapes=[
                pltpu.VMEM((far * cap, rows, SB), f32),
                pltpu.VMEM((per * rows, npair * SB), f32),
                pltpu.VMEM((npair * SB, SB), bf16),
                pltpu.VMEM((npair * SB, SB), bf16),
                pltpu.SemaphoreType.DMA((far,)),
            ],
        ),
        out_shape=[jax.ShapeDtypeStruct((rows, cols), f32)]
        + ([jax.ShapeDtypeStruct((rows, SB), f32)] * 2 if with_dot else []),
        compiler_params=params(),
        cost_estimate=cost(6 * rows * cols * npair * SB, 4 * (2 * rows * cols + far * cap * rows * SB)),
        name="beta_sum",
    )(slots, own_signs, far_signs, pair_index, vector, pair_tables, *received)
    if with_dot:
        return out[0], jnp.stack([jnp.sum(out[1]), jnp.sum(out[2])])
    return out[0], None


def finish(returned, beta_term, place, chunk, n, width, previous, extra=None):
    rows, cols = beta_term.shape
    blocks = width // SB
    steps = divisor(blocks, 2)
    wide = width // steps
    full = 1 if extra is None else 3

    def kernel(place_ref, *refs):
        refs = list(refs)
        theta_ref = None
        if extra is not None:
            theta_ref = refs.pop(0)
        fulls = refs[:full]
        parts = refs[full : full + n]
        outs = refs[full + n + (previous is not None) :]
        k = pl.program_id(0)
        for i in range(n):

            @pl.when(k == i)
            def _(i=i):
                value = fulls[0][...] + parts[i][...]
                if extra is not None:
                    value = (value - theta_ref[0] * fulls[1][...]) / fulls[2][...]
                    outs[1 + (n - i) % n][...] = value
                outs[0][...] = value

    def whole(k, g, place):
        return (0, (chunk * n + lax.rem(place[0] + n - k, n)) * steps + g)

    def only(i):
        return lambda k, g, place: (0, jnp.where(k == i, g, jnp.where(k < i, 0, steps - 1)))

    in_specs = [pl.BlockSpec((rows, wide), whole)] * full + [pl.BlockSpec((rows, wide), only(i)) for i in range(n)]
    arrays = [beta_term] + ([] if extra is None else [extra[1], extra[2]]) + list(returned)
    if extra is not None:
        in_specs = [pl.BlockSpec(memory_space=pltpu.SMEM)] + in_specs
        arrays = [extra[0]] + arrays
    aliases = {}
    if previous is not None:
        aliases = {1 + len(arrays): 0}
        in_specs = in_specs + [pl.BlockSpec(memory_space=pl.ANY)]
        arrays = arrays + [previous]
    out_specs = [pl.BlockSpec((rows, wide), whole)]
    out_shape = [jax.ShapeDtypeStruct((rows, cols), f32)]
    if extra is not None:
        out_specs += [pl.BlockSpec((rows, wide), only((n - m) % n)) for m in range(n)]
        out_shape += [jax.ShapeDtypeStruct((rows, width), f32)] * n
    out = pl.pallas_call(
        kernel,
        grid_spec=pltpu.PrefetchScalarGridSpec(
            num_scalar_prefetch=1,
            grid=(n, steps),
            in_specs=in_specs,
            out_specs=out_specs,
        ),
        out_shape=out_shape,
        input_output_aliases=aliases,
        compiler_params=params(),
        cost_estimate=cost(4 * rows * n * width, 4 * (2 * full + 2) * rows * n * width),
        name="finish" if extra is None else "correct",
    )(place, *arrays)
    return out if extra is not None else out[0]


def plan(source_blocks, phase_signs, blocks, parts, cap):
    me = lax.axis_index("beta")
    everyone = lax.all_gather(source_blocks, "beta", axis=0, tiled=True).reshape(parts, -1)
    ids = jnp.arange(parts * blocks, dtype=jnp.int32)
    need = jnp.any(everyone[:, :, None] == ids, axis=1)
    need = need.reshape(parts, parts, blocks)
    order = jnp.arange(blocks, dtype=jnp.int32)
    before = (order[:, None] < order[None, :]).astype(bf16)
    position = jnp.dot(
        need.astype(bf16).reshape(parts * parts, blocks), before, preferred_element_type=f32
    ).astype(jnp.int32).reshape(parts, parts, blocks)
    counts = jnp.sum(need.astype(jnp.int32), axis=2)
    apart = 1 - jnp.eye(parts, dtype=jnp.int32)
    rounds_needed = (jnp.max(counts * apart) + cap - 1) // cap
    partners = me ^ jnp.arange(1, parts, dtype=jnp.int32)
    send_need = need[partners, me]
    send_position = position[partners, me]
    take_position = position[me].reshape(-1)
    sources = source_blocks.T
    own = sources // blocks == me
    far_index = (sources // blocks) ^ me
    found = jnp.sum(jnp.where(sources[:, :, None] == ids, take_position, 0), axis=2)
    signs = phase_signs.T

    def round_plan(r):
        slot = jnp.arange(cap, dtype=jnp.int32)[:, None] + r * cap
        hit = send_need[:, None, :] & (send_position[:, None, :] == slot)
        lists = jnp.sum(jnp.where(hit, order, 0), axis=2)
        here = (found >= r * cap) & (found < (r + 1) * cap)
        slots = jnp.where(own, sources - me * blocks, blocks + (far_index - 1) * cap + jnp.where(here, found - r * cap, 0))
        own_signs = jnp.where(own & (r == 0), signs, 0)
        far_signs = jnp.where(~own & here, signs, 0)
        return lists, slots, own_signs, far_signs

    return rounds_needed, round_plan


def make_local(n_alpha, n_beta):
    n = n_alpha // 2

    def local(
        start_vector,
        precondition,
        alpha_hamiltonian,
        alpha_pairs,
        pair_tables,
        source_blocks,
        pair_index,
        phase_signs,
        cross_pairs,
        cross_signs,
    ):
        rows, cols = start_vector.shape
        blocks = cols // SB
        chunks = divisor(blocks // n, CHUNKS)
        width = cols // (n * chunks)
        cap = (blocks + 1) // 2
        device = lax.axis_index("alpha")
        core = lax.rem(device, 2)
        place = (device // 2).astype(jnp.int32).reshape(1)
        nq = alpha_pairs.shape[0]

        stacked = jnp.concatenate([alpha_hamiltonian[None], alpha_pairs]).reshape(nq + 1, n, 2, rows, n, 2, rows)
        flipped = stacked[:, :, ::-1, :, :, ::-1]
        chosen = jnp.where(core == 0, stacked, flipped)[:, :, :, :, :, 0]
        couplings = jnp.transpose(chosen, (2, 1, 3, 0, 4, 5)).reshape(2 * n * rows, (nq + 1) * n * rows)
        pairs_by_k = pair_index.T

        def exchange(parts):
            return [
                lax.ppermute(part, "beta", [(i, i ^ k) for i in range(n_beta)]) for k, part in enumerate(parts, 1)
            ]

        rounds_needed, round_plan = plan(source_blocks, phase_signs, blocks, n_beta, cap)
        first_plan = round_plan(0)

        def beta_round(vector, planned, with_dot):
            lists, slots, own_signs, far_signs = planned
            received = exchange(gather_blocks(vector, lists))
            return beta_sum(vector, received, slots, own_signs, far_signs, pairs_by_k, pair_tables, with_dot)

        def beta_side(vector, with_dot):
            done = beta_round(vector, first_plan, with_dot)

            def more(done):
                added = beta_round(vector, round_plan(1), with_dot)
                total = done[0] + added[0]
                if with_dot:
                    return total, jnp.stack([done[1][0] + added[1][0], done[1][1]])
                return total, None

            return lax.cond(rounds_needed > 1, more, lambda done: done, done)

        def alpha_side(own, own_chunk, sent, chunk, with_dot):
            received = rotate(sent, n)
            mine, other = alpha_partial(
                own, own_chunk, received, couplings, pair_tables, cross_pairs, cross_signs, place, chunk, n, width
            )
            other = lax.ppermute(other, "alpha", [(i, i ^ 1) for i in range(n_alpha)])
            vectors = [(own, own_chunk)] + received if with_dot else []
            joined, dot = join(mine, other, vectors, place, n, width, with_dot)
            return [joined[0]] + rotate(joined[1:], n), dot

        returned = []
        dots = []
        for c in range(chunks):
            sent = pack(start_vector, place, c, n, width)
            back, dot = alpha_side(start_vector, c, sent, c, True)
            returned.append(back)
            dots.append(dot)
        beta_term, sums = beta_side(start_vector, True)
        mine = jnp.stack([jnp.full((8, SB), sum(dots) + sums[0]), jnp.full((8, SB), sums[1])])
        both = jnp.sum(lax.all_gather(mine, ("alpha", "beta"))[:, :, 0, 0], axis=0)
        theta = (both[0] / both[1]).reshape(1)

        correction = None
        sent = []
        for c in range(chunks):
            out = finish(
                returned[c], beta_term, place, c, n, width, correction, (theta, start_vector, precondition)
            )
            correction = out[0]
            sent.append(out[1:])
        returned = [alpha_side(sent[c][0], None, sent[c][1:], c, False)[0] for c in range(chunks)]
        beta_term, _ = beta_side(correction, False)
        sigma_next = None
        for c in range(chunks):
            sigma_next = finish(returned[c], beta_term, place, c, n, width, sigma_next)
        return correction, sigma_next

    return local


def solution(mesh):
    placed = (
        P("alpha", "beta"),
        P("alpha", "beta"),
        P(),
        P(),
        P(),
        P("beta", None),
        P("beta", None),
        P("beta", None),
        P(None, "beta"),
        P(None, "beta"),
    )
    return jax.shard_map(
        make_local(mesh.shape["alpha"], mesh.shape["beta"]),
        mesh=mesh,
        in_specs=placed,
        out_specs=(P("alpha", "beta"), P("alpha", "beta")),
        check_vma=False,
    )
```

time: 1320 us -> 481 us (0.36)
  local copies, waits for them, and re-layouts: 593 us -> 45.4 us
  waiting for transfers between devices: 465 us -> 160 us
  Pallas kernels: 0 us -> 106 us
  matrix products: 91.1 us -> 0.75 us
  other arithmetic: 86 us -> 13.7 us
  starting transfers between devices: 21.2 us -> 73.4 us
  blocking collectives: 38.2 us -> 68.1 us
    all_to_all x4 -> x0, waiting for transfers between devices: 463 us -> none  [the longest x2 411 us: sigma_local(): lax.all_to_all(stacked, 'alpha', split_axis=2, concat_axis=1, tiled=True)]
    unnamed x67 -> x127, local copies, waits for them, and re-layouts: 254 us -> 19.5 us
    ppermute x0 -> x34, waiting for transfers between devices: none -> 160 us  [the longest x6 84.8 us: exchange(): lax.ppermute(part, 'beta', [(i, i ^ k) for i in range(n_beta)])]
    pallas_call x0 -> x18, Pallas kernels: none -> 106 us  [the longest x4 31.3 us: alpha_partial(): pl.pallas_call(kernel, grid_spec=pltpu.PrefetchScalarGridSpec(num_scalar_...]
    dot_general x8 -> x1, matrix products: 91.1 us -> 0.75 us  [plan(): jnp.dot(need.astype(bf16).reshape(parts * parts, blocks), before, preferr...]
    gather x15 -> x2, local copies, waits for them, and re-layouts: 88.1 us -> 3.24 us  [the longest x1 1.95 us: plan(): send_need = need[partners, me]]
    reshape x8 -> x4, local copies, waits for them, and re-layouts: 88.1 us -> 3.65 us  [the longest x1 2.16 us: local(): jnp.transpose(chosen, (2, 1, 3, 0, 4, 5))]
    all_to_all x5 -> x0, local copies, waits for them, and re-layouts: 79.3 us -> none  [the longest x3 74.6 us: sigma_local(): lax.all_to_all(stacked, 'alpha', split_axis=2, concat_axis=1, tiled=True)]
  transfers between devices with their start and end apart: 6 -> 34, of which waited for: 4 -> 11; matrix products, arithmetic and copies ran while one was open for 29% -> 9% of each run, Pallas kernels for 0% -> 21%
where the time goes in v1:
time: 481 us; the launch traced here: 473 us
  waiting for transfers between devices  160 us (33%)
  Pallas kernels  106 us (22%)
  starting transfers between devices  73.4 us (15%)
  blocking collectives  68.1 us (14%)
  local copies, waits for them, and re-layouts  45.4 us (9%)
  other arithmetic  13.7 us (3%)
  between operations  5.15 us (1%)
    ppermute x6, waiting for transfers between devices, exchange(): lax.ppermute(part, 'beta', [(i, i ^ k) for i in range(n_beta)])  84.8 us
    ppermute x24, waiting for transfers between devices, rotate(): moved.append(lax.ppermute(part, 'alpha', pairs))  75.4 us
    ppermute x24, starting transfers between devices, rotate(): moved.append(lax.ppermute(part, 'alpha', pairs))  63.2 us
    unnamed x1, blocking collectives  60.1 us
    pallas_call x4, Pallas kernels, alpha_partial(): pl.pallas_call(kernel, grid_spec=pltpu.PrefetchScalarGridSpec(num_scalar_...  31.3 us
    pallas_call x2, Pallas kernels, beta_sum(): pl.pallas_call(kernel, grid_spec=pltpu.PrefetchScalarGridSpec(num_scalar_...  29.3 us
    pallas_call x4, Pallas kernels, finish(): pl.pallas_call(kernel, grid_spec=pltpu.PrefetchScalarGridSpec(num_scalar_...  22.6 us
    unnamed x127, local copies, waits for them, and re-layouts  19.5 us
  transfers between devices with their start and end apart: 34, of which 11 were waited for; matrix products, arithmetic and copies ran while one was open for 9% of the time, Pallas kernels for 21%

profile of v1, /device:TPU:0, one launch (start us, length us, event | category | flops | bytes accessed | tf_op | source)
XLA Modules:
  0.0 472.7 jit_solution(6700258836475070651)
XLA Ops:
  0.7 1.5 pack.3
  2.1 3.1 collective-permute-start.10
  5.2 2.6 collective-permute-start.11
  8.9 1.8 collective-permute-start.7
  10.7 1.9 collective-permute-start.8
  12.7 8.1 %all-gather.1 = s32[4,192,2]{1,2,0:T(2,128)S(1)} all-gather(s32[1,192,2]{1,2,0:T(2,128)S(1)} %bitcast.26), channel_id=1, replica_groups=mesh['alpha'=8,'beta'=4] {'beta'}, dimensions={0}, use_global_device_ids=true | all-gather | bytes 7680 | tf_op jit(solution)/shard_map/all_gather | solution.py:388
  26.3 1.9 gather_fusion
  29.5 2.8 concatenate.12
  32.3 2.5 copy_dynamic-update-slice_fusion.1
  34.7 3.9 concatenate.13
  38.7 3.4 copy_dynamic-update-slice_fusion
  42.1 4.2 rev.3
  46.5 5.9 %gather_blocks.6 = (f32[96,32,128]{2,1,0:T(8,128)}, f32[96,32,128]{2,1,0:T(8,128)}, f32[96,32,128]{2,1,0:T(8,128)}) custom-call(s32[3,96]{1,0:T(4,128)S(1)} %select_reduce_fusion.3.lists_ref, f32[32,24576]{1,0:T(8,128)} %refs_2_.7), custom_call_target="tpu_custom_call" | custom-call | bytes 7864320 | tf_op jit(solution)/shard_map/gather_blocks/pallas_call | solution.py:212
  53.2 1.5 collective-permute-start.14
  54.7 4.0 collective-permute-done.7.refs_2_
  58.7 1.5 collective-permute-start.15
  60.2 1.4 collective-permute-start.16
  61.6 3.0 fusion.1
  64.6 2.2 reshape.68.refs_4_
  66.8 8.6 %alpha_partial.4 = (f32[128,3072]{1,0:T(8,128)S(1)}, f32[128,3072]{1,0:T(8,128)}) custom-call(s32[1]{0:T(128)} %bitcast.1.place_ref, s32[2,192]{1,0:T(2,128)S(1)} %copy-done.35, s32[2,192]{1,0:T(2,128)S(1)} %copy-done.37, f32[32,24576]{1,0:T(8,128)} %refs_2_.7, f32[32,3072]{1,0:T(8,128)S(1)} %collective-permute-done.6.refs_1_, ...), custom_call_target="tpu_custom_call" | custom-call | flops 1811939328 | bytes 4718592 | tf_op jit(solution)/shard_map/alpha_partial/pallas_call | solution.py:125
  75.6 7.3 %alpha_partial.5 = (f32[128,3072]{1,0:T(8,128)S(1)}, f32[128,3072]{1,0:T(8,128)}) custom-call(s32[1]{0:T(128)} %bitcast.1.place_ref, s32[2,192]{1,0:T(2,128)S(1)} %copy-done.35, s32[2,192]{1,0:T(2,128)S(1)} %copy-done.37, f32[32,24576]{1,0:T(8,128)S(1)} %copy-done.40, f32[32,3072]{1,0:T(8,128)S(1)} %collective-permute-done.10.refs_1_, ...), custom_call_target="tpu_custom_call" | custom-call | flops 1811939328 | bytes 4718592 | tf_op jit(solution)/shard_map/alpha_partial/pallas_call | solution.py:125
  88.0 2.9 collective-permute-done.14.refs_2_
  90.8 38.1 %collective-permute-done.15.refs_3_ = f32[96,32,128]{2,1,0:T(8,128)} collective-permute-done((f32[96,32,128]{2,1,0:T(8,128)}, f32[96,32,128]{2,1,0:T(8,128)}, u32[]{:S(2)}, u32[]{:S(2)}) %collective-permute-start.15) | collective-permute-done | bytes 1572896 | tf_op jit(solution)/shard_map/ppermute | solution.py:456
  128.9 16.4 %beta_sum.6 = (f32[32,24576]{1,0:T(8,128)}, f32[32,128]{1,0:T(8,128)S(1)}, f32[32,128]{1,0:T(8,128)S(1)}) custom-call(s32[2,192]{1,0:T(2,128)S(1)} %get-tuple-element.211.slots_ref, s32[2,192]{1,0:T(2,128)S(1)} %get-tuple-element.217.own_ref, s32[2,192]{1,0:T(2,128)S(1)} %get-tuple-element.208.far_ref, s32[2,192]{1,0:T(2,128)} %bitcast.31, ...), custom_call_target="tpu_custom_call" | custom-call | flops 2415919104 | bytes 11010048 | tf_op jit(solution)/shard_map/beta_sum/pallas_call | solution.py:291
  146.5 1.4 reduce_sum.105
  147.9 1.3 reduce_sum.104
  149.2 1.4 copy-done.3
  152.6 3.5 join.4
  158.5 14.7 %collective-permute-start.20 = (f32[32,3072]{1,0:T(8,128)}, f32[32,3072]{1,0:T(8,128)}, u32[]{:S(2)}, u32[]{:S(2)}) collective-permute-start(f32[32,3072]{1,0:T(8,128)} %get-tuple-element.180), channel_id=1, source_target_pairs={{0,8},{4,12},{8,16},{12,20},{16,24},{20,28},{24,0},{28,4},{1,9},{5... | collective-permute-start | bytes 1179656 | tf_op jit(solution)/shard_map/ppermute | solution.py:65
  173.1 1.3 pad_maximum_fusion.1
  174.6 3.3 collective-permute-start.21
  181.0 3.3 join.5
  186.4 2.0 collective-permute-start.17
  188.4 1.3 fusion.8
  189.7 1.4 reduce_sum.100
  194.4 60.1 %all-reduce.2 = f32[64]{0:T(128)S(1)} all-reduce(f32[64]{0:T(128)S(1)} %pad_dynamic-update-slice_fusion), channel_id=3, replica_groups=mesh['alpha'=8,'beta'=4] {'alpha','beta'}, use_global_device_ids=true, to_apply=%add.2 | all-reduce | flops 64 | bytes 512
  254.6 2.4 collective-permute-start.19
  259.9 6.0 %correct.2 = (f32[32,24576]{1,0:T(8,128)S(1)}, f32[32,3072]{1,0:T(8,128)S(1)}, f32[32,3072]{1,0:T(8,128)S(1)}, f32[32,3072]{1,0:T(8,128)S(1)}, f32[32,3072]{1,0:T(8,128)S(1)}) custom-call(s32[1]{0:T(128)} %bitcast.1.place_ref, f32[1]{0:T(128)S(6)} %div.28.refs_0_, f32[32,24576]{1,0:T(8,128)} %get-tuple-element.174.refs_1_, f32[32,24576]{1,0:T(8,128)} %refs_2_.7, ...), custom_call_target="tpu_custom_call" | custom-call | flops 1572864 | bytes 12582912 | tf_op jit(solution)/shard_map/correct/pallas_call | solution.py:369
  266.5 3.2 collective-permute-start.35
  269.8 5.4 %correct.3 = (f32[32,24576]{1,0:T(8,128)S(1)}, f32[32,3072]{1,0:T(8,128)S(1)}, f32[32,3072]{1,0:T(8,128)S(1)}, f32[32,3072]{1,0:T(8,128)S(1)}, f32[32,3072]{1,0:T(8,128)S(1)}) custom-call(s32[1]{0:T(128)} %bitcast.1.place_ref, f32[1]{0:T(128)S(6)} %div.28.refs_0_, f32[32,24576]{1,0:T(8,128)} %get-tuple-element.174.refs_1_, ...), custom_call_target="tpu_custom_call", output_to_operand_aliasing={{0}: (9, {})} | custom-call | flops 1572864 | bytes 12582912 | tf_op jit(solution)/shard_map/correct/pallas_call | solution.py:369
  276.6 1.4 collective-permute-start.27
  278.1 1.8 collective-permute-done.33.refs_1_
  281.0 28.3 %collective-permute-done.34.refs_2_ = f32[32,3072]{1,0:T(8,128)S(1)} collective-permute-done((f32[32,3072]{1,0:T(8,128)S(1)}, f32[32,3072]{1,0:T(8,128)S(1)}, u32[]{:S(2)}, u32[]{:S(2)}) %collective-permute-start.34) | collective-permute-done | bytes 393248 | tf_op jit(solution)/shard_map/ppermute | solution.py:65
  309.4 7.2 %alpha_partial.7 = (f32[128,3072]{1,0:T(8,128)S(1)}, f32[128,3072]{1,0:T(8,128)}) custom-call(s32[1]{0:T(128)} %bitcast.1.place_ref, s32[2,192]{1,0:T(2,128)S(1)} %copy-done.36, s32[2,192]{1,0:T(2,128)S(1)} %copy-done.38, f32[32,3072]{1,0:T(8,128)S(1)} %get-tuple-element.198.refs_0_, f32[32,3072]{1,0:T(8,128)S(1)} %collective-permute-done.33.refs_1_, ...), custom_call_target="tpu_custom_call" | custom-call | flops 1811939328 | bytes 4718592 | tf_op jit(solution)/shard_map/alpha_partial/pallas_call | solution.py:125
  316.6 3.2 gather_blocks.7
  320.3 2.4 collective-permute-start.24
  322.8 5.6 %collective-permute-done.27.refs_2_ = f32[32,3072]{1,0:T(8,128)S(1)} collective-permute-done((f32[32,3072]{1,0:T(8,128)S(1)}, f32[32,3072]{1,0:T(8,128)S(1)}, u32[]{:S(2)}, u32[]{:S(2)}) %collective-permute-start.27) | collective-permute-done | bytes 393248 | tf_op jit(solution)/shard_map/ppermute | solution.py:65
  328.3 2.3 collective-permute-start.25
  330.6 8.2 %alpha_partial.6 = (f32[128,3072]{1,0:T(8,128)S(1)}, f32[128,3072]{1,0:T(8,128)}) custom-call(s32[1]{0:T(128)} %bitcast.1.place_ref, s32[2,192]{1,0:T(2,128)S(1)} %copy-done.36, s32[2,192]{1,0:T(2,128)S(1)} %copy-done.38, f32[32,3072]{1,0:T(8,128)S(1)} %copy-done.34, f32[32,3072]{1,0:T(8,128)S(1)} %collective-permute-done.26.refs_1_, ...), custom_call_target="tpu_custom_call" | custom-call | flops 1811939328 | bytes 4718592 | tf_op jit(solution)/shard_map/alpha_partial/pallas_call | solution.py:125
  340.0 1.7 join.7
  341.8 5.8 %collective-permute-start.37 = (f32[32,3072]{1,0:T(8,128)}, f32[32,3072]{1,0:T(8,128)}, u32[]{:S(2)}, u32[]{:S(2)}) collective-permute-start(f32[32,3072]{1,0:T(8,128)} %get-tuple-element.205), channel_id=1, source_target_pairs={{0,8},{4,12},{8,16},{12,20},{16,24},{20,28},{24,0},{28,4},{1,9},{5... | collective-permute-start | bytes 1179656 | tf_op jit(solution)/shard_map/ppermute | solution.py:65
  347.5 9.7 %collective-permute-done.23.refs_2_ = f32[96,32,128]{2,1,0:T(8,128)S(1)} collective-permute-done((f32[96,32,128]{2,1,0:T(8,128)}, f32[96,32,128]{2,1,0:T(8,128)S(1)}, u32[]{:S(2)}, u32[]{:S(2)}) %collective-permute-start.23) | collective-permute-done | bytes 1572896 | tf_op jit(solution)/shard_map/ppermute | solution.py:456
  357.3 34.2 %collective-permute-done.24.refs_3_ = f32[96,32,128]{2,1,0:T(8,128)S(1)} collective-permute-done((f32[96,32,128]{2,1,0:T(8,128)}, f32[96,32,128]{2,1,0:T(8,128)S(1)}, u32[]{:S(2)}, u32[]{:S(2)}) %collective-permute-start.24) | collective-permute-done | bytes 1572896 | tf_op jit(solution)/shard_map/ppermute | solution.py:456
  391.5 13.0 %beta_sum.7 = f32[32,24576]{1,0:T(8,128)} custom-call(s32[2,192]{1,0:T(2,128)S(1)} %copy-done.24, s32[2,192]{1,0:T(2,128)S(1)} %copy-done.26, s32[2,192]{1,0:T(2,128)S(1)} %copy-done.22, s32[2,192]{1,0:T(2,128)S(1)} %bitcast.33, f32[32,24576]{1,0:T(8,128)S(1)} %copy-done.43, f32[4,128,128]{2,1,0:T(8,128)} %refs_5_.7, ...), custom_call_target="tpu_custom_call" | custom-call | flops 2415919104 | bytes 11010048 | tf_op jit(solution)/shard_map/beta_sum/pallas_call | solution.py:291
  404.6 10.3 %collective-permute-start.38 = (f32[32,3072]{1,0:T(8,128)}, f32[32,3072]{1,0:T(8,128)S(1)}, u32[]{:S(2)}, u32[]{:S(2)}) collective-permute-start(f32[32,3072]{1,0:T(8,128)} %copy-done.30), channel_id=1, source_target_pairs={{0,16},{4,20},{8,24},{12,28},{16,0},{20,4},{24,8},{28,12},{1,17},{... | collective-permute-start | bytes 1179656 | tf_op jit(solution)/shard_map/ppermute | solution.py:65
  414.9 3.4 collective-permute-start.39
  418.3 1.4 copy-done.1
  419.7 2.4 join.6
  422.7 3.3 collective-permute-start.32
  426.0 7.6 %collective-permute-done.38.refs_3_ = f32[32,3072]{1,0:T(8,128)S(1)} collective-permute-done((f32[32,3072]{1,0:T(8,128)}, f32[32,3072]{1,0:T(8,128)S(1)}, u32[]{:S(2)}, u32[]{:S(2)}) %collective-permute-start.38) | collective-permute-done | bytes 393248 | tf_op jit(solution)/shard_map/ppermute | solution.py:65
  433.6 5.6 %finish.2.refs_5_ = f32[32,24576]{1,0:T(8,128)} custom-call(s32[1]{0:T(128)} %bitcast.1.place_ref, f32[32,24576]{1,0:T(8,128)} %get-tuple-element.227.refs_0_, f32[32,3072]{1,0:T(8,128)S(1)} %get-tuple-element.204.refs_1_, f32[32,3072]{1,0:T(8,128)} %collective-permute-done.37.refs_2_, f32[32,3072]{1,0:T(8,128)S(1)} %collective-permute-done.38.refs_3_, ...), custom_call_target="tpu_custom_call" | custom-call | flops 1572864 | bytes 6291456 | tf_op jit(solution)/shard_map/finish/pallas_call | solution.py:369
  439.2 6.3 %collective-permute-done.30.refs_2_ = f32[32,3072]{1,0:T(8,128)S(1)} collective-permute-done((f32[32,3072]{1,0:T(8,128)S(1)}, f32[32,3072]{1,0:T(8,128)S(1)}, u32[]{:S(2)}, u32[]{:S(2)}) %collective-permute-start.30) | collective-permute-done | bytes 393248 | tf_op jit(solution)/shard_map/ppermute | solution.py:65
  445.5 21.8 %collective-permute-done.31.refs_3_ = f32[32,3072]{1,0:T(8,128)S(1)} collective-permute-done((f32[32,3072]{1,0:T(8,128)S(1)}, f32[32,3072]{1,0:T(8,128)S(1)}, u32[]{:S(2)}, u32[]{:S(2)}) %collective-permute-start.31) | collective-permute-done | bytes 393248 | tf_op jit(solution)/shard_map/ppermute | solution.py:65
  467.3 5.5 %finish.3 = f32[32,24576]{1,0:T(8,128)} custom-call(s32[1]{0:T(128)} %bitcast.1.place_ref, f32[32,24576]{1,0:T(8,128)} %get-tuple-element.227.refs_0_, f32[32,3072]{1,0:T(8,128)S(1)} %get-tuple-element.194.refs_1_, f32[32,3072]{1,0:T(8,128)S(1)} %collective-permute-done.30.refs_2_, ...), custom_call_target="tpu_custom_call", output_to_operand_aliasing={{}: (6, {})} | custom-call | flops 1572864 | bytes 6291456 | tf_op jit(solution)/shard_map/finish/pallas_call | solution.py:369
  (188 shorter events, 32.6 us)
Async XLA Ops:
  2.1 50.3 %collective-permute-start.10 = (f32[32,3072]{1,0:T(8,128)S(1)}, f32[32,3072]{1,0:T(8,128)S(1)}, u32[]{:S(2)}, u32[]{:S(2)}) collective-permute-start(f32[32,3072]{1,0:T(8,128)S(1)} %get-tuple-element.161), channel_id=1, source_target_pairs={{0,8},{4,12},{8,16},{12,20},{16,24},{20,28},{24,0},{28,4},{1,9},{5... | collective-permute-start | bytes 1179656 | tf_op jit(solution)/shard_map/ppermute | solution.py:65
  5.2 70.2 %collective-permute-start.11 = (f32[32,3072]{1,0:T(8,128)S(1)}, f32[32,3072]{1,0:T(8,128)S(1)}, u32[]{:S(2)}, u32[]{:S(2)}) collective-permute-start(f32[32,3072]{1,0:T(8,128)S(1)} %get-tuple-element.162), channel_id=1, source_target_pairs={{0,16},{4,20},{8,24},{12,28},{16,0},{20,4},{24,8},{28,12},{1,17},{... | collective-permute-start | bytes 1179656 | tf_op jit(solution)/shard_map/ppermute | solution.py:65
  8.8 44.4 %collective-permute-start.6 = (f32[32,3072]{1,0:T(8,128)}, f32[32,3072]{1,0:T(8,128)S(1)}, u32[]{:S(2)}, u32[]{:S(2)}) collective-permute-start(f32[32,3072]{1,0:T(8,128)} %get-tuple-element.155), channel_id=1, source_target_pairs={{0,8},{4,12},{8,16},{12,20},{16,24},{20,28},{24,0},{28,4},{1,9},{5... | collective-permute-start | bytes 1179656 | tf_op jit(solution)/shard_map/ppermute | solution.py:65
  8.9 49.7 %collective-permute-start.7 = (f32[32,3072]{1,0:T(8,128)}, f32[32,3072]{1,0:T(8,128)S(1)}, u32[]{:S(2)}, u32[]{:S(2)}) collective-permute-start(f32[32,3072]{1,0:T(8,128)} %get-tuple-element.156), channel_id=1, source_target_pairs={{0,16},{4,20},{8,24},{12,28},{16,0},{20,4},{24,8},{28,12},{1,17},{... | collective-permute-start | bytes 1179656 | tf_op jit(solution)/shard_map/ppermute | solution.py:65
  10.7 49.4 %collective-permute-start.8 = (f32[32,3072]{1,0:T(8,128)S(1)}, f32[32,3072]{1,0:T(8,128)S(1)}, u32[]{:S(2)}, u32[]{:S(2)}) collective-permute-start(f32[32,3072]{1,0:T(8,128)S(1)} %get-tuple-element.157), channel_id=1, source_target_pairs={{0,24},{4,28},{8,0},{12,4},{16,8},{20,12},{24,16},{28,20},{1,25},{... | collective-permute-start | bytes 1179656 | tf_op jit(solution)/shard_map/ppermute | solution.py:65
  46.5 15.1 %copy-start.45 = (f32[3,4,2,32,4,2,32]{6,4,0,3,1,2,5:T(4,128)S(1)}, f32[3,4,2,32,4,2,32]{6,4,0,3,1,2,5:T(4,128)}, u32[]{:S(2)}) copy-start(f32[3,4,2,32,4,2,32]{6,4,0,3,1,2,5:T(4,128)} %copy_dynamic-update-slice_fusion) | copy-start | bytes 2359300
  52.4 23.1 %copy-start.8 = (f32[32,3072]{1,0:T(8,128)}, f32[32,3072]{1,0:T(8,128)S(1)}, u32[]{:S(2)}) copy-start(f32[32,3072]{1,0:T(8,128)S(1)} %collective-permute-done.10.refs_1_) | copy-start | bytes 1179652
  52.4 23.1 %collective-permute-start.12 = (f32[32,3072]{1,0:T(8,128)S(1)}, f32[32,3072]{1,0:T(8,128)S(1)}, u32[]{:S(2)}, u32[]{:S(2)}) collective-permute-start(f32[32,3072]{1,0:T(8,128)S(1)} %get-tuple-element.163), channel_id=1, source_target_pairs={{0,24},{4,28},{8,0},{12,4},{16,8},{20,12},{24,16},{28,20},{1,25},{... | collective-permute-start | bytes 1179656 | tf_op jit(solution)/shard_map/ppermute | solution.py:65
  53.2 37.7 %collective-permute-start.14 = (f32[96,32,128]{2,1,0:T(8,128)}, f32[96,32,128]{2,1,0:T(8,128)}, u32[]{:S(2)}, u32[]{:S(2)}) collective-permute-start(f32[96,32,128]{2,1,0:T(8,128)} %get-tuple-element.167), channel_id=1, source_target_pairs={{0,1},{1,0},{2,3},{3,2},{4,5},{5,4},{6,7},{7,6},{8,9},{9,8},{10,11... | collective-permute-start | bytes 4718600 | tf_op jit(solution)/shard_map/ppermute | solution.py:456
  58.7 70.2 %collective-permute-start.15 = (f32[96,32,128]{2,1,0:T(8,128)}, f32[96,32,128]{2,1,0:T(8,128)}, u32[]{:S(2)}, u32[]{:S(2)}) collective-permute-start(f32[96,32,128]{2,1,0:T(8,128)} %get-tuple-element.168), channel_id=1, source_target_pairs={{0,2},{1,3},{2,0},{3,1},{4,6},{5,7},{6,4},{7,5},{8,10},{9,11},{10,... | collective-permute-start | bytes 4718600 | tf_op jit(solution)/shard_map/ppermute | solution.py:456
  60.2 68.7 %collective-permute-start.16 = (f32[96,32,128]{2,1,0:T(8,128)}, f32[96,32,128]{2,1,0:T(8,128)}, u32[]{:S(2)}, u32[]{:S(2)}) collective-permute-start(f32[96,32,128]{2,1,0:T(8,128)} %get-tuple-element.169), channel_id=1, source_target_pairs={{0,3},{1,2},{2,1},{3,0},{4,7},{5,6},{6,5},{7,4},{8,11},{9,10},{10,... | collective-permute-start | bytes 4718600 | tf_op jit(solution)/shard_map/ppermute | solution.py:456
  66.8 8.7 %copy-start.6 = (f32[256,384]{1,0:T(8,128)}, f32[256,384]{1,0:T(8,128)S(1)}, u32[]{:S(2)}) copy-start(f32[256,384]{1,0:T(8,128)S(1)} %reshape.68.refs_4_) | copy-start | bytes 1179652
  66.8 8.7 %copy-start.40 = (f32[32,24576]{1,0:T(8,128)S(1)}, f32[32,24576]{1,0:T(8,128)}, u32[]{:S(2)}) copy-start(f32[32,24576]{1,0:T(8,128)} %refs_2_.7) | copy-start | bytes 9437188
  66.8 8.7 %copy-start.46 = (f32[4,128,128]{2,1,0:T(8,128)S(1)}, f32[4,128,128]{2,1,0:T(8,128)}, u32[]{:S(2)}) copy-start(f32[4,128,128]{2,1,0:T(8,128)} %refs_5_.7) | copy-start | bytes 786436
  75.4 10.3 %copy-start.51 = (s32[192,2]{0,1:T(2,128)S(1)}, s32[192,2]{0,1:T(2,128)}, u32[]{:S(2)}) copy-start(s32[192,2]{0,1:T(2,128)} %param.19) | copy-start | bytes 4612
  75.4 73.8 %collective-permute-start.9 = (f32[128,3072]{1,0:T(8,128)}, f32[128,3072]{1,0:T(8,128)}, u32[]{:S(2)}, u32[]{:S(2)}) collective-permute-start(f32[128,3072]{1,0:T(8,128)} %get-tuple-element.159), channel_id=1, source_target_pairs={{0,4},{4,0},{8,12},{12,8},{16,20},{20,16},{24,28},{28,24},{1,5},{5... | collective-permute-start | bytes 4718600 | tf_op jit(solution)/shard_map/ppermute | solution.py:484
  82.9 95.1 %collective-permute-start.13 = (f32[128,3072]{1,0:T(8,128)}, f32[128,3072]{1,0:T(8,128)S(1)}, u32[]{:S(2)}, u32[]{:S(2)}) collective-permute-start(f32[128,3072]{1,0:T(8,128)} %get-tuple-element.165), channel_id=1, source_target_pairs={{0,4},{4,0},{8,12},{12,8},{16,20},{20,16},{24,28},{28,24},{1,5},{5... | collective-permute-start | bytes 4718600 | tf_op jit(solution)/shard_map/ppermute | solution.py:484
  86.0 59.3 %copy-start.57 = (s32[2,192]{1,0:T(2,128)}, s32[2,192]{1,0:T(2,128)S(1)}, u32[]{:S(2)}) copy-start(s32[2,192]{1,0:T(2,128)S(1)} %select_reduce_fusion.2) | copy-start | bytes 4612
  86.7 58.6 %copy-start.21 = (s32[2,192]{1,0:T(2,128)}, s32[2,192]{1,0:T(2,128)S(1)}, u32[]{:S(2)}) copy-start(s32[2,192]{1,0:T(2,128)S(1)} %get-tuple-element.208.far_ref) | copy-start | bytes 4612
  86.7 58.6 %copy-start.64 = (pred[2,192]{1,0:T(4,128)(4,1)}, pred[2,192]{1,0:T(4,128)(4,1)S(1)}, u32[]{:S(2)}) copy-start(pred[2,192]{1,0:T(4,128)(4,1)S(1)} %get-tuple-element.209) | copy-start | bytes 1156
  88.0 57.4 %copy-start.23 = (s32[2,192]{1,0:T(2,128)}, s32[2,192]{1,0:T(2,128)S(1)}, u32[]{:S(2)}) copy-start(s32[2,192]{1,0:T(2,128)S(1)} %get-tuple-element.211.slots_ref) | copy-start | bytes 4612
  88.0 57.4 %copy-start.25 = (s32[2,192]{1,0:T(2,128)}, s32[2,192]{1,0:T(2,128)S(1)}, u32[]{:S(2)}) copy-start(s32[2,192]{1,0:T(2,128)S(1)} %get-tuple-element.217.own_ref) | copy-start | bytes 4612
  158.5 96.1 %collective-permute-start.20 = (f32[32,3072]{1,0:T(8,128)}, f32[32,3072]{1,0:T(8,128)}, u32[]{:S(2)}, u32[]{:S(2)}) collective-permute-start(f32[32,3072]{1,0:T(8,128)} %get-tuple-element.180), channel_id=1, source_target_pairs={{0,8},{4,12},{8,16},{12,20},{16,24},{20,28},{24,0},{28,4},{1,9},{5... | collective-permute-start | bytes 1179656 | tf_op jit(solution)/shard_map/ppermute | solution.py:65
  174.6 84.3 %collective-permute-start.21 = (f32[32,3072]{1,0:T(8,128)}, f32[32,3072]{1,0:T(8,128)}, u32[]{:S(2)}, u32[]{:S(2)}) collective-permute-start(f32[32,3072]{1,0:T(8,128)} %copy-done.28), channel_id=1, source_target_pairs={{0,16},{4,20},{8,24},{12,28},{16,0},{20,4},{24,8},{28,12},{1,17},{... | collective-permute-start | bytes 1179656 | tf_op jit(solution)/shard_map/ppermute | solution.py:65
  178.0 80.9 %collective-permute-start.22 = (f32[32,3072]{1,0:T(8,128)}, f32[32,3072]{1,0:T(8,128)}, u32[]{:S(2)}, u32[]{:S(2)}) collective-permute-start(f32[32,3072]{1,0:T(8,128)} %copy-done.27), channel_id=1, source_target_pairs={{0,24},{4,28},{8,0},{12,4},{16,8},{20,12},{24,16},{28,20},{1,25},{... | collective-permute-start | bytes 1179656 | tf_op jit(solution)/shard_map/ppermute | solution.py:65
  186.4 80.2 %collective-permute-start.17 = (f32[32,3072]{1,0:T(8,128)}, f32[32,3072]{1,0:T(8,128)S(1)}, u32[]{:S(2)}, u32[]{:S(2)}) collective-permute-start(f32[32,3072]{1,0:T(8,128)} %get-tuple-element.176), channel_id=1, source_target_pairs={{0,8},{4,12},{8,16},{12,20},{16,24},{20,28},{24,0},{28,4},{1,9},{5... | collective-permute-start | bytes 1179656 | tf_op jit(solution)/shard_map/ppermute | solution.py:65
  191.1 78.7 %collective-permute-start.18 = (f32[32,3072]{1,0:T(8,128)}, f32[32,3072]{1,0:T(8,128)S(1)}, u32[]{:S(2)}, u32[]{:S(2)}) collective-permute-start(f32[32,3072]{1,0:T(8,128)} %copy-done.32), channel_id=1, source_target_pairs={{0,16},{4,20},{8,24},{12,28},{16,0},{20,4},{24,8},{28,12},{1,17},{... | collective-permute-start | bytes 1179656 | tf_op jit(solution)/shard_map/ppermute | solution.py:65
  254.6 15.2 %collective-permute-start.19 = (f32[32,3072]{1,0:T(8,128)}, f32[32,3072]{1,0:T(8,128)S(1)}, u32[]{:S(2)}, u32[]{:S(2)}) collective-permute-start(f32[32,3072]{1,0:T(8,128)} %copy-done.31), channel_id=1, source_target_pairs={{0,24},{4,28},{8,0},{12,4},{16,8},{20,12},{24,16},{28,20},{1,25},{... | collective-permute-start | bytes 1179656 | tf_op jit(solution)/shard_map/ppermute | solution.py:65
  259.9 9.9 %copy-start.41 = (f32[32,24576]{1,0:T(8,128)S(1)}, f32[32,24576]{1,0:T(8,128)}, u32[]{:S(2)}) copy-start(f32[32,24576]{1,0:T(8,128)} %refs_2_.7) | copy-start | bytes 9437188
  265.9 14.0 %collective-permute-start.33 = (f32[32,3072]{1,0:T(8,128)S(1)}, f32[32,3072]{1,0:T(8,128)S(1)}, u32[]{:S(2)}, u32[]{:S(2)}) collective-permute-start(f32[32,3072]{1,0:T(8,128)S(1)} %get-tuple-element.199), channel_id=1, source_target_pairs={{0,8},{4,12},{8,16},{12,20},{16,24},{20,28},{24,0},{28,4},{1,9},{5... | collective-permute-start | bytes 1179656 | tf_op jit(solution)/shard_map/ppermute | solution.py:65
  266.0 43.4 %collective-permute-start.34 = (f32[32,3072]{1,0:T(8,128)S(1)}, f32[32,3072]{1,0:T(8,128)S(1)}, u32[]{:S(2)}, u32[]{:S(2)}) collective-permute-start(f32[32,3072]{1,0:T(8,128)S(1)} %get-tuple-element.200), channel_id=1, source_target_pairs={{0,16},{4,20},{8,24},{12,28},{16,0},{20,4},{24,8},{28,12},{1,17},{... | collective-permute-start | bytes 1179656 | tf_op jit(solution)/shard_map/ppermute | solution.py:65
  266.5 42.8 %collective-permute-start.35 = (f32[32,3072]{1,0:T(8,128)S(1)}, f32[32,3072]{1,0:T(8,128)S(1)}, u32[]{:S(2)}, u32[]{:S(2)}) collective-permute-start(f32[32,3072]{1,0:T(8,128)S(1)} %get-tuple-element.201), channel_id=1, source_target_pairs={{0,24},{4,28},{8,0},{12,4},{16,8},{20,12},{24,16},{28,20},{1,25},{... | collective-permute-start | bytes 1179656 | tf_op jit(solution)/shard_map/ppermute | solution.py:65
  269.8 39.5 %copy-start.7 = (f32[256,384]{1,0:T(8,128)S(1)}, f32[256,384]{1,0:T(8,128)}, u32[]{:S(2)}) copy-start(f32[256,384]{1,0:T(8,128)} %copy-done.6) | copy-start | bytes 1179652
  269.8 39.5 %copy-start.36 = (s32[2,192]{1,0:T(2,128)S(1)}, s32[2,192]{1,0:T(2,128)}, u32[]{:S(2)}) copy-start(s32[2,192]{1,0:T(2,128)} %pairs_ref.7) | copy-start | bytes 4612
  269.8 39.5 %copy-start.38 = (s32[2,192]{1,0:T(2,128)S(1)}, s32[2,192]{1,0:T(2,128)}, u32[]{:S(2)}) copy-start(s32[2,192]{1,0:T(2,128)} %signs_ref.7) | copy-start | bytes 4612
  269.8 39.5 %copy-start.47 = (f32[4,128,128]{2,1,0:T(8,128)S(1)}, f32[4,128,128]{2,1,0:T(8,128)}, u32[]{:S(2)}) copy-start(f32[4,128,128]{2,1,0:T(8,128)} %refs_5_.7) | copy-start | bytes 786436
  276.1 43.8 %copy-start.42 = (f32[32,24576]{1,0:T(8,128)}, f32[32,24576]{1,0:T(8,128)S(1)}, u32[]{:S(2)}) copy-start(f32[32,24576]{1,0:T(8,128)S(1)} %get-tuple-element.153.v_ref.refs_0_) | copy-start | bytes 9437188
  276.1 44.2 %collective-permute-start.26 = (f32[32,3072]{1,0:T(8,128)S(1)}, f32[32,3072]{1,0:T(8,128)S(1)}, u32[]{:S(2)}, u32[]{:S(2)}) collective-permute-start(f32[32,3072]{1,0:T(8,128)S(1)} %get-tuple-element.189), channel_id=1, source_target_pairs={{0,8},{4,12},{8,16},{12,20},{16,24},{20,28},{24,0},{28,4},{1,9},{5... | collective-permute-start | bytes 1179656 | tf_op jit(solution)/shard_map/ppermute | solution.py:65
  276.6 51.7 %collective-permute-start.27 = (f32[32,3072]{1,0:T(8,128)S(1)}, f32[32,3072]{1,0:T(8,128)S(1)}, u32[]{:S(2)}, u32[]{:S(2)}) collective-permute-start(f32[32,3072]{1,0:T(8,128)S(1)} %get-tuple-element.190), channel_id=1, source_target_pairs={{0,16},{4,20},{8,24},{12,28},{16,0},{20,4},{24,8},{28,12},{1,17},{... | collective-permute-start | bytes 1179656 | tf_op jit(solution)/shard_map/ppermute | solution.py:65
  279.9 50.7 %collective-permute-start.28 = (f32[32,3072]{1,0:T(8,128)S(1)}, f32[32,3072]{1,0:T(8,128)S(1)}, u32[]{:S(2)}, u32[]{:S(2)}) collective-permute-start(f32[32,3072]{1,0:T(8,128)S(1)} %get-tuple-element.191), channel_id=1, source_target_pairs={{0,24},{4,28},{8,0},{12,4},{16,8},{20,12},{24,16},{28,20},{1,25},{... | collective-permute-start | bytes 1179656 | tf_op jit(solution)/shard_map/ppermute | solution.py:65
  316.6 23.4 %collective-permute-start.36 = (f32[128,3072]{1,0:T(8,128)}, f32[128,3072]{1,0:T(8,128)S(1)}, u32[]{:S(2)}, u32[]{:S(2)}) collective-permute-start(f32[128,3072]{1,0:T(8,128)} %get-tuple-element.203), channel_id=1, source_target_pairs={{0,4},{4,0},{8,12},{12,8},{16,20},{20,16},{24,28},{28,24},{1,5},{5... | collective-permute-start | bytes 4718600 | tf_op jit(solution)/shard_map/ppermute | solution.py:484
  316.6 14.0 %copy-start.34 = (f32[32,3072]{1,0:T(8,128)S(1)}, f32[32,3072]{1,0:T(8,128)}, u32[]{:S(2)}) copy-start(f32[32,3072]{1,0:T(8,128)} %copy-done.33) | copy-start | bytes 1179652
  319.9 37.4 %collective-permute-start.23 = (f32[96,32,128]{2,1,0:T(8,128)}, f32[96,32,128]{2,1,0:T(8,128)S(1)}, u32[]{:S(2)}, u32[]{:S(2)}) collective-permute-start(f32[96,32,128]{2,1,0:T(8,128)} %get-tuple-element.185), channel_id=1, source_target_pairs={{0,1},{1,0},{2,3},{3,2},{4,5},{5,4},{6,7},{7,6},{8,9},{9,8},{10,11... | collective-permute-start | bytes 4718600 | tf_op jit(solution)/shard_map/ppermute | solution.py:456
  320.3 71.1 %collective-permute-start.24 = (f32[96,32,128]{2,1,0:T(8,128)}, f32[96,32,128]{2,1,0:T(8,128)S(1)}, u32[]{:S(2)}, u32[]{:S(2)}) collective-permute-start(f32[96,32,128]{2,1,0:T(8,128)} %get-tuple-element.186), channel_id=1, source_target_pairs={{0,2},{1,3},{2,0},{3,1},{4,6},{5,7},{6,4},{7,5},{8,10},{9,11},{10,... | collective-permute-start | bytes 4718600 | tf_op jit(solution)/shard_map/ppermute | solution.py:456
  328.3 63.1 %collective-permute-start.25 = (f32[96,32,128]{2,1,0:T(8,128)S(1)}, f32[96,32,128]{2,1,0:T(8,128)S(1)}, u32[]{:S(2)}, u32[]{:S(2)}) collective-permute-start(f32[96,32,128]{2,1,0:T(8,128)S(1)} %get-tuple-element.187), channel_id=1, source_target_pairs={{0,3},{1,2},{2,1},{3,0},{4,7},{5,6},{6,5},{7,4},{8,11},{9,10},{10,... | collective-permute-start | bytes 4718600 | tf_op jit(solution)/shard_map/ppermute | solution.py:456
  330.6 60.8 %copy-start.68 = (s32[192,2]{0,1:T(2,128)S(1)}, s32[192,2]{0,1:T(2,128)}, u32[]{:S(2)}) copy-start(s32[192,2]{0,1:T(2,128)} %param.20) | copy-start | bytes 4612
  340.0 51.5 %copy-start.43 = (f32[32,24576]{1,0:T(8,128)S(1)}, f32[32,24576]{1,0:T(8,128)}, u32[]{:S(2)}) copy-start(f32[32,24576]{1,0:T(8,128)} %copy-done.42) | copy-start | bytes 9437188
  340.0 78.3 %collective-permute-start.29 = (f32[128,3072]{1,0:T(8,128)}, f32[128,3072]{1,0:T(8,128)}, u32[]{:S(2)}, u32[]{:S(2)}) collective-permute-start(f32[128,3072]{1,0:T(8,128)} %get-tuple-element.193), channel_id=1, source_target_pairs={{0,4},{4,0},{8,12},{12,8},{16,20},{20,16},{24,28},{28,24},{1,5},{5... | collective-permute-start | bytes 4718600 | tf_op jit(solution)/shard_map/ppermute | solution.py:484
  340.0 51.5 %copy-start.22 = (s32[2,192]{1,0:T(2,128)S(1)}, s32[2,192]{1,0:T(2,128)}, u32[]{:S(2)}) copy-start(s32[2,192]{1,0:T(2,128)} %copy-done.21) | copy-start | bytes 4612
  340.0 51.5 %copy-start.24 = (s32[2,192]{1,0:T(2,128)S(1)}, s32[2,192]{1,0:T(2,128)}, u32[]{:S(2)}) copy-start(s32[2,192]{1,0:T(2,128)} %copy-done.23) | copy-start | bytes 4612
  340.0 51.5 %copy-start.26 = (s32[2,192]{1,0:T(2,128)S(1)}, s32[2,192]{1,0:T(2,128)}, u32[]{:S(2)}) copy-start(s32[2,192]{1,0:T(2,128)} %copy-done.25) | copy-start | bytes 4612
  341.7 62.7 %copy-start.29 = (f32[32,3072]{1,0:T(8,128)}, f32[32,3072]{1,0:T(8,128)S(1)}, u32[]{:S(2)}) copy-start(f32[32,3072]{1,0:T(8,128)S(1)} %get-tuple-element.207) | copy-start | bytes 1179652
  341.7 62.7 %copy-start.30 = (f32[32,3072]{1,0:T(8,128)}, f32[32,3072]{1,0:T(8,128)S(1)}, u32[]{:S(2)}) copy-start(f32[32,3072]{1,0:T(8,128)S(1)} %get-tuple-element.206) | copy-start | bytes 1179652
  341.7 62.8 %copy-start.52 = (s32[192,2]{0,1:T(2,128)S(1)}, s32[192,2]{0,1:T(2,128)}, u32[]{:S(2)}) copy-start(s32[192,2]{0,1:T(2,128)} %param.19) | copy-start | bytes 4612
  341.7 62.8 %copy-start.55 = (s32[3,192]{1,0:T(4,128)S(1)}, s32[3,192]{1,0:T(4,128)}, u32[]{:S(2)}) copy-start(s32[3,192]{1,0:T(4,128)} %gather_fusion.1) | copy-start | bytes 6916
  341.7 62.8 %copy-start.58 = (s32[2,192]{1,0:T(2,128)S(1)}, s32[2,192]{1,0:T(2,128)}, u32[]{:S(2)}) copy-start(s32[2,192]{1,0:T(2,128)} %copy-done.57) | copy-start | bytes 4612
  341.8 62.8 %copy-start.60 = (s32[192,2]{0,1:T(2,128)S(1)}, s32[192,2]{0,1:T(2,128)}, u32[]{:S(2)}) copy-start(s32[192,2]{0,1:T(2,128)} %param.21) | copy-start | bytes 4612
  341.8 62.8 %copy-start.67 = (pred[3,192]{1,0:T(4,128)(4,1)S(1)}, pred[3,192]{1,0:T(4,128)(4,1)}, u32[]{:S(2)}) copy-start(pred[3,192]{1,0:T(4,128)(4,1)} %gather_fusion) | copy-start | bytes 1732
  341.8 81.0 %collective-permute-start.37 = (f32[32,3072]{1,0:T(8,128)}, f32[32,3072]{1,0:T(8,128)}, u32[]{:S(2)}, u32[]{:S(2)}) collective-permute-start(f32[32,3072]{1,0:T(8,128)} %get-tuple-element.205), channel_id=1, source_target_pairs={{0,8},{4,12},{8,16},{12,20},{16,24},{20,28},{24,0},{28,4},{1,9},{5... | collective-permute-start | bytes 1179656 | tf_op jit(solution)/shard_map/ppermute | solution.py:65
  404.6 29.0 %collective-permute-start.38 = (f32[32,3072]{1,0:T(8,128)}, f32[32,3072]{1,0:T(8,128)S(1)}, u32[]{:S(2)}, u32[]{:S(2)}) collective-permute-start(f32[32,3072]{1,0:T(8,128)} %copy-done.30), channel_id=1, source_target_pairs={{0,16},{4,20},{8,24},{12,28},{16,0},{20,4},{24,8},{28,12},{1,17},{... | collective-permute-start | bytes 1179656 | tf_op jit(solution)/shard_map/ppermute | solution.py:65
  414.9 18.7 %collective-permute-start.39 = (f32[32,3072]{1,0:T(8,128)}, f32[32,3072]{1,0:T(8,128)S(1)}, u32[]{:S(2)}, u32[]{:S(2)}) collective-permute-start(f32[32,3072]{1,0:T(8,128)} %copy-done.29), channel_id=1, source_target_pairs={{0,24},{4,28},{8,0},{12,4},{16,8},{20,12},{24,16},{28,20},{1,25},{... | collective-permute-start | bytes 1179656 | tf_op jit(solution)/shard_map/ppermute | solution.py:65
  422.1 23.4 %collective-permute-start.30 = (f32[32,3072]{1,0:T(8,128)S(1)}, f32[32,3072]{1,0:T(8,128)S(1)}, u32[]{:S(2)}, u32[]{:S(2)}) collective-permute-start(f32[32,3072]{1,0:T(8,128)S(1)} %get-tuple-element.195), channel_id=1, source_target_pairs={{0,8},{4,12},{8,16},{12,20},{16,24},{20,28},{24,0},{28,4},{1,9},{5... | collective-permute-start | bytes 1179656 | tf_op jit(solution)/shard_map/ppermute | solution.py:65
  422.2 45.1 %collective-permute-start.31 = (f32[32,3072]{1,0:T(8,128)S(1)}, f32[32,3072]{1,0:T(8,128)S(1)}, u32[]{:S(2)}, u32[]{:S(2)}) collective-permute-start(f32[32,3072]{1,0:T(8,128)S(1)} %get-tuple-element.196), channel_id=1, source_target_pairs={{0,16},{4,20},{8,24},{12,28},{16,0},{20,4},{24,8},{28,12},{1,17},{... | collective-permute-start | bytes 1179656 | tf_op jit(solution)/shard_map/ppermute | solution.py:65
  422.7 44.6 %collective-permute-start.32 = (f32[32,3072]{1,0:T(8,128)S(1)}, f32[32,3072]{1,0:T(8,128)S(1)}, u32[]{:S(2)}, u32[]{:S(2)}) collective-permute-start(f32[32,3072]{1,0:T(8,128)S(1)} %get-tuple-element.197), channel_id=1, source_target_pairs={{0,24},{4,28},{8,0},{12,4},{16,8},{20,12},{24,16},{28,20},{1,25},{... | collective-permute-start | bytes 1179656 | tf_op jit(solution)/shard_map/ppermute | solution.py:65
  (32 other events, 100.7 us)

commit v2 on v0

v2 whole, which is shorter than its diff:
```python
import jax
import jax.numpy as jnp
from jax import lax
from jax.experimental import pallas as pl
from jax.experimental.pallas import tpu as pltpu
from jax.sharding import PartitionSpec as P

SB = 128
CHUNKS = 1
VMEM_BYTES = 60 * 1024 * 1024
f32 = jnp.float32
bf16 = jnp.bfloat16


def params():
    return pltpu.CompilerParams(vmem_limit_bytes=VMEM_BYTES)


def divisor(number, most):
    return max(d for d in range(1, most + 1) if number % d == 0)


def halves(x):
    high = x.astype(bf16)
    return high, (x - high.astype(f32)).astype(bf16)


def mul(a, b):
    return jnp.dot(a, b, preferred_element_type=f32)


def cost(flops, count):
    return pl.CostEstimate(flops=1, bytes_accessed=1, transcendentals=0)


def prepare(alpha_hamiltonian, alpha_pairs, pair_tables, after):
    size = alpha_hamiltonian.shape[0]
    nq = alpha_pairs.shape[0]
    depth = (nq + 1) * size
    npair = pair_tables.shape[0]

    def kernel(h_ref, p_ref, t_ref, *refs):
        a_twice, a_low, t_high, t_low = refs[-4:]
        for q in range(nq + 1):
            high, low = halves(h_ref[...] if q == 0 else p_ref[q - 1])
            a_twice[:, q * size : (q + 1) * size] = high
            a_twice[:, depth + q * size : depth + (q + 1) * size] = high
            a_low[:, q * size : (q + 1) * size] = low
        for p in range(npair):
            high, low = halves(t_ref[p])
            t_high[p, :SB, :] = high
            t_high[p, SB:, :] = high
            t_low[p] = low

    shapes = [(size, 2 * depth), (size, depth), (npair, 2 * SB, SB), (npair, SB, SB)]
    return pl.pallas_call(
        kernel,
        in_specs=[pl.BlockSpec(memory_space=pltpu.VMEM)] * 3 + [pl.BlockSpec(memory_space=pl.ANY)] * len(after),
        out_specs=[pl.BlockSpec(memory_space=pltpu.VMEM)] * 4,
        out_shape=[jax.ShapeDtypeStruct(shape, bf16) for shape in shapes],
        compiler_params=params(),
        cost_estimate=cost(0, 0),
        name="prepare",
    )(alpha_hamiltonian, alpha_pairs, pair_tables, *after)


def pack(vector, chunk, parts, width):
    rows = vector.shape[0]

    def kernel(source, target):
        target[0] = source[...]

    return pl.pallas_call(
        kernel,
        grid=(parts,),
        in_specs=[pl.BlockSpec((rows, width), lambda j: (0, chunk * parts + j))],
        out_specs=pl.BlockSpec((1, rows, width), lambda j: (j, 0, 0)),
        out_shape=jax.ShapeDtypeStruct((parts, rows, width), f32),
        compiler_params=params(),
        cost_estimate=cost(0, 0),
        name="pack",
    )(vector)


def alpha_sum(columns, prepared, cross_pairs, cross_signs, device, chunk, parts, with_dot, after):
    size, width = columns.shape
    depth = prepared[1].shape[1]
    nq = cross_pairs.shape[0]
    blocks = width // SB
    per = divisor(blocks, 4)
    steps = blocks // per
    wide = per * SB

    def kernel(device_ref, pairs_ref, signs_ref, v_ref, a_twice, a_low, t_high, t_low, *refs):
        b = refs[-1]
        out_ref = refs[len(after)]
        g = pl.program_id(0)
        high, low = halves(v_ref[...])
        b[:size, :] = high
        b[depth : depth + size, :] = low
        first = (chunk * parts + device_ref[0]) * blocks + g * per
        for t in range(per):
            at = slice(t * SB, (t + 1) * SB)
            high = b[:size, at]
            both = jnp.concatenate([high, b[depth : depth + size, at]], axis=1)
            chosen = [pairs_ref[q, first + t] for q in range(nq)]
            x = mul(both, jnp.concatenate([t_high[p] for p in chosen], axis=1))
            x = x + mul(high, jnp.concatenate([t_low[p] for p in chosen], axis=1))
            for q in range(nq):
                x_high, x_low = halves(x[:, q * SB : (q + 1) * SB] * signs_ref[q, first + t].astype(f32))
                row = (q + 1) * size
                b[row : row + size, at] = x_high
                b[depth + row : depth + row + size, at] = x_low
        total = mul(a_twice[...], b[...]) + mul(a_low[...], b[:depth, :])
        out_ref[...] = total
        if with_dot:
            refs[-2][...] = jnp.sum(total * v_ref[...], axis=0, keepdims=True)

    column_spec = pl.BlockSpec((size, wide), lambda g, *_: (0, g))
    out = pl.pallas_call(
        kernel,
        grid_spec=pltpu.PrefetchScalarGridSpec(
            num_scalar_prefetch=3,
            grid=(steps,),
            in_specs=[column_spec]
            + [pl.BlockSpec(a.shape, lambda g, *_, zeros=(0,) * a.ndim: zeros) for a in prepared]
            + [pl.BlockSpec(memory_space=pl.ANY)] * len(after),
            out_specs=[column_spec] + ([pl.BlockSpec((1, wide), lambda g, *_: (0, g))] if with_dot else []),
            scratch_shapes=[pltpu.VMEM((2 * depth, wide), bf16)],
        ),
        out_shape=[jax.ShapeDtypeStruct((size, width), f32)]
        + ([jax.ShapeDtypeStruct((1, width), f32)] if with_dot else []),
        compiler_params=params(),
        cost_estimate=cost(0, 0),
        name="alpha_sum",
    )(device, cross_pairs, cross_signs, columns, *prepared, *after)
    return out[0], (out[1] if with_dot else None)


def earlier(lanes):
    row = lax.broadcasted_iota(jnp.int32, (lanes, lanes), 0)
    column = lax.broadcasted_iota(jnp.int32, (lanes, lanes), 1)
    return jnp.where(row < column, 1.0, 0.0).astype(bf16)


def mark(source_blocks, me, parts, after):
    blocks, kb = source_blocks.shape
    lanes = -(-blocks // SB) * SB
    tall = -(-parts // 8) * 8

    def kernel(me_ref, source_ref, *refs):
        marks_refs = refs[len(after) : len(after) + parts - 1]
        found_ref, held = refs[-2:]
        lane = lax.broadcasted_iota(jnp.int32, (blocks, lanes), 1)

        def hit(s, k):
            return (source_ref[:, k : k + 1] - s * blocks == lane) & (lane < blocks)

        held[...] = jnp.zeros_like(held)
        worst = jnp.zeros((1, 1), f32)
        for s in range(parts):
            needed = jnp.zeros((1, lanes), f32)
            for k in range(kb):
                needed = jnp.maximum(needed, jnp.max(jnp.where(hit(s, k), 1.0, 0.0), axis=0, keepdims=True))
            held[s : s + 1, :] = needed
            count = jnp.sum(needed, axis=1, keepdims=True)
            worst = jnp.maximum(worst, jnp.where(me_ref[0] == s, 0.0, count))
        place = mul(held[...].astype(bf16), earlier(lanes))
        for k in range(kb):
            found = jnp.zeros((blocks, 1), f32)
            for s in range(parts):
                found = found + jnp.sum(jnp.where(hit(s, k), place[s : s + 1, :], 0.0), axis=1, keepdims=True)
            found_ref[:, k : k + 1] = found.astype(jnp.int32)
        for k, marks_ref in enumerate(marks_refs, 1):
            marks_ref[...] = jnp.zeros_like(marks_ref)
            marks_ref[0:1, :] = held[pl.ds(me_ref[0] ^ k, 1), :]
            marks_ref[1:2, :] = jnp.broadcast_to(worst, (1, lanes))

    return pl.pallas_call(
        kernel,
        in_specs=[pl.BlockSpec(memory_space=pltpu.SMEM), pl.BlockSpec(memory_space=pltpu.VMEM)]
        + [pl.BlockSpec(memory_space=pl.ANY)] * len(after),
        out_specs=[pl.BlockSpec(memory_space=pltpu.VMEM)] * parts,
        out_shape=[jax.ShapeDtypeStruct((8, lanes), f32)] * (parts - 1)
        + [jax.ShapeDtypeStruct((blocks, kb), jnp.int32)],
        scratch_shapes=[pltpu.VMEM((tall, lanes), f32)],
        compiler_params=params(),
        cost_estimate=cost(0, 0),
        name="mark",
    )(me, source_blocks, *after)


def positions(marks, first, cap):
    lanes = marks[0].shape[1]
    count = len(marks)
    tall = -(-count // 8) * 8

    def kernel(*refs):
        out_ref, held = refs[-2:]
        held[...] = jnp.zeros_like(held)
        for k in range(count):
            held[k : k + 1, :] = refs[k][0:1, :]
        needed = held[...]
        slot = mul(needed.astype(bf16), earlier(lanes)).astype(jnp.int32) - first
        out_ref[...] = jnp.where((needed > 0) & (slot >= 0) & (slot < cap), slot, cap)

    return pl.pallas_call(
        kernel,
        in_specs=[pl.BlockSpec(memory_space=pltpu.VMEM)] * count,
        out_specs=pl.BlockSpec(memory_space=pltpu.VMEM),
        out_shape=jax.ShapeDtypeStruct((tall, lanes), jnp.int32),
        scratch_shapes=[pltpu.VMEM((tall, lanes), f32)],
        compiler_params=params(),
        cost_estimate=cost(0, 0),
        name="positions",
    )(*marks)


def gather_blocks(vector, slots, count, cap, after):
    rows, cols = vector.shape

    def kernel(slots_ref, v_ref, *refs):
        outs = refs[len(after) :]

        @pl.loop(0, cols // SB, unroll=4)
        def _(b):
            block = v_ref[:, pl.ds(pl.multiple_of(b * SB, SB), SB)]
            for k in range(count):
                outs[k][slots_ref[k, b]] = block

    shape = (cap + 1, rows, SB)
    return pl.pallas_call(
        kernel,
        grid_spec=pltpu.PrefetchScalarGridSpec(
            num_scalar_prefetch=1,
            grid=(1,),
            in_specs=[pl.BlockSpec(vector.shape, lambda g, *_: (0, 0))]
            + [pl.BlockSpec(memory_space=pl.ANY)] * len(after),
            out_specs=[pl.BlockSpec(shape, lambda g, *_: (0, 0, 0))] * count,
        ),
        out_shape=[jax.ShapeDtypeStruct(shape, f32)] * count,
        compiler_params=params(),
        cost_estimate=cost(0, 0),
        name="gather_blocks",
    )(slots, vector, *after)


def beta_sum(vector, received, slots, signs, pair_index, pair_tables, after, dots=None, with_dot=False):
    rows, cols = vector.shape
    blocks = cols // SB
    npair = pair_tables.shape[0]
    kb = slots.shape[0]
    far = len(received)
    each = received[0].shape[0]
    dots = [] if dots is None else dots
    per = divisor(blocks, 16)
    steps = blocks // per

    def kernel(slots_ref, sign_ref, pair_ref, *refs):
        v_ref, t_ref = refs[:2]
        r_refs = refs[2 : 2 + far]
        at = 2 + far + len(after)
        dot_refs = refs[at : at + len(dots)]
        out_ref = refs[at + len(dots)]
        pool, wide, t_high, t_low, sems = refs[-5:]
        g = pl.program_id(0)

        @pl.when(g == 0)
        def _():
            copies = [
                pltpu.make_async_copy(r_refs[i], pool.at[pl.ds(i * each, each)], sems.at[i]) for i in range(far)
            ]
            for copy in copies:
                copy.start()
            for p in range(npair):
                high, low = halves(t_ref[p])
                t_high[p * SB : (p + 1) * SB, :] = high
                t_low[p * SB : (p + 1) * SB, :] = low
            for copy in copies:
                copy.wait()

        wide[...] = jnp.zeros_like(wide)
        for t in range(per):
            target = g * per + t
            for k in range(kb):
                slot = slots_ref[k, target]
                own = v_ref[:, pl.ds(pl.multiple_of(lax.min(slot, blocks - 1) * SB, SB), SB)]
                other = pool[lax.max(slot - blocks, 0)]
                block = jnp.where(slot < blocks, own, other) * sign_ref[k, target].astype(f32)
                at = pl.ds(pl.multiple_of(pair_ref[k, target] * SB, SB), SB)
                wide[t * rows : (t + 1) * rows, at] += block
        high, low = halves(wide[...])
        total = mul(high, t_high[...]) + mul(low, t_high[...]) + mul(high, t_low[...])
        for t in range(per):
            out_ref[:, t * SB : (t + 1) * SB] = total[t * rows : (t + 1) * rows]
        if with_dot:
            sums_ref = refs[-6]
            dot = jnp.zeros((rows, SB), f32)
            square = jnp.zeros((rows, SB), f32)
            for t in range(per):
                v = v_ref[:, pl.ds(pl.multiple_of((g * per + t) * SB, SB), SB)]
                dot = dot + total[t * rows : (t + 1) * rows] * v
                square = square + v * v
            dot = jnp.sum(dot, axis=0, keepdims=True)
            square = jnp.sum(square, axis=0, keepdims=True)

            @pl.when(g == 0)
            def _():
                sums_ref[...] = jnp.zeros_like(sums_ref)

            sums_ref[0:1, :] += dot
            if dots:
                sums_ref[1:2, :] += square

            @pl.when(g == steps - 1)
            def _():
                value = sums_ref[...]
                for ref in dot_refs:
                    for at in range(0, ref.shape[1], SB):
                        first = lax.broadcasted_iota(jnp.int32, value.shape, 0) == 0
                        value = value + jnp.where(first, ref[:, at : at + SB], 0.0)
                sums_ref[...] = value

    out = pl.pallas_call(
        kernel,
        grid_spec=pltpu.PrefetchScalarGridSpec(
            num_scalar_prefetch=3,
            grid=(steps,),
            in_specs=[
                pl.BlockSpec((rows, cols), lambda g, *_: (0, 0)),
                pl.BlockSpec(pair_tables.shape, lambda g, *_: (0, 0, 0)),
            ]
            + [pl.BlockSpec(memory_space=pl.ANY)] * (far + len(after))
            + [pl.BlockSpec(dot.shape, lambda g, *_: (0, 0)) for dot in dots],
            out_specs=[pl.BlockSpec((rows, per * SB), lambda g, *_: (0, g))]
            + ([pl.BlockSpec((8, SB), lambda g, *_: (0, 0))] if with_dot else []),
            scratch_shapes=[
                pltpu.VMEM((far * each, rows, SB), f32),
                pltpu.VMEM((per * rows, npair * SB), f32),
                pltpu.VMEM((npair * SB, SB), bf16),
                pltpu.VMEM((npair * SB, SB), bf16),
                pltpu.SemaphoreType.DMA((far,)),
            ],
        ),
        out_shape=[jax.ShapeDtypeStruct((rows, cols), f32)]
        + ([jax.ShapeDtypeStruct((8, SB), f32)] if with_dot else []),
        compiler_params=params(),
        cost_estimate=cost(0, 0),
        name="beta_sum",
    )(slots, signs, pair_index, vector, pair_tables, *received, *after, *dots)
    return list(out)


def finish(returned, beta_term, chunk, parts, width, previous, extra=None):
    rows, cols = beta_term.shape
    full = 1 if extra is None else 3
    sums = [] if extra is None else extra[0]

    def kernel(*refs):
        refs = list(refs)
        if extra is not None:
            sum_refs = refs[: len(sums)]
            del refs[: len(sums)]
            theta_ref = refs.pop()

            @pl.when(pl.program_id(0) == 0)
            def _():
                total = sum_refs[0][...]
                for ref in sum_refs[1:]:
                    total = total + ref[...]
                both = [jnp.sum(total[i : i + 1], axis=1, keepdims=True) for i in range(2)]
                theta_ref[...] = jnp.broadcast_to(both[0] / both[1], theta_ref.shape)

        value = refs[0][...] + refs[full][0]
        outs = refs[full + 1 + (previous is not None) :]
        if extra is not None:
            value = (value - theta_ref[0:1, 0:1] * refs[1][...]) / refs[2][...]
            outs[1][0] = value
        outs[0][...] = value

    whole = pl.BlockSpec((rows, width), lambda j: (0, chunk * parts + j))
    part = pl.BlockSpec((1, rows, width), lambda j: (j, 0, 0))
    in_specs = [pl.BlockSpec(a.shape, lambda j: (0, 0)) for a in sums] + [whole] * full + [part]
    arrays = list(sums) + [beta_term] + ([] if extra is None else [extra[1], extra[2]]) + [returned]
    aliases = {}
    if previous is not None:
        aliases = {len(arrays): 0}
        in_specs = in_specs + [pl.BlockSpec(memory_space=pl.ANY)]
        arrays = arrays + [previous]
    out_specs = [whole]
    out_shape = [jax.ShapeDtypeStruct((rows, cols), f32)]
    if extra is not None:
        out_specs += [part]
        out_shape += [jax.ShapeDtypeStruct((parts, rows, width), f32)]
    return pl.pallas_call(
        kernel,
        grid=(parts,),
        in_specs=in_specs,
        out_specs=out_specs,
        scratch_shapes=[] if extra is None else [pltpu.VMEM((8, SB), f32)],
        out_shape=out_shape,
        input_output_aliases=aliases,
        compiler_params=params(),
        cost_estimate=cost(0, 0),
        name="finish" if extra is None else "correct",
    )(*arrays)


def make_local(n_alpha, n_beta):
    chips = n_alpha // 2

    def to_partners(parts):
        return [lax.ppermute(part, "beta", [(i, i ^ k) for i in range(n_beta)]) for k, part in enumerate(parts, 1)]

    def turn(parts):
        return lax.all_to_all(parts, "alpha", 0, 0, tiled=True)

    def local(
        start_vector,
        precondition,
        alpha_hamiltonian,
        alpha_pairs,
        pair_tables,
        source_blocks,
        pair_index,
        phase_signs,
        cross_pairs,
        cross_signs,
    ):
        rows, cols = start_vector.shape
        blocks = cols // SB
        chunks = divisor(blocks // n_alpha, CHUNKS)
        width = cols // (n_alpha * chunks)
        cap = (blocks + 1) // 2
        device = lax.axis_index("alpha").astype(jnp.int32).reshape(1)
        me = lax.axis_index("beta").astype(jnp.int32)

        sent = [pack(start_vector, c, n_alpha, width) for c in range(chunks)]
        arrived = [turn(parts) for parts in sent]

        *marks, found = mark(source_blocks, me.reshape(1), n_beta, sent[:1])
        worst = marks[0][1:2, :1]
        marks = to_partners(marks)
        for other in marks:
            worst = jnp.maximum(worst, other[1:2, :1])
        too_many = worst[0, 0] > cap
        pairs_by_k = pair_index.T

        def plan(r):
            partner = (source_blocks // blocks) ^ me
            here = (found >= r * cap) & (found < (r + 1) * cap) & (partner != 0)
            far_slot = blocks + (partner - 1) * (cap + 1) + found - r * cap
            mine = (partner == 0) & (r == 0)
            slots = jnp.where(mine, source_blocks - me * blocks, jnp.where(here, far_slot, 0))
            signs = jnp.where(mine | here, phase_signs, 0)
            return positions(marks, r * cap, cap), slots.T, signs.T

        first_plan = plan(0)

        def beta_send(vector, planned, after):
            sent = gather_blocks(vector, planned[0], n_beta - 1, cap, after)
            received = to_partners(sent)
            return received, received[:2]

        def beta_round(vector, received, planned, after, dots=None, with_dot=False):
            _, slots, signs = planned
            return beta_sum(vector, received, slots, signs, pairs_by_k, pair_tables, after, dots, with_dot)

        def beta_side(vector, received, after, dots=None, with_dot=False):
            done = beta_round(vector, received, first_plan, after, dots, with_dot)

            def more(done):
                for r in range(1, -(-blocks // cap)):
                    planned = plan(r)
                    added = beta_round(vector, beta_send(vector, planned, [])[0], planned, [], None, with_dot)
                    done = [a + b for a, b in zip(done, added)]
                return done

            return lax.cond(too_many, more, lambda done: done, done)

        def alpha_side(arrived, with_dot, after):
            sides = []
            for c, parts in enumerate(arrived):
                columns = parts.reshape(n_alpha * rows, width)
                total, dot = alpha_sum(
                    columns, prepared, cross_pairs, cross_signs, device, c, n_alpha, with_dot, after
                )
                sides.append((turn(total.reshape(n_alpha, rows, width)), dot, total))
            return sides

        received, token = beta_send(start_vector, first_plan, [])
        prepared = prepare(alpha_hamiltonian, alpha_pairs, pair_tables, [])
        sides = alpha_side(arrived, True, token)
        beta_term, sums = beta_side(start_vector, received, [], [side[1] for side in sides], True)
        for other in to_partners([sums] * (n_beta - 1)):
            sums = sums + other
        sums = sums + lax.ppermute(sums, "alpha", [(i, i ^ 1) for i in range(n_alpha)])
        all_sums = [sums]
        for k in range(1, chips):
            pairs = [(i, ((i // 2 + k) % chips) * 2 + i % 2) for i in range(n_alpha)]
            all_sums.append(lax.ppermute(sums, "alpha", pairs))

        correction = None
        arrived = []
        for c in range(chunks):
            extra = (all_sums, start_vector, precondition)
            correction, parts = finish(sides[c][0], beta_term, c, n_alpha, width, correction, extra)
            arrived.append(turn(parts))
        received, token = beta_send(correction, first_plan, [])
        sides = alpha_side(arrived, False, token)
        (beta_term,) = beta_side(correction, received, [side[2] for side in sides])
        sigma_next = None
        for c in range(chunks):
            (sigma_next,) = finish(sides[c][0], beta_term, c, n_alpha, width, sigma_next)
        return correction, sigma_next

    return local


def solution(mesh):
    placed = (
        P("alpha", "beta"),
        P("alpha", "beta"),
        P(),
        P(),
        P(),
        P("beta", None),
        P("beta", None),
        P("beta", None),
        P(None, "beta"),
        P(None, "beta"),
    )
    return jax.shard_map(
        make_local(mesh.shape["alpha"], mesh.shape["beta"]),
        mesh=mesh,
        in_specs=placed,
        out_specs=(P("alpha", "beta"), P("alpha", "beta")),
        check_vma=False,
    )
```

time: 1320 us -> 352 us (0.27)
  local copies, waits for them, and re-layouts: 593 us -> 4.27 us
  waiting for transfers between devices: 465 us -> 213 us
  matrix products: 91.1 us -> 0 us
  Pallas kernels: 0 us -> 86.6 us
  other arithmetic: 86 us -> 0.63 us
  blocking collectives: 38.2 us -> 0 us
  starting transfers between devices: 21.2 us -> 42.1 us
    all_to_all x4, waiting for transfers between devices: 463 us -> 66.3 us  [turn(): return lax.all_to_all(parts, 'alpha', 0, 0, tiled=True)]
    unnamed x67 -> x19, local copies, waits for them, and re-layouts: 254 us -> 1.36 us
    ppermute x0 -> x16, waiting for transfers between devices: none -> 147 us  [the longest x12 140 us: to_partners(): lax.ppermute(part, 'beta', [(i, i ^ k) for i in range(n_beta)])]
    dot_general x8 -> x0, matrix products: 91.1 us -> none  [the longest x2 42 us: sigma_local(): jnp.einsum('rtkc,tkcd->rtd', picked, signed_tables, precision=highest)]
    reshape x8 -> x0, local copies, waits for them, and re-layouts: 88.1 us -> none  [the longest x4 59.5 us: pair_images(): return images.reshape(row_count, block_count * NPAIR, SB)]
    gather x15 -> x0, local copies, waits for them, and re-layouts: 88.1 us -> none  [the longest x12 61.8 us: cross_terms(): picked = images[:, chosen] * signs.astype(jnp.float32)[None, :, None]]
    pallas_call x0 -> x12, Pallas kernels: none -> 86.6 us  [the longest x2 29.4 us: beta_sum(): pl.pallas_call(kernel, grid_spec=pltpu.PrefetchScalarGridSpec(num_scalar_...]
    all_to_all x5 -> x0, local copies, waits for them, and re-layouts: 79.3 us -> none  [the longest x3 74.6 us: sigma_local(): lax.all_to_all(stacked, 'alpha', split_axis=2, concat_axis=1, tiled=True)]
  transfers between devices with their start and end apart: 6 -> 20, of which waited for: 4 -> 18; matrix products, arithmetic and copies ran while one was open for 29% -> 1% of each run, Pallas kernels for 0% -> 13%
where the time goes in v2:
time: 352 us; the launch traced here: 350 us
  waiting for transfers between devices  213 us (61%)
  Pallas kernels  86.6 us (25%)
  starting transfers between devices  42.1 us (12%)
  local copies, waits for them, and re-layouts  4.27 us (1%)
    ppermute x12, waiting for transfers between devices, to_partners(): lax.ppermute(part, 'beta', [(i, i ^ k) for i in range(n_beta)])  140 us
    all_to_all x4, waiting for transfers between devices, turn(): return lax.all_to_all(parts, 'alpha', 0, 0, tiled=True)  66.3 us
    pallas_call x2, Pallas kernels, beta_sum(): pl.pallas_call(kernel, grid_spec=pltpu.PrefetchScalarGridSpec(num_scalar_...  29.4 us
    pallas_call x2, Pallas kernels, alpha_sum(): pl.pallas_call(kernel, grid_spec=pltpu.PrefetchScalarGridSpec(num_scalar_...  20.9 us
    all_to_all x4, starting transfers between devices, turn(): return lax.all_to_all(parts, 'alpha', 0, 0, tiled=True)  20.3 us
    ppermute x12, starting transfers between devices, to_partners(): lax.ppermute(part, 'beta', [(i, i ^ k) for i in range(n_beta)])  17.2 us
    pallas_call x2, Pallas kernels, finish(): pl.pallas_call(kernel, grid=(parts,), in_specs=in_specs, out_specs=out_sp...  15.3 us
    pallas_call x2, Pallas kernels, gather_blocks(): pl.pallas_call(kernel, grid_spec=pltpu.PrefetchScalarGridSpec(num_scalar_...  8.86 us
  transfers between devices with their start and end apart: 20, of which 18 were waited for; matrix products, arithmetic and copies ran while one was open for 1% of the time, Pallas kernels for 13%

profile of v2, /device:TPU:0, one launch (start us, length us, event | category | flops | bytes accessed | tf_op | source)
XLA Modules:
  0.0 350.4 jit_solution(685787504931705794)
XLA Ops:
  0.6 6.1 %pack.1.refs_0_ = f32[8,32,3072]{2,1,0:T(8,128)} custom-call(f32[32,24576]{1,0:T(8,128)} %refs_5_.1), custom_call_target="tpu_custom_call" | custom-call | flops 1 | bytes 1 | tf_op jit(solution)/shard_map/pack/pallas_call | solution.py:73
  6.7 6.5 %all-to-all-start = ((f32[8,32,3072]{2,1,0:T(8,128)}), f32[8,32,3072]{2,1,0:T(8,128)}, u32[]{:S(2)}, u32[]{:S(2)}) async-start(f32[8,32,3072]{2,1,0:T(8,128)} %pack.1.refs_0_), calls=%async_computation | async-start | bytes 6291456 | tf_op jit(solution)/shard_map/all_to_all | solution.py:416
  13.2 0.0 copy-done.3
  13.2 0.8 copy.12.source_ref
  14.0 2.9 mark.1
  16.9 1.6 collective-permute-start.7
  18.5 1.4 collective-permute-start.8
  19.9 0.5 collective-permute-start.6
  20.5 0.4 collective-permute-done.7.refs_1_
  20.9 2.4 collective-permute-done.8.refs_2_
  23.3 0.5 collective-permute-done.6.refs_0_
  23.8 0.8 positions.5.slots_ref
  24.6 0.0 copy-done
  24.6 4.5 %gather_blocks.6 = (f32[97,32,128]{2,1,0:T(8,128)}, f32[97,32,128]{2,1,0:T(8,128)}, f32[97,32,128]{2,1,0:T(8,128)}) custom-call(s32[8,256]{1,0:T(8,128)} %positions.5.slots_ref, f32[32,24576]{1,0:T(8,128)S(1)} %copy-done), custom_call_target="tpu_custom_call" | custom-call | flops 1 | bytes 1 | tf_op jit(solution)/shard_map/gather_blocks/pallas_call | solution.py:232
  29.0 1.0 collective-permute-start.9
  30.0 1.1 collective-permute-start.10
  31.1 0.0 copy-done.2
  31.1 2.4 prepare.1
  33.4 31.7 %collective-permute-done.9.refs_0_.refs_2_ = f32[97,32,128]{2,1,0:T(8,128)} collective-permute-done((f32[97,32,128]{2,1,0:T(8,128)}, f32[97,32,128]{2,1,0:T(8,128)}, u32[]{:S(2)}, u32[]{:S(2)}) %collective-permute-start.9) | collective-permute-done | bytes 1589280 | tf_op jit(solution)/shard_map/ppermute | solution.py:413
  65.2 1.0 collective-permute-done.10.refs_1_.refs_3_
  66.1 18.7 %all-to-all-done = f32[8,32,3072]{2,1,0:T(8,128)} async-done(((f32[8,32,3072]{2,1,0:T(8,128)}), f32[8,32,3072]{2,1,0:T(8,128)}, u32[]{:S(2)}, u32[]{:S(2)}) %all-to-all-start) | async-done | bytes 3145760 | tf_op jit(solution)/shard_map/all_to_all | solution.py:416
  84.8 10.5 %alpha_sum.2 = (f32[256,3072]{1,0:T(8,128)}, f32[1,3072]{1,0:T(1,128)}) custom-call(s32[1]{0:T(128)} %bitcast.9.device_ref, s32[2,192]{1,0:T(2,128)} %pairs_ref.3, s32[2,192]{1,0:T(2,128)} %signs_ref.3, f32[256,3072]{1,0:T(8,128)} %bitcast.10.v_ref, bf16[256,1536]{1,0:T(8,128)(2,1)} %get-tuple-element.116.a_twice, ...), custom_call_target="tpu_custom_call" | custom-call | flops 1 | bytes 1 | tf_op jit(solution)/shard_map/alpha_sum/pallas_call | solution.py:120
  95.4 4.6 %all-to-all-start.1 = ((f32[8,32,3072]{2,1,0:T(8,128)}), f32[8,32,3072]{2,1,0:T(8,128)}, u32[]{:S(2)}, u32[]{:S(2)}) async-start(f32[8,32,3072]{2,1,0:T(8,128)} %bitcast.21), calls=%async_computation.1 | async-start | bytes 6291456 | tf_op jit(solution)/shard_map/all_to_all | solution.py:416
  100.0 2.5 collective-permute-start.11
  102.5 1.2 slice.12
  103.7 0.1 copy.13
  103.8 0.6 fusion.2
  104.4 0.6 slice.16
  106.3 0.5 slice.17
  107.4 0.5 slice.18
  108.6 29.6 %collective-permute-done.11.refs_4_ = f32[97,32,128]{2,1,0:T(8,128)} collective-permute-done((f32[97,32,128]{2,1,0:T(8,128)}, f32[97,32,128]{2,1,0:T(8,128)}, u32[]{:S(2)}, u32[]{:S(2)}) %collective-permute-start.11) | collective-permute-done | bytes 1589280 | tf_op jit(solution)/shard_map/ppermute | solution.py:413
  138.2 0.0 copy-done.4
  138.2 15.2 %beta_sum.6 = (f32[32,24576]{1,0:T(8,128)}, f32[8,128]{1,0:T(8,128)S(1)}) custom-call(s32[2,192]{1,0:T(2,128)} %get-tuple-element.159.slots_ref, s32[2,192]{1,0:T(2,128)} %get-tuple-element.158.sign_ref, s32[2,192]{1,0:T(2,128)S(1)} %bitcast.22, f32[32,24576]{1,0:T(8,128)S(1)} %copy-done, f32[4,128,128]{2,1,0:T(8,128)S(1)} %copy-done.2, ...), custom_call_target="tpu_custom_call" | custom-call | flops 1 | bytes 1 | tf_op jit(solution)/shard_map/beta_sum/pallas_call | solution.py:324
  153.4 2.5 collective-permute-start.14
  155.9 0.5 collective-permute-start.13
  156.4 0.5 collective-permute-start.12
  157.0 1.0 collective-permute-done.14
  158.0 1.5 collective-permute-done.13
  159.5 0.5 collective-permute-done.12
  160.0 0.0 collective-permute-start.15
  160.0 1.2 collective-permute-done.15
  161.2 3.5 collective-permute-start.18
  164.7 0.0 collective-permute-start.17
  164.7 1.1 collective-permute-start.16
  165.8 0.2 collective-permute-done.18.refs_3_
  166.0 5.8 %collective-permute-done.17.refs_2_ = f32[8,128]{1,0:T(8,128)S(1)} collective-permute-done((f32[8,128]{1,0:T(8,128)S(1)}, f32[8,128]{1,0:T(8,128)S(1)}, u32[]{:S(2)}, u32[]{:S(2)}) %collective-permute-start.17) | collective-permute-done | bytes 4128 | tf_op jit(solution)/shard_map/ppermute | solution.py:501
  171.8 0.0 collective-permute-done.16.refs_1_
  171.8 0.0 all-to-all-done.1.refs_7_
  171.8 0.6 copy-done.8
  172.4 8.6 %correct.1 = (f32[32,24576]{1,0:T(8,128)}, f32[8,32,3072]{2,1,0:T(8,128)}) custom-call(f32[8,128]{1,0:T(8,128)} %copy-done.6, f32[8,128]{1,0:T(8,128)} %collective-permute-done.16.refs_1_, f32[8,128]{1,0:T(8,128)} %copy-done.8, f32[8,128]{1,0:T(8,128)} %copy-done.7, f32[32,24576]{1,0:T(8,128)} %get-tuple-element.124.refs_4_, f32[32,24576]{1,0:T(8,128)S(1)} %copy-done, ...), custom_call_target="tpu_custom_call" | custom-call | flops 1 | bytes 1 | tf_op jit(solution)/shard_map/correct/pallas_call | solution.py:395
  181.0 4.7 %all-to-all-start.2 = ((f32[8,32,3072]{2,1,0:T(8,128)}), f32[8,32,3072]{2,1,0:T(8,128)}, u32[]{:S(2)}, u32[]{:S(2)}) async-start(f32[8,32,3072]{2,1,0:T(8,128)} %get-tuple-element.130), calls=%async_computation.2 | async-start | bytes 6291456 | tf_op jit(solution)/shard_map/all_to_all | solution.py:416
  185.8 4.4 %gather_blocks.7 = (f32[97,32,128]{2,1,0:T(8,128)}, f32[97,32,128]{2,1,0:T(8,128)}, f32[97,32,128]{2,1,0:T(8,128)}) custom-call(s32[8,256]{1,0:T(8,128)} %positions.5.slots_ref, f32[32,24576]{1,0:T(8,128)S(1)} %copy-done.1), custom_call_target="tpu_custom_call" | custom-call | flops 1 | bytes 1 | tf_op jit(solution)/shard_map/gather_blocks/pallas_call | solution.py:232
  190.2 1.5 collective-permute-start.19
  191.7 1.5 collective-permute-start.20
  193.2 34.3 %collective-permute-done.19.refs_0_.refs_2_ = f32[97,32,128]{2,1,0:T(8,128)} collective-permute-done((f32[97,32,128]{2,1,0:T(8,128)}, f32[97,32,128]{2,1,0:T(8,128)}, u32[]{:S(2)}, u32[]{:S(2)}) %collective-permute-start.19) | collective-permute-done | bytes 1589280 | tf_op jit(solution)/shard_map/ppermute | solution.py:413
  227.5 1.2 collective-permute-done.20.refs_1_.refs_3_
  228.7 28.6 %all-to-all-done.2 = f32[8,32,3072]{2,1,0:T(8,128)} async-done(((f32[8,32,3072]{2,1,0:T(8,128)}), f32[8,32,3072]{2,1,0:T(8,128)}, u32[]{:S(2)}, u32[]{:S(2)}) %all-to-all-start.2) | async-done | bytes 3145760 | tf_op jit(solution)/shard_map/all_to_all | solution.py:416
  257.3 10.4 %alpha_sum.3.refs_5_ = f32[256,3072]{1,0:T(8,128)} custom-call(s32[1]{0:T(128)} %bitcast.9.device_ref, s32[2,192]{1,0:T(2,128)} %pairs_ref.3, s32[2,192]{1,0:T(2,128)} %signs_ref.3, f32[256,3072]{1,0:T(8,128)} %bitcast.12.v_ref, bf16[256,1536]{1,0:T(8,128)(2,1)} %get-tuple-element.116.a_twice, bf16[256,768]{1,0:T(8,128)(2,1)} %get-tuple-element.117.a_low, ...), custom_call_target="tpu_custom_call" | custom-call | flops 1 | bytes 1 | tf_op jit(solution)/shard_map/alpha_sum/pallas_call | solution.py:120
  267.7 4.5 %all-to-all-start.3 = ((f32[8,32,3072]{2,1,0:T(8,128)}), f32[8,32,3072]{2,1,0:T(8,128)}, u32[]{:S(2)}, u32[]{:S(2)}) async-start(f32[8,32,3072]{2,1,0:T(8,128)} %bitcast.20), calls=%async_computation.3 | async-start | bytes 6291456 | tf_op jit(solution)/shard_map/all_to_all | solution.py:416
  272.2 2.5 collective-permute-start.21
  274.7 35.7 %collective-permute-done.21.refs_4_ = f32[97,32,128]{2,1,0:T(8,128)} collective-permute-done((f32[97,32,128]{2,1,0:T(8,128)}, f32[97,32,128]{2,1,0:T(8,128)}, u32[]{:S(2)}, u32[]{:S(2)}) %collective-permute-start.21) | collective-permute-done | bytes 1589280 | tf_op jit(solution)/shard_map/ppermute | solution.py:413
  310.4 14.2 %beta_sum.7 = f32[32,24576]{1,0:T(8,128)} custom-call(s32[2,192]{1,0:T(2,128)} %get-tuple-element.159.slots_ref, s32[2,192]{1,0:T(2,128)} %get-tuple-element.158.sign_ref, s32[2,192]{1,0:T(2,128)S(1)} %bitcast.24, f32[32,24576]{1,0:T(8,128)S(1)} %copy-done.1, f32[4,128,128]{2,1,0:T(8,128)S(1)} %copy-done.2, ...), custom_call_target="tpu_custom_call" | custom-call | flops 1 | bytes 1 | tf_op jit(solution)/shard_map/beta_sum/pallas_call | solution.py:324
  324.6 19.1 %all-to-all-done.3.refs_1_ = f32[8,32,3072]{2,1,0:T(8,128)} async-done(((f32[8,32,3072]{2,1,0:T(8,128)}), f32[8,32,3072]{2,1,0:T(8,128)}, u32[]{:S(2)}, u32[]{:S(2)}) %all-to-all-start.3) | async-done | bytes 3145760 | tf_op jit(solution)/shard_map/all_to_all | solution.py:416
  343.7 6.7 %finish.1 = f32[32,24576]{1,0:T(8,128)} custom-call(f32[32,24576]{1,0:T(8,128)} %get-tuple-element.165.refs_0_, f32[8,32,3072]{2,1,0:T(8,128)} %all-to-all-done.3.refs_1_), custom_call_target="tpu_custom_call" | custom-call | flops 1 | bytes 1 | tf_op jit(solution)/shard_map/finish/pallas_call | solution.py:395
  (17 shorter events, 0.0 us)
Async XLA Ops:
  6.7 6.5 %copy-start.3 = (s32[192,2]{0,1:T(2,128)S(1)}, s32[192,2]{0,1:T(2,128)}, u32[]{:S(2)}) copy-start(s32[192,2]{0,1:T(2,128)} %param.19) | copy-start | bytes 4612
  6.7 78.1 %all-to-all-start = ((f32[8,32,3072]{2,1,0:T(8,128)}), f32[8,32,3072]{2,1,0:T(8,128)}, u32[]{:S(2)}, u32[]{:S(2)}) async-start(f32[8,32,3072]{2,1,0:T(8,128)} %pack.1.refs_0_), calls=%async_computation | async-start | bytes 6291456 | tf_op jit(solution)/shard_map/all_to_all | solution.py:416
  14.0 10.6 %copy-start = (f32[32,24576]{1,0:T(8,128)S(1)}, f32[32,24576]{1,0:T(8,128)}, u32[]{:S(2)}) copy-start(f32[32,24576]{1,0:T(8,128)} %refs_5_.1) | copy-start | bytes 9437188
  16.9 3.9 %collective-permute-start.7 = (f32[8,256]{1,0:T(8,128)}, f32[8,256]{1,0:T(8,128)S(1)}, u32[]{:S(2)}, u32[]{:S(2)}) collective-permute-start(f32[8,256]{1,0:T(8,128)} %get-tuple-element.110), channel_id=1, source_target_pairs={{0,2},{1,3},{2,0},{3,1},{4,6},{5,7},{6,4},{7,5},{8,10},{9,11},{10,... | collective-permute-start | bytes 24584 | tf_op jit(solution)/shard_map/ppermute | solution.py:413
  18.5 4.8 %collective-permute-start.8 = (f32[8,256]{1,0:T(8,128)}, f32[8,256]{1,0:T(8,128)S(1)}, u32[]{:S(2)}, u32[]{:S(2)}) collective-permute-start(f32[8,256]{1,0:T(8,128)} %get-tuple-element.111), channel_id=1, source_target_pairs={{0,3},{1,2},{2,1},{3,0},{4,7},{5,6},{6,5},{7,4},{8,11},{9,10},{10,... | collective-permute-start | bytes 24584 | tf_op jit(solution)/shard_map/ppermute | solution.py:413
  19.9 11.1 %copy-start.2 = (f32[4,128,128]{2,1,0:T(8,128)S(1)}, f32[4,128,128]{2,1,0:T(8,128)}, u32[]{:S(2)}) copy-start(f32[4,128,128]{2,1,0:T(8,128)} %refs_1_.3) | copy-start | bytes 786436
  19.9 3.9 %collective-permute-start.6 = (f32[8,256]{1,0:T(8,128)}, f32[8,256]{1,0:T(8,128)S(1)}, u32[]{:S(2)}, u32[]{:S(2)}) collective-permute-start(f32[8,256]{1,0:T(8,128)} %get-tuple-element.109), channel_id=1, source_target_pairs={{0,1},{1,0},{2,3},{3,2},{4,5},{5,4},{6,7},{7,6},{8,9},{9,8},{10,11... | collective-permute-start | bytes 24584 | tf_op jit(solution)/shard_map/ppermute | solution.py:413
  29.0 36.2 %collective-permute-start.9 = (f32[97,32,128]{2,1,0:T(8,128)}, f32[97,32,128]{2,1,0:T(8,128)}, u32[]{:S(2)}, u32[]{:S(2)}) collective-permute-start(f32[97,32,128]{2,1,0:T(8,128)} %get-tuple-element.113), channel_id=1, source_target_pairs={{0,1},{1,0},{2,3},{3,2},{4,5},{5,4},{6,7},{7,6},{8,9},{9,8},{10,11... | collective-permute-start | bytes 4767752 | tf_op jit(solution)/shard_map/ppermute | solution.py:413
  30.0 36.2 %collective-permute-start.10 = (f32[97,32,128]{2,1,0:T(8,128)}, f32[97,32,128]{2,1,0:T(8,128)}, u32[]{:S(2)}, u32[]{:S(2)}) collective-permute-start(f32[97,32,128]{2,1,0:T(8,128)} %get-tuple-element.114), channel_id=1, source_target_pairs={{0,2},{1,3},{2,0},{3,1},{4,6},{5,7},{6,4},{7,5},{8,10},{9,11},{10,... | collective-permute-start | bytes 4767752 | tf_op jit(solution)/shard_map/ppermute | solution.py:413
  95.3 8.4 %copy-start.5 = (s32[192,2]{0,1:T(2,128)S(1)}, s32[192,2]{0,1:T(2,128)}, u32[]{:S(2)}) copy-start(s32[192,2]{0,1:T(2,128)} %param.21) | copy-start | bytes 4612
  95.3 42.9 %copy-start.4 = (s32[192,2]{0,1:T(2,128)S(1)}, s32[192,2]{0,1:T(2,128)}, u32[]{:S(2)}) copy-start(s32[192,2]{0,1:T(2,128)} %param.20) | copy-start | bytes 4612
  95.4 76.5 %all-to-all-start.1 = ((f32[8,32,3072]{2,1,0:T(8,128)}), f32[8,32,3072]{2,1,0:T(8,128)}, u32[]{:S(2)}, u32[]{:S(2)}) async-start(f32[8,32,3072]{2,1,0:T(8,128)} %bitcast.21), calls=%async_computation.1 | async-start | bytes 6291456 | tf_op jit(solution)/shard_map/all_to_all | solution.py:416
  100.0 38.2 %collective-permute-start.11 = (f32[97,32,128]{2,1,0:T(8,128)}, f32[97,32,128]{2,1,0:T(8,128)}, u32[]{:S(2)}, u32[]{:S(2)}) collective-permute-start(f32[97,32,128]{2,1,0:T(8,128)} %get-tuple-element.115), channel_id=1, source_target_pairs={{0,3},{1,2},{2,1},{3,0},{4,7},{5,6},{6,5},{7,4},{8,11},{9,10},{10,... | collective-permute-start | bytes 4767752 | tf_op jit(solution)/shard_map/ppermute | solution.py:413
  153.4 4.6 %collective-permute-start.14 = (f32[8,128]{1,0:T(8,128)S(1)}, f32[8,128]{1,0:T(8,128)S(1)}, u32[]{:S(2)}, u32[]{:S(2)}) collective-permute-start(f32[8,128]{1,0:T(8,128)S(1)} %get-tuple-element.123), channel_id=1, source_target_pairs={{0,3},{1,2},{2,1},{3,0},{4,7},{5,6},{6,5},{7,4},{8,11},{9,10},{10,... | collective-permute-start | bytes 12296 | tf_op jit(solution)/shard_map/ppermute | solution.py:413
  155.9 3.6 %collective-permute-start.13 = (f32[8,128]{1,0:T(8,128)S(1)}, f32[8,128]{1,0:T(8,128)S(1)}, u32[]{:S(2)}, u32[]{:S(2)}) collective-permute-start(f32[8,128]{1,0:T(8,128)S(1)} %get-tuple-element.123), channel_id=1, source_target_pairs={{0,2},{1,3},{2,0},{3,1},{4,6},{5,7},{6,4},{7,5},{8,10},{9,11},{10,... | collective-permute-start | bytes 12296 | tf_op jit(solution)/shard_map/ppermute | solution.py:413
  156.4 3.6 %collective-permute-start.12 = (f32[8,128]{1,0:T(8,128)S(1)}, f32[8,128]{1,0:T(8,128)S(1)}, u32[]{:S(2)}, u32[]{:S(2)}) collective-permute-start(f32[8,128]{1,0:T(8,128)S(1)} %get-tuple-element.123), channel_id=1, source_target_pairs={{0,1},{1,0},{2,3},{3,2},{4,5},{5,4},{6,7},{7,6},{8,9},{9,8},{10,11... | collective-permute-start | bytes 12296 | tf_op jit(solution)/shard_map/ppermute | solution.py:413
  160.0 1.2 collective-permute-start.15
  161.2 10.6 %copy-start.6 = (f32[8,128]{1,0:T(8,128)}, f32[8,128]{1,0:T(8,128)S(1)}, u32[]{:S(2)}) copy-start(f32[8,128]{1,0:T(8,128)S(1)} %add.52.refs_0_) | copy-start | bytes 12292
  161.2 4.8 %collective-permute-start.18 = (f32[8,128]{1,0:T(8,128)S(1)}, f32[8,128]{1,0:T(8,128)S(1)}, u32[]{:S(2)}, u32[]{:S(2)}) collective-permute-start(f32[8,128]{1,0:T(8,128)S(1)} %add.52.refs_0_), channel_id=1, source_target_pairs={{0,24},{4,28},{8,0},{12,4},{16,8},{20,12},{24,16},{28,20},{1,25},{... | collective-permute-start | bytes 12296 | tf_op jit(solution)/shard_map/ppermute | solution.py:501
  164.7 7.1 %collective-permute-start.17 = (f32[8,128]{1,0:T(8,128)S(1)}, f32[8,128]{1,0:T(8,128)S(1)}, u32[]{:S(2)}, u32[]{:S(2)}) collective-permute-start(f32[8,128]{1,0:T(8,128)S(1)} %add.52.refs_0_), channel_id=1, source_target_pairs={{0,16},{4,20},{8,24},{12,28},{16,0},{20,4},{24,8},{28,12},{1,17},{... | collective-permute-start | bytes 12296 | tf_op jit(solution)/shard_map/ppermute | solution.py:501
  164.7 7.1 %collective-permute-start.16 = (f32[8,128]{1,0:T(8,128)S(1)}, f32[8,128]{1,0:T(8,128)}, u32[]{:S(2)}, u32[]{:S(2)}) collective-permute-start(f32[8,128]{1,0:T(8,128)S(1)} %add.52.refs_0_), channel_id=1, source_target_pairs={{0,8},{4,12},{8,16},{12,20},{16,24},{20,28},{24,0},{28,4},{1,9},{5... | collective-permute-start | bytes 12296 | tf_op jit(solution)/shard_map/ppermute | solution.py:501
  166.0 5.8 %copy-start.7 = (f32[8,128]{1,0:T(8,128)}, f32[8,128]{1,0:T(8,128)S(1)}, u32[]{:S(2)}) copy-start(f32[8,128]{1,0:T(8,128)S(1)} %collective-permute-done.18.refs_3_) | copy-start | bytes 12292
  171.8 0.6 copy-start.8
  181.0 4.7 %copy-start.1 = (f32[32,24576]{1,0:T(8,128)S(1)}, f32[32,24576]{1,0:T(8,128)}, u32[]{:S(2)}) copy-start(f32[32,24576]{1,0:T(8,128)} %get-tuple-element.107.v_ref.refs_0_) | copy-start | bytes 9437188
  181.0 76.3 %all-to-all-start.2 = ((f32[8,32,3072]{2,1,0:T(8,128)}), f32[8,32,3072]{2,1,0:T(8,128)}, u32[]{:S(2)}, u32[]{:S(2)}) async-start(f32[8,32,3072]{2,1,0:T(8,128)} %get-tuple-element.130), calls=%async_computation.2 | async-start | bytes 6291456 | tf_op jit(solution)/shard_map/all_to_all | solution.py:416
  190.2 37.3 %collective-permute-start.19 = (f32[97,32,128]{2,1,0:T(8,128)}, f32[97,32,128]{2,1,0:T(8,128)}, u32[]{:S(2)}, u32[]{:S(2)}) collective-permute-start(f32[97,32,128]{2,1,0:T(8,128)} %get-tuple-element.127), channel_id=1, source_target_pairs={{0,1},{1,0},{2,3},{3,2},{4,5},{5,4},{6,7},{7,6},{8,9},{9,8},{10,11... | collective-permute-start | bytes 4767752 | tf_op jit(solution)/shard_map/ppermute | solution.py:413
  191.7 37.0 %collective-permute-start.20 = (f32[97,32,128]{2,1,0:T(8,128)}, f32[97,32,128]{2,1,0:T(8,128)}, u32[]{:S(2)}, u32[]{:S(2)}) collective-permute-start(f32[97,32,128]{2,1,0:T(8,128)} %get-tuple-element.128), channel_id=1, source_target_pairs={{0,2},{1,3},{2,0},{3,1},{4,6},{5,7},{6,4},{7,5},{8,10},{9,11},{10,... | collective-permute-start | bytes 4767752 | tf_op jit(solution)/shard_map/ppermute | solution.py:413
  267.7 76.0 %all-to-all-start.3 = ((f32[8,32,3072]{2,1,0:T(8,128)}), f32[8,32,3072]{2,1,0:T(8,128)}, u32[]{:S(2)}, u32[]{:S(2)}) async-start(f32[8,32,3072]{2,1,0:T(8,128)} %bitcast.20), calls=%async_computation.3 | async-start | bytes 6291456 | tf_op jit(solution)/shard_map/all_to_all | solution.py:416
  272.2 38.2 %collective-permute-start.21 = (f32[97,32,128]{2,1,0:T(8,128)}, f32[97,32,128]{2,1,0:T(8,128)}, u32[]{:S(2)}, u32[]{:S(2)}) collective-permute-start(f32[97,32,128]{2,1,0:T(8,128)} %get-tuple-element.129), channel_id=1, source_target_pairs={{0,3},{1,2},{2,1},{3,0},{4,7},{5,6},{6,5},{7,4},{8,11},{9,10},{10,... | collective-permute-start | bytes 4767752 | tf_op jit(solution)/shard_map/ppermute | solution.py:413

commit v3 on v2

--- a/solution.py
+++ b/solution.py
@@ -6,7 +6,6 @@
 from jax.sharding import PartitionSpec as P
 
 SB = 128
-CHUNKS = 1
 VMEM_BYTES = 60 * 1024 * 1024
 f32 = jnp.float32
 bf16 = jnp.bfloat16
@@ -64,77 +63,122 @@
     )(alpha_hamiltonian, alpha_pairs, pair_tables, *after)
 
 
-def pack(vector, chunk, parts, width):
-    rows = vector.shape[0]
-
-    def kernel(source, target):
-        target[0] = source[...]
-
-    return pl.pallas_call(
-        kernel,
-        grid=(parts,),
-        in_specs=[pl.BlockSpec((rows, width), lambda j: (0, chunk * parts + j))],
-        out_specs=pl.BlockSpec((1, rows, width), lambda j: (j, 0, 0)),
+def pack(vector, parts):
+    rows, cols = vector.shape
+    width = cols // parts
+
+    def kernel(source, target, held, sems):
+        def taken(j):
+            at = pl.ds(pl.multiple_of(j * width, SB), width)
+            return pltpu.make_async_copy(source.at[:, at], held.at[j], sems.at[0, j])
+
+        def given(j):
+            return pltpu.make_async_copy(held.at[j], target.at[j], sems.at[1, j])
+
+        for j in range(parts):
+            taken(j).start()
+        for j in range(parts):
+            taken(j).wait()
+            given(j).start()
+        for j in range(parts):
+            given(j).wait()
+
+    return pl.pallas_call(
+        kernel,
+        in_specs=[pl.BlockSpec(memory_space=pl.ANY)],
+        out_specs=pl.BlockSpec(memory_space=pl.ANY),
         out_shape=jax.ShapeDtypeStruct((parts, rows, width), f32),
+        scratch_shapes=[pltpu.VMEM((parts, rows, width), f32), pltpu.SemaphoreType.DMA((2, parts))],
         compiler_params=params(),
         cost_estimate=cost(0, 0),
         name="pack",
     )(vector)
 
 
-def alpha_sum(columns, prepared, cross_pairs, cross_signs, device, chunk, parts, with_dot, after):
+def alpha_sum(columns, prepared, cross_pairs, cross_signs, device, after):
     size, width = columns.shape
     depth = prepared[1].shape[1]
     nq = cross_pairs.shape[0]
     blocks = width // SB
-    per = divisor(blocks, 4)
+    per = divisor(blocks, 8)
     steps = blocks // per
     wide = per * SB
 
-    def kernel(device_ref, pairs_ref, signs_ref, v_ref, a_twice, a_low, t_high, t_low, *refs):
-        b = refs[-1]
-        out_ref = refs[len(after)]
-        g = pl.program_id(0)
-        high, low = halves(v_ref[...])
-        b[:size, :] = high
-        b[depth : depth + size, :] = low
-        first = (chunk * parts + device_ref[0]) * blocks + g * per
-        for t in range(per):
-            at = slice(t * SB, (t + 1) * SB)
-            high = b[:size, at]
-            both = jnp.concatenate([high, b[depth : depth + size, at]], axis=1)
-            chosen = [pairs_ref[q, first + t] for q in range(nq)]
-            x = mul(both, jnp.concatenate([t_high[p] for p in chosen], axis=1))
-            x = x + mul(high, jnp.concatenate([t_low[p] for p in chosen], axis=1))
-            for q in range(nq):
-                x_high, x_low = halves(x[:, q * SB : (q + 1) * SB] * signs_ref[q, first + t].astype(f32))
-                row = (q + 1) * size
-                b[row : row + size, at] = x_high
-                b[depth + row : depth + row + size, at] = x_low
-        total = mul(a_twice[...], b[...]) + mul(a_low[...], b[:depth, :])
-        out_ref[...] = total
-        if with_dot:
-            refs[-2][...] = jnp.sum(total * v_ref[...], axis=0, keepdims=True)
-
-    column_spec = pl.BlockSpec((size, wide), lambda g, *_: (0, g))
-    out = pl.pallas_call(
-        kernel,
-        grid_spec=pltpu.PrefetchScalarGridSpec(
-            num_scalar_prefetch=3,
-            grid=(steps,),
-            in_specs=[column_spec]
-            + [pl.BlockSpec(a.shape, lambda g, *_, zeros=(0,) * a.ndim: zeros) for a in prepared]
-            + [pl.BlockSpec(memory_space=pl.ANY)] * len(after),
-            out_specs=[column_spec] + ([pl.BlockSpec((1, wide), lambda g, *_: (0, g))] if with_dot else []),
-            scratch_shapes=[pltpu.VMEM((2 * depth, wide), bf16)],
-        ),
-        out_shape=[jax.ShapeDtypeStruct((size, width), f32)]
-        + ([jax.ShapeDtypeStruct((1, width), f32)] if with_dot else []),
+    def kernel(device_ref, pairs_ref, signs_ref, v_any, *refs):
+        prepared_any = refs[:4]
+        out_any = refs[4 + len(after)]
+        v_held, out_held, a_twice, a_low, t_high, t_low, even, odd, sems, once = refs[-10:]
+
+        def at(g):
+            return pl.ds(pl.multiple_of(g * wide, SB), wide)
+
+        def taken(g):
+            return pltpu.make_async_copy(v_any.at[:, at(g)], v_held.at[g], sems.at[0, g])
+
+        def given(g):
+            return pltpu.make_async_copy(out_held.at[g], out_any.at[:, at(g)], sems.at[1, g])
+
+        held = (a_twice, a_low, t_high, t_low)
+        loads = [pltpu.make_async_copy(prepared_any[i], held[i], once.at[i]) for i in range(4)]
+        for load in loads[2:]:
+            load.start()
+        taken(0).start()
+        for load in loads[:2]:
+            load.start()
+        for g in range(1, steps):
+            taken(g).start()
+        for load in loads[2:]:
+            load.wait()
+
+        def build(g, b):
+            high, low = halves(v_held[g])
+            b[:size, :] = high
+            b[depth : depth + size, :] = low
+            first = device_ref[0] * blocks + g * per
+            for t in range(per):
+                here = slice(t * SB, (t + 1) * SB)
+                both = jnp.concatenate([high[:, here], low[:, here]], axis=1)
+                chosen = [pairs_ref[q, first + t] for q in range(nq)]
+                x = mul(both, jnp.concatenate([t_high[p] for p in chosen], axis=1))
+                x = x + mul(high[:, here], jnp.concatenate([t_low[p] for p in chosen], axis=1))
+                for q in range(nq):
+                    x_high, x_low = halves(x[:, q * SB : (q + 1) * SB] * signs_ref[q, first + t].astype(f32))
+                    row = (q + 1) * size
+                    b[row : row + size, here] = x_high
+                    b[depth + row : depth + row + size, here] = x_low
+
+        taken(0).wait()
+        build(0, even)
+        for load in loads[:2]:
+            load.wait()
+        for g in range(steps):
+            b, other = (even, odd) if g % 2 == 0 else (odd, even)
+            if g + 1 < steps:
+                taken(g + 1).wait()
+                build(g + 1, other)
+            out_held[g] = mul(a_twice[...], b[...]) + mul(a_low[...], b[:depth, :])
+            given(g).start()
+        for g in range(steps):
+            given(g).wait()
+
+    anywhere = pl.BlockSpec(memory_space=pl.ANY)
+    return pl.pallas_call(
+        kernel,
+        in_specs=[pl.BlockSpec(memory_space=pltpu.SMEM)] * 3 + [anywhere] * (5 + len(after)),
+        out_specs=anywhere,
+        out_shape=jax.ShapeDtypeStruct((size, width), f32),
+        scratch_shapes=[pltpu.VMEM((steps, size, wide), f32)] * 2
+        + [pltpu.VMEM(a.shape, bf16) for a in prepared]
+        + [
+            pltpu.VMEM((2 * depth, wide), bf16),
+            pltpu.VMEM((2 * depth, wide), bf16),
+            pltpu.SemaphoreType.DMA((2, steps)),
+            pltpu.SemaphoreType.DMA((4,)),
+        ],
         compiler_params=params(),
         cost_estimate=cost(0, 0),
         name="alpha_sum",
     )(device, cross_pairs, cross_signs, columns, *prepared, *after)
-    return out[0], (out[1] if with_dot else None)
 
 
 def earlier(lanes):
@@ -351,59 +395,78 @@
     return list(out)
 
 
-def finish(returned, beta_term, chunk, parts, width, previous, extra=None):
+def finish(returned, beta_term, extra=None):
     rows, cols = beta_term.shape
-    full = 1 if extra is None else 3
+    parts, _, width = returned.shape
     sums = [] if extra is None else extra[0]
+    wholes = [beta_term] + ([] if extra is None else [extra[1], extra[2]])
+    count = len(wholes)
+    outs = 1 if extra is None else 2
 
     def kernel(*refs):
-        refs = list(refs)
+        sum_refs = refs[: len(sums)]
+        whole_refs = refs[len(sums) : len(sums) + count]
+        part_ref = refs[len(sums) + count]
+        out_refs = refs[len(sums) + count + 1 :][:outs]
+        held, sems, out_sems = refs[-3:]
+
+        def at(j):
+            return pl.ds(pl.multiple_of(j * width, SB), width)
+
+        def taken(j):
+            copies = [
+                pltpu.make_async_copy(whole_refs[i].at[:, at(j)], held.at[i, j], sems.at[i, j]) for i in range(count)
+            ]
+            return copies + [pltpu.make_async_copy(part_ref.at[j], held.at[count, j], sems.at[count, j])]
+
+        def given(j):
+            copies = [pltpu.make_async_copy(held.at[count, j], out_refs[0].at[:, at(j)], out_sems.at[0, j])]
+            if extra is not None:
+                copies.append(pltpu.make_async_copy(held.at[count, j], out_refs[1].at[j], out_sems.at[1, j]))
+            return copies
+
+        for j in range(parts):
+            for copy in taken(j):
+                copy.start()
+        theta = None
         if extra is not None:
-            sum_refs = refs[: len(sums)]
-            del refs[: len(sums)]
-            theta_ref = refs.pop()
-
-            @pl.when(pl.program_id(0) == 0)
-            def _():
-                total = sum_refs[0][...]
-                for ref in sum_refs[1:]:
-                    total = total + ref[...]
-                both = [jnp.sum(total[i : i + 1], axis=1, keepdims=True) for i in range(2)]
-                theta_ref[...] = jnp.broadcast_to(both[0] / both[1], theta_ref.shape)
-
-        value = refs[0][...] + refs[full][0]
-        outs = refs[full + 1 + (previous is not None) :]
-        if extra is not None:
-            value = (value - theta_ref[0:1, 0:1] * refs[1][...]) / refs[2][...]
-            outs[1][0] = value
-        outs[0][...] = value
-
-    whole = pl.BlockSpec((rows, width), lambda j: (0, chunk * parts + j))
-    part = pl.BlockSpec((1, rows, width), lambda j: (j, 0, 0))
-    in_specs = [pl.BlockSpec(a.shape, lambda j: (0, 0)) for a in sums] + [whole] * full + [part]
-    arrays = list(sums) + [beta_term] + ([] if extra is None else [extra[1], extra[2]]) + [returned]
-    aliases = {}
-    if previous is not None:
-        aliases = {len(arrays): 0}
-        in_specs = in_specs + [pl.BlockSpec(memory_space=pl.ANY)]
-        arrays = arrays + [previous]
-    out_specs = [whole]
-    out_shape = [jax.ShapeDtypeStruct((rows, cols), f32)]
-    if extra is not None:
-        out_specs += [part]
-        out_shape += [jax.ShapeDtypeStruct((parts, rows, width), f32)]
-    return pl.pallas_call(
-        kernel,
-        grid=(parts,),
-        in_specs=in_specs,
-        out_specs=out_specs,
-        scratch_shapes=[] if extra is None else [pltpu.VMEM((8, SB), f32)],
-        out_shape=out_shape,
-        input_output_aliases=aliases,
+            total = sum_refs[0][...]
+            for ref in sum_refs[1:]:
+                total = total + ref[...]
+            both = [jnp.sum(total[i : i + 1], axis=1, keepdims=True) for i in range(2)]
+            theta = both[0] / both[1]
+
+        def step(j, _):
+            for copy in taken(j):
+                copy.wait()
+            value = held[0, j] + held[count, j]
+            if extra is not None:
+                value = (value - theta * held[1, j]) / held[2, j]
+            held[count, j] = value
+            for copy in given(j):
+                copy.start()
+            return 0
+
+        lax.fori_loop(0, parts, step, 0)
+        for j in range(parts):
+            for copy in given(j):
+                copy.wait()
+
+    anywhere = pl.BlockSpec(memory_space=pl.ANY)
+    return pl.pallas_call(
+        kernel,
+        in_specs=[pl.BlockSpec(memory_space=pltpu.VMEM)] * len(sums) + [anywhere] * (count + 1),
+        out_specs=[anywhere] * outs,
+        out_shape=[jax.ShapeDtypeStruct((rows, cols), f32), jax.ShapeDtypeStruct((parts, rows, width), f32)][:outs],
+        scratch_shapes=[
+            pltpu.VMEM((count + 1, parts, rows, width), f32),
+            pltpu.SemaphoreType.DMA((count + 1, parts)),
+            pltpu.SemaphoreType.DMA((outs, parts)),
+        ],
         compiler_params=params(),
         cost_estimate=cost(0, 0),
         name="finish" if extra is None else "correct",
-    )(*arrays)
+    )(*sums, *wholes, returned)
 
 
 def make_local(n_alpha, n_beta):
@@ -429,16 +492,15 @@
     ):
         rows, cols = start_vector.shape
         blocks = cols // SB
-        chunks = divisor(blocks // n_alpha, CHUNKS)
-        width = cols // (n_alpha * chunks)
+        width = cols // n_alpha
         cap = (blocks + 1) // 2
         device = lax.axis_index("alpha").astype(jnp.int32).reshape(1)
         me = lax.axis_index("beta").astype(jnp.int32)
 
-        sent = [pack(start_vector, c, n_alpha, width) for c in range(chunks)]
-        arrived = [turn(parts) for parts in sent]
-
-        *marks, found = mark(source_blocks, me.reshape(1), n_beta, sent[:1])
+        sent = pack(start_vector, n_alpha)
+        arrived = turn(sent)
+
+        *marks, found = mark(source_blocks, me.reshape(1), n_beta, [sent])
         worst = marks[0][1:2, :1]
         marks = to_partners(marks)
         for other in marks:
@@ -479,19 +541,15 @@
             return lax.cond(too_many, more, lambda done: done, done)
 
         def alpha_side(arrived, with_dot, after):
-            sides = []
-            for c, parts in enumerate(arrived):
-                columns = parts.reshape(n_alpha * rows, width)
-                total, dot = alpha_sum(
-                    columns, prepared, cross_pairs, cross_signs, device, c, n_alpha, with_dot, after
-                )
-                sides.append((turn(total.reshape(n_alpha, rows, width)), dot, total))
-            return sides
+            columns = arrived.reshape(n_alpha * rows, width)
+            total = alpha_sum(columns, prepared, cross_pairs, cross_signs, device, after)
+            dot = jnp.sum(columns * total, axis=0, keepdims=True) if with_dot else None
+            return turn(total.reshape(n_alpha, rows, width)), dot, total
 
         received, token = beta_send(start_vector, first_plan, [])
         prepared = prepare(alpha_hamiltonian, alpha_pairs, pair_tables, [])
-        sides = alpha_side(arrived, True, token)
-        beta_term, sums = beta_side(start_vector, received, [], [side[1] for side in sides], True)
+        returned, dot, _ = alpha_side(arrived, True, token)
+        beta_term, sums = beta_side(start_vector, received, [], [dot], True)
         for other in to_partners([sums] * (n_beta - 1)):
             sums = sums + other
         sums = sums + lax.ppermute(sums, "alpha", [(i, i ^ 1) for i in range(n_alpha)])
@@ -500,18 +558,12 @@
             pairs = [(i, ((i // 2 + k) % chips) * 2 + i % 2) for i in range(n_alpha)]
             all_sums.append(lax.ppermute(sums, "alpha", pairs))
 
-        correction = None
-        arrived = []
-        for c in range(chunks):
-            extra = (all_sums, start_vector, precondition)
-            correction, parts = finish(sides[c][0], beta_term, c, n_alpha, width, correction, extra)
-            arrived.append(turn(parts))
+        correction, parts = finish(returned, beta_term, (all_sums, start_vector, precondition))
+        arrived = turn(parts)
         received, token = beta_send(correction, first_plan, [])
-        sides = alpha_side(arrived, False, token)
-        (beta_term,) = beta_side(correction, received, [side[2] for side in sides])
-        sigma_next = None
-        for c in range(chunks):
-            (sigma_next,) = finish(sides[c][0], beta_term, c, n_alpha, width, sigma_next)
+        returned, _, total = alpha_side(arrived, False, token)
+        (beta_term,) = beta_side(correction, received, [total])
+        (sigma_next,) = finish(returned, beta_term)
         return correction, sigma_next
 
     return local

time: 352 us -> 342 us (0.972)
  Pallas kernels: 86.6 us -> 77.5 us
  other arithmetic: 0.63 us -> 4.42 us
    pallas_call x5, Pallas kernels: 42.4 us -> 33.2 us  [the longest x2 18.7 us: alpha_sum(): pl.pallas_call(kernel, in_specs=[pl.BlockSpec(memory_space=pltpu.SMEM)] *...]
    ppermute x12, waiting for transfers between devices: 140 us -> 136 us  [to_partners(): lax.ppermute(part, 'beta', [(i, i ^ k) for i in range(n_beta)])]
    reduce_sum x0 -> x1, other arithmetic: none -> 3.79 us  [alpha_side(): dot = jnp.sum(columns * total, axis=0, keepdims=True) if with_dot else None]
  transfers between devices with their start and end apart: 20 -> 20, of which waited for: 18 -> 18; matrix products, arithmetic and copies ran while one was open for 1% -> 2% of each run, Pallas kernels for 13% -> 13%
where the time goes in v3:
time: 342 us; the launch traced here: 341 us
  waiting for transfers between devices  210 us (61%)
  Pallas kernels  77.5 us (23%)
  starting transfers between devices  42 us (12%)
  other arithmetic  4.42 us (1%)
  local copies, waits for them, and re-layouts  4.23 us (1%)
  between operations  3.62 us (1%)
    ppermute x12, waiting for transfers between devices, to_partners(): lax.ppermute(part, 'beta', [(i, i ^ k) for i in range(n_beta)])  136 us
    all_to_all x4, waiting for transfers between devices, turn(): return lax.all_to_all(parts, 'alpha', 0, 0, tiled=True)  66.4 us
    pallas_call x2, Pallas kernels, beta_sum(): pl.pallas_call(kernel, grid_spec=pltpu.PrefetchScalarGridSpec(num_scalar_...  29.4 us
    all_to_all x4, starting transfers between devices, turn(): return lax.all_to_all(parts, 'alpha', 0, 0, tiled=True)  20.2 us
    pallas_call x2, Pallas kernels, alpha_sum(): pl.pallas_call(kernel, in_specs=[pl.BlockSpec(memory_space=pltpu.SMEM)] *...  18.7 us
    ppermute x12, starting transfers between devices, to_partners(): lax.ppermute(part, 'beta', [(i, i ^ k) for i in range(n_beta)])  17.2 us
    pallas_call x2, Pallas kernels, finish(): pl.pallas_call(kernel, in_specs=[pl.BlockSpec(memory_space=pltpu.VMEM)] *...  11.7 us
    pallas_call x2, Pallas kernels, gather_blocks(): pl.pallas_call(kernel, grid_spec=pltpu.PrefetchScalarGridSpec(num_scalar_...  8.84 us
  transfers between devices with their start and end apart: 20, of which 18 were waited for; matrix products, arithmetic and copies ran while one was open for 2% of the time, Pallas kernels for 13%

profile of v3, /device:TPU:0, one launch (start us, length us, event | category | flops | bytes accessed | tf_op | source)
XLA Modules:
  0.0 341.4 jit_solution(10003190973362519090)
XLA Ops:
  0.6 2.8 pack.1.refs_0_
  3.4 0.0 copy-start.3
  3.4 6.3 %all-to-all-start = ((f32[8,32,3072]{2,1,0:T(8,128)}), f32[8,32,3072]{2,1,0:T(8,128)}, u32[]{:S(2)}, u32[]{:S(2)}) async-start(f32[8,32,3072]{2,1,0:T(8,128)} %pack.1.refs_0_), calls=%async_computation | async-start | bytes 6291456 | tf_op jit(solution)/shard_map/all_to_all | solution.py:479
  9.8 0.8 copy.12.source_ref
  10.6 2.9 mark.1
  13.5 1.6 collective-permute-start.7
  15.1 1.4 collective-permute-start.8
  16.5 0.5 collective-permute-start.6
  17.1 0.4 collective-permute-done.7.refs_1_
  17.4 2.4 collective-permute-done.8.refs_2_
  19.9 0.5 collective-permute-done.6.refs_0_
  20.4 0.8 positions.5.slots_ref
  21.1 4.4 %gather_blocks.6 = (f32[97,32,128]{2,1,0:T(8,128)}, f32[97,32,128]{2,1,0:T(8,128)}, f32[97,32,128]{2,1,0:T(8,128)}) custom-call(s32[8,256]{1,0:T(8,128)} %positions.5.slots_ref, f32[32,24576]{1,0:T(8,128)S(1)} %copy-done), custom_call_target="tpu_custom_call" | custom-call | flops 1 | bytes 1 | tf_op jit(solution)/shard_map/gather_blocks/pallas_call | solution.py:276
  25.6 1.0 collective-permute-start.9
  26.5 1.1 collective-permute-start.10
  27.6 2.4 prepare.1
  30.0 31.7 %collective-permute-done.9.refs_4_.refs_2_ = f32[97,32,128]{2,1,0:T(8,128)} collective-permute-done((f32[97,32,128]{2,1,0:T(8,128)}, f32[97,32,128]{2,1,0:T(8,128)}, u32[]{:S(2)}, u32[]{:S(2)}) %collective-permute-start.9) | collective-permute-done | bytes 1589280 | tf_op jit(solution)/shard_map/ppermute | solution.py:476
  61.7 1.0 collective-permute-done.10.refs_5_.refs_3_
  62.7 18.7 %all-to-all-done = f32[8,32,3072]{2,1,0:T(8,128)} async-done(((f32[8,32,3072]{2,1,0:T(8,128)}), f32[8,32,3072]{2,1,0:T(8,128)}, u32[]{:S(2)}, u32[]{:S(2)}) %all-to-all-start) | async-done | bytes 3145760 | tf_op jit(solution)/shard_map/all_to_all | solution.py:479
  81.4 9.4 %alpha_sum.2 = f32[256,3072]{1,0:T(8,128)} custom-call(s32[1]{0:T(128)} %bitcast.10.device_ref, s32[2,192]{1,0:T(2,128)} %pairs_ref.3, s32[2,192]{1,0:T(2,128)} %signs_ref.3, f32[256,3072]{1,0:T(8,128)} %bitcast.9.v_any, bf16[256,1536]{1,0:T(8,128)(2,1)} %get-tuple-element.114.refs_0_, bf16[256,768]{1,0:T(8,128)(2,1)} %get-tuple-element.115.refs_1_, ...), custom_call_target="tpu_custom_call" | custom-call | flops 1 | bytes 1 | tf_op jit(solution)/shard_map/alpha_sum/pallas_call | solution.py:165
  90.8 0.0 copy-start.5
  90.8 4.5 %all-to-all-start.1 = ((f32[8,32,3072]{2,1,0:T(8,128)}), f32[8,32,3072]{2,1,0:T(8,128)}, u32[]{:S(2)}, u32[]{:S(2)}) async-start(f32[8,32,3072]{2,1,0:T(8,128)} %bitcast.23), calls=%async_computation.1 | async-start | bytes 6291456 | tf_op jit(solution)/shard_map/all_to_all | solution.py:479
  95.3 2.5 collective-permute-start.11
  97.8 1.2 slice.12
  99.0 0.1 copy.13
  99.0 0.6 fusion.2
  99.7 0.6 slice.16
  101.6 0.5 slice.17
  102.8 0.5 slice.18
  103.9 0.0 copy-start.4
  103.9 3.8 %multiply_reduce_fusion = f32[3072]{0:T(1024)} fusion(f32[256,3072]{1,0:T(8,128)} %alpha_sum.2, f32[8,32,3072]{2,1,0:T(8,128)} %all-to-all-done), kind=kLoop, calls=%fused_computation.10 | loop fusion | flops 1569792 | bytes 6303744 | tf_op jit(solution)/shard_map/reduce_sum | solution.py:546
  107.7 25.8 %collective-permute-done.11.refs_4_ = f32[97,32,128]{2,1,0:T(8,128)} collective-permute-done((f32[97,32,128]{2,1,0:T(8,128)}, f32[97,32,128]{2,1,0:T(8,128)}, u32[]{:S(2)}, u32[]{:S(2)}) %collective-permute-start.11) | collective-permute-done | bytes 1589280 | tf_op jit(solution)/shard_map/ppermute | solution.py:476
  133.5 15.2 %beta_sum.6 = (f32[32,24576]{1,0:T(8,128)}, f32[8,128]{1,0:T(8,128)S(1)}) custom-call(s32[2,192]{1,0:T(2,128)} %get-tuple-element.155.slots_ref, s32[2,192]{1,0:T(2,128)} %get-tuple-element.154.sign_ref, s32[2,192]{1,0:T(2,128)S(1)} %bitcast.25, f32[32,24576]{1,0:T(8,128)S(1)} %copy-done, f32[4,128,128]{2,1,0:T(8,128)S(1)} %copy-done.2, ...), custom_call_target="tpu_custom_call" | custom-call | flops 1 | bytes 1 | tf_op jit(solution)/shard_map/beta_sum/pallas_call | solution.py:368
  148.7 2.5 collective-permute-start.14
  151.2 0.5 collective-permute-start.13
  151.7 0.5 collective-permute-start.12
  152.2 1.0 collective-permute-done.14
  153.3 1.6 collective-permute-done.13
  154.8 0.5 collective-permute-done.12
  155.3 0.0 collective-permute-start.15
  155.3 1.2 collective-permute-done.15
  156.5 3.5 %collective-permute-start.18 = (f32[8,128]{1,0:T(8,128)S(1)}, f32[8,128]{1,0:T(8,128)S(1)}, u32[]{:S(2)}, u32[]{:S(2)}) collective-permute-start(f32[8,128]{1,0:T(8,128)S(1)} %add.52.refs_0_), channel_id=1, source_target_pairs={{0,24},{4,28},{8,0},{12,4},{16,8},{20,12},{24,16},{28,20},{1,25},{... | collective-permute-start | bytes 12296 | tf_op jit(solution)/shard_map/ppermute | solution.py:559
  160.0 0.0 collective-permute-start.17
  160.0 1.1 collective-permute-start.16
  161.1 0.2 collective-permute-done.18.refs_3_
  161.3 5.8 %collective-permute-done.17.refs_2_ = f32[8,128]{1,0:T(8,128)S(1)} collective-permute-done((f32[8,128]{1,0:T(8,128)S(1)}, f32[8,128]{1,0:T(8,128)S(1)}, u32[]{:S(2)}, u32[]{:S(2)}) %collective-permute-start.17) | collective-permute-done | bytes 4128 | tf_op jit(solution)/shard_map/ppermute | solution.py:559
  167.1 0.0 collective-permute-done.16.refs_1_
  167.1 0.6 copy-done.8
  167.7 7.3 %correct.1 = (f32[32,24576]{1,0:T(8,128)}, f32[8,32,3072]{2,1,0:T(8,128)}) custom-call(f32[8,128]{1,0:T(8,128)} %copy-done.6, f32[8,128]{1,0:T(8,128)} %collective-permute-done.16.refs_1_, f32[8,128]{1,0:T(8,128)} %copy-done.8, f32[8,128]{1,0:T(8,128)} %copy-done.7, f32[32,24576]{1,0:T(8,128)} %get-tuple-element.121.refs_4_, f32[32,24576]{1,0:T(8,128)S(1)} %copy-done, ...), custom_call_target="tpu_custom_call" | custom-call | flops 1 | bytes 1 | tf_op jit(solution)/shard_map/correct/pallas_call | solution.py:456
  175.0 0.0 copy-start.1
  175.0 4.9 %all-to-all-start.2 = ((f32[8,32,3072]{2,1,0:T(8,128)}), f32[8,32,3072]{2,1,0:T(8,128)}, u32[]{:S(2)}, u32[]{:S(2)}) async-start(f32[8,32,3072]{2,1,0:T(8,128)} %get-tuple-element.126), calls=%async_computation.2 | async-start | bytes 6291456 | tf_op jit(solution)/shard_map/all_to_all | solution.py:479
  179.9 4.4 %gather_blocks.7 = (f32[97,32,128]{2,1,0:T(8,128)}, f32[97,32,128]{2,1,0:T(8,128)}, f32[97,32,128]{2,1,0:T(8,128)}) custom-call(s32[8,256]{1,0:T(8,128)} %positions.5.slots_ref, f32[32,24576]{1,0:T(8,128)S(1)} %copy-done.1), custom_call_target="tpu_custom_call" | custom-call | flops 1 | bytes 1 | tf_op jit(solution)/shard_map/gather_blocks/pallas_call | solution.py:276
  184.3 1.5 collective-permute-start.19
  185.8 1.5 collective-permute-start.20
  187.3 34.3 %collective-permute-done.19.refs_4_.refs_2_ = f32[97,32,128]{2,1,0:T(8,128)} collective-permute-done((f32[97,32,128]{2,1,0:T(8,128)}, f32[97,32,128]{2,1,0:T(8,128)}, u32[]{:S(2)}, u32[]{:S(2)}) %collective-permute-start.19) | collective-permute-done | bytes 1589280 | tf_op jit(solution)/shard_map/ppermute | solution.py:476
  221.6 1.2 collective-permute-done.20.refs_5_.refs_3_
  222.9 28.6 %all-to-all-done.2 = f32[8,32,3072]{2,1,0:T(8,128)} async-done(((f32[8,32,3072]{2,1,0:T(8,128)}), f32[8,32,3072]{2,1,0:T(8,128)}, u32[]{:S(2)}, u32[]{:S(2)}) %all-to-all-start.2) | async-done | bytes 3145760 | tf_op jit(solution)/shard_map/all_to_all | solution.py:479
  251.4 9.4 %alpha_sum.3.refs_5_ = f32[256,3072]{1,0:T(8,128)} custom-call(s32[1]{0:T(128)} %bitcast.10.device_ref, s32[2,192]{1,0:T(2,128)} %pairs_ref.3, s32[2,192]{1,0:T(2,128)} %signs_ref.3, f32[256,3072]{1,0:T(8,128)} %bitcast.13.v_any, bf16[256,1536]{1,0:T(8,128)(2,1)} %get-tuple-element.114.refs_0_, bf16[256,768]{1,0:T(8,128)(2,1)} %get-tuple-element.115.refs_1_, ...), custom_call_target="tpu_custom_call" | custom-call | flops 1 | bytes 1 | tf_op jit(solution)/shard_map/alpha_sum/pallas_call | solution.py:165
  260.8 4.5 %all-to-all-start.3 = ((f32[8,32,3072]{2,1,0:T(8,128)}), f32[8,32,3072]{2,1,0:T(8,128)}, u32[]{:S(2)}, u32[]{:S(2)}) async-start(f32[8,32,3072]{2,1,0:T(8,128)} %bitcast.22), calls=%async_computation.3 | async-start | bytes 6291456 | tf_op jit(solution)/shard_map/all_to_all | solution.py:479
  265.3 2.5 collective-permute-start.21
  267.8 35.7 %collective-permute-done.21.refs_4_ = f32[97,32,128]{2,1,0:T(8,128)} collective-permute-done((f32[97,32,128]{2,1,0:T(8,128)}, f32[97,32,128]{2,1,0:T(8,128)}, u32[]{:S(2)}, u32[]{:S(2)}) %collective-permute-start.21) | collective-permute-done | bytes 1589280 | tf_op jit(solution)/shard_map/ppermute | solution.py:476
  303.5 14.2 %beta_sum.7 = f32[32,24576]{1,0:T(8,128)} custom-call(s32[2,192]{1,0:T(2,128)} %get-tuple-element.155.slots_ref, s32[2,192]{1,0:T(2,128)} %get-tuple-element.154.sign_ref, s32[2,192]{1,0:T(2,128)S(1)} %bitcast.27, f32[32,24576]{1,0:T(8,128)S(1)} %copy-done.1, f32[4,128,128]{2,1,0:T(8,128)S(1)} %copy-done.2, ...), custom_call_target="tpu_custom_call" | custom-call | flops 1 | bytes 1 | tf_op jit(solution)/shard_map/beta_sum/pallas_call | solution.py:368
  317.7 19.1 %all-to-all-done.3.refs_1_ = f32[8,32,3072]{2,1,0:T(8,128)} async-done(((f32[8,32,3072]{2,1,0:T(8,128)}), f32[8,32,3072]{2,1,0:T(8,128)}, u32[]{:S(2)}, u32[]{:S(2)}) %all-to-all-start.3) | async-done | bytes 3145760 | tf_op jit(solution)/shard_map/all_to_all | solution.py:479
  336.8 4.5 %finish.1 = f32[32,24576]{1,0:T(8,128)} custom-call(f32[32,24576]{1,0:T(8,128)} %get-tuple-element.161.refs_0_, f32[8,32,3072]{2,1,0:T(8,128)} %all-to-all-done.3.refs_1_), custom_call_target="tpu_custom_call" | custom-call | flops 1 | bytes 1 | tf_op jit(solution)/shard_map/finish/pallas_call | solution.py:456
  (18 shorter events, 0.1 us)
Async XLA Ops:
  3.4 6.4 %copy-start.3 = (s32[192,2]{0,1:T(2,128)S(1)}, s32[192,2]{0,1:T(2,128)}, u32[]{:S(2)}) copy-start(s32[192,2]{0,1:T(2,128)} %param.19) | copy-start | bytes 4612
  3.4 78.0 %all-to-all-start = ((f32[8,32,3072]{2,1,0:T(8,128)}), f32[8,32,3072]{2,1,0:T(8,128)}, u32[]{:S(2)}, u32[]{:S(2)}) async-start(f32[8,32,3072]{2,1,0:T(8,128)} %pack.1.refs_0_), calls=%async_computation | async-start | bytes 6291456 | tf_op jit(solution)/shard_map/all_to_all | solution.py:479
  10.5 10.6 %copy-start = (f32[32,24576]{1,0:T(8,128)S(1)}, f32[32,24576]{1,0:T(8,128)}, u32[]{:S(2)}) copy-start(f32[32,24576]{1,0:T(8,128)} %refs_5_.1) | copy-start | bytes 9437188
  13.5 3.9 %collective-permute-start.7 = (f32[8,256]{1,0:T(8,128)}, f32[8,256]{1,0:T(8,128)S(1)}, u32[]{:S(2)}, u32[]{:S(2)}) collective-permute-start(f32[8,256]{1,0:T(8,128)} %get-tuple-element.108), channel_id=1, source_target_pairs={{0,2},{1,3},{2,0},{3,1},{4,6},{5,7},{6,4},{7,5},{8,10},{9,11},{10,... | collective-permute-start | bytes 24584 | tf_op jit(solution)/shard_map/ppermute | solution.py:476
  15.1 4.8 %collective-permute-start.8 = (f32[8,256]{1,0:T(8,128)}, f32[8,256]{1,0:T(8,128)S(1)}, u32[]{:S(2)}, u32[]{:S(2)}) collective-permute-start(f32[8,256]{1,0:T(8,128)} %get-tuple-element.109), channel_id=1, source_target_pairs={{0,3},{1,2},{2,1},{3,0},{4,7},{5,6},{6,5},{7,4},{8,11},{9,10},{10,... | collective-permute-start | bytes 24584 | tf_op jit(solution)/shard_map/ppermute | solution.py:476
  16.5 11.1 %copy-start.2 = (f32[4,128,128]{2,1,0:T(8,128)S(1)}, f32[4,128,128]{2,1,0:T(8,128)}, u32[]{:S(2)}) copy-start(f32[4,128,128]{2,1,0:T(8,128)} %refs_1_.3) | copy-start | bytes 786436
  16.5 3.9 %collective-permute-start.6 = (f32[8,256]{1,0:T(8,128)}, f32[8,256]{1,0:T(8,128)S(1)}, u32[]{:S(2)}, u32[]{:S(2)}) collective-permute-start(f32[8,256]{1,0:T(8,128)} %get-tuple-element.107), channel_id=1, source_target_pairs={{0,1},{1,0},{2,3},{3,2},{4,5},{5,4},{6,7},{7,6},{8,9},{9,8},{10,11... | collective-permute-start | bytes 24584 | tf_op jit(solution)/shard_map/ppermute | solution.py:476
  25.6 36.2 %collective-permute-start.9 = (f32[97,32,128]{2,1,0:T(8,128)}, f32[97,32,128]{2,1,0:T(8,128)}, u32[]{:S(2)}, u32[]{:S(2)}) collective-permute-start(f32[97,32,128]{2,1,0:T(8,128)} %get-tuple-element.111), channel_id=1, source_target_pairs={{0,1},{1,0},{2,3},{3,2},{4,5},{5,4},{6,7},{7,6},{8,9},{9,8},{10,11... | collective-permute-start | bytes 4767752 | tf_op jit(solution)/shard_map/ppermute | solution.py:476
  26.5 36.2 %collective-permute-start.10 = (f32[97,32,128]{2,1,0:T(8,128)}, f32[97,32,128]{2,1,0:T(8,128)}, u32[]{:S(2)}, u32[]{:S(2)}) collective-permute-start(f32[97,32,128]{2,1,0:T(8,128)} %get-tuple-element.112), channel_id=1, source_target_pairs={{0,2},{1,3},{2,0},{3,1},{4,6},{5,7},{6,4},{7,5},{8,10},{9,11},{10,... | collective-permute-start | bytes 4767752 | tf_op jit(solution)/shard_map/ppermute | solution.py:476
  90.8 8.3 %copy-start.5 = (s32[192,2]{0,1:T(2,128)S(1)}, s32[192,2]{0,1:T(2,128)}, u32[]{:S(2)}) copy-start(s32[192,2]{0,1:T(2,128)} %param.21) | copy-start | bytes 4612
  90.8 76.3 %all-to-all-start.1 = ((f32[8,32,3072]{2,1,0:T(8,128)}), f32[8,32,3072]{2,1,0:T(8,128)}, u32[]{:S(2)}, u32[]{:S(2)}) async-start(f32[8,32,3072]{2,1,0:T(8,128)} %bitcast.23), calls=%async_computation.1 | async-start | bytes 6291456 | tf_op jit(solution)/shard_map/all_to_all | solution.py:479
  95.3 38.2 %collective-permute-start.11 = (f32[97,32,128]{2,1,0:T(8,128)}, f32[97,32,128]{2,1,0:T(8,128)}, u32[]{:S(2)}, u32[]{:S(2)}) collective-permute-start(f32[97,32,128]{2,1,0:T(8,128)} %get-tuple-element.113), channel_id=1, source_target_pairs={{0,3},{1,2},{2,1},{3,0},{4,7},{5,6},{6,5},{7,4},{8,11},{9,10},{10,... | collective-permute-start | bytes 4767752 | tf_op jit(solution)/shard_map/ppermute | solution.py:476
  103.9 29.6 %copy-start.4 = (s32[192,2]{0,1:T(2,128)S(1)}, s32[192,2]{0,1:T(2,128)}, u32[]{:S(2)}) copy-start(s32[192,2]{0,1:T(2,128)} %param.20) | copy-start | bytes 4612
  148.7 4.6 %collective-permute-start.14 = (f32[8,128]{1,0:T(8,128)S(1)}, f32[8,128]{1,0:T(8,128)S(1)}, u32[]{:S(2)}, u32[]{:S(2)}) collective-permute-start(f32[8,128]{1,0:T(8,128)S(1)} %get-tuple-element.120), channel_id=1, source_target_pairs={{0,3},{1,2},{2,1},{3,0},{4,7},{5,6},{6,5},{7,4},{8,11},{9,10},{10,... | collective-permute-start | bytes 12296 | tf_op jit(solution)/shard_map/ppermute | solution.py:476
  151.2 3.6 %collective-permute-start.13 = (f32[8,128]{1,0:T(8,128)S(1)}, f32[8,128]{1,0:T(8,128)S(1)}, u32[]{:S(2)}, u32[]{:S(2)}) collective-permute-start(f32[8,128]{1,0:T(8,128)S(1)} %get-tuple-element.120), channel_id=1, source_target_pairs={{0,2},{1,3},{2,0},{3,1},{4,6},{5,7},{6,4},{7,5},{8,10},{9,11},{10,... | collective-permute-start | bytes 12296 | tf_op jit(solution)/shard_map/ppermute | solution.py:476
  151.7 3.6 %collective-permute-start.12 = (f32[8,128]{1,0:T(8,128)S(1)}, f32[8,128]{1,0:T(8,128)S(1)}, u32[]{:S(2)}, u32[]{:S(2)}) collective-permute-start(f32[8,128]{1,0:T(8,128)S(1)} %get-tuple-element.120), channel_id=1, source_target_pairs={{0,1},{1,0},{2,3},{3,2},{4,5},{5,4},{6,7},{7,6},{8,9},{9,8},{10,11... | collective-permute-start | bytes 12296 | tf_op jit(solution)/shard_map/ppermute | solution.py:476
  155.3 1.2 collective-permute-start.15
  156.5 10.6 %copy-start.6 = (f32[8,128]{1,0:T(8,128)}, f32[8,128]{1,0:T(8,128)S(1)}, u32[]{:S(2)}) copy-start(f32[8,128]{1,0:T(8,128)S(1)} %add.52.refs_0_) | copy-start | bytes 12292
  156.5 4.8 %collective-permute-start.18 = (f32[8,128]{1,0:T(8,128)S(1)}, f32[8,128]{1,0:T(8,128)S(1)}, u32[]{:S(2)}, u32[]{:S(2)}) collective-permute-start(f32[8,128]{1,0:T(8,128)S(1)} %add.52.refs_0_), channel_id=1, source_target_pairs={{0,24},{4,28},{8,0},{12,4},{16,8},{20,12},{24,16},{28,20},{1,25},{... | collective-permute-start | bytes 12296 | tf_op jit(solution)/shard_map/ppermute | solution.py:559
  160.0 7.1 %collective-permute-start.17 = (f32[8,128]{1,0:T(8,128)S(1)}, f32[8,128]{1,0:T(8,128)S(1)}, u32[]{:S(2)}, u32[]{:S(2)}) collective-permute-start(f32[8,128]{1,0:T(8,128)S(1)} %add.52.refs_0_), channel_id=1, source_target_pairs={{0,16},{4,20},{8,24},{12,28},{16,0},{20,4},{24,8},{28,12},{1,17},{... | collective-permute-start | bytes 12296 | tf_op jit(solution)/shard_map/ppermute | solution.py:559
  160.0 7.1 %collective-permute-start.16 = (f32[8,128]{1,0:T(8,128)S(1)}, f32[8,128]{1,0:T(8,128)}, u32[]{:S(2)}, u32[]{:S(2)}) collective-permute-start(f32[8,128]{1,0:T(8,128)S(1)} %add.52.refs_0_), channel_id=1, source_target_pairs={{0,8},{4,12},{8,16},{12,20},{16,24},{20,28},{24,0},{28,4},{1,9},{5... | collective-permute-start | bytes 12296 | tf_op jit(solution)/shard_map/ppermute | solution.py:559
  161.3 5.8 %copy-start.7 = (f32[8,128]{1,0:T(8,128)}, f32[8,128]{1,0:T(8,128)S(1)}, u32[]{:S(2)}) copy-start(f32[8,128]{1,0:T(8,128)S(1)} %collective-permute-done.18.refs_3_) | copy-start | bytes 12292
  167.1 0.6 copy-start.8
  175.0 4.9 %copy-start.1 = (f32[32,24576]{1,0:T(8,128)S(1)}, f32[32,24576]{1,0:T(8,128)}, u32[]{:S(2)}) copy-start(f32[32,24576]{1,0:T(8,128)} %get-tuple-element.105.v_ref.refs_0_) | copy-start | bytes 9437188
  175.0 76.5 %all-to-all-start.2 = ((f32[8,32,3072]{2,1,0:T(8,128)}), f32[8,32,3072]{2,1,0:T(8,128)}, u32[]{:S(2)}, u32[]{:S(2)}) async-start(f32[8,32,3072]{2,1,0:T(8,128)} %get-tuple-element.126), calls=%async_computation.2 | async-start | bytes 6291456 | tf_op jit(solution)/shard_map/all_to_all | solution.py:479
  184.3 37.3 %collective-permute-start.19 = (f32[97,32,128]{2,1,0:T(8,128)}, f32[97,32,128]{2,1,0:T(8,128)}, u32[]{:S(2)}, u32[]{:S(2)}) collective-permute-start(f32[97,32,128]{2,1,0:T(8,128)} %get-tuple-element.123), channel_id=1, source_target_pairs={{0,1},{1,0},{2,3},{3,2},{4,5},{5,4},{6,7},{7,6},{8,9},{9,8},{10,11... | collective-permute-start | bytes 4767752 | tf_op jit(solution)/shard_map/ppermute | solution.py:476
  185.8 37.0 %collective-permute-start.20 = (f32[97,32,128]{2,1,0:T(8,128)}, f32[97,32,128]{2,1,0:T(8,128)}, u32[]{:S(2)}, u32[]{:S(2)}) collective-permute-start(f32[97,32,128]{2,1,0:T(8,128)} %get-tuple-element.124), channel_id=1, source_target_pairs={{0,2},{1,3},{2,0},{3,1},{4,6},{5,7},{6,4},{7,5},{8,10},{9,11},{10,... | collective-permute-start | bytes 4767752 | tf_op jit(solution)/shard_map/ppermute | solution.py:476
  260.8 76.0 %all-to-all-start.3 = ((f32[8,32,3072]{2,1,0:T(8,128)}), f32[8,32,3072]{2,1,0:T(8,128)}, u32[]{:S(2)}, u32[]{:S(2)}) async-start(f32[8,32,3072]{2,1,0:T(8,128)} %bitcast.22), calls=%async_computation.3 | async-start | bytes 6291456 | tf_op jit(solution)/shard_map/all_to_all | solution.py:479
  265.3 38.2 %collective-permute-start.21 = (f32[97,32,128]{2,1,0:T(8,128)}, f32[97,32,128]{2,1,0:T(8,128)}, u32[]{:S(2)}, u32[]{:S(2)}) collective-permute-start(f32[97,32,128]{2,1,0:T(8,128)} %get-tuple-element.125), channel_id=1, source_target_pairs={{0,3},{1,2},{2,1},{3,0},{4,7},{5,6},{6,5},{7,4},{8,11},{9,10},{10,... | collective-permute-start | bytes 4767752 | tf_op jit(solution)/shard_map/ppermute | solution.py:476

commit v4 on v3

--- a/solution.py
+++ b/solution.py
@@ -6,6 +6,8 @@
 from jax.sharding import PartitionSpec as P
 
 SB = 128
+SHARE = 0.375
+WORK = 20_000_000_000
 VMEM_BYTES = 60 * 1024 * 1024
 f32 = jnp.float32
 bf16 = jnp.bfloat16
@@ -29,7 +31,7 @@
 
 
 def cost(flops, count):
-    return pl.CostEstimate(flops=1, bytes_accessed=1, transcendentals=0)
+    return pl.CostEstimate(flops=max(flops, 1), bytes_accessed=max(count, 1), transcendentals=0)
 
 
 def prepare(alpha_hamiltonian, alpha_pairs, pair_tables, after):
@@ -63,60 +65,100 @@
     )(alpha_hamiltonian, alpha_pairs, pair_tables, *after)
 
 
-def pack(vector, parts):
-    rows, cols = vector.shape
-    width = cols // parts
-
-    def kernel(source, target, held, sems):
-        def taken(j):
-            at = pl.ds(pl.multiple_of(j * width, SB), width)
-            return pltpu.make_async_copy(source.at[:, at], held.at[j], sems.at[0, j])
-
-        def given(j):
-            return pltpu.make_async_copy(held.at[j], target.at[j], sems.at[1, j])
-
+def pack(vector, device, parts, wide, narrow):
+    rows = vector.shape[0]
+
+    def kernel(device_ref, source, *refs):
+        targets = refs[: 1 + parts]
+        held, few, sems = refs[-3:]
+        copies = []
         for j in range(parts):
-            taken(j).start()
-        for j in range(parts):
-            taken(j).wait()
-            given(j).start()
-        for j in range(parts):
-            given(j).wait()
-
-    return pl.pallas_call(
-        kernel,
-        in_specs=[pl.BlockSpec(memory_space=pl.ANY)],
-        out_specs=pl.BlockSpec(memory_space=pl.ANY),
-        out_shape=jax.ShapeDtypeStruct((parts, rows, width), f32),
-        scratch_shapes=[pltpu.VMEM((parts, rows, width), f32), pltpu.SemaphoreType.DMA((2, parts))],
+            copies.append((source.at[:, j * wide : (j + 1) * wide], held.at[j], targets[0].at[j]))
+        for k in range(parts):
+            at = pl.multiple_of(parts * wide + (device_ref[0] ^ k) * narrow, SB)
+            copies.append((source.at[:, pl.ds(at, narrow)], few.at[k], targets[1 + k]))
+        taken = [pltpu.make_async_copy(a, b, sems.at[0, i]) for i, (a, b, _) in enumerate(copies)]
+        given = [pltpu.make_async_copy(b, c, sems.at[1, i]) for i, (_, b, c) in enumerate(copies)]
+        for copy in taken:
+            copy.start()
+        for first, second in zip(taken, given):
+            first.wait()
+            second.start()
+        for copy in given:
+            copy.wait()
+
+    anywhere = pl.BlockSpec(memory_space=pl.ANY)
+    out = pl.pallas_call(
+        kernel,
+        in_specs=[pl.BlockSpec(memory_space=pltpu.SMEM), anywhere],
+        out_specs=[anywhere] * (1 + parts),
+        out_shape=[jax.ShapeDtypeStruct((parts, rows, wide), f32)]
+        + [jax.ShapeDtypeStruct((rows, narrow), f32)] * parts,
+        scratch_shapes=[
+            pltpu.VMEM((parts, rows, wide), f32),
+            pltpu.VMEM((parts, rows, narrow), f32),
+            pltpu.SemaphoreType.DMA((2, 2 * parts)),
+        ],
         compiler_params=params(),
         cost_estimate=cost(0, 0),
         name="pack",
-    )(vector)
-
-
-def alpha_sum(columns, prepared, cross_pairs, cross_signs, device, after):
-    size, width = columns.shape
+    )(device, vector)
+    return out[0], out[1:]
+
+
+def alpha_sum(columns, prepared, cross_pairs, cross_signs, device, start, after, work, full, offset, previous):
+    size, width = prepared[1].shape[0], columns[0].shape[1]
+    count = len(columns)
+    rows = size // count
     depth = prepared[1].shape[1]
     nq = cross_pairs.shape[0]
     blocks = width // SB
-    per = divisor(blocks, 8)
+    per = divisor(blocks, 9)
     steps = blocks // per
     wide = per * SB
 
-    def kernel(device_ref, pairs_ref, signs_ref, v_any, *refs):
-        prepared_any = refs[:4]
-        out_any = refs[4 + len(after)]
+    def kernel(device_ref, pairs_ref, signs_ref, *refs):
+        v_any = refs[:count]
+        prepared_any = refs[count : count + 4]
+        outs = refs[count + 4 + len(after) + len(previous) :][: 1 if full else count]
         v_held, out_held, a_twice, a_low, t_high, t_low, even, odd, sems, once = refs[-10:]
 
         def at(g):
             return pl.ds(pl.multiple_of(g * wide, SB), wide)
 
+        def row(k):
+            return pl.ds(pl.multiple_of((device_ref[0] ^ k) * rows, rows) if count > 1 else 0, rows)
+
+        class Several:
+            def __init__(self, copies):
+                self.copies = copies
+
+            def start(self):
+                for copy in self.copies:
+                    copy.start()
+
+            def wait(self):
+                for copy in self.copies:
+                    copy.wait()
+
         def taken(g):
-            return pltpu.make_async_copy(v_any.at[:, at(g)], v_held.at[g], sems.at[0, g])
+            return Several(
+                [
+                    pltpu.make_async_copy(v_any[k].at[:, at(g)], v_held.at[g, row(k)], sems.at[0, g, k])
+                    for k in range(count)
+                ]
+            )
 
         def given(g):
-            return pltpu.make_async_copy(out_held.at[g], out_any.at[:, at(g)], sems.at[1, g])
+            if full:
+                to = pl.ds(offset + g * wide, wide)
+                return pltpu.make_async_copy(out_held.at[g], outs[0].at[:, to], sems.at[1, g, 0])
+            return Several(
+                [
+                    pltpu.make_async_copy(out_held.at[g, row(k)], outs[k].at[:, at(g)], sems.at[1, g, k])
+                    for k in range(count)
+                ]
+            )
 
         held = (a_twice, a_low, t_high, t_low)
         loads = [pltpu.make_async_copy(prepared_any[i], held[i], once.at[i]) for i in range(4)]
@@ -134,7 +176,7 @@
             high, low = halves(v_held[g])
             b[:size, :] = high
             b[depth : depth + size, :] = low
-            first = device_ref[0] * blocks + g * per
+            first = start + device_ref[0] * blocks + g * per
             for t in range(per):
                 here = slice(t * SB, (t + 1) * SB)
                 both = jnp.concatenate([high[:, here], low[:, here]], axis=1)
@@ -164,21 +206,24 @@
     anywhere = pl.BlockSpec(memory_space=pl.ANY)
     return pl.pallas_call(
         kernel,
-        in_specs=[pl.BlockSpec(memory_space=pltpu.SMEM)] * 3 + [anywhere] * (5 + len(after)),
-        out_specs=anywhere,
-        out_shape=jax.ShapeDtypeStruct((size, width), f32),
+        in_specs=[pl.BlockSpec(memory_space=pltpu.SMEM)] * 3 + [anywhere] * (count + 4 + len(after) + len(previous)),
+        out_specs=[anywhere] * (1 if full else count),
+        out_shape=[jax.ShapeDtypeStruct((size, full), f32)]
+        if full
+        else [jax.ShapeDtypeStruct((rows, width), f32)] * count,
+        input_output_aliases={3 + count + 4 + len(after): 0} if previous else {},
         scratch_shapes=[pltpu.VMEM((steps, size, wide), f32)] * 2
         + [pltpu.VMEM(a.shape, bf16) for a in prepared]
         + [
             pltpu.VMEM((2 * depth, wide), bf16),
             pltpu.VMEM((2 * depth, wide), bf16),
-            pltpu.SemaphoreType.DMA((2, steps)),
+            pltpu.SemaphoreType.DMA((2, steps, count)),
             pltpu.SemaphoreType.DMA((4,)),
         ],
         compiler_params=params(),
-        cost_estimate=cost(0, 0),
+        cost_estimate=cost(work, work // 300),
         name="alpha_sum",
-    )(device, cross_pairs, cross_signs, columns, *prepared, *after)
+    )(device, cross_pairs, cross_signs, *columns, *prepared, *after, *previous)
 
 
 def earlier(lanes):
@@ -289,7 +334,7 @@
     )(slots, vector, *after)
 
 
-def beta_sum(vector, received, slots, signs, pair_index, pair_tables, after, dots=None, with_dot=False):
+def beta_sum(vector, received, slots, signs, pair_index, pair_tables, after, dots=None, with_dot=False, work=0):
     rows, cols = vector.shape
     blocks = cols // SB
     npair = pair_tables.shape[0]
@@ -389,84 +434,164 @@
         out_shape=[jax.ShapeDtypeStruct((rows, cols), f32)]
         + ([jax.ShapeDtypeStruct((8, SB), f32)] if with_dot else []),
         compiler_params=params(),
-        cost_estimate=cost(0, 0),
+        cost_estimate=cost(work, work // 300),
         name="beta_sum",
     )(slots, signs, pair_index, vector, pair_tables, *received, *after, *dots)
     return list(out)
 
 
-def finish(returned, beta_term, extra=None):
+def correct(returned, beta_term, device, wide, narrow, extra):
     rows, cols = beta_term.shape
-    parts, _, width = returned.shape
+    parts = returned.shape[0]
     sums = [] if extra is None else extra[0]
     wholes = [beta_term] + ([] if extra is None else [extra[1], extra[2]])
     count = len(wholes)
-    outs = 1 if extra is None else 2
-
-    def kernel(*refs):
+    sent = 0 if extra is None else 1 + parts
+
+    def kernel(device_ref, *refs):
         sum_refs = refs[: len(sums)]
-        whole_refs = refs[len(sums) : len(sums) + count]
+        whole_refs = refs[len(sums) :][:count]
         part_ref = refs[len(sums) + count]
-        out_refs = refs[len(sums) + count + 1 :][:outs]
-        held, sems, out_sems = refs[-3:]
-
-        def at(j):
-            return pl.ds(pl.multiple_of(j * width, SB), width)
-
-        def taken(j):
-            copies = [
-                pltpu.make_async_copy(whole_refs[i].at[:, at(j)], held.at[i, j], sems.at[i, j]) for i in range(count)
-            ]
-            return copies + [pltpu.make_async_copy(part_ref.at[j], held.at[count, j], sems.at[count, j])]
-
-        def given(j):
-            copies = [pltpu.make_async_copy(held.at[count, j], out_refs[0].at[:, at(j)], out_sems.at[0, j])]
-            if extra is not None:
-                copies.append(pltpu.make_async_copy(held.at[count, j], out_refs[1].at[j], out_sems.at[1, j]))
-            return copies
-
+        out_refs = refs[len(sums) + count + 1 :][: 1 + sent]
+        held, few, sems, out_sems = refs[-4:]
+        pieces = []
         for j in range(parts):
-            for copy in taken(j):
+            pieces.append((held, j, j * wide, part_ref.at[j, :, :wide], out_refs[1].at[j] if sent else None))
+        for k in range(parts):
+            place = device_ref[0] ^ k
+            at = pl.multiple_of(parts * wide + place * narrow, SB)
+            pieces.append((few, k, at, part_ref.at[place, :, wide:], out_refs[2 + k] if sent else None))
+        taken = []
+        given = []
+        for p, (buffer, j, start, part, target) in enumerate(pieces):
+            at = pl.ds(start, buffer.shape[-1])
+            taken.append(
+                [pltpu.make_async_copy(whole_refs[i].at[:, at], buffer.at[i, j], sems.at[i, p]) for i in range(count)]
+                + [pltpu.make_async_copy(part, buffer.at[count, j], sems.at[count, p])]
+            )
+            given.append([pltpu.make_async_copy(buffer.at[count, j], out_refs[0].at[:, at], out_sems.at[0, p])])
+            if sent:
+                given[-1].append(pltpu.make_async_copy(buffer.at[count, j], target, out_sems.at[1, p]))
+        for copies in taken:
+            for copy in copies:
                 copy.start()
-        theta = None
         if extra is not None:
             total = sum_refs[0][...]
             for ref in sum_refs[1:]:
                 total = total + ref[...]
             both = [jnp.sum(total[i : i + 1], axis=1, keepdims=True) for i in range(2)]
             theta = both[0] / both[1]
-
-        def step(j, _):
-            for copy in taken(j):
+        for p, (buffer, j, _, _, _) in enumerate(pieces):
+            for copy in taken[p]:
+                copy.wait()
+            value = buffer[0, j] + buffer[count, j]
+            if extra is not None:
+                value = (value - theta * buffer[1, j]) / buffer[2, j]
+            buffer[count, j] = value
+            for copy in given[p]:
+                copy.start()
+        for copies in given:
+            for copy in copies:
+                copy.wait()
+
+    anywhere = pl.BlockSpec(memory_space=pl.ANY)
+    shapes = [(rows, cols), (parts, rows, wide)] + [(rows, narrow)] * parts
+    out = pl.pallas_call(
+        kernel,
+        in_specs=[pl.BlockSpec(memory_space=pltpu.SMEM)]
+        + [pl.BlockSpec(memory_space=pltpu.VMEM)] * len(sums)
+        + [anywhere] * (count + 1),
+        out_specs=[anywhere] * (1 + sent),
+        out_shape=[jax.ShapeDtypeStruct(shape, f32) for shape in shapes[: 1 + sent]],
+        scratch_shapes=[
+            pltpu.VMEM((count + 1, parts, rows, wide), f32),
+            pltpu.VMEM((count + 1, parts, rows, narrow), f32),
+            pltpu.SemaphoreType.DMA((count + 1, 2 * parts)),
+            pltpu.SemaphoreType.DMA((2, 2 * parts)),
+        ],
+        compiler_params=params(),
+        cost_estimate=cost(0, 0),
+        name="finish" if extra is None else "correct",
+    )(device, *sums, *wholes, returned)
+    return out if extra is not None else out[0]
+
+
+def finish(returned, beta_term, device, start, previous, extra=None, work=0):
+    rows, cols = beta_term.shape
+    listed = isinstance(returned, (list, tuple))
+    arrays = list(returned) if listed else [returned]
+    parts = len(arrays) if listed else returned.shape[0]
+    width = arrays[0].shape[-1]
+    sums = [] if extra is None else extra[0]
+    wholes = [beta_term] + ([] if extra is None else [extra[1], extra[2]])
+    count = len(wholes)
+    aliased = [] if previous is None else [previous]
+    sent = [] if extra is None else arrays
+
+    def kernel(device_ref, *refs):
+        sum_refs = refs[: len(sums)]
+        whole_refs = refs[len(sums) :][:count]
+        part_refs = refs[len(sums) + count :][: len(arrays)]
+        out_refs = refs[len(sums) + count + len(arrays) + len(aliased) :][: 1 + len(sent)]
+        held, sems, out_sems = refs[-3:]
+
+        def piece(among, j):
+            return among[j] if listed else among[0].at[j]
+
+        taken = []
+        given = []
+        for j in range(parts):
+            place = device_ref[0] ^ j if listed else j
+            at = pl.ds(pl.multiple_of(start + place * width, SB), width)
+            taken.append(
+                [pltpu.make_async_copy(whole_refs[i].at[:, at], held.at[i, j], sems.at[i, j]) for i in range(count)]
+                + [pltpu.make_async_copy(piece(part_refs, j), held.at[count, j], sems.at[count, j])]
+            )
+            given.append([pltpu.make_async_copy(held.at[count, j], out_refs[0].at[:, at], out_sems.at[0, j])])
+            if sent:
+                target = piece(out_refs[1:], j)
+                given[-1].append(pltpu.make_async_copy(held.at[count, j], target, out_sems.at[1, j]))
+        for copies in taken:
+            for copy in copies:
+                copy.start()
+        if extra is not None:
+            total = sum_refs[0][...]
+            for ref in sum_refs[1:]:
+                total = total + ref[...]
+            both = [jnp.sum(total[i : i + 1], axis=1, keepdims=True) for i in range(2)]
+            theta = both[0] / both[1]
+        for j in range(parts):
+            for copy in taken[j]:
                 copy.wait()
             value = held[0, j] + held[count, j]
             if extra is not None:
                 value = (value - theta * held[1, j]) / held[2, j]
             held[count, j] = value
-            for copy in given(j):
+            for copy in given[j]:
                 copy.start()
-            return 0
-
-        lax.fori_loop(0, parts, step, 0)
-        for j in range(parts):
-            for copy in given(j):
+        for copies in given:
+            for copy in copies:
                 copy.wait()
 
     anywhere = pl.BlockSpec(memory_space=pl.ANY)
-    return pl.pallas_call(
-        kernel,
-        in_specs=[pl.BlockSpec(memory_space=pltpu.VMEM)] * len(sums) + [anywhere] * (count + 1),
-        out_specs=[anywhere] * outs,
-        out_shape=[jax.ShapeDtypeStruct((rows, cols), f32), jax.ShapeDtypeStruct((parts, rows, width), f32)][:outs],
+    out = pl.pallas_call(
+        kernel,
+        in_specs=[pl.BlockSpec(memory_space=pltpu.SMEM)]
+        + [pl.BlockSpec(memory_space=pltpu.VMEM)] * len(sums)
+        + [anywhere] * (count + len(arrays) + len(aliased)),
+        out_specs=[anywhere] * (1 + len(sent)),
+        out_shape=[jax.ShapeDtypeStruct(a.shape, f32) for a in [beta_term] + sent],
+        input_output_aliases={1 + len(sums) + count + len(arrays): 0} if aliased else {},
         scratch_shapes=[
             pltpu.VMEM((count + 1, parts, rows, width), f32),
             pltpu.SemaphoreType.DMA((count + 1, parts)),
-            pltpu.SemaphoreType.DMA((outs, parts)),
+            pltpu.SemaphoreType.DMA((2, parts)),
         ],
         compiler_params=params(),
-        cost_estimate=cost(0, 0),
+        cost_estimate=cost(work, work // 300),
         name="finish" if extra is None else "correct",
-    )(*sums, *wholes, returned)
+    )(device, *sums, *wholes, *arrays, *aliased)
+    return out[0], out[1:]
 
 
 def make_local(n_alpha, n_beta):
@@ -477,6 +602,12 @@
 
     def turn(parts):
         return lax.all_to_all(parts, "alpha", 0, 0, tiled=True)
+
+    def swap(parts):
+        moved = list(parts)
+        for k in range(n_alpha - 1, 0, -1):
+            moved[k] = lax.ppermute(parts[k], "alpha", [(i, i ^ k) for i in range(n_alpha)])
+        return moved
 
     def local(
         start_vector,
@@ -492,13 +623,17 @@
     ):
         rows, cols = start_vector.shape
         blocks = cols // SB
-        width = cols // n_alpha
+        mine = blocks // n_alpha
+        few = max(1, round(mine * SHARE))
+        wide, narrow = (mine - few) * SB, few * SB
+        border = n_alpha * wide
         cap = (blocks + 1) // 2
         device = lax.axis_index("alpha").astype(jnp.int32).reshape(1)
         me = lax.axis_index("beta").astype(jnp.int32)
 
-        sent = pack(start_vector, n_alpha)
+        sent, sent_few = pack(start_vector, device, n_alpha, wide, narrow)
         arrived = turn(sent)
+        arrived_few = swap(sent_few)
 
         *marks, found = mark(source_blocks, me.reshape(1), n_beta, [sent])
         worst = marks[0][1:2, :1]
@@ -522,14 +657,14 @@
         def beta_send(vector, planned, after):
             sent = gather_blocks(vector, planned[0], n_beta - 1, cap, after)
             received = to_partners(sent)
-            return received, received[:2]
-
-        def beta_round(vector, received, planned, after, dots=None, with_dot=False):
+            return received, (received[:2], received[2:])
+
+        def beta_round(vector, received, planned, after, dots=None, with_dot=False, work=0):
             _, slots, signs = planned
-            return beta_sum(vector, received, slots, signs, pairs_by_k, pair_tables, after, dots, with_dot)
-
-        def beta_side(vector, received, after, dots=None, with_dot=False):
-            done = beta_round(vector, received, first_plan, after, dots, with_dot)
+            return beta_sum(vector, received, slots, signs, pairs_by_k, pair_tables, after, dots, with_dot, work)
+
+        def beta_side(vector, received, after, dots=None, with_dot=False, work=0):
+            done = beta_round(vector, received, first_plan, after, dots, with_dot, work)
 
             def more(done):
                 for r in range(1, -(-blocks // cap)):
@@ -540,16 +675,19 @@
 
             return lax.cond(too_many, more, lambda done: done, done)
 
-        def alpha_side(arrived, with_dot, after):
-            columns = arrived.reshape(n_alpha * rows, width)
-            total = alpha_sum(columns, prepared, cross_pairs, cross_signs, device, after)
-            dot = jnp.sum(columns * total, axis=0, keepdims=True) if with_dot else None
-            return turn(total.reshape(n_alpha, rows, width)), dot, total
-
         received, token = beta_send(start_vector, first_plan, [])
         prepared = prepare(alpha_hamiltonian, alpha_pairs, pair_tables, [])
-        returned, dot, _ = alpha_side(arrived, True, token)
-        beta_term, sums = beta_side(start_vector, received, [], [dot], True)
+        common = (prepared, cross_pairs, cross_signs, device)
+        width = wide + narrow
+        columns = arrived.reshape(n_alpha * rows, wide)
+        first = alpha_sum([columns], *common, 0, token[0], WORK, width, 0, [])
+        (total,) = alpha_sum(arrived_few, *common, border // SB, [], 0, width, wide, first)
+        returned = turn(total.reshape(n_alpha, rows, width))
+        dots = [jnp.sum(columns * total[:, :wide], axis=0, keepdims=True)]
+        last = total[:, wide:].reshape(n_alpha, rows, narrow)
+        few = [lax.dynamic_index_in_dim(last, device[0] ^ k, 0, keepdims=False) for k in range(n_alpha)]
+        dots.append(sum(jnp.sum(a * b, axis=0, keepdims=True) for a, b in zip(arrived_few, few)))
+        beta_term, sums = beta_side(start_vector, received, [], dots, True)
         for other in to_partners([sums] * (n_beta - 1)):
             sums = sums + other
         sums = sums + lax.ppermute(sums, "alpha", [(i, i ^ 1) for i in range(n_alpha)])
@@ -558,12 +696,19 @@
             pairs = [(i, ((i // 2 + k) % chips) * 2 + i % 2) for i in range(n_alpha)]
             all_sums.append(lax.ppermute(sums, "alpha", pairs))
 
-        correction, parts = finish(returned, beta_term, (all_sums, start_vector, precondition))
+        extra = (all_sums, start_vector, precondition)
+        correction, parts, *few = correct(returned, beta_term, device, wide, narrow, extra)
         arrived = turn(parts)
+        arrived_few = swap(few)
         received, token = beta_send(correction, first_plan, [])
-        returned, _, total = alpha_side(arrived, False, token)
-        (beta_term,) = beta_side(correction, received, [total])
-        (sigma_next,) = finish(returned, beta_term)
+        columns = arrived.reshape(n_alpha * rows, wide)
+        (total,) = alpha_sum([columns], *common, 0, token[0], WORK, wide, 0, [])
+        returned = turn(total.reshape(n_alpha, rows, wide))
+        totals = alpha_sum(arrived_few, *common, border // SB, [total, *token[1]], 10 * WORK, 0, 0, [])
+        returned_few = swap(totals)
+        (beta_term,) = beta_side(correction, received, totals[:1], work=WORK)
+        sigma_next, _ = finish(returned, beta_term, device, 0, None, None, WORK)
+        sigma_next, _ = finish(returned_few, beta_term, device, border, sigma_next)
         return correction, sigma_next
 
     return local

time: 342 us -> 320 us (0.936); the launches traced: 341 us -> 315 us
  waiting for transfers between devices: 210 us -> 130 us
  starting transfers between devices: 42 us -> 79.2 us
  Pallas kernels: 77.5 us -> 89.3 us
  local copies, waits for them, and re-layouts: 4.23 us -> 8.29 us
    ppermute x12, waiting for transfers between devices: 136 us -> 53.5 us  [to_partners(): lax.ppermute(part, 'beta', [(i, i ^ k) for i in range(n_beta)])]
    ppermute x0 -> x21, waiting for transfers between devices: none -> 38.8 us  [swap(): lax.ppermute(parts[k], 'alpha', [(i, i ^ k) for i in range(n_alpha)])]
    all_to_all x4, waiting for transfers between devices: 66.4 us -> 30.6 us  [turn(): return lax.all_to_all(parts, 'alpha', 0, 0, tiled=True)]
    ppermute x0 -> x21, starting transfers between devices: none -> 33.1 us  [swap(): lax.ppermute(parts[k], 'alpha', [(i, i ^ k) for i in range(n_alpha)])]
    pallas_call x2 -> x4, Pallas kernels: 18.7 us -> 27.7 us  [alpha_sum(): pl.pallas_call(kernel, in_specs=[pl.BlockSpec(memory_space=pltpu.SMEM)] *...]
    all_to_all x4, starting transfers between devices: 20.2 us -> 24.2 us  [turn(): return lax.all_to_all(parts, 'alpha', 0, 0, tiled=True)]
    pallas_call x3 -> x4, Pallas kernels: 14.5 us -> 17.1 us  [the longest x1 8.02 us: correct(): pl.pallas_call(kernel, in_specs=[pl.BlockSpec(memory_space=pltpu.SMEM)] +...]
  transfers between devices with their start and end apart: 20 -> 41, of which waited for: 18 -> 17; matrix products, arithmetic and copies ran while one was open for 2% -> 3% of each run, Pallas kernels for 13% -> 22%
where the time goes in v4:
time: 320 us; the launch traced here: 315 us
  waiting for transfers between devices  130 us (41%)
  Pallas kernels  89.3 us (28%)
  starting transfers between devices  79.2 us (25%)
  local copies, waits for them, and re-layouts  8.29 us (3%)
  other arithmetic  4.5 us (1%)
  between operations  4.06 us (1%)
    ppermute x12, waiting for transfers between devices, to_partners(): lax.ppermute(part, 'beta', [(i, i ^ k) for i in range(n_beta)])  53.5 us
    ppermute x21, waiting for transfers between devices, swap(): lax.ppermute(parts[k], 'alpha', [(i, i ^ k) for i in range(n_alpha)])  38.8 us
    ppermute x21, starting transfers between devices, swap(): lax.ppermute(parts[k], 'alpha', [(i, i ^ k) for i in range(n_alpha)])  33.1 us
    all_to_all x4, waiting for transfers between devices, turn(): return lax.all_to_all(parts, 'alpha', 0, 0, tiled=True)  30.6 us
    pallas_call x2, Pallas kernels, beta_sum(): pl.pallas_call(kernel, grid_spec=pltpu.PrefetchScalarGridSpec(num_scalar_...  29.6 us
    pallas_call x4, Pallas kernels, alpha_sum(): pl.pallas_call(kernel, in_specs=[pl.BlockSpec(memory_space=pltpu.SMEM)] *...  27.7 us
    all_to_all x4, starting transfers between devices, turn(): return lax.all_to_all(parts, 'alpha', 0, 0, tiled=True)  24.2 us
    ppermute x12, starting transfers between devices, to_partners(): lax.ppermute(part, 'beta', [(i, i ^ k) for i in range(n_beta)])  17.1 us
  transfers between devices with their start and end apart: 41, of which 17 were waited for; matrix products, arithmetic and copies ran while one was open for 3% of the time, Pallas kernels for 22%

profile of v4, /device:TPU:0, one launch (start us, length us, event | category | flops | bytes accessed | tf_op | source)
XLA Modules:
  0.0 315.1 jit_solution(11504134854509043628)
XLA Ops:
  0.6 3.2 %pack.1 = (f32[8,32,1920]{2,1,0:T(8,128)}, f32[32,1152]{1,0:T(8,128)}, f32[32,1152]{1,0:T(8,128)}, f32[32,1152]{1,0:T(8,128)}, f32[32,1152]{1,0:T(8,128)}, /*ind...) custom-call(s32[1]{0:T(128)} %bitcast.4.device_ref, f32[32,24576]{1,0:T(8,128)} %refs_5_.1), custom_call_target="tpu_custom_call" | custom-call | flops 1 | bytes 1 | tf_op jit(solution)/shard_map/pack/pallas_call | solution.py:91
  3.9 6.6 %all-to-all-start = ((f32[8,32,1920]{2,1,0:T(8,128)}), f32[8,32,1920]{2,1,0:T(8,128)}, u32[]{:S(2)}, u32[]{:S(2)}) async-start(f32[8,32,1920]{2,1,0:T(8,128)} %get-tuple-element.132.refs_0_), calls=%async_computation | async-start | bytes 3932160 | tf_op jit(solution)/shard_map/all_to_all | solution.py:604
  10.5 0.8 copy.14.source_ref
  11.3 2.8 mark.1
  14.1 1.6 collective-permute-start.7
  15.7 1.4 collective-permute-start.8
  18.0 2.4 collective-permute-done.8.refs_2_
  21.0 0.8 positions.5.slots_ref
  21.7 4.4 %gather_blocks.6 = (f32[97,32,128]{2,1,0:T(8,128)}, f32[97,32,128]{2,1,0:T(8,128)}, f32[97,32,128]{2,1,0:T(8,128)}) custom-call(s32[8,256]{1,0:T(8,128)} %positions.5.slots_ref, f32[32,24576]{1,0:T(8,128)S(1)} %copy-done), custom_call_target="tpu_custom_call" | custom-call | flops 1 | bytes 1 | tf_op jit(solution)/shard_map/gather_blocks/pallas_call | solution.py:321
  26.2 1.0 collective-permute-start.9
  27.1 1.1 collective-permute-start.10
  28.2 2.1 collective-permute-start.13
  30.4 2.3 prepare.1
  32.7 2.6 collective-permute-start.15
  35.3 11.2 %collective-permute-done.13.refs_2_ = f32[32,1152]{1,0:T(8,128)} collective-permute-done((f32[32,1152]{1,0:T(8,128)S(1)}, f32[32,1152]{1,0:T(8,128)}, u32[]{:S(2)}, u32[]{:S(2)}) %collective-permute-start.13) | collective-permute-done | bytes 147488 | tf_op jit(solution)/shard_map/ppermute | solution.py:609
  46.6 3.7 %collective-permute-start.16 = (f32[32,1152]{1,0:T(8,128)}, f32[32,1152]{1,0:T(8,128)}, u32[]{:S(2)}, u32[]{:S(2)}) collective-permute-start(f32[32,1152]{1,0:T(8,128)} %get-tuple-element.145), channel_id=1, source_target_pairs={{0,20},{4,16},{8,28},{12,24},{16,4},{20,0},{24,12},{28,8},{1,21},{... | collective-permute-start | bytes 442376 | tf_op jit(solution)/shard_map/ppermute | solution.py:609
  50.3 12.1 %collective-permute-done.9.refs_5_.refs_2_ = f32[97,32,128]{2,1,0:T(8,128)} collective-permute-done((f32[97,32,128]{2,1,0:T(8,128)}, f32[97,32,128]{2,1,0:T(8,128)}, u32[]{:S(2)}, u32[]{:S(2)}) %collective-permute-start.9) | collective-permute-done | bytes 1589280 | tf_op jit(solution)/shard_map/ppermute | solution.py:601
  62.3 3.5 %collective-permute-start.17 = (f32[32,1152]{1,0:T(8,128)}, f32[32,1152]{1,0:T(8,128)}, u32[]{:S(2)}, u32[]{:S(2)}) collective-permute-start(f32[32,1152]{1,0:T(8,128)} %get-tuple-element.146), channel_id=1, source_target_pairs={{0,24},{4,28},{8,16},{12,20},{16,8},{20,12},{24,0},{28,4},{1,25},{... | collective-permute-start | bytes 442376 | tf_op jit(solution)/shard_map/ppermute | solution.py:609
  65.8 7.4 %alpha_sum.4.refs_12_ = f32[256,3072]{1,0:T(8,128)} custom-call(s32[1]{0:T(128)} %bitcast.4.device_ref, s32[2,192]{1,0:T(2,128)} %pairs_ref.7, s32[2,192]{1,0:T(2,128)} %signs_ref.7, f32[256,1920]{1,0:T(8,128)} %bitcast.10.refs_0_, bf16[256,1536]{1,0:T(8,128)(2,1)} %get-tuple-element.148.refs_1_.refs_8_, ...), custom_call_target="tpu_custom_call" | custom-call | flops 20000000000 | bytes 66666664 | tf_op jit(solution)/shard_map/alpha_sum/pallas_call | solution.py:207
  73.2 2.1 collective-permute-done.16.refs_5_
  75.3 6.2 %alpha_sum.5 = f32[256,3072]{1,0:T(8,128)} custom-call(s32[1]{0:T(128)} %bitcast.4.device_ref, s32[2,192]{1,0:T(2,128)} %pairs_ref.7, s32[2,192]{1,0:T(2,128)} %signs_ref.7, f32[32,1152]{1,0:T(8,128)} %get-tuple-element.140.refs_0_, f32[32,1152]{1,0:T(8,128)} %collective-permute-done.12.refs_1_, ...), custom_call_target="tpu_custom_call", output_to_operand_aliasing={{}: (15, {})} | custom-call | flops 1 | bytes 1 | tf_op jit(solution)/shard_map/alpha_sum/pallas_call | solution.py:207
  81.5 8.4 %all-to-all-start.1 = ((f32[8,32,3072]{2,1,0:T(8,128)}), f32[8,32,3072]{2,1,0:T(8,128)}, u32[]{:S(2)}, u32[]{:S(2)}) async-start(f32[8,32,3072]{2,1,0:T(8,128)} %bitcast.54), calls=%async_computation.1 | async-start | bytes 6291456 | tf_op jit(solution)/shard_map/all_to_all | solution.py:604
  89.9 2.4 collective-permute-start.11
  92.4 1.2 slice.18
  98.5 1.4 slice.28
  99.9 2.4 fusion.2
  102.9 1.5 fusion.9
  105.0 23.3 %collective-permute-done.11.refs_4_ = f32[97,32,128]{2,1,0:T(8,128)} collective-permute-done((f32[97,32,128]{2,1,0:T(8,128)}, f32[97,32,128]{2,1,0:T(8,128)}, u32[]{:S(2)}, u32[]{:S(2)}) %collective-permute-start.11) | collective-permute-done | bytes 1589280 | tf_op jit(solution)/shard_map/ppermute | solution.py:601
  128.3 15.2 %beta_sum.6 = (f32[32,24576]{1,0:T(8,128)}, f32[8,128]{1,0:T(8,128)S(1)}) custom-call(s32[2,192]{1,0:T(2,128)} %get-tuple-element.213.slots_ref, s32[2,192]{1,0:T(2,128)} %get-tuple-element.212.sign_ref, s32[2,192]{1,0:T(2,128)S(1)} %bitcast.57, f32[32,24576]{1,0:T(8,128)S(1)} %copy-done, f32[4,128,128]{2,1,0:T(8,128)S(1)} %copy-done.4, ...), custom_call_target="tpu_custom_call" | custom-call | flops 1 | bytes 1 | tf_op jit(solution)/shard_map/beta_sum/pallas_call | solution.py:413
  143.8 2.5 collective-permute-start.21
  147.3 1.0 collective-permute-done.21
  148.3 1.5 collective-permute-done.20
  150.4 1.2 collective-permute-done.22
  151.6 3.5 %collective-permute-start.25 = (f32[8,128]{1,0:T(8,128)S(1)}, f32[8,128]{1,0:T(8,128)S(1)}, u32[]{:S(2)}, u32[]{:S(2)}) collective-permute-start(f32[8,128]{1,0:T(8,128)S(1)} %add.168.refs_0_), channel_id=1, source_target_pairs={{0,24},{4,28},{8,0},{12,4},{16,8},{20,12},{24,16},{28,20},{1,25},{... | collective-permute-start | bytes 12296 | tf_op jit(solution)/shard_map/ppermute | solution.py:697
  155.1 0.8 collective-permute-start.24
  156.4 5.6 %collective-permute-done.24.refs_2_ = f32[8,128]{1,0:T(8,128)S(1)} collective-permute-done((f32[8,128]{1,0:T(8,128)S(1)}, f32[8,128]{1,0:T(8,128)S(1)}, u32[]{:S(2)}, u32[]{:S(2)}) %collective-permute-start.24) | collective-permute-done | bytes 4128 | tf_op jit(solution)/shard_map/ppermute | solution.py:697
  162.6 8.0 %correct.1 = (f32[32,24576]{1,0:T(8,128)}, f32[8,32,1920]{2,1,0:T(8,128)}, f32[32,1152]{1,0:T(8,128)}, f32[32,1152]{1,0:T(8,128)}, f32[32,1152]{1,0:T(8,128)}, /...) custom-call(s32[1]{0:T(128)} %bitcast.4.device_ref, ...), custom_call_target="tpu_custom_call" | custom-call | flops 1 | bytes 1 | tf_op jit(solution)/shard_map/correct/pallas_call | solution.py:499
  170.6 4.6 %all-to-all-start.2 = ((f32[8,32,1920]{2,1,0:T(8,128)}), f32[8,32,1920]{2,1,0:T(8,128)}, u32[]{:S(2)}, u32[]{:S(2)}) async-start(f32[8,32,1920]{2,1,0:T(8,128)} %get-tuple-element.168), calls=%async_computation.2 | async-start | bytes 3932160 | tf_op jit(solution)/shard_map/all_to_all | solution.py:604
  175.3 4.6 %gather_blocks.7 = (f32[97,32,128]{2,1,0:T(8,128)}, f32[97,32,128]{2,1,0:T(8,128)}, f32[97,32,128]{2,1,0:T(8,128)}) custom-call(s32[8,256]{1,0:T(8,128)} %positions.5.slots_ref, f32[32,24576]{1,0:T(8,128)S(1)} %copy-done.1), custom_call_target="tpu_custom_call" | custom-call | flops 1 | bytes 1 | tf_op jit(solution)/shard_map/gather_blocks/pallas_call | solution.py:321
  179.9 1.5 collective-permute-start.26
  181.4 1.5 collective-permute-start.27
  182.9 1.9 collective-permute-start.30
  185.0 2.6 collective-permute-start.32
  187.6 23.7 %collective-permute-done.30.refs_2_ = f32[32,1152]{1,0:T(8,128)S(1)} collective-permute-done((f32[32,1152]{1,0:T(8,128)S(1)}, f32[32,1152]{1,0:T(8,128)S(1)}, u32[]{:S(2)}, u32[]{:S(2)}) %collective-permute-start.30) | collective-permute-done | bytes 147488 | tf_op jit(solution)/shard_map/ppermute | solution.py:609
  211.3 3.6 %collective-permute-start.33 = (f32[32,1152]{1,0:T(8,128)}, f32[32,1152]{1,0:T(8,128)}, u32[]{:S(2)}, u32[]{:S(2)}) collective-permute-start(f32[32,1152]{1,0:T(8,128)} %get-tuple-element.165), channel_id=1, source_target_pairs={{0,20},{4,16},{8,28},{12,24},{16,4},{20,0},{24,12},{28,8},{1,21},{... | collective-permute-start | bytes 442376 | tf_op jit(solution)/shard_map/ppermute | solution.py:609
  214.9 3.3 %collective-permute-start.34 = (f32[32,1152]{1,0:T(8,128)S(1)}, f32[32,1152]{1,0:T(8,128)}, u32[]{:S(2)}, u32[]{:S(2)}) collective-permute-start(f32[32,1152]{1,0:T(8,128)S(1)} %copy-done.34), channel_id=1, source_target_pairs={{0,24},{4,28},{8,16},{12,20},{16,8},{20,12},{24,0},{28,4},{1,25},{... | collective-permute-start | bytes 442376 | tf_op jit(solution)/shard_map/ppermute | solution.py:609
  218.2 1.5 collective-permute-start.35
  219.7 2.5 collective-permute-start.28
  222.2 12.4 %all-to-all-done.2 = f32[8,32,1920]{2,1,0:T(8,128)} async-done(((f32[8,32,1920]{2,1,0:T(8,128)}), f32[8,32,1920]{2,1,0:T(8,128)}, u32[]{:S(2)}, u32[]{:S(2)}) %all-to-all-start.2) | async-done | bytes 1966112 | tf_op jit(solution)/shard_map/all_to_all | solution.py:604
  234.6 7.5 %alpha_sum.6.refs_12_ = f32[256,1920]{1,0:T(8,128)} custom-call(s32[1]{0:T(128)} %bitcast.4.device_ref, s32[2,192]{1,0:T(2,128)} %pairs_ref.7, s32[2,192]{1,0:T(2,128)} %signs_ref.7, f32[256,1920]{1,0:T(8,128)} %bitcast.21.refs_0_, bf16[256,1536]{1,0:T(8,128)(2,1)} %get-tuple-element.148.refs_1_.refs_8_, ...), custom_call_target="tpu_custom_call" | custom-call | flops 20000000000 | bytes 66666664 | tf_op jit(solution)/shard_map/alpha_sum/pallas_call | solution.py:207
  242.1 4.6 %all-to-all-start.3 = ((f32[8,32,1920]{2,1,0:T(8,128)}), f32[8,32,1920]{2,1,0:T(8,128)}, u32[]{:S(2)}, u32[]{:S(2)}) async-start(f32[8,32,1920]{2,1,0:T(8,128)} %bitcast.56), calls=%async_computation.3 | async-start | bytes 3932160 | tf_op jit(solution)/shard_map/all_to_all | solution.py:604
  246.7 11.7 %collective-permute-done.28.refs_13_.refs_4_ = f32[97,32,128]{2,1,0:T(8,128)} collective-permute-done((f32[97,32,128]{2,1,0:T(8,128)}, f32[97,32,128]{2,1,0:T(8,128)}, u32[]{:S(2)}, u32[]{:S(2)}) %collective-permute-start.28) | collective-permute-done | bytes 1589280 | tf_op jit(solution)/shard_map/ppermute | solution.py:601
  258.5 6.6 %alpha_sum.7 = (f32[32,1152]{1,0:T(8,128)}, f32[32,1152]{1,0:T(8,128)}, f32[32,1152]{1,0:T(8,128)}, f32[32,1152]{1,0:T(8,128)}, f32[32,1152]{1,0:T(8,128)}, /*in...) custom-call(s32[1]{0:T(128)} %bitcast.4.device_ref, s32[2,192]{1,0:T(2,128)} %pairs_ref.7, ...), custom_call_target="tpu_custom_call" | custom-call | flops 199999995904 | bytes 666666688 | tf_op jit(solution)/shard_map/alpha_sum/pallas_call | solution.py:207
  265.4 14.3 %beta_sum.7 = f32[32,24576]{1,0:T(8,128)} custom-call(s32[2,192]{1,0:T(2,128)} %get-tuple-element.213.slots_ref, s32[2,192]{1,0:T(2,128)} %get-tuple-element.212.sign_ref, s32[2,192]{1,0:T(2,128)S(1)} %bitcast.59, f32[32,24576]{1,0:T(8,128)S(1)} %copy-done.2, f32[4,128,128]{2,1,0:T(8,128)S(1)} %copy-done.5, f32[97,32,128]{2,1,0:T(8,128)} %copy-done.31, ...), custom_call_target="tpu_custom_call" | custom-call | flops 20000000000 | bytes 66666664 | tf_op jit(solution)/shard_map/beta_sum/pallas_call | solution.py:413
  279.9 1.7 collective-permute-start.38
  282.1 2.2 collective-permute-start.40
  284.3 1.5 collective-permute-start.41
  285.9 1.9 collective-permute-start.42
  287.7 18.1 %all-to-all-done.3.refs_1_ = f32[8,32,1920]{2,1,0:T(8,128)} async-done(((f32[8,32,1920]{2,1,0:T(8,128)}), f32[8,32,1920]{2,1,0:T(8,128)}, u32[]{:S(2)}, u32[]{:S(2)}) %all-to-all-start.3) | async-done | bytes 1966112 | tf_op jit(solution)/shard_map/all_to_all | solution.py:604
  305.9 3.5 %finish.2.refs_9_ = f32[32,24576]{1,0:T(8,128)} custom-call(s32[1]{0:T(128)} %bitcast.4.device_ref, f32[32,24576]{1,0:T(8,128)} %get-tuple-element.219.refs_0_, f32[8,32,1920]{2,1,0:T(8,128)} %all-to-all-done.3.refs_1_), custom_call_target="tpu_custom_call" | custom-call | flops 20000000000 | bytes 66666664 | tf_op jit(solution)/shard_map/finish/pallas_call | solution.py:577
  309.4 1.7 collective-permute-done.40.refs_6_
  311.2 0.6 copy-done.11
  311.9 0.7 copy-done.13
  312.5 2.4 finish.3
  (134 shorter events, 9.2 us)
Async XLA Ops:
  3.9 17.9 %copy-start = (f32[32,24576]{1,0:T(8,128)S(1)}, f32[32,24576]{1,0:T(8,128)}, u32[]{:S(2)}) copy-start(f32[32,24576]{1,0:T(8,128)} %refs_5_.1) | copy-start | bytes 9437188
  3.9 61.9 %all-to-all-start = ((f32[8,32,1920]{2,1,0:T(8,128)}), f32[8,32,1920]{2,1,0:T(8,128)}, u32[]{:S(2)}, u32[]{:S(2)}) async-start(f32[8,32,1920]{2,1,0:T(8,128)} %get-tuple-element.132.refs_0_), calls=%async_computation | async-start | bytes 3932160 | tf_op jit(solution)/shard_map/all_to_all | solution.py:604
  14.1 129.5 %copy-start.6 = (s32[192,2]{1,0:T(8,128)}, s32[192,2]{1,0:T(8,128)S(1)}, u32[]{:S(2)}) copy-start(s32[192,2]{1,0:T(8,128)S(1)} %get-tuple-element.136) | copy-start | bytes 4612
  14.1 14.1 %copy-start.39 = (f32[32,1152]{1,0:T(8,128)S(1)}, f32[32,1152]{1,0:T(8,128)}, u32[]{:S(2)}) copy-start(f32[32,1152]{1,0:T(8,128)} %get-tuple-element.141) | copy-start | bytes 442372
  14.1 14.1 %copy-start.38 = (f32[32,1152]{1,0:T(8,128)S(1)}, f32[32,1152]{1,0:T(8,128)}, u32[]{:S(2)}) copy-start(f32[32,1152]{1,0:T(8,128)} %get-tuple-element.142) | copy-start | bytes 442372
  14.1 16.3 %copy-start.4 = (f32[4,128,128]{2,1,0:T(8,128)S(1)}, f32[4,128,128]{2,1,0:T(8,128)}, u32[]{:S(2)}) copy-start(f32[4,128,128]{2,1,0:T(8,128)} %refs_1_.3) | copy-start | bytes 786436
  14.1 3.9 %collective-permute-start.7 = (f32[8,256]{1,0:T(8,128)}, f32[8,256]{1,0:T(8,128)S(1)}, u32[]{:S(2)}, u32[]{:S(2)}) collective-permute-start(f32[8,256]{1,0:T(8,128)} %get-tuple-element.134), channel_id=1, source_target_pairs={{0,2},{1,3},{2,0},{3,1},{4,6},{5,7},{6,4},{7,5},{8,10},{9,11},{10,... | collective-permute-start | bytes 24584 | tf_op jit(solution)/shard_map/ppermute | solution.py:601
  15.7 4.8 %collective-permute-start.8 = (f32[8,256]{1,0:T(8,128)}, f32[8,256]{1,0:T(8,128)S(1)}, u32[]{:S(2)}, u32[]{:S(2)}) collective-permute-start(f32[8,256]{1,0:T(8,128)} %get-tuple-element.135), channel_id=1, source_target_pairs={{0,3},{1,2},{2,1},{3,0},{4,7},{5,6},{6,5},{7,4},{8,11},{9,10},{10,... | collective-permute-start | bytes 24584 | tf_op jit(solution)/shard_map/ppermute | solution.py:601
  17.1 3.9 %collective-permute-start.6 = (f32[8,256]{1,0:T(8,128)}, f32[8,256]{1,0:T(8,128)S(1)}, u32[]{:S(2)}, u32[]{:S(2)}) collective-permute-start(f32[8,256]{1,0:T(8,128)} %get-tuple-element.133), channel_id=1, source_target_pairs={{0,1},{1,0},{2,3},{3,2},{4,5},{5,4},{6,7},{7,6},{8,9},{9,8},{10,11... | collective-permute-start | bytes 24584 | tf_op jit(solution)/shard_map/ppermute | solution.py:601
  18.0 125.5 %copy-start.14 = (f32[8,256]{1,0:T(8,128)}, f32[8,256]{1,0:T(8,128)S(1)}, u32[]{:S(2)}) copy-start(f32[8,256]{1,0:T(8,128)S(1)} %collective-permute-done.7.refs_1_) | copy-start | bytes 24580
  20.5 123.1 %copy-start.16 = (f32[8,256]{1,0:T(8,128)}, f32[8,256]{1,0:T(8,128)S(1)}, u32[]{:S(2)}) copy-start(f32[8,256]{1,0:T(8,128)S(1)} %collective-permute-done.8.refs_2_) | copy-start | bytes 24580
  21.0 122.6 %copy-start.18 = (f32[8,256]{1,0:T(8,128)}, f32[8,256]{1,0:T(8,128)S(1)}, u32[]{:S(2)}) copy-start(f32[8,256]{1,0:T(8,128)S(1)} %collective-permute-done.6.refs_0_) | copy-start | bytes 24580
  26.2 36.2 %collective-permute-start.9 = (f32[97,32,128]{2,1,0:T(8,128)}, f32[97,32,128]{2,1,0:T(8,128)}, u32[]{:S(2)}, u32[]{:S(2)}) collective-permute-start(f32[97,32,128]{2,1,0:T(8,128)} %get-tuple-element.137), channel_id=1, source_target_pairs={{0,1},{1,0},{2,3},{3,2},{4,5},{5,4},{6,7},{7,6},{8,9},{9,8},{10,11... | collective-permute-start | bytes 4767752 | tf_op jit(solution)/shard_map/ppermute | solution.py:601
  27.1 38.7 %collective-permute-start.10 = (f32[97,32,128]{2,1,0:T(8,128)}, f32[97,32,128]{2,1,0:T(8,128)}, u32[]{:S(2)}, u32[]{:S(2)}) collective-permute-start(f32[97,32,128]{2,1,0:T(8,128)} %get-tuple-element.138), channel_id=1, source_target_pairs={{0,2},{1,3},{2,0},{3,1},{4,6},{5,7},{6,4},{7,5},{8,10},{9,11},{10,... | collective-permute-start | bytes 4767752 | tf_op jit(solution)/shard_map/ppermute | solution.py:601
  28.2 4.5 %collective-permute-start.12 = (f32[32,1152]{1,0:T(8,128)S(1)}, f32[32,1152]{1,0:T(8,128)}, u32[]{:S(2)}, u32[]{:S(2)}) collective-permute-start(f32[32,1152]{1,0:T(8,128)S(1)} %copy-done.39), channel_id=1, source_target_pairs={{0,4},{4,0},{8,12},{12,8},{16,20},{20,16},{24,28},{28,24},{1,5},{5... | collective-permute-start | bytes 442376 | tf_op jit(solution)/shard_map/ppermute | solution.py:609
  28.2 18.3 %collective-permute-start.13 = (f32[32,1152]{1,0:T(8,128)S(1)}, f32[32,1152]{1,0:T(8,128)}, u32[]{:S(2)}, u32[]{:S(2)}) collective-permute-start(f32[32,1152]{1,0:T(8,128)S(1)} %copy-done.38), channel_id=1, source_target_pairs={{0,8},{4,12},{8,0},{12,4},{16,24},{20,28},{24,16},{28,20},{1,9},{5... | collective-permute-start | bytes 442376 | tf_op jit(solution)/shard_map/ppermute | solution.py:609
  30.3 42.9 %collective-permute-start.14 = (f32[32,1152]{1,0:T(8,128)}, f32[32,1152]{1,0:T(8,128)}, u32[]{:S(2)}, u32[]{:S(2)}) collective-permute-start(f32[32,1152]{1,0:T(8,128)} %get-tuple-element.143), channel_id=1, source_target_pairs={{0,12},{4,8},{8,4},{12,0},{16,28},{20,24},{24,20},{28,16},{1,13},{... | collective-permute-start | bytes 442376 | tf_op jit(solution)/shard_map/ppermute | solution.py:609
  32.7 40.5 %collective-permute-start.15 = (f32[32,1152]{1,0:T(8,128)}, f32[32,1152]{1,0:T(8,128)}, u32[]{:S(2)}, u32[]{:S(2)}) collective-permute-start(f32[32,1152]{1,0:T(8,128)} %get-tuple-element.144), channel_id=1, source_target_pairs={{0,16},{4,20},{8,24},{12,28},{16,0},{20,4},{24,8},{28,12},{1,17},{... | collective-permute-start | bytes 442376 | tf_op jit(solution)/shard_map/ppermute | solution.py:609
  46.6 28.8 %collective-permute-start.16 = (f32[32,1152]{1,0:T(8,128)}, f32[32,1152]{1,0:T(8,128)}, u32[]{:S(2)}, u32[]{:S(2)}) collective-permute-start(f32[32,1152]{1,0:T(8,128)} %get-tuple-element.145), channel_id=1, source_target_pairs={{0,20},{4,16},{8,28},{12,24},{16,4},{20,0},{24,12},{28,8},{1,21},{... | collective-permute-start | bytes 442376 | tf_op jit(solution)/shard_map/ppermute | solution.py:609
  62.3 13.0 %collective-permute-start.17 = (f32[32,1152]{1,0:T(8,128)}, f32[32,1152]{1,0:T(8,128)}, u32[]{:S(2)}, u32[]{:S(2)}) collective-permute-start(f32[32,1152]{1,0:T(8,128)} %get-tuple-element.146), channel_id=1, source_target_pairs={{0,24},{4,28},{8,16},{12,20},{16,8},{20,12},{24,0},{28,4},{1,25},{... | collective-permute-start | bytes 442376 | tf_op jit(solution)/shard_map/ppermute | solution.py:609
  65.8 9.6 %collective-permute-start.18 = (f32[32,1152]{1,0:T(8,128)}, f32[32,1152]{1,0:T(8,128)}, u32[]{:S(2)}, u32[]{:S(2)}) collective-permute-start(f32[32,1152]{1,0:T(8,128)} %get-tuple-element.147), channel_id=1, source_target_pairs={{0,28},{4,24},{8,20},{12,16},{16,12},{20,8},{24,4},{28,0},{1,29},{... | collective-permute-start | bytes 442376 | tf_op jit(solution)/shard_map/ppermute | solution.py:609
  81.5 12.1 %copy-start.22 = (s32[192,2]{0,1:T(2,128)S(1)}, s32[192,2]{0,1:T(2,128)}, u32[]{:S(2)}) copy-start(s32[192,2]{0,1:T(2,128)} %param.21) | copy-start | bytes 4612
  81.5 80.5 %all-to-all-start.1 = ((f32[8,32,3072]{2,1,0:T(8,128)}), f32[8,32,3072]{2,1,0:T(8,128)}, u32[]{:S(2)}, u32[]{:S(2)}) async-start(f32[8,32,3072]{2,1,0:T(8,128)} %bitcast.54), calls=%async_computation.1 | async-start | bytes 6291456 | tf_op jit(solution)/shard_map/all_to_all | solution.py:604
  89.9 38.4 %collective-permute-start.11 = (f32[97,32,128]{2,1,0:T(8,128)}, f32[97,32,128]{2,1,0:T(8,128)}, u32[]{:S(2)}, u32[]{:S(2)}) collective-permute-start(f32[97,32,128]{2,1,0:T(8,128)} %get-tuple-element.139), channel_id=1, source_target_pairs={{0,3},{1,2},{2,1},{3,0},{4,7},{5,6},{6,5},{7,4},{8,11},{9,10},{10,... | collective-permute-start | bytes 4767752 | tf_op jit(solution)/shard_map/ppermute | solution.py:601
  102.3 26.0 %copy-start.24 = (s32[192,2]{0,1:T(2,128)S(1)}, s32[192,2]{0,1:T(2,128)}, u32[]{:S(2)}) copy-start(s32[192,2]{0,1:T(2,128)} %param.20) | copy-start | bytes 4612
  143.8 4.6 %collective-permute-start.21 = (f32[8,128]{1,0:T(8,128)S(1)}, f32[8,128]{1,0:T(8,128)S(1)}, u32[]{:S(2)}, u32[]{:S(2)}) collective-permute-start(f32[8,128]{1,0:T(8,128)S(1)} %get-tuple-element.154), channel_id=1, source_target_pairs={{0,3},{1,2},{2,1},{3,0},{4,7},{5,6},{6,5},{7,4},{8,11},{9,10},{10,... | collective-permute-start | bytes 12296 | tf_op jit(solution)/shard_map/ppermute | solution.py:601
  146.3 3.6 %collective-permute-start.20 = (f32[8,128]{1,0:T(8,128)S(1)}, f32[8,128]{1,0:T(8,128)S(1)}, u32[]{:S(2)}, u32[]{:S(2)}) collective-permute-start(f32[8,128]{1,0:T(8,128)S(1)} %get-tuple-element.154), channel_id=1, source_target_pairs={{0,2},{1,3},{2,0},{3,1},{4,6},{5,7},{6,4},{7,5},{8,10},{9,11},{10,... | collective-permute-start | bytes 12296 | tf_op jit(solution)/shard_map/ppermute | solution.py:601
  146.8 3.6 %collective-permute-start.19 = (f32[8,128]{1,0:T(8,128)S(1)}, f32[8,128]{1,0:T(8,128)S(1)}, u32[]{:S(2)}, u32[]{:S(2)}) collective-permute-start(f32[8,128]{1,0:T(8,128)S(1)} %get-tuple-element.154), channel_id=1, source_target_pairs={{0,1},{1,0},{2,3},{3,2},{4,5},{5,4},{6,7},{7,6},{8,9},{9,8},{10,11... | collective-permute-start | bytes 12296 | tf_op jit(solution)/shard_map/ppermute | solution.py:601
  150.4 1.2 collective-permute-start.22
  151.6 10.4 %copy-start.26 = (f32[8,128]{1,0:T(8,128)}, f32[8,128]{1,0:T(8,128)S(1)}, u32[]{:S(2)}) copy-start(f32[8,128]{1,0:T(8,128)S(1)} %add.168.refs_0_) | copy-start | bytes 12292
  151.6 4.8 %collective-permute-start.25 = (f32[8,128]{1,0:T(8,128)S(1)}, f32[8,128]{1,0:T(8,128)S(1)}, u32[]{:S(2)}, u32[]{:S(2)}) collective-permute-start(f32[8,128]{1,0:T(8,128)S(1)} %add.168.refs_0_), channel_id=1, source_target_pairs={{0,24},{4,28},{8,0},{12,4},{16,8},{20,12},{24,16},{28,20},{1,25},{... | collective-permute-start | bytes 12296 | tf_op jit(solution)/shard_map/ppermute | solution.py:697
  155.1 6.9 %collective-permute-start.24 = (f32[8,128]{1,0:T(8,128)S(1)}, f32[8,128]{1,0:T(8,128)S(1)}, u32[]{:S(2)}, u32[]{:S(2)}) collective-permute-start(f32[8,128]{1,0:T(8,128)S(1)} %add.168.refs_0_), channel_id=1, source_target_pairs={{0,16},{4,20},{8,24},{12,28},{16,0},{20,4},{24,8},{28,12},{1,17},{... | collective-permute-start | bytes 12296 | tf_op jit(solution)/shard_map/ppermute | solution.py:697
  155.8 6.2 %collective-permute-start.23 = (f32[8,128]{1,0:T(8,128)S(1)}, f32[8,128]{1,0:T(8,128)S(1)}, u32[]{:S(2)}, u32[]{:S(2)}) collective-permute-start(f32[8,128]{1,0:T(8,128)S(1)} %add.168.refs_0_), channel_id=1, source_target_pairs={{0,8},{4,12},{8,16},{12,20},{16,24},{20,28},{24,0},{28,4},{1,9},{5... | collective-permute-start | bytes 12296 | tf_op jit(solution)/shard_map/ppermute | solution.py:697
  170.6 64.0 %all-to-all-start.2 = ((f32[8,32,1920]{2,1,0:T(8,128)}), f32[8,32,1920]{2,1,0:T(8,128)}, u32[]{:S(2)}, u32[]{:S(2)}) async-start(f32[8,32,1920]{2,1,0:T(8,128)} %get-tuple-element.168), calls=%async_computation.2 | async-start | bytes 3932160 | tf_op jit(solution)/shard_map/all_to_all | solution.py:604
  175.3 9.6 %copy-start.40 = (f32[32,1152]{1,0:T(8,128)S(1)}, f32[32,1152]{1,0:T(8,128)}, u32[]{:S(2)}) copy-start(f32[32,1152]{1,0:T(8,128)} %get-tuple-element.163) | copy-start | bytes 442372
  175.3 39.7 %copy-start.34 = (f32[32,1152]{1,0:T(8,128)S(1)}, f32[32,1152]{1,0:T(8,128)}, u32[]{:S(2)}) copy-start(f32[32,1152]{1,0:T(8,128)} %get-tuple-element.166) | copy-start | bytes 442372
  175.3 42.9 %copy-start.33 = (f32[32,1152]{1,0:T(8,128)S(1)}, f32[32,1152]{1,0:T(8,128)}, u32[]{:S(2)}) copy-start(f32[32,1152]{1,0:T(8,128)} %get-tuple-element.167) | copy-start | bytes 442372
  179.9 38.3 %collective-permute-start.26 = (f32[97,32,128]{2,1,0:T(8,128)}, f32[97,32,128]{2,1,0:T(8,128)S(1)}, u32[]{:S(2)}, u32[]{:S(2)}) collective-permute-start(f32[97,32,128]{2,1,0:T(8,128)} %get-tuple-element.157), channel_id=1, source_target_pairs={{0,1},{1,0},{2,3},{3,2},{4,5},{5,4},{6,7},{7,6},{8,9},{9,8},{10,11... | collective-permute-start | bytes 4767752 | tf_op jit(solution)/shard_map/ppermute | solution.py:601
  181.4 38.3 %collective-permute-start.27 = (f32[97,32,128]{2,1,0:T(8,128)}, f32[97,32,128]{2,1,0:T(8,128)S(1)}, u32[]{:S(2)}, u32[]{:S(2)}) collective-permute-start(f32[97,32,128]{2,1,0:T(8,128)} %get-tuple-element.158), channel_id=1, source_target_pairs={{0,2},{1,3},{2,0},{3,1},{4,6},{5,7},{6,4},{7,5},{8,10},{9,11},{10,... | collective-permute-start | bytes 4767752 | tf_op jit(solution)/shard_map/ppermute | solution.py:601
  182.9 2.1 collective-permute-start.29
  182.9 28.4 %collective-permute-start.30 = (f32[32,1152]{1,0:T(8,128)S(1)}, f32[32,1152]{1,0:T(8,128)S(1)}, u32[]{:S(2)}, u32[]{:S(2)}) collective-permute-start(f32[32,1152]{1,0:T(8,128)S(1)} %copy-done.41), channel_id=1, source_target_pairs={{0,8},{4,12},{8,0},{12,4},{16,24},{20,28},{24,16},{28,20},{1,9},{5... | collective-permute-start | bytes 442376 | tf_op jit(solution)/shard_map/ppermute | solution.py:609
  184.9 30.1 %collective-permute-start.31 = (f32[32,1152]{1,0:T(8,128)S(1)}, f32[32,1152]{1,0:T(8,128)S(1)}, u32[]{:S(2)}, u32[]{:S(2)}) collective-permute-start(f32[32,1152]{1,0:T(8,128)S(1)} %copy-done.40), channel_id=1, source_target_pairs={{0,12},{4,8},{8,4},{12,0},{16,28},{20,24},{24,20},{28,16},{1,13},{... | collective-permute-start | bytes 442376 | tf_op jit(solution)/shard_map/ppermute | solution.py:609
  185.0 34.7 %copy-start.35 = (f32[32,1152]{1,0:T(8,128)}, f32[32,1152]{1,0:T(8,128)S(1)}, u32[]{:S(2)}) copy-start(f32[32,1152]{1,0:T(8,128)S(1)} %collective-permute-done.29.refs_1_) | copy-start | bytes 442372
  185.0 61.7 %collective-permute-start.32 = (f32[32,1152]{1,0:T(8,128)}, f32[32,1152]{1,0:T(8,128)}, u32[]{:S(2)}, u32[]{:S(2)}) collective-permute-start(f32[32,1152]{1,0:T(8,128)} %get-tuple-element.164), channel_id=1, source_target_pairs={{0,16},{4,20},{8,24},{12,28},{16,0},{20,4},{24,8},{28,12},{1,17},{... | collective-permute-start | bytes 442376 | tf_op jit(solution)/shard_map/ppermute | solution.py:609
  211.3 35.4 %collective-permute-start.33 = (f32[32,1152]{1,0:T(8,128)}, f32[32,1152]{1,0:T(8,128)}, u32[]{:S(2)}, u32[]{:S(2)}) collective-permute-start(f32[32,1152]{1,0:T(8,128)} %get-tuple-element.165), channel_id=1, source_target_pairs={{0,20},{4,16},{8,28},{12,24},{16,4},{20,0},{24,12},{28,8},{1,21},{... | collective-permute-start | bytes 442376 | tf_op jit(solution)/shard_map/ppermute | solution.py:609
  214.9 31.8 %collective-permute-start.34 = (f32[32,1152]{1,0:T(8,128)S(1)}, f32[32,1152]{1,0:T(8,128)}, u32[]{:S(2)}, u32[]{:S(2)}) collective-permute-start(f32[32,1152]{1,0:T(8,128)S(1)} %copy-done.34), channel_id=1, source_target_pairs={{0,24},{4,28},{8,16},{12,20},{16,8},{20,12},{24,0},{28,4},{1,25},{... | collective-permute-start | bytes 442376 | tf_op jit(solution)/shard_map/ppermute | solution.py:609
  218.2 16.4 %copy-start.31 = (f32[97,32,128]{2,1,0:T(8,128)}, f32[97,32,128]{2,1,0:T(8,128)S(1)}, u32[]{:S(2)}) copy-start(f32[97,32,128]{2,1,0:T(8,128)S(1)} %collective-permute-done.26.refs_5_.refs_2_) | copy-start | bytes 4767748
  218.2 28.5 %collective-permute-start.35 = (f32[32,1152]{1,0:T(8,128)S(1)}, f32[32,1152]{1,0:T(8,128)}, u32[]{:S(2)}, u32[]{:S(2)}) collective-permute-start(f32[32,1152]{1,0:T(8,128)S(1)} %copy-done.33), channel_id=1, source_target_pairs={{0,28},{4,24},{8,20},{12,16},{16,12},{20,8},{24,4},{28,0},{1,29},{... | collective-permute-start | bytes 442376 | tf_op jit(solution)/shard_map/ppermute | solution.py:609
  219.7 15.0 %copy-start.32 = (f32[97,32,128]{2,1,0:T(8,128)}, f32[97,32,128]{2,1,0:T(8,128)S(1)}, u32[]{:S(2)}) copy-start(f32[97,32,128]{2,1,0:T(8,128)S(1)} %collective-permute-done.27.refs_6_.refs_3_) | copy-start | bytes 4767748
  219.7 38.8 %collective-permute-start.28 = (f32[97,32,128]{2,1,0:T(8,128)}, f32[97,32,128]{2,1,0:T(8,128)}, u32[]{:S(2)}, u32[]{:S(2)}) collective-permute-start(f32[97,32,128]{2,1,0:T(8,128)} %get-tuple-element.159), channel_id=1, source_target_pairs={{0,3},{1,2},{2,1},{3,0},{4,7},{5,6},{6,5},{7,4},{8,11},{9,10},{10,... | collective-permute-start | bytes 4767752 | tf_op jit(solution)/shard_map/ppermute | solution.py:601
  242.1 63.8 %all-to-all-start.3 = ((f32[8,32,1920]{2,1,0:T(8,128)}), f32[8,32,1920]{2,1,0:T(8,128)}, u32[]{:S(2)}, u32[]{:S(2)}) async-start(f32[8,32,1920]{2,1,0:T(8,128)} %bitcast.56), calls=%async_computation.3 | async-start | bytes 3932160 | tf_op jit(solution)/shard_map/all_to_all | solution.py:604
  265.1 19.3 %collective-permute-start.36 = (f32[32,1152]{1,0:T(8,128)}, f32[32,1152]{1,0:T(8,128)}, u32[]{:S(2)}, u32[]{:S(2)}) collective-permute-start(f32[32,1152]{1,0:T(8,128)} %get-tuple-element.170), channel_id=1, source_target_pairs={{0,4},{4,0},{8,12},{12,8},{16,20},{20,16},{24,28},{28,24},{1,5},{5... | collective-permute-start | bytes 442376 | tf_op jit(solution)/shard_map/ppermute | solution.py:609
  265.4 20.5 %collective-permute-start.37 = (f32[32,1152]{1,0:T(8,128)}, f32[32,1152]{1,0:T(8,128)}, u32[]{:S(2)}, u32[]{:S(2)}) collective-permute-start(f32[32,1152]{1,0:T(8,128)} %get-tuple-element.171), channel_id=1, source_target_pairs={{0,8},{4,12},{8,0},{12,4},{16,24},{20,28},{24,16},{28,20},{1,9},{5... | collective-permute-start | bytes 442376 | tf_op jit(solution)/shard_map/ppermute | solution.py:609
  265.4 14.4 %copy-start.7 = (s32[192,2]{1,0:T(8,128)S(1)}, s32[192,2]{1,0:T(8,128)}, u32[]{:S(2)}) copy-start(s32[192,2]{1,0:T(8,128)} %copy-done.6) | copy-start | bytes 4612
  265.4 14.4 %copy-start.15 = (f32[8,256]{1,0:T(8,128)S(1)}, f32[8,256]{1,0:T(8,128)}, u32[]{:S(2)}) copy-start(f32[8,256]{1,0:T(8,128)} %copy-done.14) | copy-start | bytes 24580
  265.4 14.4 %copy-start.17 = (f32[8,256]{1,0:T(8,128)S(1)}, f32[8,256]{1,0:T(8,128)}, u32[]{:S(2)}) copy-start(f32[8,256]{1,0:T(8,128)} %copy-done.16) | copy-start | bytes 24580
  265.4 14.4 %copy-start.19 = (f32[8,256]{1,0:T(8,128)S(1)}, f32[8,256]{1,0:T(8,128)}, u32[]{:S(2)}) copy-start(f32[8,256]{1,0:T(8,128)} %copy-done.18) | copy-start | bytes 24580
  265.4 14.4 %copy-start.21 = (s32[192,2]{0,1:T(2,128)S(1)}, s32[192,2]{0,1:T(2,128)}, u32[]{:S(2)}) copy-start(s32[192,2]{0,1:T(2,128)} %param.19) | copy-start | bytes 4612
  265.4 14.4 %copy-start.23 = (s32[192,2]{0,1:T(2,128)S(1)}, s32[192,2]{0,1:T(2,128)}, u32[]{:S(2)}) copy-start(s32[192,2]{0,1:T(2,128)} %param.21) | copy-start | bytes 4612
  279.9 29.5 %collective-permute-start.38 = (f32[32,1152]{1,0:T(8,128)}, f32[32,1152]{1,0:T(8,128)S(1)}, u32[]{:S(2)}, u32[]{:S(2)}) collective-permute-start(f32[32,1152]{1,0:T(8,128)} %get-tuple-element.172), channel_id=1, source_target_pairs={{0,12},{4,8},{8,4},{12,0},{16,28},{20,24},{24,20},{28,16},{1,13},{... | collective-permute-start | bytes 442376 | tf_op jit(solution)/shard_map/ppermute | solution.py:609
  281.5 27.9 %collective-permute-start.39 = (f32[32,1152]{1,0:T(8,128)}, f32[32,1152]{1,0:T(8,128)S(1)}, u32[]{:S(2)}, u32[]{:S(2)}) collective-permute-start(f32[32,1152]{1,0:T(8,128)} %get-tuple-element.173), channel_id=1, source_target_pairs={{0,16},{4,20},{8,24},{12,28},{16,0},{20,4},{24,8},{28,12},{1,17},{... | collective-permute-start | bytes 442376 | tf_op jit(solution)/shard_map/ppermute | solution.py:609
  282.1 29.0 %collective-permute-start.40 = (f32[32,1152]{1,0:T(8,128)}, f32[32,1152]{1,0:T(8,128)S(1)}, u32[]{:S(2)}, u32[]{:S(2)}) collective-permute-start(f32[32,1152]{1,0:T(8,128)} %get-tuple-element.174), channel_id=1, source_target_pairs={{0,20},{4,16},{8,28},{12,24},{16,4},{20,0},{24,12},{28,8},{1,21},{... | collective-permute-start | bytes 442376 | tf_op jit(solution)/shard_map/ppermute | solution.py:609
  284.3 26.8 %collective-permute-start.41 = (f32[32,1152]{1,0:T(8,128)}, f32[32,1152]{1,0:T(8,128)S(1)}, u32[]{:S(2)}, u32[]{:S(2)}) collective-permute-start(f32[32,1152]{1,0:T(8,128)} %get-tuple-element.175), channel_id=1, source_target_pairs={{0,24},{4,28},{8,16},{12,20},{16,8},{20,12},{24,0},{28,4},{1,25},{... | collective-permute-start | bytes 442376 | tf_op jit(solution)/shard_map/ppermute | solution.py:609
  285.9 25.3 %collective-permute-start.42 = (f32[32,1152]{1,0:T(8,128)}, f32[32,1152]{1,0:T(8,128)S(1)}, u32[]{:S(2)}, u32[]{:S(2)}) collective-permute-start(f32[32,1152]{1,0:T(8,128)} %get-tuple-element.176), channel_id=1, source_target_pairs={{0,28},{4,24},{8,20},{12,16},{16,12},{20,8},{24,4},{28,0},{1,29},{... | collective-permute-start | bytes 442376 | tf_op jit(solution)/shard_map/ppermute | solution.py:609
  (19 other events, 82.5 us)

commit v5 on v4

--- a/solution.py
+++ b/solution.py
@@ -440,27 +440,28 @@
     return list(out)
 
 
-def correct(returned, beta_term, device, wide, narrow, extra):
+def correct(returned, beta_term, device, wide, narrow, extra, previous):
     rows, cols = beta_term.shape
     parts = returned.shape[0]
     sums = [] if extra is None else extra[0]
     wholes = [beta_term] + ([] if extra is None else [extra[1], extra[2]])
     count = len(wholes)
-    sent = 0 if extra is None else 1 + parts
+    sent = parts if previous else 1
 
     def kernel(device_ref, *refs):
         sum_refs = refs[: len(sums)]
         whole_refs = refs[len(sums) :][:count]
         part_ref = refs[len(sums) + count]
-        out_refs = refs[len(sums) + count + 1 :][: 1 + sent]
-        held, few, sems, out_sems = refs[-4:]
+        out_refs = refs[len(sums) + count + 1 + len(previous) :][: 1 + sent]
+        held, sems, out_sems = refs[-3:]
         pieces = []
         for j in range(parts):
-            pieces.append((held, j, j * wide, part_ref.at[j, :, :wide], out_refs[1].at[j] if sent else None))
-        for k in range(parts):
-            place = device_ref[0] ^ k
-            at = pl.multiple_of(parts * wide + place * narrow, SB)
-            pieces.append((few, k, at, part_ref.at[place, :, wide:], out_refs[2 + k] if sent else None))
+            if previous:
+                place = device_ref[0] ^ j
+                at = pl.multiple_of(parts * wide + place * narrow, SB)
+                pieces.append((held, j, at, part_ref.at[place, :, wide:], out_refs[1 + j]))
+            else:
+                pieces.append((held, j, j * wide, part_ref.at[j, :, :wide], out_refs[1].at[j]))
         taken = []
         given = []
         for p, (buffer, j, start, part, target) in enumerate(pieces):
@@ -470,8 +471,7 @@
                 + [pltpu.make_async_copy(part, buffer.at[count, j], sems.at[count, p])]
             )
             given.append([pltpu.make_async_copy(buffer.at[count, j], out_refs[0].at[:, at], out_sems.at[0, p])])
-            if sent:
-                given[-1].append(pltpu.make_async_copy(buffer.at[count, j], target, out_sems.at[1, p]))
+            given[-1].append(pltpu.make_async_copy(buffer.at[count, j], target, out_sems.at[1, p]))
         for copies in taken:
             for copy in copies:
                 copy.start()
@@ -495,25 +495,25 @@
                 copy.wait()
 
     anywhere = pl.BlockSpec(memory_space=pl.ANY)
-    shapes = [(rows, cols), (parts, rows, wide)] + [(rows, narrow)] * parts
+    shapes = [(rows, cols)] + ([(rows, narrow)] * parts if previous else [(parts, rows, wide)])
     out = pl.pallas_call(
         kernel,
         in_specs=[pl.BlockSpec(memory_space=pltpu.SMEM)]
         + [pl.BlockSpec(memory_space=pltpu.VMEM)] * len(sums)
-        + [anywhere] * (count + 1),
+        + [anywhere] * (count + 1 + len(previous)),
         out_specs=[anywhere] * (1 + sent),
-        out_shape=[jax.ShapeDtypeStruct(shape, f32) for shape in shapes[: 1 + sent]],
+        out_shape=[jax.ShapeDtypeStruct(shape, f32) for shape in shapes],
+        input_output_aliases={1 + len(sums) + count + 1: 0} if previous else {},
         scratch_shapes=[
-            pltpu.VMEM((count + 1, parts, rows, wide), f32),
-            pltpu.VMEM((count + 1, parts, rows, narrow), f32),
-            pltpu.SemaphoreType.DMA((count + 1, 2 * parts)),
-            pltpu.SemaphoreType.DMA((2, 2 * parts)),
+            pltpu.VMEM((count + 1, parts, rows, narrow if previous else wide), f32),
+            pltpu.SemaphoreType.DMA((count + 1, parts)),
+            pltpu.SemaphoreType.DMA((2, parts)),
         ],
         compiler_params=params(),
         cost_estimate=cost(0, 0),
-        name="finish" if extra is None else "correct",
-    )(device, *sums, *wholes, returned)
-    return out if extra is not None else out[0]
+        name="correct",
+    )(device, *sums, *wholes, returned, *previous)
+    return out[0], out[1:]
 
 
 def finish(returned, beta_term, device, start, previous, extra=None, work=0):
@@ -697,8 +697,9 @@
             all_sums.append(lax.ppermute(sums, "alpha", pairs))
 
         extra = (all_sums, start_vector, precondition)
-        correction, parts, *few = correct(returned, beta_term, device, wide, narrow, extra)
+        correction, (parts,) = correct(returned, beta_term, device, wide, narrow, extra, [])
         arrived = turn(parts)
+        correction, few = correct(returned, beta_term, device, wide, narrow, extra, [correction])
         arrived_few = swap(few)
         received, token = beta_send(correction, first_plan, [])
         columns = arrived.reshape(n_alpha * rows, wide)

time: 320 us -> 317 us (level)
  waiting for transfers between devices: 130 us -> 123 us
  Pallas kernels: 89.3 us -> 92.9 us
    all_to_all x4, waiting for transfers between devices: 30.6 us -> 18.7 us  [turn(): return lax.all_to_all(parts, 'alpha', 0, 0, tiled=True)]
    ppermute x12, waiting for transfers between devices: 53.5 us -> 64.5 us  [to_partners(): lax.ppermute(part, 'beta', [(i, i ^ k) for i in range(n_beta)])]
    ppermute x21, waiting for transfers between devices: 38.8 us -> 32.9 us  [swap(): lax.ppermute(parts[k], 'alpha', [(i, i ^ k) for i in range(n_alpha)])]
    pallas_call x1 -> x2, Pallas kernels: 8.02 us -> 9.86 us  [correct(): pl.pallas_call(kernel, in_specs=[pl.BlockSpec(memory_space=pltpu.SMEM)] +...]
  transfers between devices with their start and end apart: 41 -> 41, of which waited for: 17 -> 18; matrix products, arithmetic and copies ran while one was open for 3% -> 3% of each run, Pallas kernels for 22% -> 24%
where the time goes in v5:
time: 317 us; the launch traced here: 313 us
  waiting for transfers between devices  123 us (39%)
  Pallas kernels  92.9 us (29%)
  starting transfers between devices  80 us (25%)
  local copies, waits for them, and re-layouts  8.21 us (3%)
  other arithmetic  4.51 us (1%)
  between operations  3.93 us (1%)
    ppermute x12, waiting for transfers between devices, to_partners(): lax.ppermute(part, 'beta', [(i, i ^ k) for i in range(n_beta)])  64.5 us
    ppermute x21, starting transfers between devices, swap(): lax.ppermute(parts[k], 'alpha', [(i, i ^ k) for i in range(n_alpha)])  34.1 us
    ppermute x21, waiting for transfers between devices, swap(): lax.ppermute(parts[k], 'alpha', [(i, i ^ k) for i in range(n_alpha)])  32.9 us
    pallas_call x2, Pallas kernels, beta_sum(): pl.pallas_call(kernel, grid_spec=pltpu.PrefetchScalarGridSpec(num_scalar_...  29.6 us
    pallas_call x4, Pallas kernels, alpha_sum(): pl.pallas_call(kernel, in_specs=[pl.BlockSpec(memory_space=pltpu.SMEM)] *...  27.6 us
    all_to_all x4, starting transfers between devices, turn(): return lax.all_to_all(parts, 'alpha', 0, 0, tiled=True)  23.9 us
    all_to_all x4, waiting for transfers between devices, turn(): return lax.all_to_all(parts, 'alpha', 0, 0, tiled=True)  18.7 us
    ppermute x12, starting transfers between devices, to_partners(): lax.ppermute(part, 'beta', [(i, i ^ k) for i in range(n_beta)])  17.1 us
  transfers between devices with their start and end apart: 41, of which 18 were waited for; matrix products, arithmetic and copies ran while one was open for 3% of the time, Pallas kernels for 24%

profile of v5, /device:TPU:0, one launch (start us, length us, event | category | flops | bytes accessed | tf_op | source)
XLA Modules:
  0.0 312.5 jit_solution(6493202114572771579)
XLA Ops:
  0.6 3.2 %pack.1 = (f32[8,32,1920]{2,1,0:T(8,128)}, f32[32,1152]{1,0:T(8,128)}, f32[32,1152]{1,0:T(8,128)}, f32[32,1152]{1,0:T(8,128)}, f32[32,1152]{1,0:T(8,128)}, /*ind...) custom-call(s32[1]{0:T(128)} %bitcast.4.device_ref, f32[32,24576]{1,0:T(8,128)} %refs_5_.3), custom_call_target="tpu_custom_call" | custom-call | flops 1 | bytes 1 | tf_op jit(solution)/shard_map/pack/pallas_call | solution.py:91
  3.9 6.6 %all-to-all-start = ((f32[8,32,1920]{2,1,0:T(8,128)}), f32[8,32,1920]{2,1,0:T(8,128)}, u32[]{:S(2)}, u32[]{:S(2)}) async-start(f32[8,32,1920]{2,1,0:T(8,128)} %get-tuple-element.133.refs_0_), calls=%async_computation | async-start | bytes 3932160 | tf_op jit(solution)/shard_map/all_to_all | solution.py:604
  10.5 0.8 copy.15.source_ref
  11.3 2.8 mark.1
  14.1 1.6 collective-permute-start.7
  15.7 1.4 collective-permute-start.8
  18.0 2.4 collective-permute-done.8.refs_2_
  21.0 0.8 positions.5.slots_ref
  21.7 4.4 %gather_blocks.6 = (f32[97,32,128]{2,1,0:T(8,128)}, f32[97,32,128]{2,1,0:T(8,128)}, f32[97,32,128]{2,1,0:T(8,128)}) custom-call(s32[8,256]{1,0:T(8,128)} %positions.5.slots_ref, f32[32,24576]{1,0:T(8,128)S(1)} %copy-done), custom_call_target="tpu_custom_call" | custom-call | flops 1 | bytes 1 | tf_op jit(solution)/shard_map/gather_blocks/pallas_call | solution.py:321
  26.2 1.0 collective-permute-start.9
  27.1 1.1 collective-permute-start.10
  28.2 2.1 collective-permute-start.13
  30.4 2.4 prepare.1
  32.8 2.6 collective-permute-start.15
  35.4 11.2 %collective-permute-done.13.refs_2_ = f32[32,1152]{1,0:T(8,128)} collective-permute-done((f32[32,1152]{1,0:T(8,128)S(1)}, f32[32,1152]{1,0:T(8,128)}, u32[]{:S(2)}, u32[]{:S(2)}) %collective-permute-start.13) | collective-permute-done | bytes 147488 | tf_op jit(solution)/shard_map/ppermute | solution.py:609
  46.6 3.7 %collective-permute-start.16 = (f32[32,1152]{1,0:T(8,128)}, f32[32,1152]{1,0:T(8,128)}, u32[]{:S(2)}, u32[]{:S(2)}) collective-permute-start(f32[32,1152]{1,0:T(8,128)} %get-tuple-element.146), channel_id=1, source_target_pairs={{0,20},{4,16},{8,28},{12,24},{16,4},{20,0},{24,12},{28,8},{1,21},{... | collective-permute-start | bytes 442376 | tf_op jit(solution)/shard_map/ppermute | solution.py:609
  50.3 12.1 %collective-permute-done.9.refs_5_.refs_2_ = f32[97,32,128]{2,1,0:T(8,128)} collective-permute-done((f32[97,32,128]{2,1,0:T(8,128)}, f32[97,32,128]{2,1,0:T(8,128)}, u32[]{:S(2)}, u32[]{:S(2)}) %collective-permute-start.9) | collective-permute-done | bytes 1589280 | tf_op jit(solution)/shard_map/ppermute | solution.py:601
  62.3 3.5 %collective-permute-start.17 = (f32[32,1152]{1,0:T(8,128)}, f32[32,1152]{1,0:T(8,128)}, u32[]{:S(2)}, u32[]{:S(2)}) collective-permute-start(f32[32,1152]{1,0:T(8,128)} %get-tuple-element.147), channel_id=1, source_target_pairs={{0,24},{4,28},{8,16},{12,20},{16,8},{20,12},{24,0},{28,4},{1,25},{... | collective-permute-start | bytes 442376 | tf_op jit(solution)/shard_map/ppermute | solution.py:609
  65.8 7.4 %alpha_sum.4.refs_12_ = f32[256,3072]{1,0:T(8,128)} custom-call(s32[1]{0:T(128)} %bitcast.4.device_ref, s32[2,192]{1,0:T(2,128)} %pairs_ref.7, s32[2,192]{1,0:T(2,128)} %signs_ref.7, f32[256,1920]{1,0:T(8,128)} %bitcast.10.refs_0_, bf16[256,1536]{1,0:T(8,128)(2,1)} %get-tuple-element.149.refs_1_.refs_8_, ...), custom_call_target="tpu_custom_call" | custom-call | flops 20000000000 | bytes 66666664 | tf_op jit(solution)/shard_map/alpha_sum/pallas_call | solution.py:207
  73.2 2.1 collective-permute-done.16.refs_5_
  75.3 6.2 %alpha_sum.5 = f32[256,3072]{1,0:T(8,128)} custom-call(s32[1]{0:T(128)} %bitcast.4.device_ref, s32[2,192]{1,0:T(2,128)} %pairs_ref.7, s32[2,192]{1,0:T(2,128)} %signs_ref.7, f32[32,1152]{1,0:T(8,128)} %get-tuple-element.141.refs_0_, f32[32,1152]{1,0:T(8,128)} %collective-permute-done.12.refs_1_, ...), custom_call_target="tpu_custom_call", output_to_operand_aliasing={{}: (15, {})} | custom-call | flops 1 | bytes 1 | tf_op jit(solution)/shard_map/alpha_sum/pallas_call | solution.py:207
  81.5 8.4 %all-to-all-start.1 = ((f32[8,32,3072]{2,1,0:T(8,128)}), f32[8,32,3072]{2,1,0:T(8,128)}, u32[]{:S(2)}, u32[]{:S(2)}) async-start(f32[8,32,3072]{2,1,0:T(8,128)} %bitcast.54), calls=%async_computation.1 | async-start | bytes 6291456 | tf_op jit(solution)/shard_map/all_to_all | solution.py:604
  89.9 2.4 collective-permute-start.11
  92.4 1.2 slice.18
  98.3 1.4 slice.28
  99.7 2.4 fusion.2
  102.7 1.5 fusion.9
  104.8 23.5 %collective-permute-done.11.refs_4_ = f32[97,32,128]{2,1,0:T(8,128)} collective-permute-done((f32[97,32,128]{2,1,0:T(8,128)}, f32[97,32,128]{2,1,0:T(8,128)}, u32[]{:S(2)}, u32[]{:S(2)}) %collective-permute-start.11) | collective-permute-done | bytes 1589280 | tf_op jit(solution)/shard_map/ppermute | solution.py:601
  128.3 15.2 %beta_sum.6 = (f32[32,24576]{1,0:T(8,128)}, f32[8,128]{1,0:T(8,128)S(1)}) custom-call(s32[2,192]{1,0:T(2,128)} %get-tuple-element.215.slots_ref, s32[2,192]{1,0:T(2,128)} %get-tuple-element.214.sign_ref, s32[2,192]{1,0:T(2,128)S(1)} %bitcast.57, f32[32,24576]{1,0:T(8,128)S(1)} %copy-done, f32[4,128,128]{2,1,0:T(8,128)S(1)} %copy-done.3, ...), custom_call_target="tpu_custom_call" | custom-call | flops 1 | bytes 1 | tf_op jit(solution)/shard_map/beta_sum/pallas_call | solution.py:413
  143.8 2.5 collective-permute-start.21
  147.3 1.0 collective-permute-done.21
  148.3 1.5 collective-permute-done.20
  150.4 1.2 collective-permute-done.22
  151.6 3.5 %collective-permute-start.25 = (f32[8,128]{1,0:T(8,128)S(1)}, f32[8,128]{1,0:T(8,128)S(1)}, u32[]{:S(2)}, u32[]{:S(2)}) collective-permute-start(f32[8,128]{1,0:T(8,128)S(1)} %add.168.refs_0_), channel_id=1, source_target_pairs={{0,24},{4,28},{8,0},{12,4},{16,8},{20,12},{24,16},{28,20},{1,25},{... | collective-permute-start | bytes 12296 | tf_op jit(solution)/shard_map/ppermute | solution.py:697
  155.0 0.8 collective-permute-start.24
  156.4 5.6 %collective-permute-done.24.refs_2_ = f32[8,128]{1,0:T(8,128)S(1)} collective-permute-done((f32[8,128]{1,0:T(8,128)S(1)}, f32[8,128]{1,0:T(8,128)S(1)}, u32[]{:S(2)}, u32[]{:S(2)}) %collective-permute-start.24) | collective-permute-done | bytes 4128 | tf_op jit(solution)/shard_map/ppermute | solution.py:697
  162.6 5.7 %correct.2 = (f32[32,24576]{1,0:T(8,128)}, f32[8,32,1920]{2,1,0:T(8,128)}) custom-call(s32[1]{0:T(128)} %bitcast.4.device_ref, f32[8,128]{1,0:T(8,128)} %copy-done.19, f32[8,128]{1,0:T(8,128)} %copy-done.28, f32[8,128]{1,0:T(8,128)} %copy-done.27, f32[8,128]{1,0:T(8,128)} %copy-done.26, f32[32,24576]{1,0:T(8,128)} %get-tuple-element.156.refs_4_, ...), custom_call_target="tpu_custom_call" | custom-call | flops 1 | bytes 1 | tf_op jit(solution)/shard_map/correct/pallas_call | solution.py:499
  168.3 4.3 %all-to-all-start.2 = ((f32[8,32,1920]{2,1,0:T(8,128)}), f32[8,32,1920]{2,1,0:T(8,128)}, u32[]{:S(2)}, u32[]{:S(2)}) async-start(f32[8,32,1920]{2,1,0:T(8,128)} %get-tuple-element.170), calls=%async_computation.2 | async-start | bytes 3932160 | tf_op jit(solution)/shard_map/all_to_all | solution.py:604
  172.7 4.1 %correct.3 = (f32[32,24576]{1,0:T(8,128)}, f32[32,1152]{1,0:T(8,128)}, f32[32,1152]{1,0:T(8,128)}, f32[32,1152]{1,0:T(8,128)}, f32[32,1152]{1,0:T(8,128)}, /*ind...) custom-call(s32[1]{0:T(128)} %bitcast.4.device_ref, ...), custom_call_target="tpu_custom_call", output_to_operand_aliasing={{0}: (9, {})} | custom-call | flops 1 | bytes 1 | tf_op jit(solution)/shard_map/correct/pallas_call | solution.py:499
  176.9 6.4 %gather_blocks.7 = (f32[97,32,128]{2,1,0:T(8,128)}, f32[97,32,128]{2,1,0:T(8,128)}, f32[97,32,128]{2,1,0:T(8,128)}) custom-call(s32[8,256]{1,0:T(8,128)} %positions.5.slots_ref, f32[32,24576]{1,0:T(8,128)} %get-tuple-element.131.v_ref.refs_0_), custom_call_target="tpu_custom_call" | custom-call | flops 1 | bytes 1 | tf_op jit(solution)/shard_map/gather_blocks/pallas_call | solution.py:321
  183.2 1.5 collective-permute-start.26
  184.7 1.5 collective-permute-start.27
  186.3 1.9 collective-permute-start.30
  188.3 2.6 collective-permute-start.32
  190.9 17.8 %collective-permute-done.30.refs_2_ = f32[32,1152]{1,0:T(8,128)S(1)} collective-permute-done((f32[32,1152]{1,0:T(8,128)S(1)}, f32[32,1152]{1,0:T(8,128)S(1)}, u32[]{:S(2)}, u32[]{:S(2)}) %collective-permute-start.30) | collective-permute-done | bytes 147488 | tf_op jit(solution)/shard_map/ppermute | solution.py:609
  208.7 3.6 %collective-permute-start.33 = (f32[32,1152]{1,0:T(8,128)}, f32[32,1152]{1,0:T(8,128)}, u32[]{:S(2)}, u32[]{:S(2)}) collective-permute-start(f32[32,1152]{1,0:T(8,128)} %get-tuple-element.167), channel_id=1, source_target_pairs={{0,20},{4,16},{8,28},{12,24},{16,4},{20,0},{24,12},{28,8},{1,21},{... | collective-permute-start | bytes 442376 | tf_op jit(solution)/shard_map/ppermute | solution.py:609
  212.4 3.3 %collective-permute-start.34 = (f32[32,1152]{1,0:T(8,128)S(1)}, f32[32,1152]{1,0:T(8,128)}, u32[]{:S(2)}, u32[]{:S(2)}) collective-permute-start(f32[32,1152]{1,0:T(8,128)S(1)} %copy-done.33), channel_id=1, source_target_pairs={{0,24},{4,28},{8,16},{12,20},{16,8},{20,12},{24,0},{28,4},{1,25},{... | collective-permute-start | bytes 442376 | tf_op jit(solution)/shard_map/ppermute | solution.py:609
  215.6 4.8 %collective-permute-done.26.refs_5_.refs_2_ = f32[97,32,128]{2,1,0:T(8,128)S(1)} collective-permute-done((f32[97,32,128]{2,1,0:T(8,128)}, f32[97,32,128]{2,1,0:T(8,128)S(1)}, u32[]{:S(2)}, u32[]{:S(2)}) %collective-permute-start.26) | collective-permute-done | bytes 1589280 | tf_op jit(solution)/shard_map/ppermute | solution.py:601
  220.5 2.5 collective-permute-start.35
  223.0 2.5 collective-permute-start.28
  225.5 6.5 %all-to-all-done.2 = f32[8,32,1920]{2,1,0:T(8,128)} async-done(((f32[8,32,1920]{2,1,0:T(8,128)}), f32[8,32,1920]{2,1,0:T(8,128)}, u32[]{:S(2)}, u32[]{:S(2)}) %all-to-all-start.2) | async-done | bytes 1966112 | tf_op jit(solution)/shard_map/all_to_all | solution.py:604
  232.1 7.5 %alpha_sum.6.refs_12_ = f32[256,1920]{1,0:T(8,128)} custom-call(s32[1]{0:T(128)} %bitcast.4.device_ref, s32[2,192]{1,0:T(2,128)} %pairs_ref.7, s32[2,192]{1,0:T(2,128)} %signs_ref.7, f32[256,1920]{1,0:T(8,128)} %bitcast.21.refs_0_, bf16[256,1536]{1,0:T(8,128)(2,1)} %get-tuple-element.149.refs_1_.refs_8_, ...), custom_call_target="tpu_custom_call" | custom-call | flops 20000000000 | bytes 66666664 | tf_op jit(solution)/shard_map/alpha_sum/pallas_call | solution.py:207
  239.5 4.6 %all-to-all-start.3 = ((f32[8,32,1920]{2,1,0:T(8,128)}), f32[8,32,1920]{2,1,0:T(8,128)}, u32[]{:S(2)}, u32[]{:S(2)}) async-start(f32[8,32,1920]{2,1,0:T(8,128)} %bitcast.56), calls=%async_computation.3 | async-start | bytes 3932160 | tf_op jit(solution)/shard_map/all_to_all | solution.py:604
  244.1 17.7 %collective-permute-done.28.refs_13_.refs_4_ = f32[97,32,128]{2,1,0:T(8,128)} collective-permute-done((f32[97,32,128]{2,1,0:T(8,128)}, f32[97,32,128]{2,1,0:T(8,128)}, u32[]{:S(2)}, u32[]{:S(2)}) %collective-permute-start.28) | collective-permute-done | bytes 1589280 | tf_op jit(solution)/shard_map/ppermute | solution.py:601
  261.8 6.6 %alpha_sum.7 = (f32[32,1152]{1,0:T(8,128)}, f32[32,1152]{1,0:T(8,128)}, f32[32,1152]{1,0:T(8,128)}, f32[32,1152]{1,0:T(8,128)}, f32[32,1152]{1,0:T(8,128)}, /*in...) custom-call(s32[1]{0:T(128)} %bitcast.4.device_ref, s32[2,192]{1,0:T(2,128)} %pairs_ref.7, ...), custom_call_target="tpu_custom_call" | custom-call | flops 199999995904 | bytes 666666688 | tf_op jit(solution)/shard_map/alpha_sum/pallas_call | solution.py:207
  268.7 14.3 %beta_sum.7 = f32[32,24576]{1,0:T(8,128)} custom-call(s32[2,192]{1,0:T(2,128)} %get-tuple-element.215.slots_ref, s32[2,192]{1,0:T(2,128)} %get-tuple-element.214.sign_ref, s32[2,192]{1,0:T(2,128)S(1)} %bitcast.59, f32[32,24576]{1,0:T(8,128)S(1)} %copy-done.1, f32[4,128,128]{2,1,0:T(8,128)S(1)} %copy-done.4, f32[97,32,128]{2,1,0:T(8,128)} %copy-done.30, ...), custom_call_target="tpu_custom_call" | custom-call | flops 20000000000 | bytes 66666664 | tf_op jit(solution)/shard_map/beta_sum/pallas_call | solution.py:413
  283.1 1.8 collective-permute-start.38
  284.9 2.7 collective-permute-start.40
  288.1 3.0 collective-permute-start.42
  291.1 12.2 %all-to-all-done.3.refs_1_ = f32[8,32,1920]{2,1,0:T(8,128)} async-done(((f32[8,32,1920]{2,1,0:T(8,128)}), f32[8,32,1920]{2,1,0:T(8,128)}, u32[]{:S(2)}, u32[]{:S(2)}) %all-to-all-start.3) | async-done | bytes 1966112 | tf_op jit(solution)/shard_map/all_to_all | solution.py:604
  303.3 3.5 %finish.2.refs_9_ = f32[32,24576]{1,0:T(8,128)} custom-call(s32[1]{0:T(128)} %bitcast.4.device_ref, f32[32,24576]{1,0:T(8,128)} %get-tuple-element.221.refs_0_, f32[8,32,1920]{2,1,0:T(8,128)} %all-to-all-done.3.refs_1_), custom_call_target="tpu_custom_call" | custom-call | flops 20000000000 | bytes 66666664 | tf_op jit(solution)/shard_map/finish/pallas_call | solution.py:577
  306.9 1.7 collective-permute-done.40.refs_6_
  309.3 0.7 copy-done.12
  310.0 2.4 finish.3
  (133 shorter events, 9.6 us)
Async XLA Ops:
  3.9 17.9 %copy-start = (f32[32,24576]{1,0:T(8,128)S(1)}, f32[32,24576]{1,0:T(8,128)}, u32[]{:S(2)}) copy-start(f32[32,24576]{1,0:T(8,128)} %refs_5_.3) | copy-start | bytes 9437188
  3.9 61.9 %all-to-all-start = ((f32[8,32,1920]{2,1,0:T(8,128)}), f32[8,32,1920]{2,1,0:T(8,128)}, u32[]{:S(2)}, u32[]{:S(2)}) async-start(f32[8,32,1920]{2,1,0:T(8,128)} %get-tuple-element.133.refs_0_), calls=%async_computation | async-start | bytes 3932160 | tf_op jit(solution)/shard_map/all_to_all | solution.py:604
  14.1 129.5 %copy-start.5 = (s32[192,2]{1,0:T(8,128)}, s32[192,2]{1,0:T(8,128)S(1)}, u32[]{:S(2)}) copy-start(s32[192,2]{1,0:T(8,128)S(1)} %get-tuple-element.137) | copy-start | bytes 4612
  14.1 14.1 %copy-start.38 = (f32[32,1152]{1,0:T(8,128)S(1)}, f32[32,1152]{1,0:T(8,128)}, u32[]{:S(2)}) copy-start(f32[32,1152]{1,0:T(8,128)} %get-tuple-element.142) | copy-start | bytes 442372
  14.1 14.1 %copy-start.37 = (f32[32,1152]{1,0:T(8,128)S(1)}, f32[32,1152]{1,0:T(8,128)}, u32[]{:S(2)}) copy-start(f32[32,1152]{1,0:T(8,128)} %get-tuple-element.143) | copy-start | bytes 442372
  14.1 16.3 %copy-start.3 = (f32[4,128,128]{2,1,0:T(8,128)S(1)}, f32[4,128,128]{2,1,0:T(8,128)}, u32[]{:S(2)}) copy-start(f32[4,128,128]{2,1,0:T(8,128)} %refs_1_.3) | copy-start | bytes 786436
  14.1 3.9 %collective-permute-start.7 = (f32[8,256]{1,0:T(8,128)}, f32[8,256]{1,0:T(8,128)S(1)}, u32[]{:S(2)}, u32[]{:S(2)}) collective-permute-start(f32[8,256]{1,0:T(8,128)} %get-tuple-element.135), channel_id=1, source_target_pairs={{0,2},{1,3},{2,0},{3,1},{4,6},{5,7},{6,4},{7,5},{8,10},{9,11},{10,... | collective-permute-start | bytes 24584 | tf_op jit(solution)/shard_map/ppermute | solution.py:601
  15.7 4.8 %collective-permute-start.8 = (f32[8,256]{1,0:T(8,128)}, f32[8,256]{1,0:T(8,128)S(1)}, u32[]{:S(2)}, u32[]{:S(2)}) collective-permute-start(f32[8,256]{1,0:T(8,128)} %get-tuple-element.136), channel_id=1, source_target_pairs={{0,3},{1,2},{2,1},{3,0},{4,7},{5,6},{6,5},{7,4},{8,11},{9,10},{10,... | collective-permute-start | bytes 24584 | tf_op jit(solution)/shard_map/ppermute | solution.py:601
  17.1 3.9 %collective-permute-start.6 = (f32[8,256]{1,0:T(8,128)}, f32[8,256]{1,0:T(8,128)S(1)}, u32[]{:S(2)}, u32[]{:S(2)}) collective-permute-start(f32[8,256]{1,0:T(8,128)} %get-tuple-element.134), channel_id=1, source_target_pairs={{0,1},{1,0},{2,3},{3,2},{4,5},{5,4},{6,7},{7,6},{8,9},{9,8},{10,11... | collective-permute-start | bytes 24584 | tf_op jit(solution)/shard_map/ppermute | solution.py:601
  18.0 125.5 %copy-start.13 = (f32[8,256]{1,0:T(8,128)}, f32[8,256]{1,0:T(8,128)S(1)}, u32[]{:S(2)}) copy-start(f32[8,256]{1,0:T(8,128)S(1)} %collective-permute-done.7.refs_1_) | copy-start | bytes 24580
  20.5 123.1 %copy-start.15 = (f32[8,256]{1,0:T(8,128)}, f32[8,256]{1,0:T(8,128)S(1)}, u32[]{:S(2)}) copy-start(f32[8,256]{1,0:T(8,128)S(1)} %collective-permute-done.8.refs_2_) | copy-start | bytes 24580
  21.0 122.6 %copy-start.17 = (f32[8,256]{1,0:T(8,128)}, f32[8,256]{1,0:T(8,128)S(1)}, u32[]{:S(2)}) copy-start(f32[8,256]{1,0:T(8,128)S(1)} %collective-permute-done.6.refs_0_) | copy-start | bytes 24580
  26.2 36.2 %collective-permute-start.9 = (f32[97,32,128]{2,1,0:T(8,128)}, f32[97,32,128]{2,1,0:T(8,128)}, u32[]{:S(2)}, u32[]{:S(2)}) collective-permute-start(f32[97,32,128]{2,1,0:T(8,128)} %get-tuple-element.138), channel_id=1, source_target_pairs={{0,1},{1,0},{2,3},{3,2},{4,5},{5,4},{6,7},{7,6},{8,9},{9,8},{10,11... | collective-permute-start | bytes 4767752 | tf_op jit(solution)/shard_map/ppermute | solution.py:601
  27.1 38.7 %collective-permute-start.10 = (f32[97,32,128]{2,1,0:T(8,128)}, f32[97,32,128]{2,1,0:T(8,128)}, u32[]{:S(2)}, u32[]{:S(2)}) collective-permute-start(f32[97,32,128]{2,1,0:T(8,128)} %get-tuple-element.139), channel_id=1, source_target_pairs={{0,2},{1,3},{2,0},{3,1},{4,6},{5,7},{6,4},{7,5},{8,10},{9,11},{10,... | collective-permute-start | bytes 4767752 | tf_op jit(solution)/shard_map/ppermute | solution.py:601
  28.2 4.5 %collective-permute-start.12 = (f32[32,1152]{1,0:T(8,128)S(1)}, f32[32,1152]{1,0:T(8,128)}, u32[]{:S(2)}, u32[]{:S(2)}) collective-permute-start(f32[32,1152]{1,0:T(8,128)S(1)} %copy-done.38), channel_id=1, source_target_pairs={{0,4},{4,0},{8,12},{12,8},{16,20},{20,16},{24,28},{28,24},{1,5},{5... | collective-permute-start | bytes 442376 | tf_op jit(solution)/shard_map/ppermute | solution.py:609
  28.2 18.3 %collective-permute-start.13 = (f32[32,1152]{1,0:T(8,128)S(1)}, f32[32,1152]{1,0:T(8,128)}, u32[]{:S(2)}, u32[]{:S(2)}) collective-permute-start(f32[32,1152]{1,0:T(8,128)S(1)} %copy-done.37), channel_id=1, source_target_pairs={{0,8},{4,12},{8,0},{12,4},{16,24},{20,28},{24,16},{28,20},{1,9},{5... | collective-permute-start | bytes 442376 | tf_op jit(solution)/shard_map/ppermute | solution.py:609
  30.3 42.9 %collective-permute-start.14 = (f32[32,1152]{1,0:T(8,128)}, f32[32,1152]{1,0:T(8,128)}, u32[]{:S(2)}, u32[]{:S(2)}) collective-permute-start(f32[32,1152]{1,0:T(8,128)} %get-tuple-element.144), channel_id=1, source_target_pairs={{0,12},{4,8},{8,4},{12,0},{16,28},{20,24},{24,20},{28,16},{1,13},{... | collective-permute-start | bytes 442376 | tf_op jit(solution)/shard_map/ppermute | solution.py:609
  32.8 40.5 %collective-permute-start.15 = (f32[32,1152]{1,0:T(8,128)}, f32[32,1152]{1,0:T(8,128)}, u32[]{:S(2)}, u32[]{:S(2)}) collective-permute-start(f32[32,1152]{1,0:T(8,128)} %get-tuple-element.145), channel_id=1, source_target_pairs={{0,16},{4,20},{8,24},{12,28},{16,0},{20,4},{24,8},{28,12},{1,17},{... | collective-permute-start | bytes 442376 | tf_op jit(solution)/shard_map/ppermute | solution.py:609
  46.6 28.8 %collective-permute-start.16 = (f32[32,1152]{1,0:T(8,128)}, f32[32,1152]{1,0:T(8,128)}, u32[]{:S(2)}, u32[]{:S(2)}) collective-permute-start(f32[32,1152]{1,0:T(8,128)} %get-tuple-element.146), channel_id=1, source_target_pairs={{0,20},{4,16},{8,28},{12,24},{16,4},{20,0},{24,12},{28,8},{1,21},{... | collective-permute-start | bytes 442376 | tf_op jit(solution)/shard_map/ppermute | solution.py:609
  62.3 13.0 %collective-permute-start.17 = (f32[32,1152]{1,0:T(8,128)}, f32[32,1152]{1,0:T(8,128)}, u32[]{:S(2)}, u32[]{:S(2)}) collective-permute-start(f32[32,1152]{1,0:T(8,128)} %get-tuple-element.147), channel_id=1, source_target_pairs={{0,24},{4,28},{8,16},{12,20},{16,8},{20,12},{24,0},{28,4},{1,25},{... | collective-permute-start | bytes 442376 | tf_op jit(solution)/shard_map/ppermute | solution.py:609
  65.8 9.6 %collective-permute-start.18 = (f32[32,1152]{1,0:T(8,128)}, f32[32,1152]{1,0:T(8,128)}, u32[]{:S(2)}, u32[]{:S(2)}) collective-permute-start(f32[32,1152]{1,0:T(8,128)} %get-tuple-element.148), channel_id=1, source_target_pairs={{0,28},{4,24},{8,20},{12,16},{16,12},{20,8},{24,4},{28,0},{1,29},{... | collective-permute-start | bytes 442376 | tf_op jit(solution)/shard_map/ppermute | solution.py:609
  81.5 12.1 %copy-start.22 = (s32[192,2]{0,1:T(2,128)S(1)}, s32[192,2]{0,1:T(2,128)}, u32[]{:S(2)}) copy-start(s32[192,2]{0,1:T(2,128)} %param.21) | copy-start | bytes 4612
  81.5 80.5 %all-to-all-start.1 = ((f32[8,32,3072]{2,1,0:T(8,128)}), f32[8,32,3072]{2,1,0:T(8,128)}, u32[]{:S(2)}, u32[]{:S(2)}) async-start(f32[8,32,3072]{2,1,0:T(8,128)} %bitcast.54), calls=%async_computation.1 | async-start | bytes 6291456 | tf_op jit(solution)/shard_map/all_to_all | solution.py:604
  89.9 38.4 %collective-permute-start.11 = (f32[97,32,128]{2,1,0:T(8,128)}, f32[97,32,128]{2,1,0:T(8,128)}, u32[]{:S(2)}, u32[]{:S(2)}) collective-permute-start(f32[97,32,128]{2,1,0:T(8,128)} %get-tuple-element.140), channel_id=1, source_target_pairs={{0,3},{1,2},{2,1},{3,0},{4,7},{5,6},{6,5},{7,4},{8,11},{9,10},{10,... | collective-permute-start | bytes 4767752 | tf_op jit(solution)/shard_map/ppermute | solution.py:601
  102.1 26.2 %copy-start.24 = (s32[192,2]{0,1:T(2,128)S(1)}, s32[192,2]{0,1:T(2,128)}, u32[]{:S(2)}) copy-start(s32[192,2]{0,1:T(2,128)} %param.20) | copy-start | bytes 4612
  143.8 4.6 %collective-permute-start.21 = (f32[8,128]{1,0:T(8,128)S(1)}, f32[8,128]{1,0:T(8,128)S(1)}, u32[]{:S(2)}, u32[]{:S(2)}) collective-permute-start(f32[8,128]{1,0:T(8,128)S(1)} %get-tuple-element.155), channel_id=1, source_target_pairs={{0,3},{1,2},{2,1},{3,0},{4,7},{5,6},{6,5},{7,4},{8,11},{9,10},{10,... | collective-permute-start | bytes 12296 | tf_op jit(solution)/shard_map/ppermute | solution.py:601
  146.3 3.6 %collective-permute-start.20 = (f32[8,128]{1,0:T(8,128)S(1)}, f32[8,128]{1,0:T(8,128)S(1)}, u32[]{:S(2)}, u32[]{:S(2)}) collective-permute-start(f32[8,128]{1,0:T(8,128)S(1)} %get-tuple-element.155), channel_id=1, source_target_pairs={{0,2},{1,3},{2,0},{3,1},{4,6},{5,7},{6,4},{7,5},{8,10},{9,11},{10,... | collective-permute-start | bytes 12296 | tf_op jit(solution)/shard_map/ppermute | solution.py:601
  146.8 3.6 %collective-permute-start.19 = (f32[8,128]{1,0:T(8,128)S(1)}, f32[8,128]{1,0:T(8,128)S(1)}, u32[]{:S(2)}, u32[]{:S(2)}) collective-permute-start(f32[8,128]{1,0:T(8,128)S(1)} %get-tuple-element.155), channel_id=1, source_target_pairs={{0,1},{1,0},{2,3},{3,2},{4,5},{5,4},{6,7},{7,6},{8,9},{9,8},{10,11... | collective-permute-start | bytes 12296 | tf_op jit(solution)/shard_map/ppermute | solution.py:601
  150.4 1.2 collective-permute-start.22
  151.6 4.8 %collective-permute-start.25 = (f32[8,128]{1,0:T(8,128)S(1)}, f32[8,128]{1,0:T(8,128)S(1)}, u32[]{:S(2)}, u32[]{:S(2)}) collective-permute-start(f32[8,128]{1,0:T(8,128)S(1)} %add.168.refs_0_), channel_id=1, source_target_pairs={{0,24},{4,28},{8,0},{12,4},{16,8},{20,12},{24,16},{28,20},{1,25},{... | collective-permute-start | bytes 12296 | tf_op jit(solution)/shard_map/ppermute | solution.py:697
  155.0 6.9 %collective-permute-start.24 = (f32[8,128]{1,0:T(8,128)S(1)}, f32[8,128]{1,0:T(8,128)S(1)}, u32[]{:S(2)}, u32[]{:S(2)}) collective-permute-start(f32[8,128]{1,0:T(8,128)S(1)} %add.168.refs_0_), channel_id=1, source_target_pairs={{0,16},{4,20},{8,24},{12,28},{16,0},{20,4},{24,8},{28,12},{1,17},{... | collective-permute-start | bytes 12296 | tf_op jit(solution)/shard_map/ppermute | solution.py:697
  155.8 6.2 %collective-permute-start.23 = (f32[8,128]{1,0:T(8,128)S(1)}, f32[8,128]{1,0:T(8,128)S(1)}, u32[]{:S(2)}, u32[]{:S(2)}) collective-permute-start(f32[8,128]{1,0:T(8,128)S(1)} %add.168.refs_0_), channel_id=1, source_target_pairs={{0,8},{4,12},{8,16},{12,20},{16,24},{20,28},{24,0},{28,4},{1,9},{5... | collective-permute-start | bytes 12296 | tf_op jit(solution)/shard_map/ppermute | solution.py:697
  168.3 63.7 %all-to-all-start.2 = ((f32[8,32,1920]{2,1,0:T(8,128)}), f32[8,32,1920]{2,1,0:T(8,128)}, u32[]{:S(2)}, u32[]{:S(2)}) async-start(f32[8,32,1920]{2,1,0:T(8,128)} %get-tuple-element.170), calls=%async_computation.2 | async-start | bytes 3932160 | tf_op jit(solution)/shard_map/all_to_all | solution.py:604
  176.8 11.4 %copy-start.39 = (f32[32,1152]{1,0:T(8,128)S(1)}, f32[32,1152]{1,0:T(8,128)}, u32[]{:S(2)}) copy-start(f32[32,1152]{1,0:T(8,128)} %get-tuple-element.165) | copy-start | bytes 442372
  176.8 35.5 %copy-start.33 = (f32[32,1152]{1,0:T(8,128)S(1)}, f32[32,1152]{1,0:T(8,128)}, u32[]{:S(2)}) copy-start(f32[32,1152]{1,0:T(8,128)} %get-tuple-element.168) | copy-start | bytes 442372
  176.8 43.6 %copy-start.32 = (f32[32,1152]{1,0:T(8,128)S(1)}, f32[32,1152]{1,0:T(8,128)}, u32[]{:S(2)}) copy-start(f32[32,1152]{1,0:T(8,128)} %get-tuple-element.169) | copy-start | bytes 442372
  183.2 37.2 %collective-permute-start.26 = (f32[97,32,128]{2,1,0:T(8,128)}, f32[97,32,128]{2,1,0:T(8,128)S(1)}, u32[]{:S(2)}, u32[]{:S(2)}) collective-permute-start(f32[97,32,128]{2,1,0:T(8,128)} %get-tuple-element.159), channel_id=1, source_target_pairs={{0,1},{1,0},{2,3},{3,2},{4,5},{5,4},{6,7},{7,6},{8,9},{9,8},{10,11... | collective-permute-start | bytes 4767752 | tf_op jit(solution)/shard_map/ppermute | solution.py:601
  184.7 38.3 %collective-permute-start.27 = (f32[97,32,128]{2,1,0:T(8,128)}, f32[97,32,128]{2,1,0:T(8,128)S(1)}, u32[]{:S(2)}, u32[]{:S(2)}) collective-permute-start(f32[97,32,128]{2,1,0:T(8,128)} %get-tuple-element.160), channel_id=1, source_target_pairs={{0,2},{1,3},{2,0},{3,1},{4,6},{5,7},{6,4},{7,5},{8,10},{9,11},{10,... | collective-permute-start | bytes 4767752 | tf_op jit(solution)/shard_map/ppermute | solution.py:601
  186.3 2.1 collective-permute-start.29
  186.3 22.5 %collective-permute-start.30 = (f32[32,1152]{1,0:T(8,128)S(1)}, f32[32,1152]{1,0:T(8,128)S(1)}, u32[]{:S(2)}, u32[]{:S(2)}) collective-permute-start(f32[32,1152]{1,0:T(8,128)S(1)} %copy-done.40), channel_id=1, source_target_pairs={{0,8},{4,12},{8,0},{12,4},{16,24},{20,28},{24,16},{28,20},{1,9},{5... | collective-permute-start | bytes 442376 | tf_op jit(solution)/shard_map/ppermute | solution.py:609
  188.2 24.1 %collective-permute-start.31 = (f32[32,1152]{1,0:T(8,128)S(1)}, f32[32,1152]{1,0:T(8,128)S(1)}, u32[]{:S(2)}, u32[]{:S(2)}) collective-permute-start(f32[32,1152]{1,0:T(8,128)S(1)} %copy-done.39), channel_id=1, source_target_pairs={{0,12},{4,8},{8,4},{12,0},{16,28},{20,24},{24,20},{28,16},{1,13},{... | collective-permute-start | bytes 442376 | tf_op jit(solution)/shard_map/ppermute | solution.py:609
  188.3 34.7 %copy-start.34 = (f32[32,1152]{1,0:T(8,128)}, f32[32,1152]{1,0:T(8,128)S(1)}, u32[]{:S(2)}) copy-start(f32[32,1152]{1,0:T(8,128)S(1)} %collective-permute-done.29.refs_1_) | copy-start | bytes 442372
  188.3 55.8 %collective-permute-start.32 = (f32[32,1152]{1,0:T(8,128)}, f32[32,1152]{1,0:T(8,128)}, u32[]{:S(2)}, u32[]{:S(2)}) collective-permute-start(f32[32,1152]{1,0:T(8,128)} %get-tuple-element.166), channel_id=1, source_target_pairs={{0,16},{4,20},{8,24},{12,28},{16,0},{20,4},{24,8},{28,12},{1,17},{... | collective-permute-start | bytes 442376 | tf_op jit(solution)/shard_map/ppermute | solution.py:609
  208.7 14.3 %copy-start.35 = (f32[32,1152]{1,0:T(8,128)}, f32[32,1152]{1,0:T(8,128)S(1)}, u32[]{:S(2)}) copy-start(f32[32,1152]{1,0:T(8,128)S(1)} %collective-permute-done.30.refs_2_) | copy-start | bytes 442372
  208.7 35.4 %collective-permute-start.33 = (f32[32,1152]{1,0:T(8,128)}, f32[32,1152]{1,0:T(8,128)}, u32[]{:S(2)}, u32[]{:S(2)}) collective-permute-start(f32[32,1152]{1,0:T(8,128)} %get-tuple-element.167), channel_id=1, source_target_pairs={{0,20},{4,16},{8,28},{12,24},{16,4},{20,0},{24,12},{28,8},{1,21},{... | collective-permute-start | bytes 442376 | tf_op jit(solution)/shard_map/ppermute | solution.py:609
  212.4 10.7 %copy-start.36 = (f32[32,1152]{1,0:T(8,128)}, f32[32,1152]{1,0:T(8,128)S(1)}, u32[]{:S(2)}) copy-start(f32[32,1152]{1,0:T(8,128)S(1)} %collective-permute-done.31.refs_3_) | copy-start | bytes 442372
  212.4 31.8 %collective-permute-start.34 = (f32[32,1152]{1,0:T(8,128)S(1)}, f32[32,1152]{1,0:T(8,128)}, u32[]{:S(2)}, u32[]{:S(2)}) collective-permute-start(f32[32,1152]{1,0:T(8,128)S(1)} %copy-done.33), channel_id=1, source_target_pairs={{0,24},{4,28},{8,16},{12,20},{16,8},{20,12},{24,0},{28,4},{1,25},{... | collective-permute-start | bytes 442376 | tf_op jit(solution)/shard_map/ppermute | solution.py:609
  220.5 11.6 %copy-start.30 = (f32[97,32,128]{2,1,0:T(8,128)}, f32[97,32,128]{2,1,0:T(8,128)S(1)}, u32[]{:S(2)}) copy-start(f32[97,32,128]{2,1,0:T(8,128)S(1)} %collective-permute-done.26.refs_5_.refs_2_) | copy-start | bytes 4767748
  220.5 23.7 %collective-permute-start.35 = (f32[32,1152]{1,0:T(8,128)S(1)}, f32[32,1152]{1,0:T(8,128)}, u32[]{:S(2)}, u32[]{:S(2)}) collective-permute-start(f32[32,1152]{1,0:T(8,128)S(1)} %copy-done.32), channel_id=1, source_target_pairs={{0,28},{4,24},{8,20},{12,16},{16,12},{20,8},{24,4},{28,0},{1,29},{... | collective-permute-start | bytes 442376 | tf_op jit(solution)/shard_map/ppermute | solution.py:609
  223.0 38.8 %collective-permute-start.28 = (f32[97,32,128]{2,1,0:T(8,128)}, f32[97,32,128]{2,1,0:T(8,128)}, u32[]{:S(2)}, u32[]{:S(2)}) collective-permute-start(f32[97,32,128]{2,1,0:T(8,128)} %get-tuple-element.161), channel_id=1, source_target_pairs={{0,3},{1,2},{2,1},{3,0},{4,7},{5,6},{6,5},{7,4},{8,11},{9,10},{10,... | collective-permute-start | bytes 4767752 | tf_op jit(solution)/shard_map/ppermute | solution.py:601
  239.5 63.8 %all-to-all-start.3 = ((f32[8,32,1920]{2,1,0:T(8,128)}), f32[8,32,1920]{2,1,0:T(8,128)}, u32[]{:S(2)}, u32[]{:S(2)}) async-start(f32[8,32,1920]{2,1,0:T(8,128)} %bitcast.56), calls=%async_computation.3 | async-start | bytes 3932160 | tf_op jit(solution)/shard_map/all_to_all | solution.py:604
  268.4 19.2 %collective-permute-start.36 = (f32[32,1152]{1,0:T(8,128)}, f32[32,1152]{1,0:T(8,128)}, u32[]{:S(2)}, u32[]{:S(2)}) collective-permute-start(f32[32,1152]{1,0:T(8,128)} %get-tuple-element.172), channel_id=1, source_target_pairs={{0,4},{4,0},{8,12},{12,8},{16,20},{20,16},{24,28},{28,24},{1,5},{5... | collective-permute-start | bytes 442376 | tf_op jit(solution)/shard_map/ppermute | solution.py:609
  268.6 19.5 %collective-permute-start.37 = (f32[32,1152]{1,0:T(8,128)}, f32[32,1152]{1,0:T(8,128)}, u32[]{:S(2)}, u32[]{:S(2)}) collective-permute-start(f32[32,1152]{1,0:T(8,128)} %get-tuple-element.173), channel_id=1, source_target_pairs={{0,8},{4,12},{8,0},{12,4},{16,24},{20,28},{24,16},{28,20},{1,9},{5... | collective-permute-start | bytes 442376 | tf_op jit(solution)/shard_map/ppermute | solution.py:609
  268.6 14.4 %copy-start.6 = (s32[192,2]{1,0:T(8,128)S(1)}, s32[192,2]{1,0:T(8,128)}, u32[]{:S(2)}) copy-start(s32[192,2]{1,0:T(8,128)} %copy-done.5) | copy-start | bytes 4612
  268.6 14.4 %copy-start.14 = (f32[8,256]{1,0:T(8,128)S(1)}, f32[8,256]{1,0:T(8,128)}, u32[]{:S(2)}) copy-start(f32[8,256]{1,0:T(8,128)} %copy-done.13) | copy-start | bytes 24580
  268.6 14.4 %copy-start.16 = (f32[8,256]{1,0:T(8,128)S(1)}, f32[8,256]{1,0:T(8,128)}, u32[]{:S(2)}) copy-start(f32[8,256]{1,0:T(8,128)} %copy-done.15) | copy-start | bytes 24580
  268.6 14.4 %copy-start.18 = (f32[8,256]{1,0:T(8,128)S(1)}, f32[8,256]{1,0:T(8,128)}, u32[]{:S(2)}) copy-start(f32[8,256]{1,0:T(8,128)} %copy-done.17) | copy-start | bytes 24580
  268.6 14.4 %copy-start.21 = (s32[192,2]{0,1:T(2,128)S(1)}, s32[192,2]{0,1:T(2,128)}, u32[]{:S(2)}) copy-start(s32[192,2]{0,1:T(2,128)} %param.19) | copy-start | bytes 4612
  268.7 14.4 %copy-start.23 = (s32[192,2]{0,1:T(2,128)S(1)}, s32[192,2]{0,1:T(2,128)}, u32[]{:S(2)}) copy-start(s32[192,2]{0,1:T(2,128)} %param.21) | copy-start | bytes 4612
  283.1 23.7 %collective-permute-start.38 = (f32[32,1152]{1,0:T(8,128)}, f32[32,1152]{1,0:T(8,128)S(1)}, u32[]{:S(2)}, u32[]{:S(2)}) collective-permute-start(f32[32,1152]{1,0:T(8,128)} %get-tuple-element.174), channel_id=1, source_target_pairs={{0,12},{4,8},{8,4},{12,0},{16,28},{20,24},{24,20},{28,16},{1,13},{... | collective-permute-start | bytes 442376 | tf_op jit(solution)/shard_map/ppermute | solution.py:609
  284.9 22.0 %collective-permute-start.39 = (f32[32,1152]{1,0:T(8,128)}, f32[32,1152]{1,0:T(8,128)S(1)}, u32[]{:S(2)}, u32[]{:S(2)}) collective-permute-start(f32[32,1152]{1,0:T(8,128)} %get-tuple-element.175), channel_id=1, source_target_pairs={{0,16},{4,20},{8,24},{12,28},{16,0},{20,4},{24,8},{28,12},{1,17},{... | collective-permute-start | bytes 442376 | tf_op jit(solution)/shard_map/ppermute | solution.py:609
  284.9 23.7 %collective-permute-start.40 = (f32[32,1152]{1,0:T(8,128)}, f32[32,1152]{1,0:T(8,128)S(1)}, u32[]{:S(2)}, u32[]{:S(2)}) collective-permute-start(f32[32,1152]{1,0:T(8,128)} %get-tuple-element.176), channel_id=1, source_target_pairs={{0,20},{4,16},{8,28},{12,24},{16,4},{20,0},{24,12},{28,8},{1,21},{... | collective-permute-start | bytes 442376 | tf_op jit(solution)/shard_map/ppermute | solution.py:609
  287.6 21.0 %collective-permute-start.41 = (f32[32,1152]{1,0:T(8,128)}, f32[32,1152]{1,0:T(8,128)S(1)}, u32[]{:S(2)}, u32[]{:S(2)}) collective-permute-start(f32[32,1152]{1,0:T(8,128)} %get-tuple-element.177), channel_id=1, source_target_pairs={{0,24},{4,28},{8,16},{12,20},{16,8},{20,12},{24,0},{28,4},{1,25},{... | collective-permute-start | bytes 442376 | tf_op jit(solution)/shard_map/ppermute | solution.py:609
  288.1 20.5 %collective-permute-start.42 = (f32[32,1152]{1,0:T(8,128)}, f32[32,1152]{1,0:T(8,128)S(1)}, u32[]{:S(2)}, u32[]{:S(2)}) collective-permute-start(f32[32,1152]{1,0:T(8,128)} %get-tuple-element.178), channel_id=1, source_target_pairs={{0,28},{4,24},{8,20},{12,16},{16,12},{20,8},{24,4},{28,0},{1,29},{... | collective-permute-start | bytes 442376 | tf_op jit(solution)/shard_map/ppermute | solution.py:609
  (18 other events, 87.4 us)

commit v6 on v5

--- a/solution.py
+++ b/solution.py
@@ -65,20 +65,19 @@
     )(alpha_hamiltonian, alpha_pairs, pair_tables, *after)
 
 
-def pack(vector, device, parts, wide, narrow):
+def pack(vector, device, parts, start, width, listed, after):
     rows = vector.shape[0]
 
     def kernel(device_ref, source, *refs):
-        targets = refs[: 1 + parts]
-        held, few, sems = refs[-3:]
-        copies = []
+        targets = refs[len(after) : -2]
+        held, sems = refs[-2:]
+        taken = []
+        given = []
         for j in range(parts):
-            copies.append((source.at[:, j * wide : (j + 1) * wide], held.at[j], targets[0].at[j]))
-        for k in range(parts):
-            at = pl.multiple_of(parts * wide + (device_ref[0] ^ k) * narrow, SB)
-            copies.append((source.at[:, pl.ds(at, narrow)], few.at[k], targets[1 + k]))
-        taken = [pltpu.make_async_copy(a, b, sems.at[0, i]) for i, (a, b, _) in enumerate(copies)]
-        given = [pltpu.make_async_copy(b, c, sems.at[1, i]) for i, (_, b, c) in enumerate(copies)]
+            at = pl.multiple_of(start + ((device_ref[0] ^ j) if listed else j) * width, SB)
+            target = targets[j] if listed else targets[0].at[j]
+            taken.append(pltpu.make_async_copy(source.at[:, pl.ds(at, width)], held.at[j], sems.at[0, j]))
+            given.append(pltpu.make_async_copy(held.at[j], target, sems.at[1, j]))
         for copy in taken:
             copy.start()
         for first, second in zip(taken, given):
@@ -88,22 +87,17 @@
             copy.wait()
 
     anywhere = pl.BlockSpec(memory_space=pl.ANY)
-    out = pl.pallas_call(
-        kernel,
-        in_specs=[pl.BlockSpec(memory_space=pltpu.SMEM), anywhere],
-        out_specs=[anywhere] * (1 + parts),
-        out_shape=[jax.ShapeDtypeStruct((parts, rows, wide), f32)]
-        + [jax.ShapeDtypeStruct((rows, narrow), f32)] * parts,
-        scratch_shapes=[
-            pltpu.VMEM((parts, rows, wide), f32),
-            pltpu.VMEM((parts, rows, narrow), f32),
-            pltpu.SemaphoreType.DMA((2, 2 * parts)),
-        ],
+    shapes = [(rows, width)] * parts if listed else [(parts, rows, width)]
+    return pl.pallas_call(
+        kernel,
+        in_specs=[pl.BlockSpec(memory_space=pltpu.SMEM)] + [anywhere] * (1 + len(after)),
+        out_specs=[anywhere] * len(shapes),
+        out_shape=[jax.ShapeDtypeStruct(shape, f32) for shape in shapes],
+        scratch_shapes=[pltpu.VMEM((parts, rows, width), f32), pltpu.SemaphoreType.DMA((2, parts))],
         compiler_params=params(),
         cost_estimate=cost(0, 0),
         name="pack",
-    )(device, vector)
-    return out[0], out[1:]
+    )(device, vector, *after)
 
 
 def alpha_sum(columns, prepared, cross_pairs, cross_signs, device, start, after, work, full, offset, previous):
@@ -631,8 +625,9 @@
         device = lax.axis_index("alpha").astype(jnp.int32).reshape(1)
         me = lax.axis_index("beta").astype(jnp.int32)
 
-        sent, sent_few = pack(start_vector, device, n_alpha, wide, narrow)
+        (sent,) = pack(start_vector, device, n_alpha, 0, wide, False, [])
         arrived = turn(sent)
+        sent_few = pack(start_vector, device, n_alpha, border, narrow, True, [sent])
         arrived_few = swap(sent_few)
 
         *marks, found = mark(source_blocks, me.reshape(1), n_beta, [sent])

time: 317 us -> 317 us (level)
  transfers between devices with their start and end apart: 41 -> 41, of which waited for: 18 -> 18; matrix products, arithmetic and copies ran while one was open for 3% -> 3% of each run, Pallas kernels for 24% -> 25%
where the time goes in v6:
time: 317 us; the launch traced here: 312 us
  waiting for transfers between devices  121 us (38%)
  Pallas kernels  93.6 us (30%)
  starting transfers between devices  80 us (25%)
  local copies, waits for them, and re-layouts  8.24 us (3%)
  other arithmetic  4.53 us (1%)
  between operations  4.03 us (1%)
    ppermute x12, waiting for transfers between devices, to_partners(): lax.ppermute(part, 'beta', [(i, i ^ k) for i in range(n_beta)])  64.2 us
    ppermute x21, starting transfers between devices, swap(): lax.ppermute(parts[k], 'alpha', [(i, i ^ k) for i in range(n_alpha)])  34.2 us
    ppermute x21, waiting for transfers between devices, swap(): lax.ppermute(parts[k], 'alpha', [(i, i ^ k) for i in range(n_alpha)])  31.4 us
    pallas_call x2, Pallas kernels, beta_sum(): pl.pallas_call(kernel, grid_spec=pltpu.PrefetchScalarGridSpec(num_scalar_...  29.5 us
    pallas_call x4, Pallas kernels, alpha_sum(): pl.pallas_call(kernel, in_specs=[pl.BlockSpec(memory_space=pltpu.SMEM)] *...  27.7 us
    all_to_all x4, starting transfers between devices, turn(): return lax.all_to_all(parts, 'alpha', 0, 0, tiled=True)  23.9 us
    all_to_all x4, waiting for transfers between devices, turn(): return lax.all_to_all(parts, 'alpha', 0, 0, tiled=True)  18.7 us
    ppermute x12, starting transfers between devices, to_partners(): lax.ppermute(part, 'beta', [(i, i ^ k) for i in range(n_beta)])  17.1 us
  transfers between devices with their start and end apart: 41, of which 18 were waited for; matrix products, arithmetic and copies ran while one was open for 3% of the time, Pallas kernels for 25%

profile of v6, /device:TPU:0, one launch (start us, length us, event | category | flops | bytes accessed | tf_op | source)
XLA Modules:
  0.0 311.8 jit_solution(11032202602825268218)
XLA Ops:
  0.6 2.5 pack.2.refs_0_
  3.1 6.6 %all-to-all-start = ((f32[8,32,1920]{2,1,0:T(8,128)}), f32[8,32,1920]{2,1,0:T(8,128)}, u32[]{:S(2)}, u32[]{:S(2)}) async-start(f32[8,32,1920]{2,1,0:T(8,128)} %pack.2.refs_0_), calls=%async_computation | async-start | bytes 3932160 | tf_op jit(solution)/shard_map/all_to_all | solution.py:598
  9.7 0.8 copy.15.source_ref
  10.5 2.8 mark.1
  13.3 1.6 collective-permute-start.7
  14.9 1.4 collective-permute-start.8
  17.3 2.4 collective-permute-done.8.refs_2_
  20.2 0.8 positions.5.slots_ref
  21.0 4.4 %gather_blocks.6 = (f32[97,32,128]{2,1,0:T(8,128)}, f32[97,32,128]{2,1,0:T(8,128)}, f32[97,32,128]{2,1,0:T(8,128)}) custom-call(s32[8,256]{1,0:T(8,128)} %positions.5.slots_ref, f32[32,24576]{1,0:T(8,128)S(1)} %copy-done), custom_call_target="tpu_custom_call" | custom-call | flops 1 | bytes 1 | tf_op jit(solution)/shard_map/gather_blocks/pallas_call | solution.py:315
  25.4 1.0 collective-permute-start.9
  26.3 1.1 collective-permute-start.10
  27.4 1.5 pack.3
  29.0 2.1 collective-permute-start.13
  31.2 2.3 prepare.1
  33.5 2.6 collective-permute-start.15
  36.2 9.8 %collective-permute-done.13.refs_2_ = f32[32,1152]{1,0:T(8,128)} collective-permute-done((f32[32,1152]{1,0:T(8,128)}, f32[32,1152]{1,0:T(8,128)}, u32[]{:S(2)}, u32[]{:S(2)}) %collective-permute-start.13) | collective-permute-done | bytes 147488 | tf_op jit(solution)/shard_map/ppermute | solution.py:603
  45.9 3.6 %collective-permute-start.16 = (f32[32,1152]{1,0:T(8,128)}, f32[32,1152]{1,0:T(8,128)}, u32[]{:S(2)}, u32[]{:S(2)}) collective-permute-start(f32[32,1152]{1,0:T(8,128)} %get-tuple-element.144), channel_id=1, source_target_pairs={{0,20},{4,16},{8,28},{12,24},{16,4},{20,0},{24,12},{28,8},{1,21},{... | collective-permute-start | bytes 442376 | tf_op jit(solution)/shard_map/ppermute | solution.py:603
  49.5 12.0 %collective-permute-done.9.refs_5_.refs_2_ = f32[97,32,128]{2,1,0:T(8,128)} collective-permute-done((f32[97,32,128]{2,1,0:T(8,128)}, f32[97,32,128]{2,1,0:T(8,128)}, u32[]{:S(2)}, u32[]{:S(2)}) %collective-permute-start.9) | collective-permute-done | bytes 1589280 | tf_op jit(solution)/shard_map/ppermute | solution.py:595
  61.5 3.5 %collective-permute-start.17 = (f32[32,1152]{1,0:T(8,128)}, f32[32,1152]{1,0:T(8,128)}, u32[]{:S(2)}, u32[]{:S(2)}) collective-permute-start(f32[32,1152]{1,0:T(8,128)} %get-tuple-element.145), channel_id=1, source_target_pairs={{0,24},{4,28},{8,16},{12,20},{16,8},{20,12},{24,0},{28,4},{1,25},{... | collective-permute-start | bytes 442376 | tf_op jit(solution)/shard_map/ppermute | solution.py:603
  65.0 7.4 %alpha_sum.4.refs_12_ = f32[256,3072]{1,0:T(8,128)} custom-call(s32[1]{0:T(128)} %bitcast.4.device_ref, s32[2,192]{1,0:T(2,128)} %pairs_ref.7, s32[2,192]{1,0:T(2,128)} %signs_ref.7, f32[256,1920]{1,0:T(8,128)} %bitcast.10.refs_0_, bf16[256,1536]{1,0:T(8,128)(2,1)} %get-tuple-element.147.refs_1_.refs_8_, ...), custom_call_target="tpu_custom_call" | custom-call | flops 20000000000 | bytes 66666664 | tf_op jit(solution)/shard_map/alpha_sum/pallas_call | solution.py:201
  72.4 2.1 collective-permute-done.16.refs_5_
  74.6 6.2 %alpha_sum.5 = f32[256,3072]{1,0:T(8,128)} custom-call(s32[1]{0:T(128)} %bitcast.4.device_ref, s32[2,192]{1,0:T(2,128)} %pairs_ref.7, s32[2,192]{1,0:T(2,128)} %signs_ref.7, f32[32,1152]{1,0:T(8,128)} %get-tuple-element.139.refs_0_, f32[32,1152]{1,0:T(8,128)} %collective-permute-done.12.refs_1_, ...), custom_call_target="tpu_custom_call", output_to_operand_aliasing={{}: (15, {})} | custom-call | flops 1 | bytes 1 | tf_op jit(solution)/shard_map/alpha_sum/pallas_call | solution.py:201
  80.8 8.4 %all-to-all-start.1 = ((f32[8,32,3072]{2,1,0:T(8,128)}), f32[8,32,3072]{2,1,0:T(8,128)}, u32[]{:S(2)}, u32[]{:S(2)}) async-start(f32[8,32,3072]{2,1,0:T(8,128)} %bitcast.54), calls=%async_computation.1 | async-start | bytes 6291456 | tf_op jit(solution)/shard_map/all_to_all | solution.py:598
  89.2 2.4 collective-permute-start.11
  91.6 1.2 slice.18
  97.8 1.4 slice.28
  99.1 2.4 fusion.2
  102.1 1.5 fusion.9
  104.2 23.3 %collective-permute-done.11.refs_4_ = f32[97,32,128]{2,1,0:T(8,128)} collective-permute-done((f32[97,32,128]{2,1,0:T(8,128)}, f32[97,32,128]{2,1,0:T(8,128)}, u32[]{:S(2)}, u32[]{:S(2)}) %collective-permute-start.11) | collective-permute-done | bytes 1589280 | tf_op jit(solution)/shard_map/ppermute | solution.py:595
  127.6 15.2 %beta_sum.6 = (f32[32,24576]{1,0:T(8,128)}, f32[8,128]{1,0:T(8,128)S(1)}) custom-call(s32[2,192]{1,0:T(2,128)} %get-tuple-element.213.slots_ref, s32[2,192]{1,0:T(2,128)} %get-tuple-element.212.sign_ref, s32[2,192]{1,0:T(2,128)S(1)} %bitcast.57, f32[32,24576]{1,0:T(8,128)S(1)} %copy-done, f32[4,128,128]{2,1,0:T(8,128)S(1)} %copy-done.3, ...), custom_call_target="tpu_custom_call" | custom-call | flops 1 | bytes 1 | tf_op jit(solution)/shard_map/beta_sum/pallas_call | solution.py:407
  143.0 2.5 collective-permute-start.21
  146.5 1.0 collective-permute-done.21
  147.6 1.6 collective-permute-done.20
  149.6 1.2 collective-permute-done.22
  150.8 3.5 %collective-permute-start.25 = (f32[8,128]{1,0:T(8,128)S(1)}, f32[8,128]{1,0:T(8,128)S(1)}, u32[]{:S(2)}, u32[]{:S(2)}) collective-permute-start(f32[8,128]{1,0:T(8,128)S(1)} %add.168.refs_0_), channel_id=1, source_target_pairs={{0,24},{4,28},{8,0},{12,4},{16,8},{20,12},{24,16},{28,20},{1,25},{... | collective-permute-start | bytes 12296 | tf_op jit(solution)/shard_map/ppermute | solution.py:692
  154.3 0.7 collective-permute-start.24
  155.6 5.6 %collective-permute-done.24.refs_2_ = f32[8,128]{1,0:T(8,128)S(1)} collective-permute-done((f32[8,128]{1,0:T(8,128)S(1)}, f32[8,128]{1,0:T(8,128)S(1)}, u32[]{:S(2)}, u32[]{:S(2)}) %collective-permute-start.24) | collective-permute-done | bytes 4128 | tf_op jit(solution)/shard_map/ppermute | solution.py:692
  161.8 5.7 %correct.2 = (f32[32,24576]{1,0:T(8,128)}, f32[8,32,1920]{2,1,0:T(8,128)}) custom-call(s32[1]{0:T(128)} %bitcast.4.device_ref, f32[8,128]{1,0:T(8,128)} %copy-done.19, f32[8,128]{1,0:T(8,128)} %copy-done.28, f32[8,128]{1,0:T(8,128)} %copy-done.27, f32[8,128]{1,0:T(8,128)} %copy-done.26, f32[32,24576]{1,0:T(8,128)} %get-tuple-element.154.refs_4_, ...), custom_call_target="tpu_custom_call" | custom-call | flops 1 | bytes 1 | tf_op jit(solution)/shard_map/correct/pallas_call | solution.py:493
  167.6 4.3 %all-to-all-start.2 = ((f32[8,32,1920]{2,1,0:T(8,128)}), f32[8,32,1920]{2,1,0:T(8,128)}, u32[]{:S(2)}, u32[]{:S(2)}) async-start(f32[8,32,1920]{2,1,0:T(8,128)} %get-tuple-element.168), calls=%async_computation.2 | async-start | bytes 3932160 | tf_op jit(solution)/shard_map/all_to_all | solution.py:598
  171.9 4.1 %correct.3 = (f32[32,24576]{1,0:T(8,128)}, f32[32,1152]{1,0:T(8,128)}, f32[32,1152]{1,0:T(8,128)}, f32[32,1152]{1,0:T(8,128)}, f32[32,1152]{1,0:T(8,128)}, /*ind...) custom-call(s32[1]{0:T(128)} %bitcast.4.device_ref, ...), custom_call_target="tpu_custom_call", output_to_operand_aliasing={{0}: (9, {})} | custom-call | flops 1 | bytes 1 | tf_op jit(solution)/shard_map/correct/pallas_call | solution.py:493
  176.1 6.4 %gather_blocks.7 = (f32[97,32,128]{2,1,0:T(8,128)}, f32[97,32,128]{2,1,0:T(8,128)}, f32[97,32,128]{2,1,0:T(8,128)}) custom-call(s32[8,256]{1,0:T(8,128)} %positions.5.slots_ref, f32[32,24576]{1,0:T(8,128)} %get-tuple-element.130.v_ref.refs_0_), custom_call_target="tpu_custom_call" | custom-call | flops 1 | bytes 1 | tf_op jit(solution)/shard_map/gather_blocks/pallas_call | solution.py:315
  182.5 1.5 collective-permute-start.26
  184.0 1.5 collective-permute-start.27
  185.5 1.9 collective-permute-start.30
  187.6 2.6 collective-permute-start.32
  190.2 17.8 %collective-permute-done.30.refs_2_ = f32[32,1152]{1,0:T(8,128)S(1)} collective-permute-done((f32[32,1152]{1,0:T(8,128)S(1)}, f32[32,1152]{1,0:T(8,128)S(1)}, u32[]{:S(2)}, u32[]{:S(2)}) %collective-permute-start.30) | collective-permute-done | bytes 147488 | tf_op jit(solution)/shard_map/ppermute | solution.py:603
  208.0 3.6 %collective-permute-start.33 = (f32[32,1152]{1,0:T(8,128)}, f32[32,1152]{1,0:T(8,128)}, u32[]{:S(2)}, u32[]{:S(2)}) collective-permute-start(f32[32,1152]{1,0:T(8,128)} %get-tuple-element.165), channel_id=1, source_target_pairs={{0,20},{4,16},{8,28},{12,24},{16,4},{20,0},{24,12},{28,8},{1,21},{... | collective-permute-start | bytes 442376 | tf_op jit(solution)/shard_map/ppermute | solution.py:603
  211.6 3.3 %collective-permute-start.34 = (f32[32,1152]{1,0:T(8,128)S(1)}, f32[32,1152]{1,0:T(8,128)}, u32[]{:S(2)}, u32[]{:S(2)}) collective-permute-start(f32[32,1152]{1,0:T(8,128)S(1)} %copy-done.33), channel_id=1, source_target_pairs={{0,24},{4,28},{8,16},{12,20},{16,8},{20,12},{24,0},{28,4},{1,25},{... | collective-permute-start | bytes 442376 | tf_op jit(solution)/shard_map/ppermute | solution.py:603
  214.9 4.8 %collective-permute-done.26.refs_5_.refs_2_ = f32[97,32,128]{2,1,0:T(8,128)S(1)} collective-permute-done((f32[97,32,128]{2,1,0:T(8,128)}, f32[97,32,128]{2,1,0:T(8,128)S(1)}, u32[]{:S(2)}, u32[]{:S(2)}) %collective-permute-start.26) | collective-permute-done | bytes 1589280 | tf_op jit(solution)/shard_map/ppermute | solution.py:595
  219.7 2.5 collective-permute-start.35
  222.3 2.5 collective-permute-start.28
  224.8 6.5 %all-to-all-done.2 = f32[8,32,1920]{2,1,0:T(8,128)} async-done(((f32[8,32,1920]{2,1,0:T(8,128)}), f32[8,32,1920]{2,1,0:T(8,128)}, u32[]{:S(2)}, u32[]{:S(2)}) %all-to-all-start.2) | async-done | bytes 1966112 | tf_op jit(solution)/shard_map/all_to_all | solution.py:598
  231.3 7.5 %alpha_sum.6.refs_12_ = f32[256,1920]{1,0:T(8,128)} custom-call(s32[1]{0:T(128)} %bitcast.4.device_ref, s32[2,192]{1,0:T(2,128)} %pairs_ref.7, s32[2,192]{1,0:T(2,128)} %signs_ref.7, f32[256,1920]{1,0:T(8,128)} %bitcast.21.refs_0_, bf16[256,1536]{1,0:T(8,128)(2,1)} %get-tuple-element.147.refs_1_.refs_8_, ...), custom_call_target="tpu_custom_call" | custom-call | flops 20000000000 | bytes 66666664 | tf_op jit(solution)/shard_map/alpha_sum/pallas_call | solution.py:201
  238.8 4.6 %all-to-all-start.3 = ((f32[8,32,1920]{2,1,0:T(8,128)}), f32[8,32,1920]{2,1,0:T(8,128)}, u32[]{:S(2)}, u32[]{:S(2)}) async-start(f32[8,32,1920]{2,1,0:T(8,128)} %bitcast.56), calls=%async_computation.3 | async-start | bytes 3932160 | tf_op jit(solution)/shard_map/all_to_all | solution.py:598
  243.4 17.6 %collective-permute-done.28.refs_13_.refs_4_ = f32[97,32,128]{2,1,0:T(8,128)} collective-permute-done((f32[97,32,128]{2,1,0:T(8,128)}, f32[97,32,128]{2,1,0:T(8,128)}, u32[]{:S(2)}, u32[]{:S(2)}) %collective-permute-start.28) | collective-permute-done | bytes 1589280 | tf_op jit(solution)/shard_map/ppermute | solution.py:595
  261.1 6.6 %alpha_sum.7 = (f32[32,1152]{1,0:T(8,128)}, f32[32,1152]{1,0:T(8,128)}, f32[32,1152]{1,0:T(8,128)}, f32[32,1152]{1,0:T(8,128)}, f32[32,1152]{1,0:T(8,128)}, /*in...) custom-call(s32[1]{0:T(128)} %bitcast.4.device_ref, s32[2,192]{1,0:T(2,128)} %pairs_ref.7, ...), custom_call_target="tpu_custom_call" | custom-call | flops 199999995904 | bytes 666666688 | tf_op jit(solution)/shard_map/alpha_sum/pallas_call | solution.py:201
  267.9 14.3 %beta_sum.7 = f32[32,24576]{1,0:T(8,128)} custom-call(s32[2,192]{1,0:T(2,128)} %get-tuple-element.213.slots_ref, s32[2,192]{1,0:T(2,128)} %get-tuple-element.212.sign_ref, s32[2,192]{1,0:T(2,128)S(1)} %bitcast.59, f32[32,24576]{1,0:T(8,128)S(1)} %copy-done.1, f32[4,128,128]{2,1,0:T(8,128)S(1)} %copy-done.4, f32[97,32,128]{2,1,0:T(8,128)} %copy-done.30, ...), custom_call_target="tpu_custom_call" | custom-call | flops 20000000000 | bytes 66666664 | tf_op jit(solution)/shard_map/beta_sum/pallas_call | solution.py:407
  282.3 1.8 collective-permute-start.38
  284.2 2.6 collective-permute-start.40
  287.3 3.1 collective-permute-start.42
  290.4 12.2 %all-to-all-done.3.refs_1_ = f32[8,32,1920]{2,1,0:T(8,128)} async-done(((f32[8,32,1920]{2,1,0:T(8,128)}), f32[8,32,1920]{2,1,0:T(8,128)}, u32[]{:S(2)}, u32[]{:S(2)}) %all-to-all-start.3) | async-done | bytes 1966112 | tf_op jit(solution)/shard_map/all_to_all | solution.py:598
  302.6 3.5 %finish.2.refs_9_ = f32[32,24576]{1,0:T(8,128)} custom-call(s32[1]{0:T(128)} %bitcast.4.device_ref, f32[32,24576]{1,0:T(8,128)} %get-tuple-element.219.refs_0_, f32[8,32,1920]{2,1,0:T(8,128)} %all-to-all-done.3.refs_1_), custom_call_target="tpu_custom_call" | custom-call | flops 20000000000 | bytes 66666664 | tf_op jit(solution)/shard_map/finish/pallas_call | solution.py:571
  306.1 1.7 collective-permute-done.40.refs_6_
  309.2 2.4 finish.3
  (130 shorter events, 10.4 us)
Async XLA Ops:
  3.1 17.8 %copy-start = (f32[32,24576]{1,0:T(8,128)S(1)}, f32[32,24576]{1,0:T(8,128)}, u32[]{:S(2)}) copy-start(f32[32,24576]{1,0:T(8,128)} %refs_5_.3) | copy-start | bytes 9437188
  3.1 61.9 %all-to-all-start = ((f32[8,32,1920]{2,1,0:T(8,128)}), f32[8,32,1920]{2,1,0:T(8,128)}, u32[]{:S(2)}, u32[]{:S(2)}) async-start(f32[8,32,1920]{2,1,0:T(8,128)} %pack.2.refs_0_), calls=%async_computation | async-start | bytes 3932160 | tf_op jit(solution)/shard_map/all_to_all | solution.py:598
  13.3 129.4 %copy-start.5 = (s32[192,2]{1,0:T(8,128)}, s32[192,2]{1,0:T(8,128)S(1)}, u32[]{:S(2)}) copy-start(s32[192,2]{1,0:T(8,128)S(1)} %get-tuple-element.135) | copy-start | bytes 4612
  13.3 3.9 %collective-permute-start.7 = (f32[8,256]{1,0:T(8,128)}, f32[8,256]{1,0:T(8,128)S(1)}, u32[]{:S(2)}, u32[]{:S(2)}) collective-permute-start(f32[8,256]{1,0:T(8,128)} %get-tuple-element.133), channel_id=1, source_target_pairs={{0,2},{1,3},{2,0},{3,1},{4,6},{5,7},{6,4},{7,5},{8,10},{9,11},{10,... | collective-permute-start | bytes 24584 | tf_op jit(solution)/shard_map/ppermute | solution.py:595
  14.9 4.8 %collective-permute-start.8 = (f32[8,256]{1,0:T(8,128)}, f32[8,256]{1,0:T(8,128)S(1)}, u32[]{:S(2)}, u32[]{:S(2)}) collective-permute-start(f32[8,256]{1,0:T(8,128)} %get-tuple-element.134), channel_id=1, source_target_pairs={{0,3},{1,2},{2,1},{3,0},{4,7},{5,6},{6,5},{7,4},{8,11},{9,10},{10,... | collective-permute-start | bytes 24584 | tf_op jit(solution)/shard_map/ppermute | solution.py:595
  16.3 3.9 %collective-permute-start.6 = (f32[8,256]{1,0:T(8,128)}, f32[8,256]{1,0:T(8,128)S(1)}, u32[]{:S(2)}, u32[]{:S(2)}) collective-permute-start(f32[8,256]{1,0:T(8,128)} %get-tuple-element.132), channel_id=1, source_target_pairs={{0,1},{1,0},{2,3},{3,2},{4,5},{5,4},{6,7},{7,6},{8,9},{9,8},{10,11... | collective-permute-start | bytes 24584 | tf_op jit(solution)/shard_map/ppermute | solution.py:595
  17.3 125.5 %copy-start.13 = (f32[8,256]{1,0:T(8,128)}, f32[8,256]{1,0:T(8,128)S(1)}, u32[]{:S(2)}) copy-start(f32[8,256]{1,0:T(8,128)S(1)} %collective-permute-done.7.refs_1_) | copy-start | bytes 24580
  19.7 123.1 %copy-start.15 = (f32[8,256]{1,0:T(8,128)}, f32[8,256]{1,0:T(8,128)S(1)}, u32[]{:S(2)}) copy-start(f32[8,256]{1,0:T(8,128)S(1)} %collective-permute-done.8.refs_2_) | copy-start | bytes 24580
  20.2 122.6 %copy-start.17 = (f32[8,256]{1,0:T(8,128)}, f32[8,256]{1,0:T(8,128)S(1)}, u32[]{:S(2)}) copy-start(f32[8,256]{1,0:T(8,128)S(1)} %collective-permute-done.6.refs_0_) | copy-start | bytes 24580
  25.4 36.2 %collective-permute-start.9 = (f32[97,32,128]{2,1,0:T(8,128)}, f32[97,32,128]{2,1,0:T(8,128)}, u32[]{:S(2)}, u32[]{:S(2)}) collective-permute-start(f32[97,32,128]{2,1,0:T(8,128)} %get-tuple-element.136), channel_id=1, source_target_pairs={{0,1},{1,0},{2,3},{3,2},{4,5},{5,4},{6,7},{7,6},{8,9},{9,8},{10,11... | collective-permute-start | bytes 4767752 | tf_op jit(solution)/shard_map/ppermute | solution.py:595
  26.3 38.7 %collective-permute-start.10 = (f32[97,32,128]{2,1,0:T(8,128)}, f32[97,32,128]{2,1,0:T(8,128)}, u32[]{:S(2)}, u32[]{:S(2)}) collective-permute-start(f32[97,32,128]{2,1,0:T(8,128)} %get-tuple-element.137), channel_id=1, source_target_pairs={{0,2},{1,3},{2,0},{3,1},{4,6},{5,7},{6,4},{7,5},{8,10},{9,11},{10,... | collective-permute-start | bytes 4767752 | tf_op jit(solution)/shard_map/ppermute | solution.py:595
  29.0 4.6 %collective-permute-start.12 = (f32[32,1152]{1,0:T(8,128)}, f32[32,1152]{1,0:T(8,128)}, u32[]{:S(2)}, u32[]{:S(2)}) collective-permute-start(f32[32,1152]{1,0:T(8,128)} %get-tuple-element.140), channel_id=1, source_target_pairs={{0,4},{4,0},{8,12},{12,8},{16,20},{20,16},{24,28},{28,24},{1,5},{5... | collective-permute-start | bytes 442376 | tf_op jit(solution)/shard_map/ppermute | solution.py:603
  29.0 16.9 %collective-permute-start.13 = (f32[32,1152]{1,0:T(8,128)}, f32[32,1152]{1,0:T(8,128)}, u32[]{:S(2)}, u32[]{:S(2)}) collective-permute-start(f32[32,1152]{1,0:T(8,128)} %get-tuple-element.141), channel_id=1, source_target_pairs={{0,8},{4,12},{8,0},{12,4},{16,24},{20,28},{24,16},{28,20},{1,9},{5... | collective-permute-start | bytes 442376 | tf_op jit(solution)/shard_map/ppermute | solution.py:603
  31.1 41.3 %collective-permute-start.14 = (f32[32,1152]{1,0:T(8,128)}, f32[32,1152]{1,0:T(8,128)}, u32[]{:S(2)}, u32[]{:S(2)}) collective-permute-start(f32[32,1152]{1,0:T(8,128)} %get-tuple-element.142), channel_id=1, source_target_pairs={{0,12},{4,8},{8,4},{12,0},{16,28},{20,24},{24,20},{28,16},{1,13},{... | collective-permute-start | bytes 442376 | tf_op jit(solution)/shard_map/ppermute | solution.py:603
  33.5 38.9 %collective-permute-start.15 = (f32[32,1152]{1,0:T(8,128)}, f32[32,1152]{1,0:T(8,128)}, u32[]{:S(2)}, u32[]{:S(2)}) collective-permute-start(f32[32,1152]{1,0:T(8,128)} %get-tuple-element.143), channel_id=1, source_target_pairs={{0,16},{4,20},{8,24},{12,28},{16,0},{20,4},{24,8},{28,12},{1,17},{... | collective-permute-start | bytes 442376 | tf_op jit(solution)/shard_map/ppermute | solution.py:603
  45.9 28.7 %collective-permute-start.16 = (f32[32,1152]{1,0:T(8,128)}, f32[32,1152]{1,0:T(8,128)}, u32[]{:S(2)}, u32[]{:S(2)}) collective-permute-start(f32[32,1152]{1,0:T(8,128)} %get-tuple-element.144), channel_id=1, source_target_pairs={{0,20},{4,16},{8,28},{12,24},{16,4},{20,0},{24,12},{28,8},{1,21},{... | collective-permute-start | bytes 442376 | tf_op jit(solution)/shard_map/ppermute | solution.py:603
  61.5 13.1 %collective-permute-start.17 = (f32[32,1152]{1,0:T(8,128)}, f32[32,1152]{1,0:T(8,128)}, u32[]{:S(2)}, u32[]{:S(2)}) collective-permute-start(f32[32,1152]{1,0:T(8,128)} %get-tuple-element.145), channel_id=1, source_target_pairs={{0,24},{4,28},{8,16},{12,20},{16,8},{20,12},{24,0},{28,4},{1,25},{... | collective-permute-start | bytes 442376 | tf_op jit(solution)/shard_map/ppermute | solution.py:603
  65.0 9.6 %collective-permute-start.18 = (f32[32,1152]{1,0:T(8,128)}, f32[32,1152]{1,0:T(8,128)}, u32[]{:S(2)}, u32[]{:S(2)}) collective-permute-start(f32[32,1152]{1,0:T(8,128)} %get-tuple-element.146), channel_id=1, source_target_pairs={{0,28},{4,24},{8,20},{12,16},{16,12},{20,8},{24,4},{28,0},{1,29},{... | collective-permute-start | bytes 442376 | tf_op jit(solution)/shard_map/ppermute | solution.py:603
  80.8 12.1 %copy-start.22 = (s32[192,2]{0,1:T(2,128)S(1)}, s32[192,2]{0,1:T(2,128)}, u32[]{:S(2)}) copy-start(s32[192,2]{0,1:T(2,128)} %param.21) | copy-start | bytes 4612
  80.8 80.4 %all-to-all-start.1 = ((f32[8,32,3072]{2,1,0:T(8,128)}), f32[8,32,3072]{2,1,0:T(8,128)}, u32[]{:S(2)}, u32[]{:S(2)}) async-start(f32[8,32,3072]{2,1,0:T(8,128)} %bitcast.54), calls=%async_computation.1 | async-start | bytes 6291456 | tf_op jit(solution)/shard_map/all_to_all | solution.py:598
  89.2 38.4 %collective-permute-start.11 = (f32[97,32,128]{2,1,0:T(8,128)}, f32[97,32,128]{2,1,0:T(8,128)}, u32[]{:S(2)}, u32[]{:S(2)}) collective-permute-start(f32[97,32,128]{2,1,0:T(8,128)} %get-tuple-element.138), channel_id=1, source_target_pairs={{0,3},{1,2},{2,1},{3,0},{4,7},{5,6},{6,5},{7,4},{8,11},{9,10},{10,... | collective-permute-start | bytes 4767752 | tf_op jit(solution)/shard_map/ppermute | solution.py:595
  101.5 26.0 %copy-start.24 = (s32[192,2]{0,1:T(2,128)S(1)}, s32[192,2]{0,1:T(2,128)}, u32[]{:S(2)}) copy-start(s32[192,2]{0,1:T(2,128)} %param.20) | copy-start | bytes 4612
  143.0 4.6 %collective-permute-start.21 = (f32[8,128]{1,0:T(8,128)S(1)}, f32[8,128]{1,0:T(8,128)S(1)}, u32[]{:S(2)}, u32[]{:S(2)}) collective-permute-start(f32[8,128]{1,0:T(8,128)S(1)} %get-tuple-element.153), channel_id=1, source_target_pairs={{0,3},{1,2},{2,1},{3,0},{4,7},{5,6},{6,5},{7,4},{8,11},{9,10},{10,... | collective-permute-start | bytes 12296 | tf_op jit(solution)/shard_map/ppermute | solution.py:595
  145.5 3.6 %collective-permute-start.20 = (f32[8,128]{1,0:T(8,128)S(1)}, f32[8,128]{1,0:T(8,128)S(1)}, u32[]{:S(2)}, u32[]{:S(2)}) collective-permute-start(f32[8,128]{1,0:T(8,128)S(1)} %get-tuple-element.153), channel_id=1, source_target_pairs={{0,2},{1,3},{2,0},{3,1},{4,6},{5,7},{6,4},{7,5},{8,10},{9,11},{10,... | collective-permute-start | bytes 12296 | tf_op jit(solution)/shard_map/ppermute | solution.py:595
  146.0 3.6 %collective-permute-start.19 = (f32[8,128]{1,0:T(8,128)S(1)}, f32[8,128]{1,0:T(8,128)S(1)}, u32[]{:S(2)}, u32[]{:S(2)}) collective-permute-start(f32[8,128]{1,0:T(8,128)S(1)} %get-tuple-element.153), channel_id=1, source_target_pairs={{0,1},{1,0},{2,3},{3,2},{4,5},{5,4},{6,7},{7,6},{8,9},{9,8},{10,11... | collective-permute-start | bytes 12296 | tf_op jit(solution)/shard_map/ppermute | solution.py:595
  149.6 1.2 collective-permute-start.22
  150.8 10.4 %copy-start.19 = (f32[8,128]{1,0:T(8,128)}, f32[8,128]{1,0:T(8,128)S(1)}, u32[]{:S(2)}) copy-start(f32[8,128]{1,0:T(8,128)S(1)} %add.168.refs_0_) | copy-start | bytes 12292
  150.8 4.8 %collective-permute-start.25 = (f32[8,128]{1,0:T(8,128)S(1)}, f32[8,128]{1,0:T(8,128)S(1)}, u32[]{:S(2)}, u32[]{:S(2)}) collective-permute-start(f32[8,128]{1,0:T(8,128)S(1)} %add.168.refs_0_), channel_id=1, source_target_pairs={{0,24},{4,28},{8,0},{12,4},{16,8},{20,12},{24,16},{28,20},{1,25},{... | collective-permute-start | bytes 12296 | tf_op jit(solution)/shard_map/ppermute | solution.py:692
  154.3 7.0 %collective-permute-start.24 = (f32[8,128]{1,0:T(8,128)S(1)}, f32[8,128]{1,0:T(8,128)S(1)}, u32[]{:S(2)}, u32[]{:S(2)}) collective-permute-start(f32[8,128]{1,0:T(8,128)S(1)} %add.168.refs_0_), channel_id=1, source_target_pairs={{0,16},{4,20},{8,24},{12,28},{16,0},{20,4},{24,8},{28,12},{1,17},{... | collective-permute-start | bytes 12296 | tf_op jit(solution)/shard_map/ppermute | solution.py:692
  155.0 6.2 %collective-permute-start.23 = (f32[8,128]{1,0:T(8,128)S(1)}, f32[8,128]{1,0:T(8,128)S(1)}, u32[]{:S(2)}, u32[]{:S(2)}) collective-permute-start(f32[8,128]{1,0:T(8,128)S(1)} %add.168.refs_0_), channel_id=1, source_target_pairs={{0,8},{4,12},{8,16},{12,20},{16,24},{20,28},{24,0},{28,4},{1,9},{5... | collective-permute-start | bytes 12296 | tf_op jit(solution)/shard_map/ppermute | solution.py:692
  167.6 63.7 %all-to-all-start.2 = ((f32[8,32,1920]{2,1,0:T(8,128)}), f32[8,32,1920]{2,1,0:T(8,128)}, u32[]{:S(2)}, u32[]{:S(2)}) async-start(f32[8,32,1920]{2,1,0:T(8,128)} %get-tuple-element.168), calls=%async_computation.2 | async-start | bytes 3932160 | tf_op jit(solution)/shard_map/all_to_all | solution.py:598
  176.1 9.5 %copy-start.39 = (f32[32,1152]{1,0:T(8,128)S(1)}, f32[32,1152]{1,0:T(8,128)}, u32[]{:S(2)}) copy-start(f32[32,1152]{1,0:T(8,128)} %get-tuple-element.161) | copy-start | bytes 442372
  176.1 9.5 %copy-start.38 = (f32[32,1152]{1,0:T(8,128)S(1)}, f32[32,1152]{1,0:T(8,128)}, u32[]{:S(2)}) copy-start(f32[32,1152]{1,0:T(8,128)} %get-tuple-element.162) | copy-start | bytes 442372
  176.1 11.4 %copy-start.37 = (f32[32,1152]{1,0:T(8,128)S(1)}, f32[32,1152]{1,0:T(8,128)}, u32[]{:S(2)}) copy-start(f32[32,1152]{1,0:T(8,128)} %get-tuple-element.163) | copy-start | bytes 442372
  176.1 35.5 %copy-start.33 = (f32[32,1152]{1,0:T(8,128)S(1)}, f32[32,1152]{1,0:T(8,128)}, u32[]{:S(2)}) copy-start(f32[32,1152]{1,0:T(8,128)} %get-tuple-element.166) | copy-start | bytes 442372
  176.1 43.6 %copy-start.32 = (f32[32,1152]{1,0:T(8,128)S(1)}, f32[32,1152]{1,0:T(8,128)}, u32[]{:S(2)}) copy-start(f32[32,1152]{1,0:T(8,128)} %get-tuple-element.167) | copy-start | bytes 442372
  182.5 37.2 %collective-permute-start.26 = (f32[97,32,128]{2,1,0:T(8,128)}, f32[97,32,128]{2,1,0:T(8,128)S(1)}, u32[]{:S(2)}, u32[]{:S(2)}) collective-permute-start(f32[97,32,128]{2,1,0:T(8,128)} %get-tuple-element.157), channel_id=1, source_target_pairs={{0,1},{1,0},{2,3},{3,2},{4,5},{5,4},{6,7},{7,6},{8,9},{9,8},{10,11... | collective-permute-start | bytes 4767752 | tf_op jit(solution)/shard_map/ppermute | solution.py:595
  184.0 38.3 %collective-permute-start.27 = (f32[97,32,128]{2,1,0:T(8,128)}, f32[97,32,128]{2,1,0:T(8,128)S(1)}, u32[]{:S(2)}, u32[]{:S(2)}) collective-permute-start(f32[97,32,128]{2,1,0:T(8,128)} %get-tuple-element.158), channel_id=1, source_target_pairs={{0,2},{1,3},{2,0},{3,1},{4,6},{5,7},{6,4},{7,5},{8,10},{9,11},{10,... | collective-permute-start | bytes 4767752 | tf_op jit(solution)/shard_map/ppermute | solution.py:595
  185.5 2.1 collective-permute-start.29
  185.5 22.5 %collective-permute-start.30 = (f32[32,1152]{1,0:T(8,128)S(1)}, f32[32,1152]{1,0:T(8,128)S(1)}, u32[]{:S(2)}, u32[]{:S(2)}) collective-permute-start(f32[32,1152]{1,0:T(8,128)S(1)} %copy-done.38), channel_id=1, source_target_pairs={{0,8},{4,12},{8,0},{12,4},{16,24},{20,28},{24,16},{28,20},{1,9},{5... | collective-permute-start | bytes 442376 | tf_op jit(solution)/shard_map/ppermute | solution.py:603
  187.5 24.1 %collective-permute-start.31 = (f32[32,1152]{1,0:T(8,128)S(1)}, f32[32,1152]{1,0:T(8,128)S(1)}, u32[]{:S(2)}, u32[]{:S(2)}) collective-permute-start(f32[32,1152]{1,0:T(8,128)S(1)} %copy-done.37), channel_id=1, source_target_pairs={{0,12},{4,8},{8,4},{12,0},{16,28},{20,24},{24,20},{28,16},{1,13},{... | collective-permute-start | bytes 442376 | tf_op jit(solution)/shard_map/ppermute | solution.py:603
  187.6 34.7 %copy-start.34 = (f32[32,1152]{1,0:T(8,128)}, f32[32,1152]{1,0:T(8,128)S(1)}, u32[]{:S(2)}) copy-start(f32[32,1152]{1,0:T(8,128)S(1)} %collective-permute-done.29.refs_1_) | copy-start | bytes 442372
  187.6 55.8 %collective-permute-start.32 = (f32[32,1152]{1,0:T(8,128)}, f32[32,1152]{1,0:T(8,128)}, u32[]{:S(2)}, u32[]{:S(2)}) collective-permute-start(f32[32,1152]{1,0:T(8,128)} %get-tuple-element.164), channel_id=1, source_target_pairs={{0,16},{4,20},{8,24},{12,28},{16,0},{20,4},{24,8},{28,12},{1,17},{... | collective-permute-start | bytes 442376 | tf_op jit(solution)/shard_map/ppermute | solution.py:603
  208.0 14.3 %copy-start.35 = (f32[32,1152]{1,0:T(8,128)}, f32[32,1152]{1,0:T(8,128)S(1)}, u32[]{:S(2)}) copy-start(f32[32,1152]{1,0:T(8,128)S(1)} %collective-permute-done.30.refs_2_) | copy-start | bytes 442372
  208.0 35.4 %collective-permute-start.33 = (f32[32,1152]{1,0:T(8,128)}, f32[32,1152]{1,0:T(8,128)}, u32[]{:S(2)}, u32[]{:S(2)}) collective-permute-start(f32[32,1152]{1,0:T(8,128)} %get-tuple-element.165), channel_id=1, source_target_pairs={{0,20},{4,16},{8,28},{12,24},{16,4},{20,0},{24,12},{28,8},{1,21},{... | collective-permute-start | bytes 442376 | tf_op jit(solution)/shard_map/ppermute | solution.py:603
  211.6 10.7 %copy-start.36 = (f32[32,1152]{1,0:T(8,128)}, f32[32,1152]{1,0:T(8,128)S(1)}, u32[]{:S(2)}) copy-start(f32[32,1152]{1,0:T(8,128)S(1)} %collective-permute-done.31.refs_3_) | copy-start | bytes 442372
  211.6 31.8 %collective-permute-start.34 = (f32[32,1152]{1,0:T(8,128)S(1)}, f32[32,1152]{1,0:T(8,128)}, u32[]{:S(2)}, u32[]{:S(2)}) collective-permute-start(f32[32,1152]{1,0:T(8,128)S(1)} %copy-done.33), channel_id=1, source_target_pairs={{0,24},{4,28},{8,16},{12,20},{16,8},{20,12},{24,0},{28,4},{1,25},{... | collective-permute-start | bytes 442376 | tf_op jit(solution)/shard_map/ppermute | solution.py:603
  219.7 11.6 %copy-start.30 = (f32[97,32,128]{2,1,0:T(8,128)}, f32[97,32,128]{2,1,0:T(8,128)S(1)}, u32[]{:S(2)}) copy-start(f32[97,32,128]{2,1,0:T(8,128)S(1)} %collective-permute-done.26.refs_5_.refs_2_) | copy-start | bytes 4767748
  219.7 23.7 %collective-permute-start.35 = (f32[32,1152]{1,0:T(8,128)S(1)}, f32[32,1152]{1,0:T(8,128)}, u32[]{:S(2)}, u32[]{:S(2)}) collective-permute-start(f32[32,1152]{1,0:T(8,128)S(1)} %copy-done.32), channel_id=1, source_target_pairs={{0,28},{4,24},{8,20},{12,16},{16,12},{20,8},{24,4},{28,0},{1,29},{... | collective-permute-start | bytes 442376 | tf_op jit(solution)/shard_map/ppermute | solution.py:603
  222.3 38.8 %collective-permute-start.28 = (f32[97,32,128]{2,1,0:T(8,128)}, f32[97,32,128]{2,1,0:T(8,128)}, u32[]{:S(2)}, u32[]{:S(2)}) collective-permute-start(f32[97,32,128]{2,1,0:T(8,128)} %get-tuple-element.159), channel_id=1, source_target_pairs={{0,3},{1,2},{2,1},{3,0},{4,7},{5,6},{6,5},{7,4},{8,11},{9,10},{10,... | collective-permute-start | bytes 4767752 | tf_op jit(solution)/shard_map/ppermute | solution.py:595
  238.8 63.8 %all-to-all-start.3 = ((f32[8,32,1920]{2,1,0:T(8,128)}), f32[8,32,1920]{2,1,0:T(8,128)}, u32[]{:S(2)}, u32[]{:S(2)}) async-start(f32[8,32,1920]{2,1,0:T(8,128)} %bitcast.56), calls=%async_computation.3 | async-start | bytes 3932160 | tf_op jit(solution)/shard_map/all_to_all | solution.py:598
  267.7 19.1 %collective-permute-start.36 = (f32[32,1152]{1,0:T(8,128)}, f32[32,1152]{1,0:T(8,128)}, u32[]{:S(2)}, u32[]{:S(2)}) collective-permute-start(f32[32,1152]{1,0:T(8,128)} %get-tuple-element.170), channel_id=1, source_target_pairs={{0,4},{4,0},{8,12},{12,8},{16,20},{20,16},{24,28},{28,24},{1,5},{5... | collective-permute-start | bytes 442376 | tf_op jit(solution)/shard_map/ppermute | solution.py:603
  267.8 19.5 %collective-permute-start.37 = (f32[32,1152]{1,0:T(8,128)}, f32[32,1152]{1,0:T(8,128)}, u32[]{:S(2)}, u32[]{:S(2)}) collective-permute-start(f32[32,1152]{1,0:T(8,128)} %get-tuple-element.171), channel_id=1, source_target_pairs={{0,8},{4,12},{8,0},{12,4},{16,24},{20,28},{24,16},{28,20},{1,9},{5... | collective-permute-start | bytes 442376 | tf_op jit(solution)/shard_map/ppermute | solution.py:603
  267.9 14.4 %copy-start.6 = (s32[192,2]{1,0:T(8,128)S(1)}, s32[192,2]{1,0:T(8,128)}, u32[]{:S(2)}) copy-start(s32[192,2]{1,0:T(8,128)} %copy-done.5) | copy-start | bytes 4612
  267.9 14.4 %copy-start.14 = (f32[8,256]{1,0:T(8,128)S(1)}, f32[8,256]{1,0:T(8,128)}, u32[]{:S(2)}) copy-start(f32[8,256]{1,0:T(8,128)} %copy-done.13) | copy-start | bytes 24580
  267.9 14.4 %copy-start.16 = (f32[8,256]{1,0:T(8,128)S(1)}, f32[8,256]{1,0:T(8,128)}, u32[]{:S(2)}) copy-start(f32[8,256]{1,0:T(8,128)} %copy-done.15) | copy-start | bytes 24580
  267.9 14.4 %copy-start.18 = (f32[8,256]{1,0:T(8,128)S(1)}, f32[8,256]{1,0:T(8,128)}, u32[]{:S(2)}) copy-start(f32[8,256]{1,0:T(8,128)} %copy-done.17) | copy-start | bytes 24580
  267.9 14.4 %copy-start.21 = (s32[192,2]{0,1:T(2,128)S(1)}, s32[192,2]{0,1:T(2,128)}, u32[]{:S(2)}) copy-start(s32[192,2]{0,1:T(2,128)} %param.19) | copy-start | bytes 4612
  267.9 14.4 %copy-start.23 = (s32[192,2]{0,1:T(2,128)S(1)}, s32[192,2]{0,1:T(2,128)}, u32[]{:S(2)}) copy-start(s32[192,2]{0,1:T(2,128)} %param.21) | copy-start | bytes 4612
  282.3 23.8 %collective-permute-start.38 = (f32[32,1152]{1,0:T(8,128)}, f32[32,1152]{1,0:T(8,128)S(1)}, u32[]{:S(2)}, u32[]{:S(2)}) collective-permute-start(f32[32,1152]{1,0:T(8,128)} %get-tuple-element.172), channel_id=1, source_target_pairs={{0,12},{4,8},{8,4},{12,0},{16,28},{20,24},{24,20},{28,16},{1,13},{... | collective-permute-start | bytes 442376 | tf_op jit(solution)/shard_map/ppermute | solution.py:603
  284.2 22.0 %collective-permute-start.39 = (f32[32,1152]{1,0:T(8,128)}, f32[32,1152]{1,0:T(8,128)S(1)}, u32[]{:S(2)}, u32[]{:S(2)}) collective-permute-start(f32[32,1152]{1,0:T(8,128)} %get-tuple-element.173), channel_id=1, source_target_pairs={{0,16},{4,20},{8,24},{12,28},{16,0},{20,4},{24,8},{28,12},{1,17},{... | collective-permute-start | bytes 442376 | tf_op jit(solution)/shard_map/ppermute | solution.py:603
  284.2 23.7 %collective-permute-start.40 = (f32[32,1152]{1,0:T(8,128)}, f32[32,1152]{1,0:T(8,128)S(1)}, u32[]{:S(2)}, u32[]{:S(2)}) collective-permute-start(f32[32,1152]{1,0:T(8,128)} %get-tuple-element.174), channel_id=1, source_target_pairs={{0,20},{4,16},{8,28},{12,24},{16,4},{20,0},{24,12},{28,8},{1,21},{... | collective-permute-start | bytes 442376 | tf_op jit(solution)/shard_map/ppermute | solution.py:603
  286.8 21.1 %collective-permute-start.41 = (f32[32,1152]{1,0:T(8,128)}, f32[32,1152]{1,0:T(8,128)S(1)}, u32[]{:S(2)}, u32[]{:S(2)}) collective-permute-start(f32[32,1152]{1,0:T(8,128)} %get-tuple-element.175), channel_id=1, source_target_pairs={{0,24},{4,28},{8,16},{12,20},{16,8},{20,12},{24,0},{28,4},{1,25},{... | collective-permute-start | bytes 442376 | tf_op jit(solution)/shard_map/ppermute | solution.py:603
  287.3 20.5 %collective-permute-start.42 = (f32[32,1152]{1,0:T(8,128)}, f32[32,1152]{1,0:T(8,128)S(1)}, u32[]{:S(2)}, u32[]{:S(2)}) collective-permute-start(f32[32,1152]{1,0:T(8,128)} %get-tuple-element.176), channel_id=1, source_target_pairs={{0,28},{4,24},{8,20},{12,16},{16,12},{20,8},{24,4},{28,0},{1,29},{... | collective-permute-start | bytes 442376 | tf_op jit(solution)/shard_map/ppermute | solution.py:603
  (16 other events, 62.8 us)

commit v7 on v6

--- a/solution.py
+++ b/solution.py
@@ -41,11 +41,10 @@
     npair = pair_tables.shape[0]
 
     def kernel(h_ref, p_ref, t_ref, *refs):
-        a_twice, a_low, t_high, t_low = refs[-4:]
+        a_high, a_low, t_high, t_low = refs[-4:]
         for q in range(nq + 1):
             high, low = halves(h_ref[...] if q == 0 else p_ref[q - 1])
-            a_twice[:, q * size : (q + 1) * size] = high
-            a_twice[:, depth + q * size : depth + (q + 1) * size] = high
+            a_high[:, q * size : (q + 1) * size] = high
             a_low[:, q * size : (q + 1) * size] = low
         for p in range(npair):
             high, low = halves(t_ref[p])
@@ -53,7 +52,7 @@
             t_high[p, SB:, :] = high
             t_low[p] = low
 
-    shapes = [(size, 2 * depth), (size, depth), (npair, 2 * SB, SB), (npair, SB, SB)]
+    shapes = [(size, depth), (size, depth), (npair, 2 * SB, SB), (npair, SB, SB)]
     return pl.pallas_call(
         kernel,
         in_specs=[pl.BlockSpec(memory_space=pltpu.VMEM)] * 3 + [pl.BlockSpec(memory_space=pl.ANY)] * len(after),
@@ -115,7 +114,7 @@
         v_any = refs[:count]
         prepared_any = refs[count : count + 4]
         outs = refs[count + 4 + len(after) + len(previous) :][: 1 if full else count]
-        v_held, out_held, a_twice, a_low, t_high, t_low, even, odd, sems, once = refs[-10:]
+        v_held, out_held, a_high, a_low, t_high, t_low, even, odd, sems, once = refs[-10:]
 
         def at(g):
             return pl.ds(pl.multiple_of(g * wide, SB), wide)
@@ -154,7 +153,7 @@
                 ]
             )
 
-        held = (a_twice, a_low, t_high, t_low)
+        held = (a_high, a_low, t_high, t_low)
         loads = [pltpu.make_async_copy(prepared_any[i], held[i], once.at[i]) for i in range(4)]
         for load in loads[2:]:
             load.start()
@@ -192,7 +191,7 @@
             if g + 1 < steps:
                 taken(g + 1).wait()
                 build(g + 1, other)
-            out_held[g] = mul(a_twice[...], b[...]) + mul(a_low[...], b[:depth, :])
+            out_held[g] = mul(a_high[...], b[:depth, :]) + mul(a_high[...], b[depth:, :]) + mul(a_low[...], b[:depth, :])
             given(g).start()
         for g in range(steps):
             given(g).wait()

time: 317 us -> 316 us (level)
  no operation moved by 1% of the time
where the time goes in v7:
time: 316 us; the launch traced here: 312 us
  waiting for transfers between devices  121 us (38%)
  Pallas kernels  93.3 us (30%)
  starting transfers between devices  80 us (25%)
  local copies, waits for them, and re-layouts  8.24 us (3%)
  other arithmetic  4.51 us (1%)
  between operations  4.04 us (1%)
    ppermute x12, waiting for transfers between devices, to_partners(): lax.ppermute(part, 'beta', [(i, i ^ k) for i in range(n_beta)])  64.2 us
    ppermute x21, starting transfers between devices, swap(): lax.ppermute(parts[k], 'alpha', [(i, i ^ k) for i in range(n_alpha)])  34.1 us
    ppermute x21, waiting for transfers between devices, swap(): lax.ppermute(parts[k], 'alpha', [(i, i ^ k) for i in range(n_alpha)])  31.6 us
    pallas_call x2, Pallas kernels, beta_sum(): pl.pallas_call(kernel, grid_spec=pltpu.PrefetchScalarGridSpec(num_scalar_...  29.5 us
    pallas_call x4, Pallas kernels, alpha_sum(): pl.pallas_call(kernel, in_specs=[pl.BlockSpec(memory_space=pltpu.SMEM)] *...  27.4 us
    all_to_all x4, starting transfers between devices, turn(): return lax.all_to_all(parts, 'alpha', 0, 0, tiled=True)  23.9 us
    all_to_all x4, waiting for transfers between devices, turn(): return lax.all_to_all(parts, 'alpha', 0, 0, tiled=True)  18.9 us
    ppermute x12, starting transfers between devices, to_partners(): lax.ppermute(part, 'beta', [(i, i ^ k) for i in range(n_beta)])  17.1 us
  transfers between devices with their start and end apart: 41, of which 18 were waited for; matrix products, arithmetic and copies ran while one was open for 3% of the time, Pallas kernels for 25%

profile of v7, /device:TPU:0, one launch (start us, length us, event | category | flops | bytes accessed | tf_op | source)
XLA Modules:
  0.0 311.7 jit_solution(12018775243533737438)
XLA Ops:
  0.6 2.5 pack.2.refs_0_
  3.1 6.6 %all-to-all-start = ((f32[8,32,1920]{2,1,0:T(8,128)}), f32[8,32,1920]{2,1,0:T(8,128)}, u32[]{:S(2)}, u32[]{:S(2)}) async-start(f32[8,32,1920]{2,1,0:T(8,128)} %pack.2.refs_0_), calls=%async_computation | async-start | bytes 3932160 | tf_op jit(solution)/shard_map/all_to_all | solution.py:597
  9.7 0.8 copy.15.source_ref
  10.5 2.8 mark.1
  13.3 1.6 collective-permute-start.7
  14.9 1.4 collective-permute-start.8
  17.3 2.4 collective-permute-done.8.refs_2_
  20.2 0.8 positions.5.slots_ref
  21.0 4.4 %gather_blocks.6 = (f32[97,32,128]{2,1,0:T(8,128)}, f32[97,32,128]{2,1,0:T(8,128)}, f32[97,32,128]{2,1,0:T(8,128)}) custom-call(s32[8,256]{1,0:T(8,128)} %positions.5.slots_ref, f32[32,24576]{1,0:T(8,128)S(1)} %copy-done), custom_call_target="tpu_custom_call" | custom-call | flops 1 | bytes 1 | tf_op jit(solution)/shard_map/gather_blocks/pallas_call | solution.py:314
  25.4 1.0 collective-permute-start.9
  26.3 1.1 collective-permute-start.10
  27.4 1.5 pack.3
  29.0 2.1 collective-permute-start.13
  31.2 2.2 prepare.1
  33.4 2.6 collective-permute-start.15
  36.0 9.9 %collective-permute-done.13.refs_2_ = f32[32,1152]{1,0:T(8,128)} collective-permute-done((f32[32,1152]{1,0:T(8,128)}, f32[32,1152]{1,0:T(8,128)}, u32[]{:S(2)}, u32[]{:S(2)}) %collective-permute-start.13) | collective-permute-done | bytes 147488 | tf_op jit(solution)/shard_map/ppermute | solution.py:602
  45.9 3.6 %collective-permute-start.16 = (f32[32,1152]{1,0:T(8,128)}, f32[32,1152]{1,0:T(8,128)}, u32[]{:S(2)}, u32[]{:S(2)}) collective-permute-start(f32[32,1152]{1,0:T(8,128)} %get-tuple-element.144), channel_id=1, source_target_pairs={{0,20},{4,16},{8,28},{12,24},{16,4},{20,0},{24,12},{28,8},{1,21},{... | collective-permute-start | bytes 442376 | tf_op jit(solution)/shard_map/ppermute | solution.py:602
  49.5 12.0 %collective-permute-done.9.refs_5_.refs_2_ = f32[97,32,128]{2,1,0:T(8,128)} collective-permute-done((f32[97,32,128]{2,1,0:T(8,128)}, f32[97,32,128]{2,1,0:T(8,128)}, u32[]{:S(2)}, u32[]{:S(2)}) %collective-permute-start.9) | collective-permute-done | bytes 1589280 | tf_op jit(solution)/shard_map/ppermute | solution.py:594
  61.5 3.5 %collective-permute-start.17 = (f32[32,1152]{1,0:T(8,128)}, f32[32,1152]{1,0:T(8,128)}, u32[]{:S(2)}, u32[]{:S(2)}) collective-permute-start(f32[32,1152]{1,0:T(8,128)} %get-tuple-element.145), channel_id=1, source_target_pairs={{0,24},{4,28},{8,16},{12,20},{16,8},{20,12},{24,0},{28,4},{1,25},{... | collective-permute-start | bytes 442376 | tf_op jit(solution)/shard_map/ppermute | solution.py:602
  65.0 7.4 %alpha_sum.4.refs_12_ = f32[256,3072]{1,0:T(8,128)} custom-call(s32[1]{0:T(128)} %bitcast.4.device_ref, s32[2,192]{1,0:T(2,128)} %pairs_ref.7, s32[2,192]{1,0:T(2,128)} %signs_ref.7, f32[256,1920]{1,0:T(8,128)} %bitcast.10.refs_0_, bf16[256,768]{1,0:T(8,128)(2,1)} %get-tuple-element.147.refs_1_.refs_8_, bf16[256,768]{1,0:T(8,128)(2,1)} %get-tuple-element.148.refs_2_.refs_9_, ...), custom_call_target="tpu_custom_call" | custom-call | flops 20000000000 | bytes 66666664 | tf_op jit(solution)/shard_map/alpha_sum/pallas_call | solution.py:200
  72.5 2.1 collective-permute-done.16.refs_5_
  74.6 6.1 %alpha_sum.5 = f32[256,3072]{1,0:T(8,128)} custom-call(s32[1]{0:T(128)} %bitcast.4.device_ref, s32[2,192]{1,0:T(2,128)} %pairs_ref.7, s32[2,192]{1,0:T(2,128)} %signs_ref.7, f32[32,1152]{1,0:T(8,128)} %get-tuple-element.139.refs_0_, f32[32,1152]{1,0:T(8,128)} %collective-permute-done.12.refs_1_, ...), custom_call_target="tpu_custom_call", output_to_operand_aliasing={{}: (15, {})} | custom-call | flops 1 | bytes 1 | tf_op jit(solution)/shard_map/alpha_sum/pallas_call | solution.py:200
  80.7 8.4 %all-to-all-start.1 = ((f32[8,32,3072]{2,1,0:T(8,128)}), f32[8,32,3072]{2,1,0:T(8,128)}, u32[]{:S(2)}, u32[]{:S(2)}) async-start(f32[8,32,3072]{2,1,0:T(8,128)} %bitcast.54), calls=%async_computation.1 | async-start | bytes 6291456 | tf_op jit(solution)/shard_map/all_to_all | solution.py:597
  89.1 2.4 collective-permute-start.11
  91.5 1.2 slice.18
  97.7 1.4 slice.28
  99.0 2.4 fusion.2
  102.0 1.5 fusion.9
  104.1 23.3 %collective-permute-done.11.refs_4_ = f32[97,32,128]{2,1,0:T(8,128)} collective-permute-done((f32[97,32,128]{2,1,0:T(8,128)}, f32[97,32,128]{2,1,0:T(8,128)}, u32[]{:S(2)}, u32[]{:S(2)}) %collective-permute-start.11) | collective-permute-done | bytes 1589280 | tf_op jit(solution)/shard_map/ppermute | solution.py:594
  127.4 15.2 %beta_sum.6 = (f32[32,24576]{1,0:T(8,128)}, f32[8,128]{1,0:T(8,128)S(1)}) custom-call(s32[2,192]{1,0:T(2,128)} %get-tuple-element.213.slots_ref, s32[2,192]{1,0:T(2,128)} %get-tuple-element.212.sign_ref, s32[2,192]{1,0:T(2,128)S(1)} %bitcast.57, f32[32,24576]{1,0:T(8,128)S(1)} %copy-done, f32[4,128,128]{2,1,0:T(8,128)S(1)} %copy-done.3, ...), custom_call_target="tpu_custom_call" | custom-call | flops 1 | bytes 1 | tf_op jit(solution)/shard_map/beta_sum/pallas_call | solution.py:406
  142.9 2.5 collective-permute-start.21
  146.4 1.0 collective-permute-done.21
  147.4 1.5 collective-permute-done.20
  149.5 1.2 collective-permute-done.22
  150.7 3.5 %collective-permute-start.25 = (f32[8,128]{1,0:T(8,128)S(1)}, f32[8,128]{1,0:T(8,128)S(1)}, u32[]{:S(2)}, u32[]{:S(2)}) collective-permute-start(f32[8,128]{1,0:T(8,128)S(1)} %add.168.refs_0_), channel_id=1, source_target_pairs={{0,24},{4,28},{8,0},{12,4},{16,8},{20,12},{24,16},{28,20},{1,25},{... | collective-permute-start | bytes 12296 | tf_op jit(solution)/shard_map/ppermute | solution.py:691
  154.1 0.7 collective-permute-start.24
  155.5 5.6 %collective-permute-done.24.refs_2_ = f32[8,128]{1,0:T(8,128)S(1)} collective-permute-done((f32[8,128]{1,0:T(8,128)S(1)}, f32[8,128]{1,0:T(8,128)S(1)}, u32[]{:S(2)}, u32[]{:S(2)}) %collective-permute-start.24) | collective-permute-done | bytes 4128 | tf_op jit(solution)/shard_map/ppermute | solution.py:691
  161.7 5.7 %correct.2 = (f32[32,24576]{1,0:T(8,128)}, f32[8,32,1920]{2,1,0:T(8,128)}) custom-call(s32[1]{0:T(128)} %bitcast.4.device_ref, f32[8,128]{1,0:T(8,128)} %copy-done.19, f32[8,128]{1,0:T(8,128)} %copy-done.28, f32[8,128]{1,0:T(8,128)} %copy-done.27, f32[8,128]{1,0:T(8,128)} %copy-done.26, f32[32,24576]{1,0:T(8,128)} %get-tuple-element.154.refs_4_, ...), custom_call_target="tpu_custom_call" | custom-call | flops 1 | bytes 1 | tf_op jit(solution)/shard_map/correct/pallas_call | solution.py:492
  167.5 4.3 %all-to-all-start.2 = ((f32[8,32,1920]{2,1,0:T(8,128)}), f32[8,32,1920]{2,1,0:T(8,128)}, u32[]{:S(2)}, u32[]{:S(2)}) async-start(f32[8,32,1920]{2,1,0:T(8,128)} %get-tuple-element.168), calls=%async_computation.2 | async-start | bytes 3932160 | tf_op jit(solution)/shard_map/all_to_all | solution.py:597
  171.8 4.1 %correct.3 = (f32[32,24576]{1,0:T(8,128)}, f32[32,1152]{1,0:T(8,128)}, f32[32,1152]{1,0:T(8,128)}, f32[32,1152]{1,0:T(8,128)}, f32[32,1152]{1,0:T(8,128)}, /*ind...) custom-call(s32[1]{0:T(128)} %bitcast.4.device_ref, ...), custom_call_target="tpu_custom_call", output_to_operand_aliasing={{0}: (9, {})} | custom-call | flops 1 | bytes 1 | tf_op jit(solution)/shard_map/correct/pallas_call | solution.py:492
  176.0 6.4 %gather_blocks.7 = (f32[97,32,128]{2,1,0:T(8,128)}, f32[97,32,128]{2,1,0:T(8,128)}, f32[97,32,128]{2,1,0:T(8,128)}) custom-call(s32[8,256]{1,0:T(8,128)} %positions.5.slots_ref, f32[32,24576]{1,0:T(8,128)} %get-tuple-element.130.v_ref.refs_0_), custom_call_target="tpu_custom_call" | custom-call | flops 1 | bytes 1 | tf_op jit(solution)/shard_map/gather_blocks/pallas_call | solution.py:314
  182.4 1.5 collective-permute-start.26
  183.9 1.5 collective-permute-start.27
  185.4 1.9 collective-permute-start.30
  187.5 2.6 collective-permute-start.32
  190.1 17.8 %collective-permute-done.30.refs_2_ = f32[32,1152]{1,0:T(8,128)S(1)} collective-permute-done((f32[32,1152]{1,0:T(8,128)S(1)}, f32[32,1152]{1,0:T(8,128)S(1)}, u32[]{:S(2)}, u32[]{:S(2)}) %collective-permute-start.30) | collective-permute-done | bytes 147488 | tf_op jit(solution)/shard_map/ppermute | solution.py:602
  207.9 3.6 %collective-permute-start.33 = (f32[32,1152]{1,0:T(8,128)}, f32[32,1152]{1,0:T(8,128)}, u32[]{:S(2)}, u32[]{:S(2)}) collective-permute-start(f32[32,1152]{1,0:T(8,128)} %get-tuple-element.165), channel_id=1, source_target_pairs={{0,20},{4,16},{8,28},{12,24},{16,4},{20,0},{24,12},{28,8},{1,21},{... | collective-permute-start | bytes 442376 | tf_op jit(solution)/shard_map/ppermute | solution.py:602
  211.5 3.3 %collective-permute-start.34 = (f32[32,1152]{1,0:T(8,128)S(1)}, f32[32,1152]{1,0:T(8,128)}, u32[]{:S(2)}, u32[]{:S(2)}) collective-permute-start(f32[32,1152]{1,0:T(8,128)S(1)} %copy-done.33), channel_id=1, source_target_pairs={{0,24},{4,28},{8,16},{12,20},{16,8},{20,12},{24,0},{28,4},{1,25},{... | collective-permute-start | bytes 442376 | tf_op jit(solution)/shard_map/ppermute | solution.py:602
  214.8 4.9 %collective-permute-done.26.refs_5_.refs_2_ = f32[97,32,128]{2,1,0:T(8,128)S(1)} collective-permute-done((f32[97,32,128]{2,1,0:T(8,128)}, f32[97,32,128]{2,1,0:T(8,128)S(1)}, u32[]{:S(2)}, u32[]{:S(2)}) %collective-permute-start.26) | collective-permute-done | bytes 1589280 | tf_op jit(solution)/shard_map/ppermute | solution.py:594
  219.6 2.5 collective-permute-start.35
  222.2 2.5 collective-permute-start.28
  224.7 6.5 %all-to-all-done.2 = f32[8,32,1920]{2,1,0:T(8,128)} async-done(((f32[8,32,1920]{2,1,0:T(8,128)}), f32[8,32,1920]{2,1,0:T(8,128)}, u32[]{:S(2)}, u32[]{:S(2)}) %all-to-all-start.2) | async-done | bytes 1966112 | tf_op jit(solution)/shard_map/all_to_all | solution.py:597
  231.2 7.5 %alpha_sum.6.refs_12_ = f32[256,1920]{1,0:T(8,128)} custom-call(s32[1]{0:T(128)} %bitcast.4.device_ref, s32[2,192]{1,0:T(2,128)} %pairs_ref.7, s32[2,192]{1,0:T(2,128)} %signs_ref.7, f32[256,1920]{1,0:T(8,128)} %bitcast.21.refs_0_, bf16[256,768]{1,0:T(8,128)(2,1)} %get-tuple-element.147.refs_1_.refs_8_, bf16[256,768]{1,0:T(8,128)(2,1)} %get-tuple-element.148.refs_2_.refs_9_, ...), custom_call_target="tpu_custom_call" | custom-call | flops 20000000000 | bytes 66666664 | tf_op jit(solution)/shard_map/alpha_sum/pallas_call | solution.py:200
  238.7 4.6 %all-to-all-start.3 = ((f32[8,32,1920]{2,1,0:T(8,128)}), f32[8,32,1920]{2,1,0:T(8,128)}, u32[]{:S(2)}, u32[]{:S(2)}) async-start(f32[8,32,1920]{2,1,0:T(8,128)} %bitcast.56), calls=%async_computation.3 | async-start | bytes 3932160 | tf_op jit(solution)/shard_map/all_to_all | solution.py:597
  243.3 17.6 %collective-permute-done.28.refs_13_.refs_4_ = f32[97,32,128]{2,1,0:T(8,128)} collective-permute-done((f32[97,32,128]{2,1,0:T(8,128)}, f32[97,32,128]{2,1,0:T(8,128)}, u32[]{:S(2)}, u32[]{:S(2)}) %collective-permute-start.28) | collective-permute-done | bytes 1589280 | tf_op jit(solution)/shard_map/ppermute | solution.py:594
  261.0 6.4 %alpha_sum.7 = (f32[32,1152]{1,0:T(8,128)}, f32[32,1152]{1,0:T(8,128)}, f32[32,1152]{1,0:T(8,128)}, f32[32,1152]{1,0:T(8,128)}, f32[32,1152]{1,0:T(8,128)}, /*in...) custom-call(s32[1]{0:T(128)} %bitcast.4.device_ref, s32[2,192]{1,0:T(2,128)} %pairs_ref.7, ...), custom_call_target="tpu_custom_call" | custom-call | flops 199999995904 | bytes 666666688 | tf_op jit(solution)/shard_map/alpha_sum/pallas_call | solution.py:200
  267.7 14.3 %beta_sum.7 = f32[32,24576]{1,0:T(8,128)} custom-call(s32[2,192]{1,0:T(2,128)} %get-tuple-element.213.slots_ref, s32[2,192]{1,0:T(2,128)} %get-tuple-element.212.sign_ref, s32[2,192]{1,0:T(2,128)S(1)} %bitcast.59, f32[32,24576]{1,0:T(8,128)S(1)} %copy-done.1, f32[4,128,128]{2,1,0:T(8,128)S(1)} %copy-done.4, f32[97,32,128]{2,1,0:T(8,128)} %copy-done.30, ...), custom_call_target="tpu_custom_call" | custom-call | flops 20000000000 | bytes 66666664 | tf_op jit(solution)/shard_map/beta_sum/pallas_call | solution.py:406
  282.1 1.8 collective-permute-start.38
  283.9 2.7 collective-permute-start.40
  287.1 3.0 collective-permute-start.42
  290.1 12.4 %all-to-all-done.3.refs_1_ = f32[8,32,1920]{2,1,0:T(8,128)} async-done(((f32[8,32,1920]{2,1,0:T(8,128)}), f32[8,32,1920]{2,1,0:T(8,128)}, u32[]{:S(2)}, u32[]{:S(2)}) %all-to-all-start.3) | async-done | bytes 1966112 | tf_op jit(solution)/shard_map/all_to_all | solution.py:597
  302.5 3.5 %finish.2.refs_9_ = f32[32,24576]{1,0:T(8,128)} custom-call(s32[1]{0:T(128)} %bitcast.4.device_ref, f32[32,24576]{1,0:T(8,128)} %get-tuple-element.219.refs_0_, f32[8,32,1920]{2,1,0:T(8,128)} %all-to-all-done.3.refs_1_), custom_call_target="tpu_custom_call" | custom-call | flops 20000000000 | bytes 66666664 | tf_op jit(solution)/shard_map/finish/pallas_call | solution.py:570
  306.0 1.7 collective-permute-done.40.refs_6_
  309.1 2.4 finish.3
  (130 shorter events, 10.3 us)
Async XLA Ops:
  3.1 17.8 %copy-start = (f32[32,24576]{1,0:T(8,128)S(1)}, f32[32,24576]{1,0:T(8,128)}, u32[]{:S(2)}) copy-start(f32[32,24576]{1,0:T(8,128)} %refs_5_.3) | copy-start | bytes 9437188
  3.1 61.9 %all-to-all-start = ((f32[8,32,1920]{2,1,0:T(8,128)}), f32[8,32,1920]{2,1,0:T(8,128)}, u32[]{:S(2)}, u32[]{:S(2)}) async-start(f32[8,32,1920]{2,1,0:T(8,128)} %pack.2.refs_0_), calls=%async_computation | async-start | bytes 3932160 | tf_op jit(solution)/shard_map/all_to_all | solution.py:597
  13.3 129.3 %copy-start.5 = (s32[192,2]{1,0:T(8,128)}, s32[192,2]{1,0:T(8,128)S(1)}, u32[]{:S(2)}) copy-start(s32[192,2]{1,0:T(8,128)S(1)} %get-tuple-element.135) | copy-start | bytes 4612
  13.3 3.9 %collective-permute-start.7 = (f32[8,256]{1,0:T(8,128)}, f32[8,256]{1,0:T(8,128)S(1)}, u32[]{:S(2)}, u32[]{:S(2)}) collective-permute-start(f32[8,256]{1,0:T(8,128)} %get-tuple-element.133), channel_id=1, source_target_pairs={{0,2},{1,3},{2,0},{3,1},{4,6},{5,7},{6,4},{7,5},{8,10},{9,11},{10,... | collective-permute-start | bytes 24584 | tf_op jit(solution)/shard_map/ppermute | solution.py:594
  14.9 4.8 %collective-permute-start.8 = (f32[8,256]{1,0:T(8,128)}, f32[8,256]{1,0:T(8,128)S(1)}, u32[]{:S(2)}, u32[]{:S(2)}) collective-permute-start(f32[8,256]{1,0:T(8,128)} %get-tuple-element.134), channel_id=1, source_target_pairs={{0,3},{1,2},{2,1},{3,0},{4,7},{5,6},{6,5},{7,4},{8,11},{9,10},{10,... | collective-permute-start | bytes 24584 | tf_op jit(solution)/shard_map/ppermute | solution.py:594
  16.3 3.9 %collective-permute-start.6 = (f32[8,256]{1,0:T(8,128)}, f32[8,256]{1,0:T(8,128)S(1)}, u32[]{:S(2)}, u32[]{:S(2)}) collective-permute-start(f32[8,256]{1,0:T(8,128)} %get-tuple-element.132), channel_id=1, source_target_pairs={{0,1},{1,0},{2,3},{3,2},{4,5},{5,4},{6,7},{7,6},{8,9},{9,8},{10,11... | collective-permute-start | bytes 24584 | tf_op jit(solution)/shard_map/ppermute | solution.py:594
  17.3 125.4 %copy-start.13 = (f32[8,256]{1,0:T(8,128)}, f32[8,256]{1,0:T(8,128)S(1)}, u32[]{:S(2)}) copy-start(f32[8,256]{1,0:T(8,128)S(1)} %collective-permute-done.7.refs_1_) | copy-start | bytes 24580
  19.7 123.0 %copy-start.15 = (f32[8,256]{1,0:T(8,128)}, f32[8,256]{1,0:T(8,128)S(1)}, u32[]{:S(2)}) copy-start(f32[8,256]{1,0:T(8,128)S(1)} %collective-permute-done.8.refs_2_) | copy-start | bytes 24580
  20.2 122.5 %copy-start.17 = (f32[8,256]{1,0:T(8,128)}, f32[8,256]{1,0:T(8,128)S(1)}, u32[]{:S(2)}) copy-start(f32[8,256]{1,0:T(8,128)S(1)} %collective-permute-done.6.refs_0_) | copy-start | bytes 24580
  25.4 36.2 %collective-permute-start.9 = (f32[97,32,128]{2,1,0:T(8,128)}, f32[97,32,128]{2,1,0:T(8,128)}, u32[]{:S(2)}, u32[]{:S(2)}) collective-permute-start(f32[97,32,128]{2,1,0:T(8,128)} %get-tuple-element.136), channel_id=1, source_target_pairs={{0,1},{1,0},{2,3},{3,2},{4,5},{5,4},{6,7},{7,6},{8,9},{9,8},{10,11... | collective-permute-start | bytes 4767752 | tf_op jit(solution)/shard_map/ppermute | solution.py:594
  26.3 38.7 %collective-permute-start.10 = (f32[97,32,128]{2,1,0:T(8,128)}, f32[97,32,128]{2,1,0:T(8,128)}, u32[]{:S(2)}, u32[]{:S(2)}) collective-permute-start(f32[97,32,128]{2,1,0:T(8,128)} %get-tuple-element.137), channel_id=1, source_target_pairs={{0,2},{1,3},{2,0},{3,1},{4,6},{5,7},{6,4},{7,5},{8,10},{9,11},{10,... | collective-permute-start | bytes 4767752 | tf_op jit(solution)/shard_map/ppermute | solution.py:594
  29.0 4.5 %collective-permute-start.12 = (f32[32,1152]{1,0:T(8,128)}, f32[32,1152]{1,0:T(8,128)}, u32[]{:S(2)}, u32[]{:S(2)}) collective-permute-start(f32[32,1152]{1,0:T(8,128)} %get-tuple-element.140), channel_id=1, source_target_pairs={{0,4},{4,0},{8,12},{12,8},{16,20},{20,16},{24,28},{28,24},{1,5},{5... | collective-permute-start | bytes 442376 | tf_op jit(solution)/shard_map/ppermute | solution.py:602
  29.0 16.9 %collective-permute-start.13 = (f32[32,1152]{1,0:T(8,128)}, f32[32,1152]{1,0:T(8,128)}, u32[]{:S(2)}, u32[]{:S(2)}) collective-permute-start(f32[32,1152]{1,0:T(8,128)} %get-tuple-element.141), channel_id=1, source_target_pairs={{0,8},{4,12},{8,0},{12,4},{16,24},{20,28},{24,16},{28,20},{1,9},{5... | collective-permute-start | bytes 442376 | tf_op jit(solution)/shard_map/ppermute | solution.py:602
  31.1 41.3 %collective-permute-start.14 = (f32[32,1152]{1,0:T(8,128)}, f32[32,1152]{1,0:T(8,128)}, u32[]{:S(2)}, u32[]{:S(2)}) collective-permute-start(f32[32,1152]{1,0:T(8,128)} %get-tuple-element.142), channel_id=1, source_target_pairs={{0,12},{4,8},{8,4},{12,0},{16,28},{20,24},{24,20},{28,16},{1,13},{... | collective-permute-start | bytes 442376 | tf_op jit(solution)/shard_map/ppermute | solution.py:602
  33.4 39.0 %collective-permute-start.15 = (f32[32,1152]{1,0:T(8,128)}, f32[32,1152]{1,0:T(8,128)}, u32[]{:S(2)}, u32[]{:S(2)}) collective-permute-start(f32[32,1152]{1,0:T(8,128)} %get-tuple-element.143), channel_id=1, source_target_pairs={{0,16},{4,20},{8,24},{12,28},{16,0},{20,4},{24,8},{28,12},{1,17},{... | collective-permute-start | bytes 442376 | tf_op jit(solution)/shard_map/ppermute | solution.py:602
  45.9 28.7 %collective-permute-start.16 = (f32[32,1152]{1,0:T(8,128)}, f32[32,1152]{1,0:T(8,128)}, u32[]{:S(2)}, u32[]{:S(2)}) collective-permute-start(f32[32,1152]{1,0:T(8,128)} %get-tuple-element.144), channel_id=1, source_target_pairs={{0,20},{4,16},{8,28},{12,24},{16,4},{20,0},{24,12},{28,8},{1,21},{... | collective-permute-start | bytes 442376 | tf_op jit(solution)/shard_map/ppermute | solution.py:602
  61.5 13.1 %collective-permute-start.17 = (f32[32,1152]{1,0:T(8,128)}, f32[32,1152]{1,0:T(8,128)}, u32[]{:S(2)}, u32[]{:S(2)}) collective-permute-start(f32[32,1152]{1,0:T(8,128)} %get-tuple-element.145), channel_id=1, source_target_pairs={{0,24},{4,28},{8,16},{12,20},{16,8},{20,12},{24,0},{28,4},{1,25},{... | collective-permute-start | bytes 442376 | tf_op jit(solution)/shard_map/ppermute | solution.py:602
  65.0 9.6 %collective-permute-start.18 = (f32[32,1152]{1,0:T(8,128)}, f32[32,1152]{1,0:T(8,128)}, u32[]{:S(2)}, u32[]{:S(2)}) collective-permute-start(f32[32,1152]{1,0:T(8,128)} %get-tuple-element.146), channel_id=1, source_target_pairs={{0,28},{4,24},{8,20},{12,16},{16,12},{20,8},{24,4},{28,0},{1,29},{... | collective-permute-start | bytes 442376 | tf_op jit(solution)/shard_map/ppermute | solution.py:602
  80.7 12.1 %copy-start.22 = (s32[192,2]{0,1:T(2,128)S(1)}, s32[192,2]{0,1:T(2,128)}, u32[]{:S(2)}) copy-start(s32[192,2]{0,1:T(2,128)} %param.21) | copy-start | bytes 4612
  80.7 80.4 %all-to-all-start.1 = ((f32[8,32,3072]{2,1,0:T(8,128)}), f32[8,32,3072]{2,1,0:T(8,128)}, u32[]{:S(2)}, u32[]{:S(2)}) async-start(f32[8,32,3072]{2,1,0:T(8,128)} %bitcast.54), calls=%async_computation.1 | async-start | bytes 6291456 | tf_op jit(solution)/shard_map/all_to_all | solution.py:597
  89.1 38.4 %collective-permute-start.11 = (f32[97,32,128]{2,1,0:T(8,128)}, f32[97,32,128]{2,1,0:T(8,128)}, u32[]{:S(2)}, u32[]{:S(2)}) collective-permute-start(f32[97,32,128]{2,1,0:T(8,128)} %get-tuple-element.138), channel_id=1, source_target_pairs={{0,3},{1,2},{2,1},{3,0},{4,7},{5,6},{6,5},{7,4},{8,11},{9,10},{10,... | collective-permute-start | bytes 4767752 | tf_op jit(solution)/shard_map/ppermute | solution.py:594
  101.4 26.0 %copy-start.24 = (s32[192,2]{0,1:T(2,128)S(1)}, s32[192,2]{0,1:T(2,128)}, u32[]{:S(2)}) copy-start(s32[192,2]{0,1:T(2,128)} %param.20) | copy-start | bytes 4612
  142.9 4.6 %collective-permute-start.21 = (f32[8,128]{1,0:T(8,128)S(1)}, f32[8,128]{1,0:T(8,128)S(1)}, u32[]{:S(2)}, u32[]{:S(2)}) collective-permute-start(f32[8,128]{1,0:T(8,128)S(1)} %get-tuple-element.153), channel_id=1, source_target_pairs={{0,3},{1,2},{2,1},{3,0},{4,7},{5,6},{6,5},{7,4},{8,11},{9,10},{10,... | collective-permute-start | bytes 12296 | tf_op jit(solution)/shard_map/ppermute | solution.py:594
  145.4 3.6 %collective-permute-start.20 = (f32[8,128]{1,0:T(8,128)S(1)}, f32[8,128]{1,0:T(8,128)S(1)}, u32[]{:S(2)}, u32[]{:S(2)}) collective-permute-start(f32[8,128]{1,0:T(8,128)S(1)} %get-tuple-element.153), channel_id=1, source_target_pairs={{0,2},{1,3},{2,0},{3,1},{4,6},{5,7},{6,4},{7,5},{8,10},{9,11},{10,... | collective-permute-start | bytes 12296 | tf_op jit(solution)/shard_map/ppermute | solution.py:594
  145.9 3.6 %collective-permute-start.19 = (f32[8,128]{1,0:T(8,128)S(1)}, f32[8,128]{1,0:T(8,128)S(1)}, u32[]{:S(2)}, u32[]{:S(2)}) collective-permute-start(f32[8,128]{1,0:T(8,128)S(1)} %get-tuple-element.153), channel_id=1, source_target_pairs={{0,1},{1,0},{2,3},{3,2},{4,5},{5,4},{6,7},{7,6},{8,9},{9,8},{10,11... | collective-permute-start | bytes 12296 | tf_op jit(solution)/shard_map/ppermute | solution.py:594
  149.5 1.2 collective-permute-start.22
  150.7 10.4 %copy-start.19 = (f32[8,128]{1,0:T(8,128)}, f32[8,128]{1,0:T(8,128)S(1)}, u32[]{:S(2)}) copy-start(f32[8,128]{1,0:T(8,128)S(1)} %add.168.refs_0_) | copy-start | bytes 12292
  150.7 4.8 %collective-permute-start.25 = (f32[8,128]{1,0:T(8,128)S(1)}, f32[8,128]{1,0:T(8,128)S(1)}, u32[]{:S(2)}, u32[]{:S(2)}) collective-permute-start(f32[8,128]{1,0:T(8,128)S(1)} %add.168.refs_0_), channel_id=1, source_target_pairs={{0,24},{4,28},{8,0},{12,4},{16,8},{20,12},{24,16},{28,20},{1,25},{... | collective-permute-start | bytes 12296 | tf_op jit(solution)/shard_map/ppermute | solution.py:691
  154.1 7.0 %collective-permute-start.24 = (f32[8,128]{1,0:T(8,128)S(1)}, f32[8,128]{1,0:T(8,128)S(1)}, u32[]{:S(2)}, u32[]{:S(2)}) collective-permute-start(f32[8,128]{1,0:T(8,128)S(1)} %add.168.refs_0_), channel_id=1, source_target_pairs={{0,16},{4,20},{8,24},{12,28},{16,0},{20,4},{24,8},{28,12},{1,17},{... | collective-permute-start | bytes 12296 | tf_op jit(solution)/shard_map/ppermute | solution.py:691
  154.9 6.2 %collective-permute-start.23 = (f32[8,128]{1,0:T(8,128)S(1)}, f32[8,128]{1,0:T(8,128)S(1)}, u32[]{:S(2)}, u32[]{:S(2)}) collective-permute-start(f32[8,128]{1,0:T(8,128)S(1)} %add.168.refs_0_), channel_id=1, source_target_pairs={{0,8},{4,12},{8,16},{12,20},{16,24},{20,28},{24,0},{28,4},{1,9},{5... | collective-permute-start | bytes 12296 | tf_op jit(solution)/shard_map/ppermute | solution.py:691
  167.5 63.7 %all-to-all-start.2 = ((f32[8,32,1920]{2,1,0:T(8,128)}), f32[8,32,1920]{2,1,0:T(8,128)}, u32[]{:S(2)}, u32[]{:S(2)}) async-start(f32[8,32,1920]{2,1,0:T(8,128)} %get-tuple-element.168), calls=%async_computation.2 | async-start | bytes 3932160 | tf_op jit(solution)/shard_map/all_to_all | solution.py:597
  176.0 9.5 %copy-start.39 = (f32[32,1152]{1,0:T(8,128)S(1)}, f32[32,1152]{1,0:T(8,128)}, u32[]{:S(2)}) copy-start(f32[32,1152]{1,0:T(8,128)} %get-tuple-element.161) | copy-start | bytes 442372
  176.0 9.5 %copy-start.38 = (f32[32,1152]{1,0:T(8,128)S(1)}, f32[32,1152]{1,0:T(8,128)}, u32[]{:S(2)}) copy-start(f32[32,1152]{1,0:T(8,128)} %get-tuple-element.162) | copy-start | bytes 442372
  176.0 11.4 %copy-start.37 = (f32[32,1152]{1,0:T(8,128)S(1)}, f32[32,1152]{1,0:T(8,128)}, u32[]{:S(2)}) copy-start(f32[32,1152]{1,0:T(8,128)} %get-tuple-element.163) | copy-start | bytes 442372
  176.0 35.5 %copy-start.33 = (f32[32,1152]{1,0:T(8,128)S(1)}, f32[32,1152]{1,0:T(8,128)}, u32[]{:S(2)}) copy-start(f32[32,1152]{1,0:T(8,128)} %get-tuple-element.166) | copy-start | bytes 442372
  176.0 43.6 %copy-start.32 = (f32[32,1152]{1,0:T(8,128)S(1)}, f32[32,1152]{1,0:T(8,128)}, u32[]{:S(2)}) copy-start(f32[32,1152]{1,0:T(8,128)} %get-tuple-element.167) | copy-start | bytes 442372
  182.4 37.2 %collective-permute-start.26 = (f32[97,32,128]{2,1,0:T(8,128)}, f32[97,32,128]{2,1,0:T(8,128)S(1)}, u32[]{:S(2)}, u32[]{:S(2)}) collective-permute-start(f32[97,32,128]{2,1,0:T(8,128)} %get-tuple-element.157), channel_id=1, source_target_pairs={{0,1},{1,0},{2,3},{3,2},{4,5},{5,4},{6,7},{7,6},{8,9},{9,8},{10,11... | collective-permute-start | bytes 4767752 | tf_op jit(solution)/shard_map/ppermute | solution.py:594
  183.9 38.3 %collective-permute-start.27 = (f32[97,32,128]{2,1,0:T(8,128)}, f32[97,32,128]{2,1,0:T(8,128)S(1)}, u32[]{:S(2)}, u32[]{:S(2)}) collective-permute-start(f32[97,32,128]{2,1,0:T(8,128)} %get-tuple-element.158), channel_id=1, source_target_pairs={{0,2},{1,3},{2,0},{3,1},{4,6},{5,7},{6,4},{7,5},{8,10},{9,11},{10,... | collective-permute-start | bytes 4767752 | tf_op jit(solution)/shard_map/ppermute | solution.py:594
  185.4 2.1 collective-permute-start.29
  185.4 22.5 %collective-permute-start.30 = (f32[32,1152]{1,0:T(8,128)S(1)}, f32[32,1152]{1,0:T(8,128)S(1)}, u32[]{:S(2)}, u32[]{:S(2)}) collective-permute-start(f32[32,1152]{1,0:T(8,128)S(1)} %copy-done.38), channel_id=1, source_target_pairs={{0,8},{4,12},{8,0},{12,4},{16,24},{20,28},{24,16},{28,20},{1,9},{5... | collective-permute-start | bytes 442376 | tf_op jit(solution)/shard_map/ppermute | solution.py:602
  187.4 24.1 %collective-permute-start.31 = (f32[32,1152]{1,0:T(8,128)S(1)}, f32[32,1152]{1,0:T(8,128)S(1)}, u32[]{:S(2)}, u32[]{:S(2)}) collective-permute-start(f32[32,1152]{1,0:T(8,128)S(1)} %copy-done.37), channel_id=1, source_target_pairs={{0,12},{4,8},{8,4},{12,0},{16,28},{20,24},{24,20},{28,16},{1,13},{... | collective-permute-start | bytes 442376 | tf_op jit(solution)/shard_map/ppermute | solution.py:602
  187.5 34.7 %copy-start.34 = (f32[32,1152]{1,0:T(8,128)}, f32[32,1152]{1,0:T(8,128)S(1)}, u32[]{:S(2)}) copy-start(f32[32,1152]{1,0:T(8,128)S(1)} %collective-permute-done.29.refs_1_) | copy-start | bytes 442372
  187.5 55.8 %collective-permute-start.32 = (f32[32,1152]{1,0:T(8,128)}, f32[32,1152]{1,0:T(8,128)}, u32[]{:S(2)}, u32[]{:S(2)}) collective-permute-start(f32[32,1152]{1,0:T(8,128)} %get-tuple-element.164), channel_id=1, source_target_pairs={{0,16},{4,20},{8,24},{12,28},{16,0},{20,4},{24,8},{28,12},{1,17},{... | collective-permute-start | bytes 442376 | tf_op jit(solution)/shard_map/ppermute | solution.py:602
  207.9 14.3 %copy-start.35 = (f32[32,1152]{1,0:T(8,128)}, f32[32,1152]{1,0:T(8,128)S(1)}, u32[]{:S(2)}) copy-start(f32[32,1152]{1,0:T(8,128)S(1)} %collective-permute-done.30.refs_2_) | copy-start | bytes 442372
  207.9 35.4 %collective-permute-start.33 = (f32[32,1152]{1,0:T(8,128)}, f32[32,1152]{1,0:T(8,128)}, u32[]{:S(2)}, u32[]{:S(2)}) collective-permute-start(f32[32,1152]{1,0:T(8,128)} %get-tuple-element.165), channel_id=1, source_target_pairs={{0,20},{4,16},{8,28},{12,24},{16,4},{20,0},{24,12},{28,8},{1,21},{... | collective-permute-start | bytes 442376 | tf_op jit(solution)/shard_map/ppermute | solution.py:602
  211.5 10.7 %copy-start.36 = (f32[32,1152]{1,0:T(8,128)}, f32[32,1152]{1,0:T(8,128)S(1)}, u32[]{:S(2)}) copy-start(f32[32,1152]{1,0:T(8,128)S(1)} %collective-permute-done.31.refs_3_) | copy-start | bytes 442372
  211.5 31.8 %collective-permute-start.34 = (f32[32,1152]{1,0:T(8,128)S(1)}, f32[32,1152]{1,0:T(8,128)}, u32[]{:S(2)}, u32[]{:S(2)}) collective-permute-start(f32[32,1152]{1,0:T(8,128)S(1)} %copy-done.33), channel_id=1, source_target_pairs={{0,24},{4,28},{8,16},{12,20},{16,8},{20,12},{24,0},{28,4},{1,25},{... | collective-permute-start | bytes 442376 | tf_op jit(solution)/shard_map/ppermute | solution.py:602
  219.6 11.6 %copy-start.30 = (f32[97,32,128]{2,1,0:T(8,128)}, f32[97,32,128]{2,1,0:T(8,128)S(1)}, u32[]{:S(2)}) copy-start(f32[97,32,128]{2,1,0:T(8,128)S(1)} %collective-permute-done.26.refs_5_.refs_2_) | copy-start | bytes 4767748
  219.6 23.7 %collective-permute-start.35 = (f32[32,1152]{1,0:T(8,128)S(1)}, f32[32,1152]{1,0:T(8,128)}, u32[]{:S(2)}, u32[]{:S(2)}) collective-permute-start(f32[32,1152]{1,0:T(8,128)S(1)} %copy-done.32), channel_id=1, source_target_pairs={{0,28},{4,24},{8,20},{12,16},{16,12},{20,8},{24,4},{28,0},{1,29},{... | collective-permute-start | bytes 442376 | tf_op jit(solution)/shard_map/ppermute | solution.py:602
  222.2 38.8 %collective-permute-start.28 = (f32[97,32,128]{2,1,0:T(8,128)}, f32[97,32,128]{2,1,0:T(8,128)}, u32[]{:S(2)}, u32[]{:S(2)}) collective-permute-start(f32[97,32,128]{2,1,0:T(8,128)} %get-tuple-element.159), channel_id=1, source_target_pairs={{0,3},{1,2},{2,1},{3,0},{4,7},{5,6},{6,5},{7,4},{8,11},{9,10},{10,... | collective-permute-start | bytes 4767752 | tf_op jit(solution)/shard_map/ppermute | solution.py:594
  238.7 63.8 %all-to-all-start.3 = ((f32[8,32,1920]{2,1,0:T(8,128)}), f32[8,32,1920]{2,1,0:T(8,128)}, u32[]{:S(2)}, u32[]{:S(2)}) async-start(f32[8,32,1920]{2,1,0:T(8,128)} %bitcast.56), calls=%async_computation.3 | async-start | bytes 3932160 | tf_op jit(solution)/shard_map/all_to_all | solution.py:597
  267.4 19.2 %collective-permute-start.36 = (f32[32,1152]{1,0:T(8,128)}, f32[32,1152]{1,0:T(8,128)}, u32[]{:S(2)}, u32[]{:S(2)}) collective-permute-start(f32[32,1152]{1,0:T(8,128)} %get-tuple-element.170), channel_id=1, source_target_pairs={{0,4},{4,0},{8,12},{12,8},{16,20},{20,16},{24,28},{28,24},{1,5},{5... | collective-permute-start | bytes 442376 | tf_op jit(solution)/shard_map/ppermute | solution.py:602
  267.6 19.5 %collective-permute-start.37 = (f32[32,1152]{1,0:T(8,128)}, f32[32,1152]{1,0:T(8,128)}, u32[]{:S(2)}, u32[]{:S(2)}) collective-permute-start(f32[32,1152]{1,0:T(8,128)} %get-tuple-element.171), channel_id=1, source_target_pairs={{0,8},{4,12},{8,0},{12,4},{16,24},{20,28},{24,16},{28,20},{1,9},{5... | collective-permute-start | bytes 442376 | tf_op jit(solution)/shard_map/ppermute | solution.py:602
  267.6 14.4 %copy-start.6 = (s32[192,2]{1,0:T(8,128)S(1)}, s32[192,2]{1,0:T(8,128)}, u32[]{:S(2)}) copy-start(s32[192,2]{1,0:T(8,128)} %copy-done.5) | copy-start | bytes 4612
  267.6 14.4 %copy-start.14 = (f32[8,256]{1,0:T(8,128)S(1)}, f32[8,256]{1,0:T(8,128)}, u32[]{:S(2)}) copy-start(f32[8,256]{1,0:T(8,128)} %copy-done.13) | copy-start | bytes 24580
  267.6 14.4 %copy-start.16 = (f32[8,256]{1,0:T(8,128)S(1)}, f32[8,256]{1,0:T(8,128)}, u32[]{:S(2)}) copy-start(f32[8,256]{1,0:T(8,128)} %copy-done.15) | copy-start | bytes 24580
  267.6 14.4 %copy-start.18 = (f32[8,256]{1,0:T(8,128)S(1)}, f32[8,256]{1,0:T(8,128)}, u32[]{:S(2)}) copy-start(f32[8,256]{1,0:T(8,128)} %copy-done.17) | copy-start | bytes 24580
  267.7 14.4 %copy-start.21 = (s32[192,2]{0,1:T(2,128)S(1)}, s32[192,2]{0,1:T(2,128)}, u32[]{:S(2)}) copy-start(s32[192,2]{0,1:T(2,128)} %param.19) | copy-start | bytes 4612
  267.7 14.4 %copy-start.23 = (s32[192,2]{0,1:T(2,128)S(1)}, s32[192,2]{0,1:T(2,128)}, u32[]{:S(2)}) copy-start(s32[192,2]{0,1:T(2,128)} %param.21) | copy-start | bytes 4612
  282.1 23.9 %collective-permute-start.38 = (f32[32,1152]{1,0:T(8,128)}, f32[32,1152]{1,0:T(8,128)S(1)}, u32[]{:S(2)}, u32[]{:S(2)}) collective-permute-start(f32[32,1152]{1,0:T(8,128)} %get-tuple-element.172), channel_id=1, source_target_pairs={{0,12},{4,8},{8,4},{12,0},{16,28},{20,24},{24,20},{28,16},{1,13},{... | collective-permute-start | bytes 442376 | tf_op jit(solution)/shard_map/ppermute | solution.py:602
  283.9 22.1 %collective-permute-start.39 = (f32[32,1152]{1,0:T(8,128)}, f32[32,1152]{1,0:T(8,128)S(1)}, u32[]{:S(2)}, u32[]{:S(2)}) collective-permute-start(f32[32,1152]{1,0:T(8,128)} %get-tuple-element.173), channel_id=1, source_target_pairs={{0,16},{4,20},{8,24},{12,28},{16,0},{20,4},{24,8},{28,12},{1,17},{... | collective-permute-start | bytes 442376 | tf_op jit(solution)/shard_map/ppermute | solution.py:602
  283.9 23.8 %collective-permute-start.40 = (f32[32,1152]{1,0:T(8,128)}, f32[32,1152]{1,0:T(8,128)S(1)}, u32[]{:S(2)}, u32[]{:S(2)}) collective-permute-start(f32[32,1152]{1,0:T(8,128)} %get-tuple-element.174), channel_id=1, source_target_pairs={{0,20},{4,16},{8,28},{12,24},{16,4},{20,0},{24,12},{28,8},{1,21},{... | collective-permute-start | bytes 442376 | tf_op jit(solution)/shard_map/ppermute | solution.py:602
  286.6 21.2 %collective-permute-start.41 = (f32[32,1152]{1,0:T(8,128)}, f32[32,1152]{1,0:T(8,128)S(1)}, u32[]{:S(2)}, u32[]{:S(2)}) collective-permute-start(f32[32,1152]{1,0:T(8,128)} %get-tuple-element.175), channel_id=1, source_target_pairs={{0,24},{4,28},{8,16},{12,20},{16,8},{20,12},{24,0},{28,4},{1,25},{... | collective-permute-start | bytes 442376 | tf_op jit(solution)/shard_map/ppermute | solution.py:602
  287.1 20.7 %collective-permute-start.42 = (f32[32,1152]{1,0:T(8,128)}, f32[32,1152]{1,0:T(8,128)S(1)}, u32[]{:S(2)}, u32[]{:S(2)}) collective-permute-start(f32[32,1152]{1,0:T(8,128)} %get-tuple-element.176), channel_id=1, source_target_pairs={{0,28},{4,24},{8,20},{12,16},{16,12},{20,8},{24,4},{28,0},{1,29},{... | collective-permute-start | bytes 442376 | tf_op jit(solution)/shard_map/ppermute | solution.py:602
  (16 other events, 62.4 us)
